TPU v7x, 32 devices: a whole 2x2x4 slice. The times are simulated.
32 devices in a mesh: dp: 8 (over y, x, core), ctx: 4 (over z).
Axes of the slice: x: 2, y: 2, z: 4, core: 2. Of those that a mesh axis runs over, the one named last changes fastest.
Arguments:
- tokens: bfloat16 [16, 1024, 768], P('dp', 'ctx'), may hold values from -6 to 6
- segment_ids: int32 [16, 1024], P('dp', 'ctx'), may hold values from 0 to 2, as said below
- prompt_slots: int32 [16, 1024], P('dp', 'ctx'), may hold values from -1 to 99, as said below
- cotangent: bfloat16 [16, 1024, 768], P('dp', 'ctx'), may hold values from -6 to 6
- w_query: bfloat16 [768, 768], replicated, may hold values from -0.0390625 to 0.0390625
- w_key: bfloat16 [768, 768], replicated, may hold values from -0.21875 to 0.21875
- w_value: bfloat16 [768, 768], replicated, may hold values from -0.21875 to 0.21875
- w_output: bfloat16 [768, 768], replicated, may hold values from -0.4375 to 0.4375
- w_inner: bfloat16 [768, 3072], replicated, may hold values from -0.21875 to 0.21875
- w_outer: bfloat16 [3072, 768], replicated, may hold values from -0.15625 to 0.15625
- gain_first: float32 [768], replicated, may hold values from 0.1 to 1.9
- gain_second: float32 [768], replicated, may hold values from 0.1 to 1.9
- bias_table: float32 [32, 12], replicated, may hold values from -4 to 4
- prompt: float32 [128, 768], P('dp', 'ctx'), may hold values from -6 to 6
- first_moment: float32 [128, 768], P('dp', 'ctx'), may hold values from -2 to 2
- second_moment: float32 [128, 768], P('dp', 'ctx'), may hold values from 0.0005 to 0.005
Outputs:
- output: bfloat16 [16, 1024, 768], P('dp', 'ctx')
- prompt_new: float32 [128, 768], P('dp', 'ctx')
- first_new: float32 [128, 768], P('dp', 'ctx')
- second_new: float32 [128, 768], P('dp', 'ctx')
Inputs may be any that keep to these rules, and one draw needn't show every extreme that they name: `segment_ids`: within a row the numbers never fall; each row holds 3 segments of at least 101 positions each, filling the row. `prompt_slots`: the first 100 positions of each segment hold 0 to 99 in order; all other positions hold -1.
All inputs are finite; a program needn't handle non-finite values.
Results may differ from a plain program's by a relative error of at most 0.015.
The roundings to bfloat16 on the way count: a program that leaves them out, or rounds other values in their place, can miss the bound.
Values may be sent and summed in bfloat16 or wider, within the bound.
No kernel may reach another device: no remote copies, remote signals or barrier semaphores. Data moves between devices by JAX's collectives and lax.ppermute only.
A program may use at most 192 MiB of HBM per device.

v0:
```python
import jax
import jax.numpy as jnp
from jax import lax
from jax.sharding import PartitionSpec as P

D = 768
PROMPT = 100


highest = lax.Precision.HIGHEST
norm_eps = 1e-06
beta_first = 0.9
beta_second = 0.999
adam_eps = 1e-08
learn_rate = 0.1
first_fix = 1.0 - 0.9**8
second_fix = 1.0 - 0.999**8
far_marks = (12, 16, 23, 32, 46, 64, 91)


def bucket_ids(offset):
    distance = jnp.abs(offset)
    passed = sum(((distance >= boundary).astype(jnp.int32) for boundary in far_marks))
    far_ids = jnp.minimum(8 + passed, 15)
    return jnp.where(distance < 8, distance, far_ids) + 16 * (offset > 0).astype(jnp.int32)


def rms_norm(values, gain_vector):
    return (
        values
        * lax.rsqrt(jnp.mean(values * values, axis=-1, keepdims=True) + norm_eps)
        * gain_vector
    )


def norm_back(values, gain_vector, grad_in):
    pull_back = jax.vjp(lambda inputs: rms_norm(inputs, gain_vector), values)[1]
    return pull_back(grad_in)[0]


def bias_block(bias_table, query_places, key_places):
    buckets = bucket_ids(key_places[None, :] - query_places[:, None])
    choose = (buckets[:, :, None] == jnp.arange(bias_table.shape[0], dtype=jnp.int32)).astype(
        jnp.float32
    )
    return jnp.einsum("qkb,bh->hqk", choose, bias_table, precision=highest)


def split_heads(values, head_count):
    return values.reshape(values.shape[0], head_count, -1)


def score_rows(query_heads, key_heads, score_bias, same_row):
    scores = (
        jnp.einsum("qhd,khd->hqk", query_heads, key_heads, preferred_element_type=jnp.float32)
        + score_bias
    )
    return jnp.where(same_row[None], scores, -1000000000.0)


def pair_terms(
    query_row, key_row, value_row, grad_row, same_row, log_total, score_bias, head_count, inner_sum
):
    query_heads = split_heads(query_row, head_count)
    key_heads = split_heads(key_row, head_count)
    value_heads = split_heads(value_row, head_count)
    grad_heads = split_heads(grad_row, head_count)
    scores = score_rows(query_heads, key_heads, score_bias, same_row)
    soft_probs = jnp.exp(scores - log_total[..., None])
    grad_probs = jnp.einsum(
        "qhd,khd->hqk", grad_heads, value_heads, preferred_element_type=jnp.float32
    )
    inner_sum = jnp.sum(soft_probs * grad_probs, axis=-1)
    grad_scores = (soft_probs * (grad_probs - inner_sum[..., None])).astype(jnp.bfloat16)
    return (query_heads, key_heads, grad_heads, soft_probs, grad_scores, inner_sum)


def on_device(
    tokens,
    segment_ids,
    prompt_slots,
    cotangent,
    w_query,
    w_key,
    w_value,
    w_output,
    w_inner,
    w_outer,
    gain_first,
    gain_second,
    bias_table,
    prompt,
    first_moment,
    second_moment,
):
    row_count, local_len, model_width = tokens.shape
    head_count = bias_table.shape[1]
    seq_len = local_len * lax.axis_size("ctx")
    pad_rows = prompt.shape[0] * lax.axis_size("dp")
    column_part = lax.all_gather(prompt.astype(jnp.bfloat16), "ctx", axis=1, tiled=True)
    sent_prompt = lax.all_gather(column_part, "dp", axis=0, tiled=True)
    flat_slots = prompt_slots.reshape(-1)
    choose = (flat_slots[:, None] == jnp.arange(pad_rows, dtype=jnp.int32)[None, :]).astype(
        jnp.bfloat16
    )
    picked = jnp.dot(choose, sent_prompt, preferred_element_type=jnp.float32)
    hidden = jnp.where(
        (flat_slots >= 0)[:, None], picked, tokens.reshape(-1, model_width).astype(jnp.float32)
    )
    normed_low = rms_norm(hidden, gain_first).astype(jnp.bfloat16)
    query_all = jnp.dot(normed_low, w_query, preferred_element_type=jnp.float32).astype(
        jnp.bfloat16
    )
    key_all = jnp.dot(normed_low, w_key, preferred_element_type=jnp.float32).astype(jnp.bfloat16)
    value_all = jnp.dot(normed_low, w_value, preferred_element_type=jnp.float32).astype(
        jnp.bfloat16
    )
    query_rows = query_all.reshape(row_count, local_len, model_width)
    key_local = key_all.reshape(row_count, local_len, model_width)
    value_local = value_all.reshape(row_count, local_len, model_width)
    seg_low = segment_ids.astype(jnp.bfloat16)
    key_rows, value_rows, seg_rows = (
        lax.all_gather(key_local, "ctx", axis=1, tiled=True),
        lax.all_gather(value_local, "ctx", axis=1, tiled=True),
        lax.all_gather(seg_low, "ctx", axis=1, tiled=True),
    )
    query_places = lax.axis_index("ctx") * local_len + jnp.arange(local_len, dtype=jnp.int32)
    key_places = jnp.arange(seq_len, dtype=jnp.int32)
    score_bias = bias_block(bias_table, query_places, key_places)
    same_rows = seg_low[:, :, None] == seg_rows[:, None, :]

    def attend_row(row_items):
        query_row, key_row, value_row, same_row = row_items
        scores = score_rows(
            split_heads(query_row, head_count),
            split_heads(key_row, head_count),
            score_bias,
            same_row,
        )
        largest = jnp.max(scores, axis=-1, keepdims=True)
        raised = jnp.exp(scores - largest)
        denominator = jnp.sum(raised, axis=-1, keepdims=True)
        soft_weights = (raised / denominator).astype(jnp.bfloat16)
        log_total = largest[..., 0] + jnp.log(denominator[..., 0])
        mixed_heads = jnp.einsum(
            "hqk,khd->qhd",
            soft_weights,
            split_heads(value_row, head_count),
            preferred_element_type=jnp.float32,
        )
        return (mixed_heads.reshape(local_len, model_width).astype(jnp.bfloat16), log_total)

    mixed_rows, log_totals = lax.map(attend_row, (query_rows, key_rows, value_rows, same_rows))
    attended = jnp.dot(
        mixed_rows.reshape(-1, model_width), w_output, preferred_element_type=jnp.float32
    )
    after_attn = hidden + attended
    normed_second = rms_norm(after_attn, gain_second).astype(jnp.bfloat16)
    inner_pre = jnp.dot(normed_second, w_inner, preferred_element_type=jnp.float32)
    activated = jax.nn.relu(inner_pre).astype(jnp.bfloat16)
    outer_out = jnp.dot(activated, w_outer, preferred_element_type=jnp.float32)
    output = (
        (after_attn + outer_out).astype(jnp.bfloat16).reshape(row_count, local_len, model_width)
    )
    cot_flat = cotangent.reshape(-1, model_width)
    grad_activated = jnp.dot(cot_flat, w_outer.T, preferred_element_type=jnp.float32)
    grad_inner = jnp.where(inner_pre > 0, grad_activated, 0.0).astype(jnp.bfloat16)
    grad_normed_second = jnp.dot(grad_inner, w_inner.T, preferred_element_type=jnp.float32)
    grad_after = cot_flat.astype(jnp.float32) + norm_back(
        after_attn, gain_second, grad_normed_second
    )
    grad_mixed = jnp.dot(
        grad_after.astype(jnp.bfloat16), w_output.T, preferred_element_type=jnp.float32
    ).astype(jnp.bfloat16)
    grad_rows = grad_mixed.reshape(row_count, local_len, model_width)

    def back_scatter(row_items):
        query_row, key_row, value_row, grad_row, same_row, log_total = row_items
        query_heads, key_heads, grad_heads, soft_probs, grad_scores, unused_sum = pair_terms(
            query_row,
            key_row,
            value_row,
            grad_row,
            same_row,
            log_total,
            score_bias,
            head_count,
            None,
        )
        query_grad = jnp.einsum(
            "hqk,khd->qhd", grad_scores, key_heads, preferred_element_type=jnp.float32
        ).reshape(local_len, model_width)
        key_grad = jnp.einsum(
            "hqk,qhd->khd", grad_scores, query_heads, preferred_element_type=jnp.float32
        ).reshape(seq_len, model_width)
        value_grad = jnp.einsum(
            "hqk,qhd->khd",
            soft_probs.astype(jnp.bfloat16),
            grad_heads,
            preferred_element_type=jnp.float32,
        ).reshape(seq_len, model_width)
        return (query_grad, key_grad, value_grad)

    query_grads, key_parts, value_parts = lax.map(
        back_scatter, (query_rows, key_rows, value_rows, grad_rows, same_rows, log_totals)
    )
    key_grads, value_grads = (
        lax.psum_scatter(
            key_parts.astype(jnp.bfloat16), "ctx", scatter_dimension=1, tiled=True
        ).astype(jnp.float32),
        lax.psum_scatter(
            value_parts.astype(jnp.bfloat16), "ctx", scatter_dimension=1, tiled=True
        ).astype(jnp.float32),
    )
    query_low = query_grads.reshape(-1, model_width).astype(jnp.bfloat16)
    key_low = key_grads.reshape(-1, model_width).astype(jnp.bfloat16)
    value_low = value_grads.reshape(-1, model_width).astype(jnp.bfloat16)
    grad_normed_first = jnp.dot(query_low, w_query.T, preferred_element_type=jnp.float32)
    grad_normed_first = grad_normed_first + jnp.dot(
        key_low, w_key.T, preferred_element_type=jnp.float32
    )
    grad_normed_first = grad_normed_first + jnp.dot(
        value_low, w_value.T, preferred_element_type=jnp.float32
    )
    grad_hidden = grad_after + norm_back(hidden, gain_first, grad_normed_first)
    prompt_grad = jnp.einsum(
        "tp,td->pd", choose.astype(jnp.float32), grad_hidden, precision=highest
    )
    grad_group = lax.psum_scatter(
        prompt_grad.astype(jnp.bfloat16), "ctx", scatter_dimension=1, tiled=True
    )
    grad_own = lax.psum_scatter(grad_group, "dp", scatter_dimension=0, tiled=True).astype(
        jnp.float32
    )
    square_sum = lax.psum(jnp.sum(grad_own * grad_own), ("dp", "ctx"))
    max_norm = 0.5 * jnp.sqrt(jnp.float32(PROMPT * D))
    norm_total = jnp.sqrt(square_sum)
    clipped = grad_own * (max_norm / jnp.maximum(norm_total, max_norm))
    first_new = beta_first * first_moment + (1.0 - beta_first) * clipped
    second_new = beta_second * second_moment + (1.0 - beta_second) * clipped * clipped
    prompt_new = prompt - learn_rate * (first_new / first_fix) / (
        jnp.sqrt(second_new / second_fix) + adam_eps
    )
    return (output, prompt_new, first_new, second_new)


def solution(mesh):
    placed = (
        P("dp", "ctx", None),
        P("dp", "ctx"),
        P("dp", "ctx"),
        P("dp", "ctx", None),
        P(),
        P(),
        P(),
        P(),
        P(),
        P(),
        P(),
        P(),
        P(),
        P("dp", "ctx"),
        P("dp", "ctx"),
        P("dp", "ctx"),
    )
    return jax.shard_map(
        on_device,
        mesh=mesh,
        in_specs=placed,
        out_specs=(P("dp", "ctx", None), P("dp", "ctx"), P("dp", "ctx"), P("dp", "ctx")),
        check_vma=False,
    )
```

profile of v0, /device:TPU:0, one launch (start us, length us, event | category | flops | bytes accessed | tf_op | source)
XLA Modules:
  0.0 555.5 jit_solution(8104855041204266140)
XLA Ops:
  8.7 14.8 %all-gather = bf16[4,192,16]{1,2,0:T(8,128)(2,1)S(1)} all-gather(bf16[1,192,16]{1,2,0:T(8,128)(2,1)S(1)} %convert_bitcast_fusion), channel_id=1, replica_groups=mesh['dp'=8,'ctx'=4] {'ctx'}, dimensions={0}, use_global_device_ids=true | all-gather | bytes 30720 | tf_op jit(solution)/shard_map/all_gather | solution.py:100
  23.6 9.3 %all_gather.16 = bf16[128,768]{1,0:T(8,128)(2,1)S(1)} all-gather(bf16[16,768]{1,0:T(8,128)(2,1)S(1)} %bitcast.163), channel_id=1, replica_groups=mesh['dp'=8,'ctx'=4] {'dp'}, dimensions={0}, use_global_device_ids=true | all-gather | bytes 221184 | tf_op jit(solution)/shard_map/all_gather | solution.py:101
  39.0 1.9 convolution_convert_fusion.3
  42.2 2.3 convolution_convert_fusion.2
  46.8 16.8 %fusion.7 = f32[12,256,1024]{2,0,1:T(8,128)} fusion(s32[256,1024]{1,0:T(8,128)S(1)} %fusion.19, f32[32,12]{0,1:T(8,128)S(1)} %copy-done.35), kind=kOutput, calls=%fused_computation.29 | convolution fusion | flops 1216348160 | bytes 13633024 | tf_op jit(solution)/shard_map/qkb,bh->hqk/dot_general | solution.py:46
  63.6 17.7 %copy.79 = f32[12,256,1024]{2,1,0:T(8,128)} copy(f32[12,256,1024]{2,0,1:T(8,128)} %fusion.7) | data formatting | bytes 25165824 | tf_op jit(solution)/shard_map/while | solution.py:153
  81.3 11.1 %all_gather.18 = bf16[2,1024]{1,0:T(2,128)(2,1)S(1)} all-gather(bf16[2,256]{1,0:T(2,128)(2,1)S(1)} %convert_element_type.156), channel_id=1, replica_groups=mesh['dp'=8,'ctx'=4] {'ctx'}, dimensions={1}, use_global_device_ids=true | all-gather | bytes 5120 | tf_op jit(solution)/shard_map/all_gather | solution.py:125
  93.6 8.9 %all-gather.6.cloned.1.call-done = bf16[2,1024,768]{1,2,0:T(8,128)(2,1)} async-done(((bf16[2,256,768]{1,2,0:T(8,128)(2,1)}), bf16[2,1024,768]{1,2,0:T(8,128)(2,1)}) %all-gather.6.cloned.1.call-update) | async-done | bytes 3145744 | tf_op jit(solution)/shard_map/all_gather | solution.py:123
  102.5 63.2 %all-gather.4.cloned.1.call-done = bf16[2,1024,768]{1,2,0:T(8,128)(2,1)} async-done(((bf16[2,256,768]{1,2,0:T(8,128)(2,1)}), bf16[2,1024,768]{1,2,0:T(8,128)(2,1)}) %all-gather.4.cloned.1.call-update) | async-done | bytes 3145744 | tf_op jit(solution)/shard_map/all_gather | solution.py:124
  165.7 35.3 %while.26 = (s32[]{:T(128)}, bf16[2,256,768]{2,1,0:T(8,128)(2,1)}, f32[2,12,256]{2,1,0:T(8,128)}, bf16[2,1024,768]{1,2,0:T(8,128)(2,1)}, pred[2,256,1024]{2,1,0:...) while((s32[]{:T(128)}, bf16[2,256,768]{2,1,0:T(8,128)(2,1)}, ...), condition=%wide.region_4.5_spmd, body=%wide.region_1.4_spmd.sunk | while | flops 830665728 | bytes 63803512 | solution.py:153
  168.0 2.2 constant_dynamic-slice_fusion.13
  170.2 6.0 %fusion.110 = (f32[12,256]{1,0:T(8,128)S(1)}, f32[12,256,1024]{2,1,0:T(8,128)S(1)}) fusion(f32[12,256,1024]{2,1,0:T(8,128)} %get-tuple-element.413, bf16[256,12,64]{0,2,1:T(8,128)(2,1)S(1)} %bitcast.154, bf16[1024,12,64]{0,2,1:T(8,128)(2,1)S(1)} %bitcast.146, pred[256,1024]{1,0:T(8,128)(4,1)S(1)} %dynamic-slice_bitcast_fusion.6), kind=kOutput, calls=%fused_computation.99.clone.1 | convolution fusion | flops 412087296 | bytes 27406336 | tf_op jit(solution)/shard_map/while/body/eval_jaxpr/qhd,khd->hqk/dot_general | solution.py:55
  176.2 2.6 fusion.111
  178.8 3.1 fusion.112
  185.5 2.2 constant_dynamic-slice_fusion.13
  187.7 6.0 %fusion.110 = (f32[12,256]{1,0:T(8,128)S(1)}, f32[12,256,1024]{2,1,0:T(8,128)S(1)}) fusion(f32[12,256,1024]{2,1,0:T(8,128)} %get-tuple-element.413, bf16[256,12,64]{0,2,1:T(8,128)(2,1)S(1)} %bitcast.154, bf16[1024,12,64]{0,2,1:T(8,128)(2,1)S(1)} %bitcast.146, pred[256,1024]{1,0:T(8,128)(4,1)S(1)} %dynamic-slice_bitcast_fusion.6), kind=kOutput, calls=%fused_computation.99.clone.1 | convolution fusion | flops 412087296 | bytes 27406336 | tf_op jit(solution)/shard_map/while/body/eval_jaxpr/qhd,khd->hqk/dot_general | solution.py:55
  193.7 2.6 fusion.111
  196.3 3.1 fusion.112
  201.0 2.2 multiply_reduce_fusion.3
  203.6 4.7 fusion.29
  208.2 12.4 %multiply_reduce_fusion.2 = (f32[512]{0:T(512)S(1)}, f32[512,768]{1,0:T(8,128)}) fusion(f32[512,768]{1,0:T(8,128)} %copy-done.13, f32[768]{0:T(1024)S(1)} %copy-done.22, bf16[768,3072]{1,0:T(8,128)(2,1)} %param.28, f32[512,3072]{1,0:T(8,128)} %fusion.29, bf16[512,768]{1,0:T(8,128)(2,1)S(1)} %bitcast.156, bf16[3072,768]{1,0:T(8,128)(2,1)} %param.29), kind=kOutput, calls=%fused_computation.45 | convolution fusion | flops 4837735936 | bytes 19665920 | tf_op jit(solution)/shard_map/dot_general | solution.py:168
  220.6 1.8 fusion.10
  222.4 1.7 convolution_convert_fusion
  224.2 92.9 %while.27 = (s32[]{:T(128)}, bf16[2,256,768]{2,1,0:T(8,128)(2,1)}, bf16[2,1024,768]{2,1,0:T(8,128)(2,1)}, bf16[2,1024,768]{2,1,0:T(8,128)(2,1)}, bf16[2,1024,768...) while((s32[]{:T(128)}, bf16[2,256,768]{2,1,0:T(8,128)(2,1)}, ...), condition=%wide.region_9.10_spmd, body=%wide.region_7.9_spmd.sunk | while | flops 2041574400 | bytes 178188688 | solution.py:204
  229.3 1.7 constant_dynamic-slice_fusion.17
  232.9 6.4 %fusion.123 = f32[12,256,1024]{2,1,0:T(8,128)} fusion(bf16[256,12,64]{0,2,1:T(8,128)(2,1)S(1)} %bitcast.150, bf16[1024,12,64]{0,2,1:T(8,128)(2,1)S(1)} %bitcast.147), kind=kOutput, calls=%fused_computation.100.clone.1 | convolution fusion | flops 402653184 | bytes 14548992 | tf_op jit(solution)/shard_map/while/body/eval_jaxpr/qhd,khd->hqk/dot_general | solution.py:70
  239.4 11.2 %multiply_reduce_fusion.6 = (f32[12,256]{1,0:T(8,128)S(1)}, f32[12,256,1024]{2,1,0:T(8,128)S(1)}) fusion(f32[12,256,1024]{2,1,0:T(8,128)} %fusion.123, f32[12,256]{1,0:T(8,128)S(1)} %dynamic-slice_bitcast_fusion.7, f32[12,256,1024]{2,1,0:T(8,128)} %get-tuple-element.446, bf16[256,12,64]{0,2,1:T(8,128)(2,1)S(1)} %bitcast.148, ...), kind=kOutput, calls=%fused_computation.13.clone.1 | convolution fusion | flops 418378752 | bytes 40001536 | tf_op jit(solution)/shard_map/while/body/eval_jaxpr/qhd,khd->hqk/dot_general | solution.py:55
  250.6 5.5 multiply_convert_fusion.5
  256.1 2.4 fusion.125
  258.5 2.8 fusion.124
  267.5 3.2 constant_dynamic-update-slice_fusion.9
  275.5 1.7 constant_dynamic-slice_fusion.17
  279.1 6.4 %fusion.123 = f32[12,256,1024]{2,1,0:T(8,128)} fusion(bf16[256,12,64]{0,2,1:T(8,128)(2,1)S(1)} %bitcast.150, bf16[1024,12,64]{0,2,1:T(8,128)(2,1)S(1)} %bitcast.147), kind=kOutput, calls=%fused_computation.100.clone.1 | convolution fusion | flops 402653184 | bytes 14548992 | tf_op jit(solution)/shard_map/while/body/eval_jaxpr/qhd,khd->hqk/dot_general | solution.py:70
  285.5 11.2 %multiply_reduce_fusion.6 = (f32[12,256]{1,0:T(8,128)S(1)}, f32[12,256,1024]{2,1,0:T(8,128)S(1)}) fusion(f32[12,256,1024]{2,1,0:T(8,128)} %fusion.123, f32[12,256]{1,0:T(8,128)S(1)} %dynamic-slice_bitcast_fusion.7, f32[12,256,1024]{2,1,0:T(8,128)} %get-tuple-element.446, bf16[256,12,64]{0,2,1:T(8,128)(2,1)S(1)} %bitcast.148, ...), kind=kOutput, calls=%fused_computation.13.clone.1 | convolution fusion | flops 418378752 | bytes 40001536 | tf_op jit(solution)/shard_map/while/body/eval_jaxpr/qhd,khd->hqk/dot_general | solution.py:55
  296.8 5.5 multiply_convert_fusion.5
  302.3 2.4 fusion.125
  304.7 2.8 fusion.124
  313.7 3.3 constant_dynamic-update-slice_fusion.9
  318.4 1.9 fusion.52
  320.3 55.3 %reduce-scatter.7.cloned.1.call-done = bf16[2,256,768]{2,1,0:T(8,128)(2,1)} async-done(((bf16[2,1024,768]{2,1,0:T(8,128)(2,1)}), bf16[2,256,768]{2,1,0:T(8,128)(2,1)}) %reduce-scatter.7.cloned.1.call-update) | async-done | bytes 786448 | tf_op jit(solution)/shard_map/reduce_scatter | solution.py:208
  375.6 3.6 fusion.53
  379.3 58.8 %reduce-scatter.9.cloned.1.call-done = bf16[2,256,768]{2,1,0:T(8,128)(2,1)} async-done(((bf16[2,1024,768]{2,1,0:T(8,128)(2,1)}), bf16[2,256,768]{2,1,0:T(8,128)(2,1)}) %reduce-scatter.9.cloned.1.call-update) | async-done | bytes 786448 | tf_op jit(solution)/shard_map/reduce_scatter | solution.py:211
  438.1 3.1 multiply_reduce_fusion.1
  441.3 2.5 fusion.16
  443.8 19.5 %reduce-scatter.11.cloned.1.call-done = bf16[128,192]{0,1:T(8,128)(2,1)} async-done(((bf16[128,768]{0,1:T(8,128)(2,1)}), bf16[128,192]{0,1:T(8,128)(2,1)}) %reduce-scatter.11.cloned.1.call-update) | async-done | bytes 49168 | tf_op jit(solution)/shard_map/reduce_scatter | solution.py:229
  464.9 33.6 %reduce-scatter.13.cloned.1.call-done = bf16[16,192]{1,0:T(8,128)(2,1)} async-done(((bf16[128,192]{1,0:T(8,128)(2,1)}), bf16[16,192]{1,0:T(8,128)(2,1)}) %reduce-scatter.13.cloned.1.call-update) | async-done | bytes 6160 | tf_op jit(solution)/shard_map/reduce_scatter | solution.py:232
  499.8 7.7 %add_convert_fusion = bf16[512,768]{1,0:T(8,128)(2,1)} fusion(f32[512,768]{1,0:T(8,128)S(1)} %copy-done.15, bf16[3072,768]{1,0:T(8,128)(2,1)} %param.29, f32[512,3072]{1,0:T(8,128)} %fusion.29), kind=kOutput, calls=%fused_computation.46 | convolution fusion | flops 2419851264 | bytes 13369344 | tf_op jit(solution)/shard_map/dot_general | solution.py:161
  507.5 39.5 %psum.7 = f32[]{:T(128)} all-reduce(f32[]{:T(128)} %fusion.39), channel_id=1, replica_groups=mesh['dp'=8,'ctx'=4] {'dp','ctx'}, use_global_device_ids=true, to_apply=%region_16.17 | all-reduce | flops 1 | bytes 8 | tf_op jit(solution)/shard_map/psum | solution.py:235
  (165 shorter events, 50.5 us)
Async XLA Ops:
  7.2 193.8 %copy-start = (bf16[768,768]{1,0:T(8,128)(2,1)S(1)}, bf16[768,768]{1,0:T(8,128)(2,1)}, u32[]{:S(2)}) copy-start(bf16[768,768]{1,0:T(8,128)(2,1)} %param.27) | copy-start | bytes 3538948
  7.2 28.0 %copy-start.31 = (f32[768]{0:T(1024)S(1)}, f32[768]{0:T(1024)}, u32[]{:S(2)}) copy-start(f32[768]{0:T(1024)} %param.30) | copy-start | bytes 9220
  7.2 95.3 %all-gather.6.cloned.1.call-start = ((), (), s32[]{:S(2)}) async-start(), calls=%async_computation.5 | async-start | bytes 3932160 | tf_op jit(solution)/shard_map/all_gather | solution.py:123
  8.0 26.6 %copy-start.25 = (s32[1,2,2,128]{3,1,2,0:T(2,128)}, s32[1,2,2,128]{3,1,2,0:T(2,128)S(1)}, u32[]{:S(2)}) copy-start(s32[1,2,2,128]{3,1,2,0:T(2,128)S(1)} %copy.104) | copy-start | bytes 6148
  34.6 2.9 copy-start.9
  34.6 2.1 copy-start.38
  35.2 2.4 copy-start.27
  38.8 126.9 %all-gather.4.cloned.1.call-start = ((), (), s32[]{:S(2)}) async-start(), calls=%async_computation.4 | async-start | bytes 3932160 | tf_op jit(solution)/shard_map/all_gather | solution.py:124
  42.1 333.6 %reduce-scatter.7.cloned.1.call-start = ((), (), s32[]{:S(2)}) async-start(), calls=%async_computation.6 | async-start | bytes 3932160 | tf_op jit(solution)/shard_map/reduce_scatter | solution.py:208
  44.5 2.3 copy-start.35
  165.7 35.3 %copy-start.10 = (f32[512,768]{1,0:T(8,128)S(1)}, f32[512,768]{1,0:T(8,128)}, u32[]{:S(2)}) copy-start(f32[512,768]{1,0:T(8,128)} %copy-done.9) | copy-start | bytes 4718596
  201.0 2.6 copy-start.18
  201.0 2.6 copy-start.22
  203.1 5.1 copy-start.13
  203.6 4.7 copy-start.20
  208.2 12.4 %copy-start.14 = (f32[512,768]{1,0:T(8,128)S(1)}, f32[512,768]{1,0:T(8,128)}, u32[]{:S(2)}) copy-start(f32[512,768]{1,0:T(8,128)} %copy-done.13) | copy-start | bytes 4718596
  222.4 1.7 copy-start.16
  228.1 4.8 copy-start.5
  229.3 2.4 copy-start.7
  250.6 5.5 copy-start.6
  256.1 2.4 copy-start.2
  262.6 1.6 copy-start.8
  262.6 2.5 copy-start.3
  265.1 1.6 copy-start.12
  265.1 2.4 copy-start.4
  274.3 4.8 copy-start.5
  275.5 2.4 copy-start.7
  296.8 5.5 copy-start.6
  302.3 2.4 copy-start.2
  308.8 1.6 copy-start.8
  308.8 2.5 copy-start.3
  311.3 1.6 copy-start.12
  311.3 2.4 copy-start.4
  317.0 121.1 %reduce-scatter.9.cloned.1.call-start = ((), (), s32[]{:S(2)}) async-start(), calls=%async_computation.7 | async-start | bytes 3932160 | tf_op jit(solution)/shard_map/reduce_scatter | solution.py:211
  317.6 145.7 %reduce-scatter.11.cloned.1.call-start = ((), (), s32[]{:S(2)}) async-start(), calls=%async_computation.8 | async-start | bytes 245760 | tf_op jit(solution)/shard_map/reduce_scatter | solution.py:229
  375.6 62.5 %copy-start.11 = (f32[512,768]{1,0:T(8,128)S(1)}, f32[512,768]{1,0:T(8,128)}, u32[]{:S(2)}) copy-start(f32[512,768]{1,0:T(8,128)} %copy-done.9) | copy-start | bytes 4718596
  375.6 62.5 %copy-start.32 = (f32[768]{0:T(1024)S(1)}, f32[768]{0:T(1024)}, u32[]{:S(2)}) copy-start(f32[768]{0:T(1024)} %param.30) | copy-start | bytes 9220
  438.1 3.1 copy-start.30
  438.1 3.1 copy-start.17
  438.1 3.1 copy-start.26
  438.1 3.1 copy-start.28
  441.3 58.5 %copy-start.15 = (f32[512,768]{1,0:T(8,128)S(1)}, f32[512,768]{1,0:T(8,128)}, u32[]{:S(2)}) copy-start(f32[512,768]{1,0:T(8,128)} %copy-done.13) | copy-start | bytes 4718596
  443.8 54.7 %reduce-scatter.13.cloned.1.call-start = ((), (), s32[]{:S(2)}) async-start(), calls=%async_computation.9 | async-start | bytes 73728 | tf_op jit(solution)/shard_map/reduce_scatter | solution.py:232
  499.8 48.0 %copy-start.23 = (f32[16,192]{1,0:T(8,128)S(1)}, f32[16,192]{1,0:T(8,128)}, u32[]{:S(2)}) copy-start(f32[16,192]{1,0:T(8,128)} %param.33) | copy-start | bytes 36868
  499.8 48.0 %copy-start.24 = (bf16[16,192]{1,0:T(8,128)(2,1)S(1)}, bf16[16,192]{1,0:T(8,128)(2,1)}, u32[]{:S(2)}) copy-start(bf16[16,192]{1,0:T(8,128)(2,1)} %reduce-scatter.13.cloned.1.call-done) | copy-start | bytes 18436
  499.8 48.1 %copy-start.33 = (f32[16,192]{1,0:T(8,128)S(1)}, f32[16,192]{1,0:T(8,128)}, u32[]{:S(2)}) copy-start(f32[16,192]{1,0:T(8,128)} %param.34) | copy-start | bytes 36868
  499.8 48.1 %copy-start.34 = (f32[16,192]{1,0:T(8,128)S(1)}, f32[16,192]{1,0:T(8,128)}, u32[]{:S(2)}) copy-start(f32[16,192]{1,0:T(8,128)} %param.35) | copy-start | bytes 36868
  499.8 48.7 %copy-start.1 = (bf16[768,768]{1,0:T(8,128)(2,1)S(1)}, bf16[768,768]{1,0:T(8,128)(2,1)}, u32[]{:S(2)}) copy-start(bf16[768,768]{1,0:T(8,128)(2,1)} %param.27) | copy-start | bytes 3538948
  (5 other events, 5.5 us)
Sparse Core Ops, SparseCore 0:
  38.9 63.5 all-gather.5
  104.0 61.5 all-gather.3
  317.2 58.4 reduce-scatter.6
  377.8 60.2 reduce-scatter.8
  443.9 19.3 reduce-scatter.10
  467.0 31.3 reduce-scatter.12
where the time goes:
time: 561 us; the launch traced here: 556 us
  waiting for transfers between devices  240 us (43%)
  matrix products  129 us (23%)
  blocking collectives  74.7 us (13%)
  local copies, waits for them, and re-layouts  70.1 us (12%)
  other arithmetic  24.6 us (4%)
  between operations  15.4 us (3%)
    all_gather x1, waiting for transfers between devices, on_device(): lax.all_gather(value_local, 'ctx', axis=1, tiled=True)  63.2 us
    reduce_scatter x1, waiting for transfers between devices, on_device(): lax.psum_scatter(value_parts.astype(jnp.bfloat16), 'ctx', scatter_dimensi...  58.8 us
    reduce_scatter x1, waiting for transfers between devices, on_device(): lax.psum_scatter(key_parts.astype(jnp.bfloat16), 'ctx', scatter_dimension...  55.3 us
    psum x1, blocking collectives, on_device(): square_sum = lax.psum(jnp.sum(grad_own * grad_own), ('dp', 'ctx'))  39.5 us
    dot_general x4, matrix products, score_rows(): jnp.einsum('qhd,khd->hqk', query_heads, key_heads, preferred_element_type...  34.3 us
    reduce_scatter x1, waiting for transfers between devices, on_device(): lax.psum_scatter(grad_group, 'dp', scatter_dimension=0, tiled=True)  33.6 us
    reduce_scatter x1, waiting for transfers between devices, on_device(): lax.psum_scatter(prompt_grad.astype(jnp.bfloat16), 'ctx', scatter_dimensi...  19.5 us
    while x2, local copies, waits for them, and re-layouts, on_device(): lax.map(attend_row, (query_rows, key_rows, value_rows, same_rows))  18.8 us
  transfers between devices with their start and end apart: 6, of which 6 were waited for; matrix products, arithmetic and copies ran while one was open for 9% of the time, Pallas kernels for 0%

commit v1 on v0

v1 whole, which is shorter than its diff:
```python
import functools

import jax
import jax.numpy as jnp
import numpy as np
from jax import lax
from jax.experimental import pallas as pl
from jax.experimental.pallas import tpu as pltpu
from jax.sharding import PartitionSpec as P

PROMPT = 100
HEAD = 64
PAIR = 2 * HEAD
BLK = 128
QROWS = 256
norm_eps = 1e-06
beta_first = 0.9
beta_second = 0.999
adam_eps = 1e-08
learn_rate = 0.1
first_fix = 1.0 - 0.9**8
second_fix = 1.0 - 0.999**8
far_marks = (12, 16, 23, 32, 46, 64, 91)
f32 = jnp.float32
bf16 = jnp.bfloat16
i32 = jnp.int32
MASKED = -float(2**30)
AXES = ("dp", "ctx")
MIB = 1 << 20


def bucket_table(offset):
    distance = np.abs(offset)
    passed = sum((distance >= mark).astype(np.int32) for mark in far_marks)
    far_ids = np.minimum(8 + passed, 15)
    return np.where(distance < 8, distance, far_ids) + 16 * (offset > 0).astype(np.int32)


def dot_nn(a, b):
    return lax.dot_general(a, b, (((1,), (0,)), ((), ())), preferred_element_type=f32)


def dot_nt(a, b):
    return lax.dot_general(a, b, (((1,), (1,)), ((), ())), preferred_element_type=f32)


def dot_tn(a, b):
    return lax.dot_general(a, b, (((0,), (0,)), ((), ())), preferred_element_type=f32)


def split_two(values):
    high = values.astype(bf16)
    return high, (values - high.astype(f32)).astype(bf16)


def inv_rms(values):
    return lax.rsqrt(jnp.mean(values * values, axis=-1, keepdims=True) + norm_eps)


def segment_of(place, first, second):
    seg = (place >= first).astype(i32) + (place >= second).astype(i32)
    start = jnp.where(seg == 0, 0, jnp.where(seg == 1, first, second))
    return seg, place - start


def vmem_spec():
    return pl.BlockSpec(memory_space=pltpu.VMEM)


def smem_spec():
    return pl.BlockSpec(memory_space=pltpu.SMEM)


def any_spec():
    return pl.BlockSpec(memory_space=pl.ANY)


def out(shape, dtype):
    return jax.ShapeDtypeStruct(shape, dtype)


def params(mib):
    return pltpu.CompilerParams(vmem_limit_bytes=mib * MIB)


def cost(flops, nbytes, trans=0):
    return pl.CostEstimate(flops=int(flops), bytes_accessed=int(nbytes), transcendentals=int(trans))


def pick_piece(pieces, turn, j):
    count = len(pieces)
    place = lax.rem(turn - j + count, count)
    picked = pieces[0][...]
    for k in range(1, count):
        picked = jnp.where(place == k, pieces[k][...], picked)
    return picked


def bias_kernel(base_ref, tile_ref, table_ref):
    heads = tile_ref.shape[0]
    for h in range(heads):
        row = jnp.broadcast_to(base_ref[h : h + 1, :], (BLK, 4 * BLK))
        spread = pltpu.roll(row, 0, 1, stride=1, stride_axis=0)
        low, mid, top = (spread[:, k * BLK : (k + 1) * BLK] for k in (1, 2, 3))
        tile_ref[h, 0] = low
        tile_ref[h, 1] = mid
        tile_ref[h, 2] = top
        mid_high, mid_low = split_two(mid)
        low_high, low_low = split_two(low)
        table_ref[h, 0:BLK, :] = mid_high
        table_ref[h, BLK : 2 * BLK, :] = low_high
        table_ref[h, 2 * BLK : 3 * BLK, :] = mid_low
        table_ref[h, 3 * BLK : 4 * BLK, :] = low_low


def first_kernel(count, piece, sc_ref, *refs):
    pieces = refs[:count]
    (prompt_ref, gain_ref, wq_ref, wk_ref, wv_ref, hid_ref, q_ref, k_ref, v_ref, kp_ref, vp_ref, norm_ref) = refs[count:]
    half, turn, first, second = (sc_ref[n] for n in range(4))
    half_len = count * piece
    gain = gain_ref[...]
    slots = lax.broadcasted_iota(i32, (1, BLK), 1)
    for j in range(count):
        rows = slice(j * piece, (j + 1) * piece)
        place = half * half_len + j * piece + lax.broadcasted_iota(i32, (piece, 1), 0)
        inside = segment_of(place, first, second)[1]
        shown = inside < PROMPT
        choose = jnp.where((inside == slots) & shown, 1.0, 0.0).astype(bf16)
        picked = dot_nn(choose, prompt_ref[...])
        hidden = jnp.where(shown, picked, pick_piece(pieces, turn, j).astype(f32))
        hid_ref[rows, :] = hidden.astype(bf16)
        norm_ref[rows, :] = (hidden * inv_rms(hidden) * gain).astype(bf16)
    hidden = prompt_ref[...].astype(f32)
    norm_ref[half_len : half_len + BLK, :] = (hidden * inv_rms(hidden) * gain).astype(bf16)
    wide = 2 * BLK

    @pl.loop(0, wq_ref.shape[1] // wide)
    def _(t):
        cols = pl.ds(pl.multiple_of(t * wide, wide), wide)
        q_ref[:, cols] = dot_nn(norm_ref[0:half_len, :], wq_ref[:, cols]).astype(bf16)
        keys = dot_nn(norm_ref[...], wk_ref[:, cols]).astype(bf16)
        k_ref[:, cols] = keys[:half_len]
        kp_ref[:, cols] = keys[half_len:]
        vals = dot_nn(norm_ref[...], wv_ref[:, cols]).astype(bf16)
        v_ref[:, cols] = vals[:half_len]
        vp_ref[:, cols] = vals[half_len:]


def forward_kernel(count, piece, sc_ref, tab_ref, *refs):
    pieces = refs[:count]
    (
        q_ref, k_ref, v_ref, kp_ref, vp_ref, hid_ref, gain_first_ref, gain_second_ref, wk_ref, wv_ref, wo_ref, wi_ref,
        tile_ref, table_ref,
        e_ref, kall_ref, vall_ref, mixed_ref, inv_ref, after_ref, act_ref,
        norm_ref, e_buf, sems,
    ) = refs[count:]
    half, turn, first, second = (sc_ref[n] for n in range(4))
    half_len = count * piece
    width = q_ref.shape[1]
    keys_all = 2 * half_len + BLK
    gain = gain_first_ref[...]
    for j in range(count):
        tok = pick_piece(pieces, turn, j).astype(f32)
        norm_ref[j * piece : (j + 1) * piece, :] = (tok * inv_rms(tok) * gain).astype(bf16)
    wide = 2 * BLK

    @pl.loop(0, width // wide)
    def _(t):
        cols = pl.ds(pl.multiple_of(t * wide, wide), wide)
        kall_ref[half_len : 2 * half_len, cols] = dot_nn(norm_ref[...], wk_ref[:, cols]).astype(bf16)
        vall_ref[half_len : 2 * half_len, cols] = dot_nn(norm_ref[...], wv_ref[:, cols]).astype(bf16)
        kall_ref[0:half_len, cols] = k_ref[:, cols]
        vall_ref[0:half_len, cols] = v_ref[:, cols]
        kall_ref[2 * half_len :, cols] = kp_ref[:, cols]
        vall_ref[2 * half_len :, cols] = vp_ref[:, cols]

    lane = lax.broadcasted_iota(i32, (1, PAIR), 1)
    low_lane = lane < HEAD
    lane_seg = lax.rem(lane, HEAD)
    spot = lax.broadcasted_iota(i32, (half_len, 1), 0)
    own_seg, own_inside = segment_of(half * half_len + spot, first, second)
    par_seg, par_inside = segment_of((1 - half) * half_len + spot, first, second)
    q_aug = jnp.where(own_seg == lane_seg, 1.0, 0.0).astype(bf16)

    def key_aug(seg, inside):
        closed = ((seg != lane_seg) | (inside < PROMPT)) & (lane_seg < 3)
        return jnp.where(closed, MASKED, 0.0).astype(bf16)

    slot = lax.broadcasted_iota(i32, (BLK, 1), 0)
    k_aug = jnp.concatenate(
        [
            key_aug(own_seg, own_inside),
            key_aug(par_seg, par_inside),
            jnp.where((slot >= PROMPT) & (lane_seg < 3), MASKED, 0.0).astype(bf16),
        ],
        axis=0,
    )
    far = lax.rem(lax.broadcasted_iota(i32, (1, 4 * BLK), 1), 2 * BLK)
    spread = jnp.where(jnp.minimum(own_inside, 2 * BLK - 1) == far, 1.0, 0.0).astype(bf16)
    blocks = half_len // BLK
    per = QROWS // BLK

    def e_copy(hp, at):
        return pltpu.make_async_copy(e_buf.at[at], e_ref.at[pl.ds(2 * hp, 2)], sems.at[at])

    @pl.loop(0, width // PAIR)
    def _(hp):
        at = lax.rem(hp, 2)

        @pl.when(hp >= 2)
        def _():
            e_copy(hp - 2, at).wait()

        cols = pl.ds(pl.multiple_of(hp * PAIR, PAIR), PAIR)
        q_pair, k_pair, v_pair = q_ref[:, cols], kall_ref[:, cols], vall_ref[:, cols]
        results = []
        for s in range(2):
            h = 2 * hp + s
            keep = low_lane if s == 0 else jnp.logical_not(low_lane)
            q_e = jnp.where(keep, q_pair, q_aug)
            k_e = jnp.where(keep, k_pair, k_aug)
            v_e = jnp.where(keep, v_pair, jnp.ones((), bf16))
            back_far, ahead_far = tab_ref[15, h], tab_ref[31, h]
            other_far = jnp.where(half == 0, ahead_far, back_far)
            table = table_ref[h]
            head_rows = []
            for qt in range(half_len // QROWS):
                qrows = slice(qt * QROWS, (qt + 1) * QROWS)
                raw = dot_nt(q_e[qrows], k_e)
                prompt_bias = dot_nn(spread[qrows], table)
                e_rows = []
                for sub in range(per):
                    qb = qt * per + sub
                    rr = slice(sub * BLK, (sub + 1) * BLK)
                    parts, consts = [], []
                    for kb in range(2 * blocks):
                        part = raw[rr, kb * BLK : (kb + 1) * BLK]
                        const = None
                        if kb < blocks:
                            gap = kb - qb
                            if abs(gap) <= 1:
                                part = part + tile_ref[h, gap + 1]
                            else:
                                const = 0 if gap < 0 else 1
                        elif qb == blocks - 1 and kb == blocks:
                            part = part + jnp.where(half == 0, tile_ref[h, 2], back_far)
                        elif qb == 0 and kb == 2 * blocks - 1:
                            part = part + jnp.where(half == 0, ahead_far, tile_ref[h, 0])
                        else:
                            const = 2
                        parts.append(part)
                        consts.append(const)
                    parts.append(raw[rr, 2 * blocks * BLK :] + prompt_bias[rr])
                    consts.append(None)
                    values = (back_far, ahead_far, other_far)
                    best = None
                    for group in (None, 0, 1, 2):
                        members = [p for p, c in zip(parts, consts) if c == group]
                        if not members:
                            continue
                        top = functools.reduce(jnp.maximum, members)
                        if group is not None:
                            top = top + values[group]
                        best = top if best is None else jnp.maximum(best, top)
                    peak = jnp.max(best, axis=1, keepdims=True)
                    shifts = [peak - value for value in values]
                    e_rows.append(
                        jnp.concatenate(
                            [
                                jnp.exp(p - (peak if c is None else shifts[c])).astype(bf16)
                                for p, c in zip(parts, consts)
                            ],
                            axis=1,
                        )
                    )
                raised = jnp.concatenate(e_rows, axis=0)
                e_buf[at, s, qrows, :] = raised
                head_rows.append(dot_nn(raised, v_e))
            results.append(jnp.concatenate(head_rows, axis=0))
        sums = pltpu.roll(jnp.where(low_lane, results[1], results[0]), HEAD, 1)
        inv = 1.0 / sums
        inv_ref[:, cols] = inv
        mixed_ref[:, cols] = (jnp.where(low_lane, results[0], results[1]) * inv).astype(bf16)
        e_copy(hp, at).start()

    for rest in range(2):
        e_copy(width // PAIR - 2 + rest, rest).wait()

    @pl.loop(0, half_len // BLK)
    def _(t):
        rows = pl.ds(pl.multiple_of(t * BLK, BLK), BLK)
        after = hid_ref[rows, :].astype(f32) + dot_nn(mixed_ref[rows, :], wo_ref[...])
        after_ref[rows, :] = after
        norm_ref[rows, :] = (after * inv_rms(after) * gain_second_ref[...]).astype(bf16)

    @pl.loop(0, wi_ref.shape[1] // wide)
    def _(t):
        cols = pl.ds(pl.multiple_of(t * wide, wide), wide)
        act_ref[:, cols] = jnp.maximum(dot_nn(norm_ref[...], wi_ref[:, cols]), 0.0).astype(bf16)


def backward_kernel(count, piece, sc_ref, *refs):
    cots = refs[:count]
    (
        act_ref, after_ref, mixed_ref, inv_ref, q_ref, kall_ref, vall_ref, prompt_ref, gain_first_ref, gain_second_ref,
        wout_ref, wi_ref, wo_ref, wq_ref, wk_ref, wv_ref, e_hbm,
        grad_ref,
        e_ref, cot_ref, acc_ref, do_ref, delta_ref, dq_ref, gk_ref, gv_ref, sem,
    ) = refs[count:]
    fetch = pltpu.make_async_copy(e_hbm, e_ref, sem)
    fetch.start()
    half, turn, first, second = (sc_ref[n] for n in range(4))
    half_len = count * piece
    width = q_ref.shape[1]
    for j in range(count):
        cot_ref[j * piece : (j + 1) * piece, :] = pick_piece(cots, turn, j)
    wide = 4 * BLK
    acc_ref[...] = jnp.zeros_like(acc_ref)

    @pl.loop(0, wi_ref.shape[1] // wide)
    def _(t):
        cols = pl.ds(pl.multiple_of(t * wide, wide), wide)
        grad_act = dot_nt(cot_ref[...], wout_ref[cols, :])
        grad_inner = jnp.where(act_ref[:, cols] > 0, grad_act, 0.0).astype(bf16)
        acc_ref[...] += dot_nt(grad_inner, wi_ref[:, cols])

    gain = gain_second_ref[...]

    @pl.loop(0, half_len // BLK)
    def _(t):
        rows = pl.ds(pl.multiple_of(t * BLK, BLK), BLK)
        after = after_ref[rows, :]
        scale = inv_rms(after)
        pulled = gain * acc_ref[rows, :]
        along = jnp.mean(after * pulled, axis=-1, keepdims=True)
        grad_after = cot_ref[rows, :].astype(f32) + scale * pulled - after * (scale * scale * scale * along)
        acc_ref[rows, :] = grad_after
        grad_mixed = dot_nt(grad_after.astype(bf16), wo_ref[...])
        do_ref[rows, :] = (grad_mixed * inv_ref[rows, :]).astype(bf16)

    fetch.wait()
    lane = lax.broadcasted_iota(i32, (1, PAIR), 1)
    low_lane = lane < HEAD
    lane_at = lax.rem(lane, HEAD)

    @pl.loop(0, width // PAIR)
    def _(hp):
        cols = pl.ds(pl.multiple_of(hp * PAIR, PAIR), PAIR)
        q_pair, k_pair, v_pair, do_pair = q_ref[:, cols], kall_ref[:, cols], vall_ref[:, cols], do_ref[:, cols]
        inner = do_pair.astype(f32) * mixed_ref[:, cols].astype(f32)
        dqs, dks, dvs = [], [], []
        for s in range(2):
            keep = low_lane if s == 0 else jnp.logical_not(low_lane)
            delta = jnp.sum(jnp.where(keep, inner, 0.0), axis=1, keepdims=True)
            high, low = split_two(-delta)
            aug = jnp.where(lane_at == 0, high, jnp.where(lane_at == 1, low, jnp.zeros((), bf16)))
            do_e = jnp.where(keep, do_pair, aug)
            v_e = jnp.where(keep, v_pair, jnp.ones((), bf16))
            dq, dk, dv = [], None, None
            for qt in range(half_len // QROWS):
                qrows = slice(qt * QROWS, (qt + 1) * QROWS)
                raised = e_ref[2 * hp + s, qrows, :]
                grad_probs = dot_nt(do_e[qrows], v_e)
                grad_scores = (raised.astype(f32) * grad_probs).astype(bf16)
                dq.append(dot_nn(grad_scores, k_pair))
                dk_now = dot_tn(grad_scores[:, 2 * half_len :], q_pair[qrows])
                dv_now = dot_tn(raised[:, 2 * half_len :], do_pair[qrows])
                dk = dk_now if dk is None else dk + dk_now
                dv = dv_now if dv is None else dv + dv_now
            dqs.append(jnp.concatenate(dq, axis=0))
            dks.append(dk)
            dvs.append(dv)
        dq_ref[:, cols] = jnp.where(low_lane, dqs[0], dqs[1]).astype(bf16)
        gk_ref[:, cols] = jnp.where(low_lane, dks[0], dks[1]).astype(bf16)
        gv_ref[:, cols] = jnp.where(low_lane, dvs[0], dvs[1]).astype(bf16)

    spot = lax.broadcasted_iota(i32, (1, half_len), 1)
    inside = segment_of(half * half_len + spot, first, second)[1]
    slots = lax.broadcasted_iota(i32, (BLK, 1), 0)
    choose = jnp.where((inside == slots) & (inside < PROMPT), 1.0, 0.0).astype(bf16)
    gq = dot_nn(choose, dq_ref[...]).astype(bf16)
    pulled = dot_nt(gq, wq_ref[...]) + dot_nt(gk_ref[...], wk_ref[...]) + dot_nt(gv_ref[...], wv_ref[...])
    high, low = split_two(acc_ref[...])
    direct = dot_nn(choose, high) + dot_nn(choose, low)
    hidden = prompt_ref[...].astype(f32)
    scale = inv_rms(hidden)
    pulled = gain_first_ref[...] * pulled
    along = jnp.mean(hidden * pulled, axis=-1, keepdims=True)
    grad_ref[...] = direct + scale * pulled - hidden * (scale * scale * scale * along)


def output_kernel(act_ref, after_ref, wout_ref, out_ref):
    wide = 2 * BLK

    @pl.loop(0, out_ref.shape[1] // wide)
    def _(t):
        cols = pl.ds(pl.multiple_of(t * wide, wide), wide)
        out_ref[:, cols] = (after_ref[:, cols] + dot_nn(act_ref[...], wout_ref[:, cols])).astype(bf16)


def on_device(
    sizes, tokens, segment_ids, prompt_slots, cotangent, w_query, w_key, w_value, w_output, w_inner, w_outer,
    gain_first, gain_second, bias_table, prompt, first_moment, second_moment,
):
    n_dp, n_ctx = sizes
    count, piece, width = tokens.shape
    half_len = count * piece
    heads = bias_table.shape[1]
    dp, ctx = lax.axis_index("dp"), lax.axis_index("ctx")
    core, turn = lax.rem(dp, 2), lax.rem(ctx, count)

    def permute(value, target):
        pairs = []
        for d in range(n_dp):
            for z in range(n_ctx):
                d2, z2 = target(d, z)
                pairs.append((d * n_ctx + z, d2 * n_ctx + z2))
        return lax.ppermute(value, AXES, pairs)

    def swap_dp(value, bit):
        return permute(value, lambda d, z: (d ^ bit, z))

    def swap_ctx(value, bit):
        return permute(value, lambda d, z: (d, z ^ bit))

    def there(k):
        return lambda d, z: (2 * (d // 2) + z // count, (d % 2) * count + (z + k) % count)

    def send_pieces(rows):
        return [
            permute(lax.dynamic_index_in_dim(rows, lax.rem(ctx + k, count), keepdims=False), there(k))
            for k in range(count)
        ]

    own = send_pieces(tokens)
    partner = [swap_dp(piece_rows, 1) for piece_rows in own]
    cot_rows, partner = lax.optimization_barrier((cotangent, partner))
    cots = send_pieces(cot_rows)

    rows_own, cols_own = prompt.shape
    tallies = jnp.concatenate(
        [jnp.sum((segment_ids <= n).astype(f32), axis=1) for n in range(2)]
    )
    tally_row = jnp.zeros((8, cols_own), f32).at[0, : 2 * count].set(tallies)
    block = jnp.concatenate([prompt, tally_row], axis=0).astype(bf16)
    block = jnp.concatenate([jnp.where(ctx == n, block, 0) for n in range(n_ctx)], axis=1)
    bit = 1
    while bit < n_ctx:
        block = block + swap_ctx(block, bit)
        bit *= 2
    other = swap_dp(block, 1)

    def joined(mine, theirs, up):
        return jnp.where(up, jnp.concatenate([theirs, mine], 0), jnp.concatenate([mine, theirs], 0))

    tally_mine, tally_theirs = (
        jnp.sum(b[rows_own].astype(f32).reshape(n_ctx, cols_own)[:, : 2 * count], axis=0).reshape(2, count)
        for b in (block, other)
    )
    tally = jnp.where(ctx // count == core, tally_mine, tally_theirs)
    marks = lax.dynamic_index_in_dim(tally, turn, axis=1, keepdims=False).astype(i32)
    scalars = jnp.concatenate([jnp.stack([core, turn]).astype(i32), marks])
    sent = joined(block[:rows_own], other[:rows_own], core == 1)
    bit = 2
    while bit < n_dp:
        sent = joined(sent, swap_dp(sent, bit), (dp & bit) != 0)
        bit *= 2

    choose = (np.arange(bias_table.shape[0])[:, None] == bucket_table(np.arange(4 * BLK) - 2 * BLK)[None]).astype(np.float32)
    base = lax.dot_general(
        bias_table, jnp.asarray(choose), (((0,), (0,)), ((), ())), precision=lax.Precision.HIGHEST
    )
    tiles, table = pl.pallas_call(
        bias_kernel,
        out_shape=(out((heads, 3, BLK, BLK), f32), out((heads, 4 * BLK, BLK), bf16)),
        compiler_params=params(24),
        cost_estimate=cost(1e6, 4e6),
    )(base)

    gain_1, gain_2 = gain_first[None], gain_second[None]
    act_like = out((half_len, width), bf16)
    pair_like = out((BLK, width), bf16)
    hid, q, k, v, kp, vp = pl.pallas_call(
        functools.partial(first_kernel, count, piece),
        out_shape=(act_like, act_like, act_like, act_like, pair_like, pair_like),
        in_specs=[smem_spec()] + [vmem_spec()] * (count + 5),
        out_specs=[vmem_spec()] * 6,
        scratch_shapes=[pltpu.VMEM((half_len + BLK, width), bf16)],
        compiler_params=params(32),
        cost_estimate=cost(6 * half_len * width * width, 8e6),
    )(scalars, *own, sent, gain_1, w_query, w_key, w_value)

    keys_all = 2 * half_len + BLK
    hidden_ff = w_inner.shape[1]
    e, kall, vall, mixed, inv, after, act = pl.pallas_call(
        functools.partial(forward_kernel, count, piece),
        out_shape=(
            out((heads, half_len, keys_all), bf16),
            out((keys_all, width), bf16),
            out((keys_all, width), bf16),
            act_like,
            out((half_len, width), f32),
            out((half_len, width), f32),
            out((half_len, hidden_ff), bf16),
        ),
        in_specs=[smem_spec(), smem_spec()] + [vmem_spec()] * (count + 14),
        out_specs=[any_spec()] + [vmem_spec()] * 6,
        scratch_shapes=[
            pltpu.VMEM((half_len, width), bf16),
            pltpu.VMEM((2, 2, half_len, keys_all), bf16),
            pltpu.SemaphoreType.DMA((2,)),
        ],
        compiler_params=params(56),
        cost_estimate=cost(3e10, 4e7, heads * half_len * keys_all),
    )(
        scalars, bias_table, *partner, q, k, v, kp, vp, hid, gain_1, gain_2, w_key, w_value, w_output, w_inner, tiles,
        table,
    )

    grad = pl.pallas_call(
        functools.partial(backward_kernel, count, piece),
        out_shape=out((BLK, width), f32),
        in_specs=[smem_spec()] + [vmem_spec()] * (count + 16) + [any_spec()],
        out_specs=vmem_spec(),
        scratch_shapes=[
            pltpu.VMEM((heads, half_len, keys_all), bf16),
            pltpu.VMEM((half_len, width), bf16),
            pltpu.VMEM((half_len, width), f32),
            pltpu.VMEM((half_len, width), bf16),
            pltpu.VMEM((8, BLK), f32),
            pltpu.VMEM((half_len, width), bf16),
            pltpu.VMEM((BLK, width), bf16),
            pltpu.VMEM((BLK, width), bf16),
            pltpu.SemaphoreType.DMA,
        ],
        compiler_params=params(60),
        cost_estimate=cost(3e10, 4e7),
    )(
        scalars, *cots, act, after, mixed, inv, q, kall, vall, sent, gain_1, gain_2, w_outer, w_inner, w_output, w_query,
        w_key, w_value, e,
    )

    rows_out = pl.pallas_call(
        output_kernel,
        out_shape=act_like,
        compiler_params=params(32),
        cost_estimate=cost(2 * half_len * width * hidden_ff, 1e7),
    )(act, after, w_outer)

    halves = rows_out.reshape(count, piece, width)
    got = [
        permute(lax.dynamic_index_in_dim(halves, lax.rem(turn - k + count, count), keepdims=False), back_of(count, k))
        for k in range(count)
    ]
    order = [lax.rem(ctx + j, count) for j in range(count)]
    output = jnp.stack(
        [functools.reduce(lambda a, k: jnp.where(order[k] == r, got[k], a), range(1, count), got[0]) for r in range(count)]
    )

    per = rows_own
    grad = grad[: per * n_dp]
    bit = 1
    keep = grad.reshape(1, n_dp, per, width)
    while bit < n_dp:
        left = keep.shape[1]
        view = keep.reshape(left // 2, 2, per, width)
        up = (dp & bit) != 0
        mine = jnp.where(up, view[:, 1], view[:, 0])
        theirs = jnp.where(up, view[:, 0], view[:, 1])
        keep = (mine + swap_dp(theirs.astype(bf16), bit).astype(f32))[None]
        bit *= 2
    total = keep.reshape(per, width)
    bit = 1
    while bit < n_ctx:
        total = total + swap_ctx(total.astype(bf16), bit).astype(f32)
        bit *= 2
    square = jnp.full((8, BLK), jnp.sum(total * total), f32)
    bit = 1
    while bit < n_dp:
        square = square + swap_dp(square, bit)
        bit *= 2
    max_norm = 0.5 * jnp.sqrt(f32(PROMPT * width))
    norm_total = jnp.sqrt(square[0, 0])
    grad_own = lax.dynamic_slice_in_dim(total, ctx * cols_own, cols_own, axis=1)
    clipped = grad_own * (max_norm / jnp.maximum(norm_total, max_norm))
    first_new = beta_first * first_moment + (1.0 - beta_first) * clipped
    second_new = beta_second * second_moment + (1.0 - beta_second) * clipped * clipped
    prompt_new = prompt - learn_rate * (first_new / first_fix) / (jnp.sqrt(second_new / second_fix) + adam_eps)
    return (output, prompt_new, first_new, second_new)


def back_of(count, k):
    def target(d, z):
        half, c, r = d % 2, z // count, z % count
        return (2 * (d // 2) + c, half * count + (r - k) % count)

    return target


def solution(mesh):
    rows, cols = P("dp", "ctx", None), P("dp", "ctx")
    placed = (rows, cols, cols, rows) + (P(),) * 9 + (cols,) * 3
    return jax.shard_map(
        functools.partial(on_device, (mesh.shape["dp"], mesh.shape["ctx"])),
        mesh=mesh,
        in_specs=placed,
        out_specs=(rows, cols, cols, cols),
        check_vma=False,
    )
```

time: 561 us -> 173 us (0.31)
  the two profiles are of different devices: /device:TPU:0 before, /device:TPU:16 now
where the time goes in v1:
time: 173 us
  Pallas kernels  75.1 us (43%)
  waiting for transfers between devices  41.6 us (24%)
  starting transfers between devices  27.9 us (16%)
  local copies, waits for them, and re-layouts  17.8 us (10%)
  other arithmetic  8.08 us (5%)
  between operations  1.88 us (1%)
    ppermute x21, waiting for transfers between devices, permute(): return lax.ppermute(value, AXES, pairs)  41.6 us
    pallas_call x1, Pallas kernels, on_device(): pl.pallas_call(functools.partial(forward_kernel, count, piece), out_shape...  35.8 us
    pallas_call x1, Pallas kernels, on_device(): pl.pallas_call(functools.partial(backward_kernel, count, piece), out_shap...  31 us
    ppermute x21, starting transfers between devices, permute(): return lax.ppermute(value, AXES, pairs)  27.9 us
    unnamed x59, local copies, waits for them, and re-layouts  13.6 us
    pallas_call x1, Pallas kernels, on_device(): pl.pallas_call(functools.partial(first_kernel, count, piece), out_shape=(...  4.5 us
  transfers between devices with their start and end apart: 21, of which 11 were waited for; matrix products, arithmetic and copies ran while one was open for 4% of the time, Pallas kernels for 26%

profile of v1, /device:TPU:16, one launch (start us, length us, event | category | flops | bytes accessed | tf_op | source)
XLA Modules:
  0.0 172.6 jit_solution(9990103894764546638)
XLA Ops:
  0.7 0.9 fusion.10
  1.6 0.7 convert.17
  2.5 1.6 collective-permute-start
  4.1 2.0 %dynamic-slice_bitcast_fusion.4 = (bf16[256,768]{1,0:T(8,128)(2,1)}, bf16[256,768]{1,0:T(8,128)(2,1)}) fusion(bf16[2,256,768]{2,1,0:T(8,128)(2,1)} %param.19, s32[]{:T(128)S(6)} %select_n.178, s32[]{:T(128)S(6)} %select_n.177), kind=kLoop, calls=%fused_computation.8 | loop fusion | bytes 1572872 | tf_op jit(solution)/shard_map/jit(dynamic_index_in_dim)/squeeze | solution.py:431
  6.2 1.9 %collective-permute-start.3 = (bf16[256,768]{1,0:T(8,128)(2,1)}, bf16[256,768]{1,0:T(8,128)(2,1)S(1)}, u32[]{:S(2)}, u32[]{:S(2)}) collective-permute-start(bf16[256,768]{1,0:T(8,128)(2,1)} %get-tuple-element.68), channel_id=1, source_target_pairs={{0,0},{1,1},{2,4},{3,5},{4,2},{5,3},{6,6},{7,7},{8,8},{9,9},{10,12... | collective-permute-start | bytes 1179656 | tf_op jit(solution)/shard_map/ppermute | solution.py:418
  8.1 1.7 collective-permute-start.5
  10.1 0.7 copy.25.tab_ref
  11.4 0.9 shard_map.184
  12.3 1.4 copy-done.6
  13.7 14.0 %collective-permute-done.1 = bf16[24,768]{1,0:T(8,128)(2,1)S(1)} collective-permute-done((bf16[24,768]{1,0:T(8,128)(2,1)S(1)}, bf16[24,768]{1,0:T(8,128)(2,1)S(1)}, u32[]{:S(2)}, u32[]{:S(2)}) %collective-permute-start.1) | collective-permute-done | bytes 36896 | tf_op jit(solution)/shard_map/ppermute | solution.py:418
  28.0 1.1 collective-permute-done.2
  29.1 1.6 collective-permute-start.7
  31.0 2.2 %collective-permute-done.7 = bf16[32,768]{1,0:T(8,128)(2,1)S(1)} collective-permute-done((bf16[32,768]{1,0:T(8,128)(2,1)S(1)}, bf16[32,768]{1,0:T(8,128)(2,1)S(1)}, u32[]{:S(2)}, u32[]{:S(2)}) %collective-permute-start.7) | collective-permute-done | bytes 49184 | tf_op jit(solution)/shard_map/ppermute | solution.py:418
  33.2 1.6 collective-permute-start.8
  35.4 2.5 %collective-permute-done.8 = bf16[64,768]{1,0:T(8,128)(2,1)S(1)} collective-permute-done((bf16[64,768]{1,0:T(8,128)(2,1)S(1)}, bf16[64,768]{1,0:T(8,128)(2,1)S(1)}, u32[]{:S(2)}, u32[]{:S(2)}) %collective-permute-start.8) | collective-permute-done | bytes 98336 | tf_op jit(solution)/shard_map/ppermute | solution.py:418
  38.0 1.3 copy-done.9
  39.2 1.3 copy-done.10
  40.5 4.5 %shard_map.183 = (bf16[512,768]{1,0:T(8,128)(2,1)S(1)}, bf16[512,768]{1,0:T(8,128)(2,1)S(1)}, bf16[512,768]{1,0:T(8,128)(2,1)S(1)}, bf16[512,768]{1,0:T(8,128)(2...) custom-call(s32[4]{0:T(128)S(1)} %pad_add_fusion.sc_ref, ...), custom_call_target="tpu_custom_call" | custom-call | flops 1811939328 | bytes 8000000 | tf_op jit(solution)/shard_map/pallas_call | solution.py:483
  45.1 0.9 copy-done.11
  46.0 0.9 copy-done.12
  46.8 0.9 copy-done.13
  47.7 0.9 copy-done.14
  49.4 2.9 %collective-permute-start.11 = (bf16[256,768]{1,0:T(8,128)(2,1)S(1)}, bf16[256,768]{1,0:T(8,128)(2,1)S(1)}, u32[]{:S(2)}, u32[]{:S(2)}) collective-permute-start(bf16[256,768]{1,0:T(8,128)(2,1)S(1)} %get-tuple-element.62), channel_id=1, source_target_pairs={{0,0},{1,1},{2,4},{3,5},{4,2},{5,3},{6,6},{7,7},{8,8},{9,9},{10,12... | collective-permute-start | bytes 1179656 | tf_op jit(solution)/shard_map/ppermute | solution.py:418
  52.3 3.2 %collective-permute-start.12 = (bf16[256,768]{1,0:T(8,128)(2,1)S(1)}, bf16[256,768]{1,0:T(8,128)(2,1)S(1)}, u32[]{:S(2)}, u32[]{:S(2)}) collective-permute-start(bf16[256,768]{1,0:T(8,128)(2,1)S(1)} %get-tuple-element.61), channel_id=1, source_target_pairs={{0,1},{1,0},{2,5},{3,4},{4,3},{5,2},{6,7},{7,6},{8,9},{9,8},{10,13... | collective-permute-start | bytes 1179656 | tf_op jit(solution)/shard_map/ppermute | solution.py:418
  55.6 35.8 %shard_map.185 = (bf16[12,512,1152]{2,1,0:T(8,128)(2,1)}, bf16[1152,768]{1,0:T(8,128)(2,1)}, bf16[1152,768]{1,0:T(8,128)(2,1)}, bf16[512,768]{1,0:T(8,128)(2,1)}...) custom-call(s32[4]{0:T(128)} %copy-done.5, f32[32,12]{1,0:T(8,128)} %copy.25.tab_ref, ...), custom_call_target="tpu_custom_call" | custom-call | flops 30000001024 | bytes 40000000 | tf_op jit(solution)/shard_map/pallas_call | solution.py:495
  91.5 0.8 copy-done.28
  92.4 31.0 %shard_map.187 = f32[128,768]{1,0:T(8,128)} custom-call(s32[4]{0:T(128)} %copy-done.5, bf16[256,768]{1,0:T(8,128)(2,1)} %copy-done.27, bf16[256,768]{1,0:T(8,128)(2,1)} %copy-done.28, bf16[512,3072]{1,0:T(8,128)(2,1)} %get-tuple-element.44.act_ref.refs_2_, f32[512,768]{1,0:T(8,128)} %get-tuple-element.45.after_ref.refs_3_, ...), custom_call_target="tpu_custom_call" | custom-call | flops 30000001024 | bytes 40000000 | tf_op jit(solution)/shard_map/pallas_call | solution.py:520
  123.4 1.1 fusion
  124.5 1.3 collective-permute-done.13
  125.8 1.1 bitcast_add_fusion
  126.9 1.5 collective-permute-start.14
  128.4 2.6 %collective-permute-done.14 = bf16[2,16,768]{2,1,0:T(8,128)(2,1)S(1)} collective-permute-done((bf16[2,16,768]{2,1,0:T(8,128)(2,1)S(1)}, bf16[2,16,768]{2,1,0:T(8,128)(2,1)S(1)}, u32[]{:S(2)}, u32[]{:S(2)}) %collective-permute-start.14) | collective-permute-done | bytes 49184 | tf_op jit(solution)/shard_map/ppermute | solution.py:418
  131.1 1.6 collective-permute-start.15
  132.6 2.3 %collective-permute-done.15 = bf16[1,16,768]{2,1,0:T(8,128)(2,1)S(1)} collective-permute-done((bf16[1,16,768]{2,1,0:T(8,128)(2,1)S(1)}, bf16[1,16,768]{2,1,0:T(8,128)(2,1)S(1)}, u32[]{:S(2)}, u32[]{:S(2)}) %collective-permute-start.15) | collective-permute-done | bytes 24608 | tf_op jit(solution)/shard_map/ppermute | solution.py:418
  135.1 2.3 %copy-done = bf16[3072,768]{1,0:T(8,128)(2,1)S(1)} copy-done((bf16[3072,768]{1,0:T(8,128)(2,1)S(1)}, bf16[3072,768]{1,0:T(8,128)(2,1)}, u32[]{:S(2)}) %copy-start) | copy-done | bytes 4718616
  137.5 1.4 copy-done.2
  138.9 3.0 %shard_map.186 = bf16[512,768]{1,0:T(8,128)(2,1)S(1)} custom-call(bf16[512,3072]{1,0:T(8,128)(2,1)S(1)} %copy-done.1, f32[512,768]{1,0:T(8,128)S(1)} %copy-done.2, bf16[3072,768]{1,0:T(8,128)(2,1)S(1)} %copy-done), custom_call_target="tpu_custom_call" | custom-call | flops 2415919104 | bytes 10000000 | tf_op jit(solution)/shard_map/pallas_call | solution.py:543
  141.9 1.5 collective-permute-start.17
  143.5 2.1 %collective-permute-start.10 = (bf16[256,768]{1,0:T(8,128)(2,1)S(1)}, bf16[256,768]{1,0:T(8,128)(2,1)S(1)}, u32[]{:S(2)}, u32[]{:S(2)}) collective-permute-start(bf16[256,768]{1,0:T(8,128)(2,1)S(1)} %get-tuple-element.65), channel_id=1, source_target_pairs={{0,0},{1,1},{2,4},{3,5},{4,2},{5,3},{6,6},{7,7},{8,8},{9,9},{10,12... | collective-permute-start | bytes 1179656 | tf_op jit(solution)/shard_map/ppermute | solution.py:418
  145.6 2.7 %collective-permute-start.9 = (bf16[256,768]{1,0:T(8,128)(2,1)S(1)}, bf16[256,768]{1,0:T(8,128)(2,1)S(1)}, u32[]{:S(2)}, u32[]{:S(2)}) collective-permute-start(bf16[256,768]{1,0:T(8,128)(2,1)S(1)} %get-tuple-element.66), channel_id=1, source_target_pairs={{0,1},{1,0},{2,5},{3,4},{4,3},{5,2},{6,7},{7,6},{8,9},{9,8},{10,13... | collective-permute-start | bytes 1179656 | tf_op jit(solution)/shard_map/ppermute | solution.py:418
  149.6 1.1 collective-permute-done.18
  151.4 1.5 collective-permute-start.19
  152.9 6.3 %collective-permute-done.10 = bf16[256,768]{1,0:T(8,128)(2,1)S(1)} collective-permute-done((bf16[256,768]{1,0:T(8,128)(2,1)S(1)}, bf16[256,768]{1,0:T(8,128)(2,1)S(1)}, u32[]{:S(2)}, u32[]{:S(2)}) %collective-permute-start.10) | collective-permute-done | bytes 393248 | tf_op jit(solution)/shard_map/ppermute | solution.py:418
  159.3 7.0 %collective-permute-done.9 = bf16[256,768]{1,0:T(8,128)(2,1)S(1)} collective-permute-done((bf16[256,768]{1,0:T(8,128)(2,1)S(1)}, bf16[256,768]{1,0:T(8,128)(2,1)S(1)}, u32[]{:S(2)}, u32[]{:S(2)}) %collective-permute-start.9) | collective-permute-done | bytes 393248 | tf_op jit(solution)/shard_map/ppermute | solution.py:418
  167.0 1.6 collective-permute-start.20
  168.5 0.9 pad_maximum_fusion
  169.5 1.1 collective-permute-done.20
  171.9 0.7 divide_subtract_fusion
  (101 shorter events, 6.9 us)
Async XLA Ops:
  0.6 9.3 %copy-start.19 = (f32[32,512]{1,0:T(8,128)S(1)}, f32[32,512]{1,0:T(8,128)}, u32[]{:S(2)}) copy-start(f32[32,512]{1,0:T(8,128)} %constant.118.clone) | copy-start | bytes 196612
  0.6 9.3 %copy-start.20 = (f32[32,12]{0,1:T(8,128)S(1)}, f32[32,12]{0,1:T(8,128)}, u32[]{:S(2)}) copy-start(f32[32,12]{0,1:T(8,128)} %param.30) | copy-start | bytes 4612
  0.7 10.2 %copy-start.23 = (f32[768]{0:T(1024)S(1)}, f32[768]{0:T(1024)}, u32[]{:S(2)}) copy-start(f32[768]{0:T(1024)} %param.28) | copy-start | bytes 9220
  0.7 10.2 %copy-start.24 = (f32[768]{0:T(1024)S(1)}, f32[768]{0:T(1024)}, u32[]{:S(2)}) copy-start(f32[768]{0:T(1024)} %param.29) | copy-start | bytes 9220
  0.7 37.3 %copy-start.8 = (bf16[768,768]{1,0:T(8,128)(2,1)S(1)}, bf16[768,768]{1,0:T(8,128)(2,1)}, u32[]{:S(2)}) copy-start(bf16[768,768]{1,0:T(8,128)(2,1)} %refs_15_.1) | copy-start | bytes 3538948
  2.5 7.3 %collective-permute-start = (bf16[24,768]{1,0:T(8,128)(2,1)S(1)}, bf16[24,768]{1,0:T(8,128)(2,1)S(1)}, u32[]{:S(2)}, u32[]{:S(2)}) collective-permute-start(bf16[24,768]{1,0:T(8,128)(2,1)S(1)} %pad_maximum_fusion.1), channel_id=1, source_target_pairs={{0,1},{1,0},{2,3},{3,2},{4,5},{5,4},{6,7},{7,6},{8,9},{9,8},{10,11... | collective-permute-start | bytes 110600 | tf_op jit(solution)/shard_map/ppermute | solution.py:418
  6.2 28.6 %collective-permute-start.3 = (bf16[256,768]{1,0:T(8,128)(2,1)}, bf16[256,768]{1,0:T(8,128)(2,1)S(1)}, u32[]{:S(2)}, u32[]{:S(2)}) collective-permute-start(bf16[256,768]{1,0:T(8,128)(2,1)} %get-tuple-element.68), channel_id=1, source_target_pairs={{0,0},{1,1},{2,4},{3,5},{4,2},{5,3},{6,6},{7,7},{8,8},{9,9},{10,12... | collective-permute-start | bytes 1179656 | tf_op jit(solution)/shard_map/ppermute | solution.py:418
  8.1 26.7 %collective-permute-start.5 = (bf16[256,768]{1,0:T(8,128)(2,1)}, bf16[256,768]{1,0:T(8,128)(2,1)}, u32[]{:S(2)}, u32[]{:S(2)}) collective-permute-start(bf16[256,768]{1,0:T(8,128)(2,1)} %get-tuple-element.67), channel_id=1, source_target_pairs={{0,1},{1,0},{2,5},{3,4},{4,3},{5,2},{6,7},{7,6},{8,9},{9,8},{10,13... | collective-permute-start | bytes 1179656 | tf_op jit(solution)/shard_map/ppermute | solution.py:418
  9.9 17.9 %collective-permute-start.1 = (bf16[24,768]{1,0:T(8,128)(2,1)S(1)}, bf16[24,768]{1,0:T(8,128)(2,1)S(1)}, u32[]{:S(2)}, u32[]{:S(2)}) collective-permute-start(bf16[24,768]{1,0:T(8,128)(2,1)S(1)} %fusion.18), channel_id=1, source_target_pairs={{0,2},{1,3},{2,0},{3,1},{4,6},{5,7},{6,4},{7,5},{8,10},{9,11},{10,... | collective-permute-start | bytes 110600 | tf_op jit(solution)/shard_map/ppermute | solution.py:418
  10.8 34.2 %copy-start.4 = (f32[1,768]{1,0:T(1,128)}, f32[1,768]{1,0:T(1,128)S(1)}, u32[]{:S(2)}) copy-start(f32[1,768]{1,0:T(1,128)S(1)} %broadcast_in_dim.21.refs_3_.refs_8_.refs_10_) | copy-start | bytes 9220
  12.3 1.4 copy-start.6
  13.7 31.3 %copy-start.7 = (bf16[12,512,128]{2,1,0:T(8,128)(2,1)}, bf16[12,512,128]{2,1,0:T(8,128)(2,1)S(1)}, u32[]{:S(2)}) copy-start(bf16[12,512,128]{2,1,0:T(8,128)(2,1)S(1)} %get-tuple-element.43.refs_15_) | copy-start | bytes 4718596
  27.8 1.3 collective-permute-start.2
  29.1 4.2 %collective-permute-start.7 = (bf16[32,768]{1,0:T(8,128)(2,1)S(1)}, bf16[32,768]{1,0:T(8,128)(2,1)S(1)}, u32[]{:S(2)}, u32[]{:S(2)}) collective-permute-start(bf16[32,768]{1,0:T(8,128)(2,1)S(1)} %maximum_select_fusion.2), channel_id=1, source_target_pairs={{0,8},{1,9},{2,10},{3,11},{4,12},{5,13},{6,14},{7,15},{8,0},{9,1},... | collective-permute-start | bytes 147464 | tf_op jit(solution)/shard_map/ppermute | solution.py:418
  33.2 4.7 %collective-permute-start.8 = (bf16[64,768]{1,0:T(8,128)(2,1)S(1)}, bf16[64,768]{1,0:T(8,128)(2,1)S(1)}, u32[]{:S(2)}, u32[]{:S(2)}) collective-permute-start(bf16[64,768]{1,0:T(8,128)(2,1)S(1)} %maximum_select_fusion.1), channel_id=1, source_target_pairs={{0,16},{1,17},{2,18},{3,19},{4,20},{5,21},{6,22},{7,23},{8,24},{9,... | collective-permute-start | bytes 294920 | tf_op jit(solution)/shard_map/ppermute | solution.py:418
  34.8 14.5 %collective-permute-start.4 = (bf16[256,768]{1,0:T(8,128)(2,1)S(1)}, bf16[256,768]{1,0:T(8,128)(2,1)S(1)}, u32[]{:S(2)}, u32[]{:S(2)}) collective-permute-start(bf16[256,768]{1,0:T(8,128)(2,1)S(1)} %collective-permute-done.3.refs_0_), channel_id=1, source_target_pairs={{0,4},{1,5},{2,6},{3,7},{4,0},{5,1},{6,2},{7,3},{8,12},{9,13},{10,... | collective-permute-start | bytes 1179656 | tf_op jit(solution)/shard_map/ppermute | solution.py:418
  34.8 14.5 %collective-permute-start.6 = (bf16[256,768]{1,0:T(8,128)(2,1)}, bf16[256,768]{1,0:T(8,128)(2,1)S(1)}, u32[]{:S(2)}, u32[]{:S(2)}) collective-permute-start(bf16[256,768]{1,0:T(8,128)(2,1)} %collective-permute-done.5.refs_1_), channel_id=1, source_target_pairs={{0,4},{1,5},{2,6},{3,7},{4,0},{5,1},{6,2},{7,3},{8,12},{9,13},{10,... | collective-permute-start | bytes 1179656 | tf_op jit(solution)/shard_map/ppermute | solution.py:418
  35.4 9.6 %copy-start.5 = (s32[4]{0:T(128)}, s32[4]{0:T(128)S(1)}, u32[]{:S(2)}) copy-start(s32[4]{0:T(128)S(1)} %pad_add_fusion.sc_ref) | copy-start | bytes 52
  38.0 1.3 copy-start.9
  39.2 1.3 copy-start.10
  40.5 4.5 %copy-start.3 = (bf16[128,768]{1,0:T(8,128)(2,1)}, bf16[128,768]{1,0:T(8,128)(2,1)S(1)}, u32[]{:S(2)}) copy-start(bf16[128,768]{1,0:T(8,128)(2,1)S(1)} %maximum_select_fusion.refs_2_.refs_9_) | copy-start | bytes 589828
  40.5 8.8 %copy-start.17 = (bf16[2,256,768]{2,1,0:T(8,128)(2,1)S(1)}, bf16[2,256,768]{2,1,0:T(8,128)(2,1)}, u32[]{:S(2)}) copy-start(bf16[2,256,768]{2,1,0:T(8,128)(2,1)} %param.21) | copy-start | bytes 2359300
  45.1 0.9 copy-start.11
  46.0 0.9 copy-start.12
  46.8 0.9 copy-start.13
  47.7 0.9 copy-start.14
  49.3 6.3 %copy-start.16 = (bf16[128,768]{1,0:T(8,128)(2,1)}, bf16[128,768]{1,0:T(8,128)(2,1)S(1)}, u32[]{:S(2)}) copy-start(bf16[128,768]{1,0:T(8,128)(2,1)S(1)} %get-tuple-element.40.refs_6_) | copy-start | bytes 589828
  49.3 6.3 %copy-start.25 = (bf16[256,768]{1,0:T(8,128)(2,1)}, bf16[256,768]{1,0:T(8,128)(2,1)S(1)}, u32[]{:S(2)}) copy-start(bf16[256,768]{1,0:T(8,128)(2,1)S(1)} %collective-permute-done.4.refs_0_) | copy-start | bytes 1179652
  49.3 6.3 %copy-start.26 = (bf16[256,768]{1,0:T(8,128)(2,1)}, bf16[256,768]{1,0:T(8,128)(2,1)S(1)}, u32[]{:S(2)}) copy-start(bf16[256,768]{1,0:T(8,128)(2,1)S(1)} %collective-permute-done.6.refs_1_) | copy-start | bytes 1179652
  49.4 42.0 %collective-permute-start.11 = (bf16[256,768]{1,0:T(8,128)(2,1)S(1)}, bf16[256,768]{1,0:T(8,128)(2,1)S(1)}, u32[]{:S(2)}, u32[]{:S(2)}) collective-permute-start(bf16[256,768]{1,0:T(8,128)(2,1)S(1)} %get-tuple-element.62), channel_id=1, source_target_pairs={{0,0},{1,1},{2,4},{3,5},{4,2},{5,3},{6,6},{7,7},{8,8},{9,9},{10,12... | collective-permute-start | bytes 1179656 | tf_op jit(solution)/shard_map/ppermute | solution.py:418
  52.3 39.1 %collective-permute-start.12 = (bf16[256,768]{1,0:T(8,128)(2,1)S(1)}, bf16[256,768]{1,0:T(8,128)(2,1)S(1)}, u32[]{:S(2)}, u32[]{:S(2)}) collective-permute-start(bf16[256,768]{1,0:T(8,128)(2,1)S(1)} %get-tuple-element.61), channel_id=1, source_target_pairs={{0,1},{1,0},{2,5},{3,4},{4,3},{5,2},{6,7},{7,6},{8,9},{9,8},{10,13... | collective-permute-start | bytes 1179656 | tf_op jit(solution)/shard_map/ppermute | solution.py:418
  91.4 1.0 copy-start.27
  92.4 42.8 %copy-start.1 = (bf16[512,3072]{1,0:T(8,128)(2,1)S(1)}, bf16[512,3072]{1,0:T(8,128)(2,1)}, u32[]{:S(2)}) copy-start(bf16[512,3072]{1,0:T(8,128)(2,1)} %get-tuple-element.44.act_ref.refs_2_) | copy-start | bytes 9437188
  124.4 1.4 collective-permute-start.13
  126.9 4.2 %collective-permute-start.14 = (bf16[2,16,768]{2,1,0:T(8,128)(2,1)S(1)}, bf16[2,16,768]{2,1,0:T(8,128)(2,1)S(1)}, u32[]{:S(2)}, u32[]{:S(2)}) collective-permute-start(bf16[2,16,768]{2,1,0:T(8,128)(2,1)S(1)} %fusion.4), channel_id=1, source_target_pairs={{0,8},{1,9},{2,10},{3,11},{4,12},{5,13},{6,14},{7,15},{8,0},{9,1},... | collective-permute-start | bytes 147464 | tf_op jit(solution)/shard_map/ppermute | solution.py:418
  131.1 3.9 %collective-permute-start.15 = (bf16[1,16,768]{2,1,0:T(8,128)(2,1)S(1)}, bf16[1,16,768]{2,1,0:T(8,128)(2,1)S(1)}, u32[]{:S(2)}, u32[]{:S(2)}) collective-permute-start(bf16[1,16,768]{2,1,0:T(8,128)(2,1)S(1)} %fusion.6), channel_id=1, source_target_pairs={{0,16},{1,17},{2,18},{3,19},{4,20},{5,21},{6,22},{7,23},{8,24},{9,... | collective-permute-start | bytes 73736 | tf_op jit(solution)/shard_map/ppermute | solution.py:418
  135.0 6.9 %collective-permute-start.16 = (bf16[16,768]{1,0:T(8,128)(2,1)S(1)}, bf16[16,768]{1,0:T(8,128)(2,1)S(1)}, u32[]{:S(2)}, u32[]{:S(2)}) collective-permute-start(bf16[16,768]{1,0:T(8,128)(2,1)S(1)} %get-tuple-element.59), channel_id=1, source_target_pairs={{0,1},{1,0},{2,3},{3,2},{4,5},{5,4},{6,7},{7,6},{8,9},{9,8},{10,11... | collective-permute-start | bytes 73736 | tf_op jit(solution)/shard_map/ppermute | solution.py:418
  135.1 2.3 %copy-start = (bf16[3072,768]{1,0:T(8,128)(2,1)S(1)}, bf16[3072,768]{1,0:T(8,128)(2,1)}, u32[]{:S(2)}) copy-start(bf16[3072,768]{1,0:T(8,128)(2,1)} %refs_12_.3) | copy-start | bytes 14155780
  137.5 1.4 copy-start.2
  141.9 6.3 %collective-permute-start.17 = (bf16[16,768]{1,0:T(8,128)(2,1)S(1)}, bf16[16,768]{1,0:T(8,128)(2,1)S(1)}, u32[]{:S(2)}, u32[]{:S(2)}) collective-permute-start(bf16[16,768]{1,0:T(8,128)(2,1)S(1)} %fusion.5), channel_id=1, source_target_pairs={{0,2},{1,3},{2,0},{3,1},{4,6},{5,7},{6,4},{7,5},{8,10},{9,11},{10,... | collective-permute-start | bytes 73736 | tf_op jit(solution)/shard_map/ppermute | solution.py:418
  143.5 28.4 %copy-start.18 = (f32[16,192]{1,0:T(8,128)S(1)}, f32[16,192]{1,0:T(8,128)}, u32[]{:S(2)}) copy-start(f32[16,192]{1,0:T(8,128)} %param.31) | copy-start | bytes 36868
  143.5 28.4 %copy-start.21 = (f32[16,192]{1,0:T(8,128)S(1)}, f32[16,192]{1,0:T(8,128)}, u32[]{:S(2)}) copy-start(f32[16,192]{1,0:T(8,128)} %param.32) | copy-start | bytes 36868
  143.5 28.4 %copy-start.22 = (f32[16,192]{1,0:T(8,128)S(1)}, f32[16,192]{1,0:T(8,128)}, u32[]{:S(2)}) copy-start(f32[16,192]{1,0:T(8,128)} %param.33) | copy-start | bytes 36868
  143.5 15.8 %collective-permute-start.10 = (bf16[256,768]{1,0:T(8,128)(2,1)S(1)}, bf16[256,768]{1,0:T(8,128)(2,1)S(1)}, u32[]{:S(2)}, u32[]{:S(2)}) collective-permute-start(bf16[256,768]{1,0:T(8,128)(2,1)S(1)} %get-tuple-element.65), channel_id=1, source_target_pairs={{0,0},{1,1},{2,4},{3,5},{4,2},{5,3},{6,6},{7,7},{8,8},{9,9},{10,12... | collective-permute-start | bytes 1179656 | tf_op jit(solution)/shard_map/ppermute | solution.py:418
  145.6 20.7 %collective-permute-start.9 = (bf16[256,768]{1,0:T(8,128)(2,1)S(1)}, bf16[256,768]{1,0:T(8,128)(2,1)S(1)}, u32[]{:S(2)}, u32[]{:S(2)}) collective-permute-start(bf16[256,768]{1,0:T(8,128)(2,1)S(1)} %get-tuple-element.66), channel_id=1, source_target_pairs={{0,1},{1,0},{2,5},{3,4},{4,3},{5,2},{6,7},{7,6},{8,9},{9,8},{10,13... | collective-permute-start | bytes 1179656 | tf_op jit(solution)/shard_map/ppermute | solution.py:418
  149.5 1.2 collective-permute-start.18
  151.4 14.9 %collective-permute-start.19 = (f32[8,128]{1,0:T(8,128)S(1)}, f32[8,128]{1,0:T(8,128)S(1)}, u32[]{:S(2)}, u32[]{:S(2)}) collective-permute-start(f32[8,128]{1,0:T(8,128)S(1)} %broadcast_add_fusion), channel_id=1, source_target_pairs={{0,8},{1,9},{2,10},{3,11},{4,12},{5,13},{6,14},{7,15},{8,0},{9,1},... | collective-permute-start | bytes 12296 | tf_op jit(solution)/shard_map/ppermute | solution.py:418
  167.0 3.7 %collective-permute-start.20 = (f32[8,128]{1,0:T(8,128)S(1)}, f32[8,128]{1,0:T(8,128)S(1)}, u32[]{:S(2)}, u32[]{:S(2)}) collective-permute-start(f32[8,128]{1,0:T(8,128)S(1)} %fusion.17), channel_id=1, source_target_pairs={{0,16},{1,17},{2,18},{3,19},{4,20},{5,21},{6,22},{7,23},{8,24},{9,... | collective-permute-start | bytes 12296 | tf_op jit(solution)/shard_map/ppermute | solution.py:418
  (2 other events, 1.5 us)

commit v2 on v1

--- a/solution.py
+++ b/solution.py
@@ -27,6 +27,7 @@
 MASKED = -float(2**30)
 AXES = ("dp", "ctx")
 MIB = 1 << 20
+A_MIB, F_MIB, B_MIB = 6, 12, 13
 
 
 def bucket_table(offset):
@@ -77,6 +78,18 @@
 
 def out(shape, dtype):
     return jax.ShapeDtypeStruct(shape, dtype)
+
+
+def held(shape, dtype):
+    return pltpu.VMEM(shape, dtype)
+
+
+def in_vmem(value):
+    return pltpu.with_memory_space_constraint(value, pltpu.VMEM)
+
+
+def in_hbm(value):
+    return pltpu.with_memory_space_constraint(value, pltpu.HBM)
 
 
 def params(mib):
@@ -96,7 +109,38 @@
     return picked
 
 
-def bias_kernel(base_ref, tile_ref, table_ref):
+def slot_of(index, count):
+    return lax.rem(index + 2 * count, count)
+
+
+def pack_kernel(count, tokens_ref, seg_ref, prompt_ref, *refs):
+    pieces, (block_ref, wide_ref, sems) = refs[:count], refs[count:]
+    ctx = lax.axis_index("ctx")
+    copies = [
+        pltpu.make_async_copy(tokens_ref.at[slot_of(ctx + k, count)], pieces[k], sems.at[k]) for k in range(count)
+    ]
+    for copy in copies:
+        copy.start()
+    rows = prompt_ref.shape[0]
+    wide_ref[...] = jnp.zeros_like(wide_ref)
+    wide_ref[0:rows, :] = prompt_ref[...]
+    for n in range(2):
+        tally = jnp.sum((seg_ref[...] <= n).astype(f32), axis=1, keepdims=True)
+        wide_ref[rows + n * count : rows + (n + 1) * count, :] = jnp.broadcast_to(tally, (count, prompt_ref.shape[1]))
+    block_ref[...] = wide_ref[...].astype(bf16)
+    for copy in copies:
+        copy.wait()
+
+
+def prepare_kernel(count, base_ref, cot_ref, *refs):
+    weights, (tile_ref, table_ref) = refs[:6], refs[6:8]
+    pieces, kept, sems = refs[8 : 8 + count], refs[8 + count : 14 + count], refs[14 + count]
+    ctx = lax.axis_index("ctx")
+    copies = [pltpu.make_async_copy(weights[n], kept[n], sems.at[n]) for n in range(6)] + [
+        pltpu.make_async_copy(cot_ref.at[slot_of(ctx + k, count)], pieces[k], sems.at[6 + k]) for k in range(count)
+    ]
+    for copy in copies:
+        copy.start()
     heads = tile_ref.shape[0]
     for h in range(heads):
         row = jnp.broadcast_to(base_ref[h : h + 1, :], (BLK, 4 * BLK))
@@ -111,13 +155,33 @@
         table_ref[h, BLK : 2 * BLK, :] = low_high
         table_ref[h, 2 * BLK : 3 * BLK, :] = mid_low
         table_ref[h, 3 * BLK : 4 * BLK, :] = low_low
-
-
-def first_kernel(count, piece, sc_ref, *refs):
-    pieces = refs[:count]
-    (prompt_ref, gain_ref, wq_ref, wk_ref, wv_ref, hid_ref, q_ref, k_ref, v_ref, kp_ref, vp_ref, norm_ref) = refs[count:]
-    half, turn, first, second = (sc_ref[n] for n in range(4))
+    for copy in copies:
+        copy.wait()
+
+
+def places(count):
+    return lax.rem(lax.axis_index("dp"), 2), lax.rem(lax.axis_index("ctx"), count)
+
+
+def first_kernel(count, piece, rows_own, *refs):
+    own = refs[:count]
+    (
+        block_ref, other_ref, prompt_ref, gain_ref, wq_ref, wk_ref, wv_ref,
+        marks_ref, hid_ref, q_ref, kall_ref, vall_ref, norm_ref,
+    ) = refs[count:]
+    half, turn = places(count)
     half_len = count * piece
+    width = q_ref.shape[1]
+    mine = lax.div(lax.axis_index("ctx"), count) == half
+    line = jnp.where(mine, block_ref[...], other_ref[...]).astype(f32)
+    line_row = lax.broadcasted_iota(i32, (line.shape[0], 1), 0)
+    marks = []
+    for n in range(2):
+        tally = jnp.where(line_row == rows_own + n * count + turn, line, 0.0)
+        tally = jnp.sum(jnp.sum(tally, axis=1, keepdims=True), axis=0, keepdims=True)
+        marks.append((tally * (1.0 / (width // lax.axis_size("ctx"))) + 0.5).astype(i32))
+        marks_ref[n : n + 1, :] = jnp.broadcast_to(marks[n], (1, BLK))
+    first, second = marks
     gain = gain_ref[...]
     slots = lax.broadcasted_iota(i32, (1, BLK), 1)
     for j in range(count):
@@ -127,40 +191,38 @@
         shown = inside < PROMPT
         choose = jnp.where((inside == slots) & shown, 1.0, 0.0).astype(bf16)
         picked = dot_nn(choose, prompt_ref[...])
-        hidden = jnp.where(shown, picked, pick_piece(pieces, turn, j).astype(f32))
+        hidden = jnp.where(shown, picked, pick_piece(own, turn, j).astype(f32))
         hid_ref[rows, :] = hidden.astype(bf16)
         norm_ref[rows, :] = (hidden * inv_rms(hidden) * gain).astype(bf16)
     hidden = prompt_ref[...].astype(f32)
-    norm_ref[half_len : half_len + BLK, :] = (hidden * inv_rms(hidden) * gain).astype(bf16)
+    norm_ref[half_len:, :] = (hidden * inv_rms(hidden) * gain).astype(bf16)
     wide = 2 * BLK
 
-    @pl.loop(0, wq_ref.shape[1] // wide)
+    @pl.loop(0, width // wide)
     def _(t):
         cols = pl.ds(pl.multiple_of(t * wide, wide), wide)
         q_ref[:, cols] = dot_nn(norm_ref[0:half_len, :], wq_ref[:, cols]).astype(bf16)
-        keys = dot_nn(norm_ref[...], wk_ref[:, cols]).astype(bf16)
-        k_ref[:, cols] = keys[:half_len]
-        kp_ref[:, cols] = keys[half_len:]
-        vals = dot_nn(norm_ref[...], wv_ref[:, cols]).astype(bf16)
-        v_ref[:, cols] = vals[:half_len]
-        vp_ref[:, cols] = vals[half_len:]
-
-
-def forward_kernel(count, piece, sc_ref, tab_ref, *refs):
-    pieces = refs[:count]
+        for all_ref, weight_ref in ((kall_ref, wk_ref), (vall_ref, wv_ref)):
+            made = dot_nn(norm_ref[...], weight_ref[:, cols]).astype(bf16)
+            all_ref[0:half_len, cols] = made[:half_len]
+            all_ref[2 * half_len :, cols] = made[half_len:]
+
+
+def forward_kernel(count, piece, tab_ref, *refs):
+    partner = refs[:count]
     (
-        q_ref, k_ref, v_ref, kp_ref, vp_ref, hid_ref, gain_first_ref, gain_second_ref, wk_ref, wv_ref, wo_ref, wi_ref,
-        tile_ref, table_ref,
-        e_ref, kall_ref, vall_ref, mixed_ref, inv_ref, after_ref, act_ref,
-        norm_ref, e_buf, sems,
-    ) = refs[count:]
-    half, turn, first, second = (sc_ref[n] for n in range(4))
+        marks_ref, q_ref, hid_ref, kown_ref, vown_ref, gain_first_ref, gain_second_ref, wk_ref, wv_ref, wo_ref, wi_ref,
+        wout_ref, tile_ref, table_ref,
+    ) = refs[count : count + 14]
+    e_ref, kall_ref, vall_ref, mixed_ref, inv_ref, after_ref, act_ref = refs[count + 14 : count + 21]
+    going, (norm_ref, e_buf, sems) = refs[count + 21 : 2 * count + 21], refs[2 * count + 21 :]
+    half, turn = places(count)
+    first, second = marks_ref[0:1, 0:1], marks_ref[1:2, 0:1]
     half_len = count * piece
     width = q_ref.shape[1]
-    keys_all = 2 * half_len + BLK
     gain = gain_first_ref[...]
     for j in range(count):
-        tok = pick_piece(pieces, turn, j).astype(f32)
+        tok = pick_piece(partner, turn, j).astype(f32)
         norm_ref[j * piece : (j + 1) * piece, :] = (tok * inv_rms(tok) * gain).astype(bf16)
     wide = 2 * BLK
 
@@ -169,10 +231,6 @@
         cols = pl.ds(pl.multiple_of(t * wide, wide), wide)
         kall_ref[half_len : 2 * half_len, cols] = dot_nn(norm_ref[...], wk_ref[:, cols]).astype(bf16)
         vall_ref[half_len : 2 * half_len, cols] = dot_nn(norm_ref[...], wv_ref[:, cols]).astype(bf16)
-        kall_ref[0:half_len, cols] = k_ref[:, cols]
-        vall_ref[0:half_len, cols] = v_ref[:, cols]
-        kall_ref[2 * half_len :, cols] = kp_ref[:, cols]
-        vall_ref[2 * half_len :, cols] = vp_ref[:, cols]
 
     lane = lax.broadcasted_iota(i32, (1, PAIR), 1)
     low_lane = lane < HEAD
@@ -200,16 +258,15 @@
     blocks = half_len // BLK
     per = QROWS // BLK
 
-    def e_copy(hp, at):
-        return pltpu.make_async_copy(e_buf.at[at], e_ref.at[pl.ds(2 * hp, 2)], sems.at[at])
+    def e_copy(hp):
+        at = lax.rem(hp, 2)
+        return pltpu.make_async_copy(e_buf.at[at], e_ref.at[hp], sems.at[at])
 
     @pl.loop(0, width // PAIR)
     def _(hp):
-        at = lax.rem(hp, 2)
-
         @pl.when(hp >= 2)
         def _():
-            e_copy(hp - 2, at).wait()
+            e_copy(hp - 2).wait()
 
         cols = pl.ds(pl.multiple_of(hp * PAIR, PAIR), PAIR)
         q_pair, k_pair, v_pair = q_ref[:, cols], kall_ref[:, cols], vall_ref[:, cols]
@@ -274,17 +331,14 @@
                         )
                     )
                 raised = jnp.concatenate(e_rows, axis=0)
-                e_buf[at, s, qrows, :] = raised
+                e_buf[lax.rem(hp, 2), s, qrows, :] = raised
                 head_rows.append(dot_nn(raised, v_e))
             results.append(jnp.concatenate(head_rows, axis=0))
         sums = pltpu.roll(jnp.where(low_lane, results[1], results[0]), HEAD, 1)
         inv = 1.0 / sums
         inv_ref[:, cols] = inv
         mixed_ref[:, cols] = (jnp.where(low_lane, results[0], results[1]) * inv).astype(bf16)
-        e_copy(hp, at).start()
-
-    for rest in range(2):
-        e_copy(width // PAIR - 2 + rest, rest).wait()
+        e_copy(hp).start()
 
     @pl.loop(0, half_len // BLK)
     def _(t):
@@ -298,20 +352,42 @@
         cols = pl.ds(pl.multiple_of(t * wide, wide), wide)
         act_ref[:, cols] = jnp.maximum(dot_nn(norm_ref[...], wi_ref[:, cols]), 0.0).astype(bf16)
 
-
-def backward_kernel(count, piece, sc_ref, *refs):
+    @pl.loop(0, width // wide)
+    def _(t):
+        cols = pl.ds(pl.multiple_of(t * wide, wide), wide)
+        made = (after_ref[:, cols] + dot_nn(act_ref[...], wout_ref[:, cols])).astype(bf16)
+        made = [made[j * piece : (j + 1) * piece] for j in range(count)]
+        for k in range(count):
+            place = slot_of(turn - k, count)
+            sent = made[0]
+            for j in range(1, count):
+                sent = jnp.where(place == j, made[j], sent)
+            going[k][:, cols] = sent
+
+    for hp in range(width // PAIR - 2, width // PAIR):
+        e_copy(hp).wait()
+
+
+def backward_kernel(count, piece, *refs):
     cots = refs[:count]
     (
-        act_ref, after_ref, mixed_ref, inv_ref, q_ref, kall_ref, vall_ref, prompt_ref, gain_first_ref, gain_second_ref,
-        wout_ref, wi_ref, wo_ref, wq_ref, wk_ref, wv_ref, e_hbm,
+        marks_ref, act_ref, after_ref, mixed_ref, inv_ref, q_ref, kall_ref, vall_ref, prompt_ref, gain_first_ref, gain_second_ref,
+        wout_ref, wi_ref, wo_ref, wq_ref, wk_ref, wv_ref, e_ref,
         grad_ref,
-        e_ref, cot_ref, acc_ref, do_ref, delta_ref, dq_ref, gk_ref, gv_ref, sem,
+        cot_ref, acc_ref, do_ref, dq_ref, gk_ref, gv_ref, e_buf, sems,
     ) = refs[count:]
-    fetch = pltpu.make_async_copy(e_hbm, e_ref, sem)
-    fetch.start()
-    half, turn, first, second = (sc_ref[n] for n in range(4))
+    half, turn = places(count)
+    first, second = marks_ref[0:1, 0:1], marks_ref[1:2, 0:1]
     half_len = count * piece
     width = q_ref.shape[1]
+    pairs = width // PAIR
+
+    def e_copy(hp):
+        at = lax.rem(hp, 2)
+        return pltpu.make_async_copy(e_ref.at[hp], e_buf.at[at], sems.at[at])
+
+    for hp in range(2):
+        e_copy(hp).start()
     for j in range(count):
         cot_ref[j * piece : (j + 1) * piece, :] = pick_piece(cots, turn, j)
     wide = 4 * BLK
@@ -338,13 +414,13 @@
         grad_mixed = dot_nt(grad_after.astype(bf16), wo_ref[...])
         do_ref[rows, :] = (grad_mixed * inv_ref[rows, :]).astype(bf16)
 
-    fetch.wait()
     lane = lax.broadcasted_iota(i32, (1, PAIR), 1)
     low_lane = lane < HEAD
     lane_at = lax.rem(lane, HEAD)
 
     @pl.loop(0, width // PAIR)
     def _(hp):
+        e_copy(hp).wait()
         cols = pl.ds(pl.multiple_of(hp * PAIR, PAIR), PAIR)
         q_pair, k_pair, v_pair, do_pair = q_ref[:, cols], kall_ref[:, cols], vall_ref[:, cols], do_ref[:, cols]
         inner = do_pair.astype(f32) * mixed_ref[:, cols].astype(f32)
@@ -359,7 +435,7 @@
             dq, dk, dv = [], None, None
             for qt in range(half_len // QROWS):
                 qrows = slice(qt * QROWS, (qt + 1) * QROWS)
-                raised = e_ref[2 * hp + s, qrows, :]
+                raised = e_buf[lax.rem(hp, 2), s, qrows, :]
                 grad_probs = dot_nt(do_e[qrows], v_e)
                 grad_scores = (raised.astype(f32) * grad_probs).astype(bf16)
                 dq.append(dot_nn(grad_scores, k_pair))
@@ -374,6 +450,10 @@
         gk_ref[:, cols] = jnp.where(low_lane, dks[0], dks[1]).astype(bf16)
         gv_ref[:, cols] = jnp.where(low_lane, dvs[0], dvs[1]).astype(bf16)
 
+        @pl.when(hp + 2 < pairs)
+        def _():
+            e_copy(hp + 2).start()
+
     spot = lax.broadcasted_iota(i32, (1, half_len), 1)
     inside = segment_of(half * half_len + spot, first, second)[1]
     slots = lax.broadcasted_iota(i32, (BLK, 1), 0)
@@ -389,15 +469,6 @@
     grad_ref[...] = direct + scale * pulled - hidden * (scale * scale * scale * along)
 
 
-def output_kernel(act_ref, after_ref, wout_ref, out_ref):
-    wide = 2 * BLK
-
-    @pl.loop(0, out_ref.shape[1] // wide)
-    def _(t):
-        cols = pl.ds(pl.multiple_of(t * wide, wide), wide)
-        out_ref[:, cols] = (after_ref[:, cols] + dot_nn(act_ref[...], wout_ref[:, cols])).astype(bf16)
-
-
 def on_device(
     sizes, tokens, segment_ids, prompt_slots, cotangent, w_query, w_key, w_value, w_output, w_inner, w_outer,
     gain_first, gain_second, bias_table, prompt, first_moment, second_moment,
@@ -407,7 +478,7 @@
     half_len = count * piece
     heads = bias_table.shape[1]
     dp, ctx = lax.axis_index("dp"), lax.axis_index("ctx")
-    core, turn = lax.rem(dp, 2), lax.rem(ctx, count)
+    core = lax.rem(dp, 2)
 
     def permute(value, target):
         pairs = []
@@ -426,162 +497,149 @@
     def there(k):
         return lambda d, z: (2 * (d // 2) + z // count, (d % 2) * count + (z + k) % count)
 
-    def send_pieces(rows):
-        return [
-            permute(lax.dynamic_index_in_dim(rows, lax.rem(ctx + k, count), keepdims=False), there(k))
-            for k in range(count)
-        ]
-
-    own = send_pieces(tokens)
-    partner = [swap_dp(piece_rows, 1) for piece_rows in own]
-    cot_rows, partner = lax.optimization_barrier((cotangent, partner))
-    cots = send_pieces(cot_rows)
+    def in_order(parts, me, axis):
+        ordered = []
+        for place in range(len(parts)):
+            picked = parts[0]
+            for n in range(1, len(parts)):
+                picked = jnp.where((me ^ n) == place, parts[n], picked)
+            ordered.append(picked)
+        return jnp.concatenate(ordered, axis=axis)
 
     rows_own, cols_own = prompt.shape
-    tallies = jnp.concatenate(
-        [jnp.sum((segment_ids <= n).astype(f32), axis=1) for n in range(2)]
-    )
-    tally_row = jnp.zeros((8, cols_own), f32).at[0, : 2 * count].set(tallies)
-    block = jnp.concatenate([prompt, tally_row], axis=0).astype(bf16)
-    block = jnp.concatenate([jnp.where(ctx == n, block, 0) for n in range(n_ctx)], axis=1)
-    bit = 1
-    while bit < n_ctx:
-        block = block + swap_ctx(block, bit)
-        bit *= 2
+    piece_like = held((piece, width), bf16)
+    packed = pl.pallas_call(
+        functools.partial(pack_kernel, count),
+        out_shape=[piece_like] * count + [held((rows_own + 8, cols_own), bf16)],
+        in_specs=[any_spec(), vmem_spec(), vmem_spec()],
+        out_specs=[vmem_spec()] * (count + 1),
+        scratch_shapes=[pltpu.VMEM((rows_own + 8, cols_own), f32), pltpu.SemaphoreType.DMA((count,))],
+        compiler_params=params(4),
+        cost_estimate=cost(1e5, 2e6),
+    )(in_hbm(tokens), segment_ids, prompt)
+
+    block = packed[count]
+    blocks = [block] + [swap_ctx(block, n) for n in range(1, n_ctx)]
+    own = [permute(packed[k], there(k)) for k in range(count)]
+    block = in_order(blocks, ctx, 1)
     other = swap_dp(block, 1)
-
-    def joined(mine, theirs, up):
-        return jnp.where(up, jnp.concatenate([theirs, mine], 0), jnp.concatenate([mine, theirs], 0))
-
-    tally_mine, tally_theirs = (
-        jnp.sum(b[rows_own].astype(f32).reshape(n_ctx, cols_own)[:, : 2 * count], axis=0).reshape(2, count)
-        for b in (block, other)
-    )
-    tally = jnp.where(ctx // count == core, tally_mine, tally_theirs)
-    marks = lax.dynamic_index_in_dim(tally, turn, axis=1, keepdims=False).astype(i32)
-    scalars = jnp.concatenate([jnp.stack([core, turn]).astype(i32), marks])
-    sent = joined(block[:rows_own], other[:rows_own], core == 1)
-    bit = 2
-    while bit < n_dp:
-        sent = joined(sent, swap_dp(sent, bit), (dp & bit) != 0)
-        bit *= 2
+    chip_rows = in_order([block[:rows_own], other[:rows_own]], core, 0)
+    sent = in_order([chip_rows] + [swap_dp(chip_rows, 2 * n) for n in range(1, n_dp // 2)], dp // 2, 0)
 
     choose = (np.arange(bias_table.shape[0])[:, None] == bucket_table(np.arange(4 * BLK) - 2 * BLK)[None]).astype(np.float32)
     base = lax.dot_general(
         bias_table, jnp.asarray(choose), (((0,), (0,)), ((), ())), precision=lax.Precision.HIGHEST
     )
-    tiles, table = pl.pallas_call(
-        bias_kernel,
-        out_shape=(out((heads, 3, BLK, BLK), f32), out((heads, 4 * BLK, BLK), bf16)),
-        compiler_params=params(24),
-        cost_estimate=cost(1e6, 4e6),
-    )(base)
+    weights = (w_query, w_key, w_value, w_output, w_inner, w_outer)
+    prepared = pl.pallas_call(
+        functools.partial(prepare_kernel, count),
+        out_shape=[held((heads, 3, BLK, BLK), f32), held((heads, 4 * BLK, BLK), bf16)]
+        + [piece_like] * count
+        + [held(w.shape, bf16) for w in weights],
+        in_specs=[vmem_spec()] + [any_spec()] * 7,
+        out_specs=[vmem_spec()] * (8 + count),
+        scratch_shapes=[pltpu.SemaphoreType.DMA((6 + count,))],
+        compiler_params=params(4),
+        cost_estimate=cost(1e6, 1.5e7),
+    )(base, in_hbm(cotangent), *[in_hbm(w) for w in weights])
+    tiles, table = prepared[:2]
+    cot_pieces = prepared[2 : 2 + count]
+    w_q, w_k, w_v, w_o, w_i, w_out = prepared[2 + count :]
 
     gain_1, gain_2 = gain_first[None], gain_second[None]
-    act_like = out((half_len, width), bf16)
-    pair_like = out((BLK, width), bf16)
-    hid, q, k, v, kp, vp = pl.pallas_call(
-        functools.partial(first_kernel, count, piece),
-        out_shape=(act_like, act_like, act_like, act_like, pair_like, pair_like),
-        in_specs=[smem_spec()] + [vmem_spec()] * (count + 5),
-        out_specs=[vmem_spec()] * 6,
-        scratch_shapes=[pltpu.VMEM((half_len + BLK, width), bf16)],
-        compiler_params=params(32),
-        cost_estimate=cost(6 * half_len * width * width, 8e6),
-    )(scalars, *own, sent, gain_1, w_query, w_key, w_value)
-
     keys_all = 2 * half_len + BLK
     hidden_ff = w_inner.shape[1]
-    e, kall, vall, mixed, inv, after, act = pl.pallas_call(
+    partner = [swap_dp(piece_rows, 1) for piece_rows in own]
+    marks, hid, q, kall, vall = pl.pallas_call(
+        functools.partial(first_kernel, count, piece, rows_own),
+        out_shape=[
+            held((8, BLK), i32),
+            held((half_len, width), bf16),
+            held((half_len, width), bf16),
+            held((keys_all, width), bf16),
+            held((keys_all, width), bf16),
+        ],
+        in_specs=[vmem_spec()] * (count + 7),
+        out_specs=[vmem_spec()] * 5,
+        scratch_shapes=[pltpu.VMEM((half_len + BLK, width), bf16)],
+        compiler_params=params(A_MIB),
+        cost_estimate=cost(6 * half_len * width * width, 8e6),
+    )(*own, block, other, sent, gain_1, w_q, w_k, w_v)
+
+    cot_pieces, q = lax.optimization_barrier((cot_pieces, q))
+    cots = [permute(cot_pieces[k], there(k)) for k in range(count)]
+
+    made = pl.pallas_call(
         functools.partial(forward_kernel, count, piece),
-        out_shape=(
-            out((heads, half_len, keys_all), bf16),
-            out((keys_all, width), bf16),
-            out((keys_all, width), bf16),
-            act_like,
-            out((half_len, width), f32),
-            out((half_len, width), f32),
-            out((half_len, hidden_ff), bf16),
-        ),
-        in_specs=[smem_spec(), smem_spec()] + [vmem_spec()] * (count + 14),
-        out_specs=[any_spec()] + [vmem_spec()] * 6,
+        out_shape=[
+            pltpu.HBM((heads // 2, 2, half_len, keys_all), bf16),
+            held((keys_all, width), bf16),
+            held((keys_all, width), bf16),
+            held((half_len, width), bf16),
+            held((half_len, width), f32),
+            held((half_len, width), f32),
+            held((half_len, hidden_ff), bf16),
+        ]
+        + [piece_like] * count,
+        in_specs=[smem_spec()] + [vmem_spec()] * (count + 14),
+        out_specs=[any_spec()] + [vmem_spec()] * (6 + count),
         scratch_shapes=[
             pltpu.VMEM((half_len, width), bf16),
             pltpu.VMEM((2, 2, half_len, keys_all), bf16),
             pltpu.SemaphoreType.DMA((2,)),
         ],
-        compiler_params=params(56),
+        input_output_aliases={count + 4: 1, count + 5: 2},
+        compiler_params=params(F_MIB),
         cost_estimate=cost(3e10, 4e7, heads * half_len * keys_all),
     )(
-        scalars, bias_table, *partner, q, k, v, kp, vp, hid, gain_1, gain_2, w_key, w_value, w_output, w_inner, tiles,
-        table,
+        bias_table, *partner, marks, q, hid, kall, vall, gain_1, gain_2, w_k, w_v, w_o, w_i, w_out, tiles, table,
     )
+    e, kall, vall, mixed, inv, after, act = made[:7]
+    got = [permute(made[7 + k], back_of(count, k)) for k in range(count)]
 
     grad = pl.pallas_call(
         functools.partial(backward_kernel, count, piece),
-        out_shape=out((BLK, width), f32),
-        in_specs=[smem_spec()] + [vmem_spec()] * (count + 16) + [any_spec()],
+        out_shape=held((BLK, width), f32),
+        in_specs=[vmem_spec()] * (count + 17) + [any_spec()],
         out_specs=vmem_spec(),
         scratch_shapes=[
-            pltpu.VMEM((heads, half_len, keys_all), bf16),
             pltpu.VMEM((half_len, width), bf16),
             pltpu.VMEM((half_len, width), f32),
             pltpu.VMEM((half_len, width), bf16),
-            pltpu.VMEM((8, BLK), f32),
             pltpu.VMEM((half_len, width), bf16),
             pltpu.VMEM((BLK, width), bf16),
             pltpu.VMEM((BLK, width), bf16),
-            pltpu.SemaphoreType.DMA,
+            pltpu.VMEM((2, 2, half_len, keys_all), bf16),
+            pltpu.SemaphoreType.DMA((2,)),
         ],
-        compiler_params=params(60),
+        compiler_params=params(B_MIB),
         cost_estimate=cost(3e10, 4e7),
     )(
-        scalars, *cots, act, after, mixed, inv, q, kall, vall, sent, gain_1, gain_2, w_outer, w_inner, w_output, w_query,
-        w_key, w_value, e,
+        *cots, marks, act, after, mixed, inv, q, kall, vall, sent, gain_1, gain_2, w_out, w_i, w_o, w_q, w_k, w_v, in_hbm(e),
     )
 
-    rows_out = pl.pallas_call(
-        output_kernel,
-        out_shape=act_like,
-        compiler_params=params(32),
-        cost_estimate=cost(2 * half_len * width * hidden_ff, 1e7),
-    )(act, after, w_outer)
-
-    halves = rows_out.reshape(count, piece, width)
-    got = [
-        permute(lax.dynamic_index_in_dim(halves, lax.rem(turn - k + count, count), keepdims=False), back_of(count, k))
-        for k in range(count)
-    ]
+    got, grad = lax.optimization_barrier((got, grad))
     order = [lax.rem(ctx + j, count) for j in range(count)]
     output = jnp.stack(
         [functools.reduce(lambda a, k: jnp.where(order[k] == r, got[k], a), range(1, count), got[0]) for r in range(count)]
     )
 
     per = rows_own
-    grad = grad[: per * n_dp]
-    bit = 1
-    keep = grad.reshape(1, n_dp, per, width)
-    while bit < n_dp:
-        left = keep.shape[1]
-        view = keep.reshape(left // 2, 2, per, width)
-        up = (dp & bit) != 0
-        mine = jnp.where(up, view[:, 1], view[:, 0])
-        theirs = jnp.where(up, view[:, 0], view[:, 1])
-        keep = (mine + swap_dp(theirs.astype(bf16), bit).astype(f32))[None]
-        bit *= 2
-    total = keep.reshape(per, width)
-    bit = 1
-    while bit < n_ctx:
-        total = total + swap_ctx(total.astype(bf16), bit).astype(f32)
-        bit *= 2
+    view = grad.reshape(n_dp // 2, 2, per, width)
+    mine = jnp.where(core == 1, view[:, 1], view[:, 0])
+    theirs = jnp.where(core == 1, view[:, 0], view[:, 1]).astype(bf16)
+    total = (mine + swap_dp(theirs, 1).astype(f32)).reshape(n_dp // 2 * per, width)
+    plane = total.astype(bf16)
+    for n in range(1, n_dp // 2):
+        total = total + swap_dp(plane, 2 * n).astype(f32)
+    line = total.astype(bf16)
+    for n in range(1, n_ctx):
+        total = total + swap_ctx(line, n).astype(f32)
     square = jnp.full((8, BLK), jnp.sum(total * total), f32)
-    bit = 1
-    while bit < n_dp:
-        square = square + swap_dp(square, bit)
-        bit *= 2
+    square = square + swap_dp(square, 1)
     max_norm = 0.5 * jnp.sqrt(f32(PROMPT * width))
     norm_total = jnp.sqrt(square[0, 0])
-    grad_own = lax.dynamic_slice_in_dim(total, ctx * cols_own, cols_own, axis=1)
+    grad_own = lax.dynamic_slice(total, (dp // 2 * per, ctx * cols_own), (per, cols_own))
     clipped = grad_own * (max_norm / jnp.maximum(norm_total, max_norm))
     first_new = beta_first * first_moment + (1.0 - beta_first) * clipped
     second_new = beta_second * second_moment + (1.0 - beta_second) * clipped * clipped

time: 173 us -> 125 us (0.72)
  the two profiles are of different devices: /device:TPU:16 before, /device:TPU:0 now
where the time goes in v2:
time: 125 us
  Pallas kernels  61.8 us (49%)
  starting transfers between devices  35 us (28%)
  waiting for transfers between devices  17 us (14%)
  local copies, waits for them, and re-layouts  4.73 us (4%)
  other arithmetic  3.39 us (3%)
  between operations  1.71 us (1%)
    ppermute x23, starting transfers between devices, permute(): return lax.ppermute(value, AXES, pairs)  35 us
    pallas_call x1, Pallas kernels, on_device(): pl.pallas_call(functools.partial(forward_kernel, count, piece), out_shape...  29.1 us
    pallas_call x1, Pallas kernels, on_device(): pl.pallas_call(functools.partial(backward_kernel, count, piece), out_shap...  21.7 us
    ppermute x23, waiting for transfers between devices, permute(): return lax.ppermute(value, AXES, pairs)  17 us
    pallas_call x1, Pallas kernels, on_device(): pl.pallas_call(functools.partial(prepare_kernel, count), out_shape=[held(...  6.24 us
    pallas_call x1, Pallas kernels, on_device(): pl.pallas_call(functools.partial(first_kernel, count, piece, rows_own), o...  3.56 us
  transfers between devices with their start and end apart: 23, of which 10 were waited for; matrix products, arithmetic and copies ran while one was open for 3% of the time, Pallas kernels for 49%

profile of v2, /device:TPU:0, one launch (start us, length us, event | category | flops | bytes accessed | tf_op | source)
XLA Modules:
  0.0 124.6 jit_solution(11782037510210244176)
XLA Ops:
  0.6 0.7 copy-done
  1.4 0.7 copy-done.2
  2.0 1.1 shard_map.183
  3.2 5.1 %collective-permute-start.4 = (bf16[24,192]{1,0:T(8,128)(2,1)S(1)}, bf16[24,192]{1,0:T(8,128)(2,1)S(1)}, u32[]{:S(2)}, u32[]{:S(2)}) collective-permute-start(bf16[24,192]{1,0:T(8,128)(2,1)S(1)} %get-tuple-element.39), channel_id=1, source_target_pairs={{0,3},{1,2},{2,1},{3,0},{4,7},{5,6},{6,5},{7,4},{8,11},{9,10},{10,... | collective-permute-start | bytes 27656 | tf_op jit(solution)/shard_map/ppermute | solution.py:489
  8.3 0.6 collective-permute-start.6
  8.9 1.0 collective-permute-done.4
  10.0 2.9 %collective-permute-done.5 = bf16[24,192]{1,0:T(8,128)(2,1)S(1)} collective-permute-done((bf16[24,192]{1,0:T(8,128)(2,1)S(1)}, bf16[24,192]{1,0:T(8,128)(2,1)S(1)}, u32[]{:S(2)}, u32[]{:S(2)}) %collective-permute-start.5) | collective-permute-done | bytes 9248 | tf_op jit(solution)/shard_map/ppermute | solution.py:489
  12.9 0.1 pad_maximum_fusion.3.refs_2_
  13.0 0.7 collective-permute-start
  13.7 0.1 collective-permute-start.2
  13.8 0.4 collective-permute-done.7.refs_3_
  14.3 1.6 %collective-permute-start.10 = (bf16[32,768]{1,0:T(8,128)(2,1)S(1)}, bf16[32,768]{1,0:T(8,128)(2,1)S(1)}, u32[]{:S(2)}, u32[]{:S(2)}) collective-permute-start(bf16[32,768]{1,0:T(8,128)(2,1)S(1)} %pad_maximum_fusion.2), channel_id=1, source_target_pairs={{0,8},{1,9},{2,10},{3,11},{4,12},{5,13},{6,14},{7,15},{8,0},{9,1},... | collective-permute-start | bytes 147464 | tf_op jit(solution)/shard_map/ppermute | solution.py:489
  15.8 1.5 %collective-permute-start.8 = (bf16[32,768]{1,0:T(8,128)(2,1)S(1)}, bf16[32,768]{1,0:T(8,128)(2,1)S(1)}, u32[]{:S(2)}, u32[]{:S(2)}) collective-permute-start(bf16[32,768]{1,0:T(8,128)(2,1)S(1)} %pad_maximum_fusion.2), channel_id=1, source_target_pairs={{0,24},{1,25},{2,26},{3,27},{4,28},{5,29},{6,30},{7,31},{8,16},{9,... | collective-permute-start | bytes 147464 | tf_op jit(solution)/shard_map/ppermute | solution.py:489
  17.3 0.5 collective-permute-start.9
  17.8 1.0 convolution_bitcast_fusion.base_ref
  18.9 0.8 copy.22.tab_ref
  19.7 0.7 broadcast_in_dim.9.refs_5_.refs_7_.refs_11_
  20.4 0.7 broadcast_in_dim.10.refs_8_.refs_12_
  21.0 6.2 %shard_map.184 = (f32[12,3,128,128]{3,2,1,0:T(8,128)S(1)}, bf16[12,512,128]{2,1,0:T(8,128)(2,1)S(1)}, bf16[256,768]{1,0:T(8,128)(2,1)S(1)}, bf16[256,768]{1,0:T(...) custom-call(f32[12,512]{1,0:T(8,128)S(1)} %convolution_bitcast_fusio, ...), custom_call_target="tpu_custom_call" | custom-call | flops 1000000 | bytes 15000000 | tf_op jit(solution)/shard_map/pallas_call | solution.py:534
  27.4 4.1 %collective-permute-start.1 = (bf16[256,768]{1,0:T(8,128)(2,1)S(1)}, bf16[256,768]{1,0:T(8,128)(2,1)S(1)}, u32[]{:S(2)}, u32[]{:S(2)}) collective-permute-start(bf16[256,768]{1,0:T(8,128)(2,1)S(1)} %collective-permute-done.refs_0_), channel_id=1, source_target_pairs={{0,4},{1,5},{2,6},{3,7},{4,0},{5,1},{6,2},{7,3},{8,12},{9,13},{10,... | collective-permute-start | bytes 1179656 | tf_op jit(solution)/shard_map/ppermute | solution.py:489
  31.6 3.6 %shard_map.185 = (s32[8,128]{1,0:T(8,128)S(1)}, bf16[512,768]{1,0:T(8,128)(2,1)S(1)}, bf16[512,768]{1,0:T(8,128)(2,1)S(1)}, bf16[1152,768]{1,0:T(8,128)(2,1)S(1)}, bf16[1152,768]{1,0:T(8,128)(2,1)S(1)}) custom-call(bf16[256,768]{1,0:T(8,128)(2,1)S(1)} %collective-permute-done.refs_0_, bf16[256,768]{1,0:T(8,128)(2,1)S(1)} %collective-permute-done.2.refs_1_, ...), custom_call_target="tpu_custom_call" | custom-call | flops 1811939328 | bytes 8000000 | tf_op jit(solution)/shard_map/pallas_call | solution.py:553
  35.2 0.7 collective-permute-start.13
  35.9 4.8 %collective-permute-start.14 = (bf16[256,768]{1,0:T(8,128)(2,1)S(1)}, bf16[256,768]{1,0:T(8,128)(2,1)S(1)}, u32[]{:S(2)}, u32[]{:S(2)}) collective-permute-start(bf16[256,768]{1,0:T(8,128)(2,1)S(1)} %get-tuple-element.59), channel_id=1, source_target_pairs={{0,1},{1,0},{2,5},{3,4},{4,3},{5,2},{6,7},{7,6},{8,9},{9,8},{10,13... | collective-permute-start | bytes 1179656 | tf_op jit(solution)/shard_map/ppermute | solution.py:489
  40.7 29.1 %shard_map.186 = (bf16[6,2,512,1152]{3,2,1,0:T(8,128)(2,1)}, bf16[1152,768]{1,0:T(8,128)(2,1)S(1)}, bf16[1152,768]{1,0:T(8,128)(2,1)S(1)}, bf16[512,768]{1,0:T(8...) custom-call(f32[32,12]{1,0:T(8,128)S(1)} %copy.22.tab_ref, ...), custom_call_target="tpu_custom_call", output_to_operand_aliasing={{1}: (6, {}), {2}: (7, {})} | custom-call | flops 30000001024 | bytes 40000000 | tf_op jit(solution)/shard_map/pallas_call | solution.py:572
  69.8 0.9 collective-permute-start.11
  70.7 0.1 collective-permute-start.12
  70.8 21.7 %shard_map.187 = f32[128,768]{1,0:T(8,128)S(1)} custom-call(bf16[256,768]{1,0:T(8,128)(2,1)S(1)} %collective-permute-done.13.refs_0_, bf16[256,768]{1,0:T(8,128)(2,1)S(1)} %collective-permute-done.14.refs_1_, s32[8,128]{1,0:T(8,128)S(1)} %get-tuple-element.43.refs_2_, bf16[512,3072]{1,0:T(8,128)(2,1)S(1)} %get-tuple-element.60.refs_3_, ...), custom_call_target="tpu_custom_call" | custom-call | flops 30000001024 | bytes 40000000 | tf_op jit(solution)/shard_map/pallas_call | solution.py:600
  92.6 6.1 %collective-permute-start.15 = (bf16[4,16,768]{2,1,0:T(8,128)(2,1)S(1)}, bf16[4,16,768]{2,1,0:T(8,128)(2,1)S(1)}, u32[]{:S(2)}, u32[]{:S(2)}) collective-permute-start(bf16[4,16,768]{2,1,0:T(8,128)(2,1)S(1)} %fusion.4), channel_id=1, source_target_pairs={{0,4},{1,5},{2,6},{3,7},{4,0},{5,1},{6,2},{7,3},{8,12},{9,13},{10,... | collective-permute-start | bytes 294920 | tf_op jit(solution)/shard_map/ppermute | solution.py:489
  98.7 0.9 collective-permute-done.15
  99.7 1.6 %collective-permute-start.16 = (bf16[64,768]{1,0:T(8,128)(2,1)S(1)}, bf16[64,768]{1,0:T(8,128)(2,1)S(1)}, u32[]{:S(2)}, u32[]{:S(2)}) collective-permute-start(bf16[64,768]{1,0:T(8,128)(2,1)S(1)} %bitcast_convert_fusion), channel_id=1, source_target_pairs={{0,8},{1,9},{2,10},{3,11},{4,12},{5,13},{6,14},{7,15},{8,0},{9,1},... | collective-permute-start | bytes 294920 | tf_op jit(solution)/shard_map/ppermute | solution.py:489
  101.3 1.5 %collective-permute-start.17 = (bf16[64,768]{1,0:T(8,128)(2,1)S(1)}, bf16[64,768]{1,0:T(8,128)(2,1)S(1)}, u32[]{:S(2)}, u32[]{:S(2)}) collective-permute-start(bf16[64,768]{1,0:T(8,128)(2,1)S(1)} %bitcast_convert_fusion), channel_id=1, source_target_pairs={{0,16},{1,17},{2,18},{3,19},{4,20},{5,21},{6,22},{7,23},{8,24},{9,... | collective-permute-start | bytes 294920 | tf_op jit(solution)/shard_map/ppermute | solution.py:489
  102.8 0.5 collective-permute-start.18
  103.3 1.6 %collective-permute-done.16 = bf16[64,768]{1,0:T(8,128)(2,1)S(1)} collective-permute-done((bf16[64,768]{1,0:T(8,128)(2,1)S(1)}, bf16[64,768]{1,0:T(8,128)(2,1)S(1)}, u32[]{:S(2)}, u32[]{:S(2)}) %collective-permute-start.16) | collective-permute-done | bytes 98336 | tf_op jit(solution)/shard_map/ppermute | solution.py:489
  104.8 2.4 %collective-permute-done.17 = bf16[64,768]{1,0:T(8,128)(2,1)S(1)} collective-permute-done((bf16[64,768]{1,0:T(8,128)(2,1)S(1)}, bf16[64,768]{1,0:T(8,128)(2,1)S(1)}, u32[]{:S(2)}, u32[]{:S(2)}) %collective-permute-start.17) | collective-permute-done | bytes 98336 | tf_op jit(solution)/shard_map/ppermute | solution.py:489
  107.2 1.1 collective-permute-done.18
  108.4 1.8 %collective-permute-start.19 = (bf16[64,768]{1,0:T(8,128)(2,1)S(1)}, bf16[64,768]{1,0:T(8,128)(2,1)S(1)}, u32[]{:S(2)}, u32[]{:S(2)}) collective-permute-start(bf16[64,768]{1,0:T(8,128)(2,1)S(1)} %fusion.6), channel_id=1, source_target_pairs={{0,1},{1,0},{2,3},{3,2},{4,5},{5,4},{6,7},{7,6},{8,9},{9,8},{10,11... | collective-permute-start | bytes 294920 | tf_op jit(solution)/shard_map/ppermute | solution.py:489
  110.1 1.1 collective-permute-start.20
  111.3 1.6 %collective-permute-start.21 = (bf16[64,768]{1,0:T(8,128)(2,1)S(1)}, bf16[64,768]{1,0:T(8,128)(2,1)S(1)}, u32[]{:S(2)}, u32[]{:S(2)}) collective-permute-start(bf16[64,768]{1,0:T(8,128)(2,1)S(1)} %fusion.6), channel_id=1, source_target_pairs={{0,3},{1,2},{2,1},{3,0},{4,7},{5,6},{6,5},{7,4},{8,11},{9,10},{10,... | collective-permute-start | bytes 294920 | tf_op jit(solution)/shard_map/ppermute | solution.py:489
  112.9 0.3 collective-permute-done.19
  113.2 6.2 %collective-permute-done.20 = bf16[64,768]{1,0:T(8,128)(2,1)S(1)} collective-permute-done((bf16[64,768]{1,0:T(8,128)(2,1)S(1)}, bf16[64,768]{1,0:T(8,128)(2,1)S(1)}, u32[]{:S(2)}, u32[]{:S(2)}) %collective-permute-start.20) | collective-permute-done | bytes 98336 | tf_op jit(solution)/shard_map/ppermute | solution.py:489
  119.3 0.7 multiply_reduce_fusion
  120.0 0.6 broadcast_in_dim.11
  120.7 0.1 collective-permute-start.22
  120.8 0.9 pad_maximum_fusion
  121.7 0.2 collective-permute-done.22
  121.9 0.6 broadcast_add_fusion
  122.6 0.5 slice.21
  123.9 0.7 divide_subtract_fusion
  (35 shorter events, 0.4 us)
Async XLA Ops:
  0.6 0.7 copy-start
  1.4 0.7 copy-start.2
  3.2 6.8 %collective-permute-start.4 = (bf16[24,192]{1,0:T(8,128)(2,1)S(1)}, bf16[24,192]{1,0:T(8,128)(2,1)S(1)}, u32[]{:S(2)}, u32[]{:S(2)}) collective-permute-start(bf16[24,192]{1,0:T(8,128)(2,1)S(1)} %get-tuple-element.39), channel_id=1, source_target_pairs={{0,3},{1,2},{2,1},{3,0},{4,7},{5,6},{6,5},{7,4},{8,11},{9,10},{10,... | collective-permute-start | bytes 27656 | tf_op jit(solution)/shard_map/ppermute | solution.py:489
  8.3 4.6 %collective-permute-start.5 = (bf16[24,192]{1,0:T(8,128)(2,1)S(1)}, bf16[24,192]{1,0:T(8,128)(2,1)S(1)}, u32[]{:S(2)}, u32[]{:S(2)}) collective-permute-start(bf16[24,192]{1,0:T(8,128)(2,1)S(1)} %get-tuple-element.39), channel_id=1, source_target_pairs={{0,2},{1,3},{2,0},{3,1},{4,6},{5,7},{6,4},{7,5},{8,10},{9,11},{10,... | collective-permute-start | bytes 27656 | tf_op jit(solution)/shard_map/ppermute | solution.py:489
  8.3 4.6 %collective-permute-start.6 = (bf16[24,192]{1,0:T(8,128)(2,1)S(1)}, bf16[24,192]{1,0:T(8,128)(2,1)S(1)}, u32[]{:S(2)}, u32[]{:S(2)}) collective-permute-start(bf16[24,192]{1,0:T(8,128)(2,1)S(1)} %get-tuple-element.39), channel_id=1, source_target_pairs={{0,1},{1,0},{2,3},{3,2},{4,5},{5,4},{6,7},{7,6},{8,9},{9,8},{10,11... | collective-permute-start | bytes 27656 | tf_op jit(solution)/shard_map/ppermute | solution.py:489
  13.0 1.2 %collective-permute-start.7 = (bf16[24,768]{1,0:T(8,128)(2,1)S(1)}, bf16[24,768]{1,0:T(8,128)(2,1)S(1)}, u32[]{:S(2)}, u32[]{:S(2)}) collective-permute-start(bf16[24,768]{1,0:T(8,128)(2,1)S(1)} %pad_maximum_fusion.3.refs_2_), channel_id=1, source_target_pairs={{0,4},{1,5},{2,6},{3,7},{4,0},{5,1},{6,2},{7,3},{8,12},{9,13},{10,... | collective-permute-start | bytes 110600 | tf_op jit(solution)/shard_map/ppermute | solution.py:489
  13.0 14.3 %collective-permute-start = (bf16[256,768]{1,0:T(8,128)(2,1)S(1)}, bf16[256,768]{1,0:T(8,128)(2,1)S(1)}, u32[]{:S(2)}, u32[]{:S(2)}) collective-permute-start(bf16[256,768]{1,0:T(8,128)(2,1)S(1)} %get-tuple-element.37), channel_id=1, source_target_pairs={{0,0},{1,1},{2,4},{3,5},{4,2},{5,3},{6,6},{7,7},{8,8},{9,9},{10,12... | collective-permute-start | bytes 1179656 | tf_op jit(solution)/shard_map/ppermute | solution.py:489
  13.7 17.8 %collective-permute-start.2 = (bf16[256,768]{1,0:T(8,128)(2,1)S(1)}, bf16[256,768]{1,0:T(8,128)(2,1)S(1)}, u32[]{:S(2)}, u32[]{:S(2)}) collective-permute-start(bf16[256,768]{1,0:T(8,128)(2,1)S(1)} %get-tuple-element.38), channel_id=1, source_target_pairs={{0,1},{1,0},{2,5},{3,4},{4,3},{5,2},{6,7},{7,6},{8,9},{9,8},{10,13... | collective-permute-start | bytes 1179656 | tf_op jit(solution)/shard_map/ppermute | solution.py:489
  14.3 13.0 %collective-permute-start.10 = (bf16[32,768]{1,0:T(8,128)(2,1)S(1)}, bf16[32,768]{1,0:T(8,128)(2,1)S(1)}, u32[]{:S(2)}, u32[]{:S(2)}) collective-permute-start(bf16[32,768]{1,0:T(8,128)(2,1)S(1)} %pad_maximum_fusion.2), channel_id=1, source_target_pairs={{0,8},{1,9},{2,10},{3,11},{4,12},{5,13},{6,14},{7,15},{8,0},{9,1},... | collective-permute-start | bytes 147464 | tf_op jit(solution)/shard_map/ppermute | solution.py:489
  15.8 11.5 %collective-permute-start.8 = (bf16[32,768]{1,0:T(8,128)(2,1)S(1)}, bf16[32,768]{1,0:T(8,128)(2,1)S(1)}, u32[]{:S(2)}, u32[]{:S(2)}) collective-permute-start(bf16[32,768]{1,0:T(8,128)(2,1)S(1)} %pad_maximum_fusion.2), channel_id=1, source_target_pairs={{0,24},{1,25},{2,26},{3,27},{4,28},{5,29},{6,30},{7,31},{8,16},{9,... | collective-permute-start | bytes 147464 | tf_op jit(solution)/shard_map/ppermute | solution.py:489
  17.3 10.0 %collective-permute-start.9 = (bf16[32,768]{1,0:T(8,128)(2,1)S(1)}, bf16[32,768]{1,0:T(8,128)(2,1)S(1)}, u32[]{:S(2)}, u32[]{:S(2)}) collective-permute-start(bf16[32,768]{1,0:T(8,128)(2,1)S(1)} %pad_maximum_fusion.2), channel_id=1, source_target_pairs={{0,16},{1,17},{2,18},{3,19},{4,20},{5,21},{6,22},{7,23},{8,24},{9,... | collective-permute-start | bytes 147464 | tf_op jit(solution)/shard_map/ppermute | solution.py:489
  27.4 13.3 %collective-permute-start.1 = (bf16[256,768]{1,0:T(8,128)(2,1)S(1)}, bf16[256,768]{1,0:T(8,128)(2,1)S(1)}, u32[]{:S(2)}, u32[]{:S(2)}) collective-permute-start(bf16[256,768]{1,0:T(8,128)(2,1)S(1)} %collective-permute-done.refs_0_), channel_id=1, source_target_pairs={{0,4},{1,5},{2,6},{3,7},{4,0},{5,1},{6,2},{7,3},{8,12},{9,13},{10,... | collective-permute-start | bytes 1179656 | tf_op jit(solution)/shard_map/ppermute | solution.py:489
  31.5 9.2 %collective-permute-start.3 = (bf16[256,768]{1,0:T(8,128)(2,1)S(1)}, bf16[256,768]{1,0:T(8,128)(2,1)S(1)}, u32[]{:S(2)}, u32[]{:S(2)}) collective-permute-start(bf16[256,768]{1,0:T(8,128)(2,1)S(1)} %collective-permute-done.2.refs_1_), channel_id=1, source_target_pairs={{0,4},{1,5},{2,6},{3,7},{4,0},{5,1},{6,2},{7,3},{8,12},{9,13},{10,... | collective-permute-start | bytes 1179656 | tf_op jit(solution)/shard_map/ppermute | solution.py:489
  35.2 35.6 %collective-permute-start.13 = (bf16[256,768]{1,0:T(8,128)(2,1)S(1)}, bf16[256,768]{1,0:T(8,128)(2,1)S(1)}, u32[]{:S(2)}, u32[]{:S(2)}) collective-permute-start(bf16[256,768]{1,0:T(8,128)(2,1)S(1)} %get-tuple-element.58), channel_id=1, source_target_pairs={{0,0},{1,1},{2,4},{3,5},{4,2},{5,3},{6,6},{7,7},{8,8},{9,9},{10,12... | collective-permute-start | bytes 1179656 | tf_op jit(solution)/shard_map/ppermute | solution.py:489
  35.9 34.9 %collective-permute-start.14 = (bf16[256,768]{1,0:T(8,128)(2,1)S(1)}, bf16[256,768]{1,0:T(8,128)(2,1)S(1)}, u32[]{:S(2)}, u32[]{:S(2)}) collective-permute-start(bf16[256,768]{1,0:T(8,128)(2,1)S(1)} %get-tuple-element.59), channel_id=1, source_target_pairs={{0,1},{1,0},{2,5},{3,4},{4,3},{5,2},{6,7},{7,6},{8,9},{9,8},{10,13... | collective-permute-start | bytes 1179656 | tf_op jit(solution)/shard_map/ppermute | solution.py:489
  69.8 22.7 %collective-permute-start.11 = (bf16[256,768]{1,0:T(8,128)(2,1)S(1)}, bf16[256,768]{1,0:T(8,128)(2,1)S(1)}, u32[]{:S(2)}, u32[]{:S(2)}) collective-permute-start(bf16[256,768]{1,0:T(8,128)(2,1)S(1)} %get-tuple-element.56), channel_id=1, source_target_pairs={{0,0},{1,1},{2,4},{3,5},{4,2},{5,3},{6,6},{7,7},{8,8},{9,9},{10,12... | collective-permute-start | bytes 1179656 | tf_op jit(solution)/shard_map/ppermute | solution.py:489
  70.7 21.9 %collective-permute-start.12 = (bf16[256,768]{1,0:T(8,128)(2,1)S(1)}, bf16[256,768]{1,0:T(8,128)(2,1)S(1)}, u32[]{:S(2)}, u32[]{:S(2)}) collective-permute-start(bf16[256,768]{1,0:T(8,128)(2,1)S(1)} %get-tuple-element.57), channel_id=1, source_target_pairs={{0,1},{1,0},{2,5},{3,4},{4,3},{5,2},{6,7},{7,6},{8,9},{9,8},{10,13... | collective-permute-start | bytes 1179656 | tf_op jit(solution)/shard_map/ppermute | solution.py:489
  92.6 7.1 %collective-permute-start.15 = (bf16[4,16,768]{2,1,0:T(8,128)(2,1)S(1)}, bf16[4,16,768]{2,1,0:T(8,128)(2,1)S(1)}, u32[]{:S(2)}, u32[]{:S(2)}) collective-permute-start(bf16[4,16,768]{2,1,0:T(8,128)(2,1)S(1)} %fusion.4), channel_id=1, source_target_pairs={{0,4},{1,5},{2,6},{3,7},{4,0},{5,1},{6,2},{7,3},{8,12},{9,13},{10,... | collective-permute-start | bytes 294920 | tf_op jit(solution)/shard_map/ppermute | solution.py:489
  99.7 5.1 %collective-permute-start.16 = (bf16[64,768]{1,0:T(8,128)(2,1)S(1)}, bf16[64,768]{1,0:T(8,128)(2,1)S(1)}, u32[]{:S(2)}, u32[]{:S(2)}) collective-permute-start(bf16[64,768]{1,0:T(8,128)(2,1)S(1)} %bitcast_convert_fusion), channel_id=1, source_target_pairs={{0,8},{1,9},{2,10},{3,11},{4,12},{5,13},{6,14},{7,15},{8,0},{9,1},... | collective-permute-start | bytes 294920 | tf_op jit(solution)/shard_map/ppermute | solution.py:489
  101.3 5.9 %collective-permute-start.17 = (bf16[64,768]{1,0:T(8,128)(2,1)S(1)}, bf16[64,768]{1,0:T(8,128)(2,1)S(1)}, u32[]{:S(2)}, u32[]{:S(2)}) collective-permute-start(bf16[64,768]{1,0:T(8,128)(2,1)S(1)} %bitcast_convert_fusion), channel_id=1, source_target_pairs={{0,16},{1,17},{2,18},{3,19},{4,20},{5,21},{6,22},{7,23},{8,24},{9,... | collective-permute-start | bytes 294920 | tf_op jit(solution)/shard_map/ppermute | solution.py:489
  102.8 5.5 %collective-permute-start.18 = (bf16[64,768]{1,0:T(8,128)(2,1)S(1)}, bf16[64,768]{1,0:T(8,128)(2,1)S(1)}, u32[]{:S(2)}, u32[]{:S(2)}) collective-permute-start(bf16[64,768]{1,0:T(8,128)(2,1)S(1)} %bitcast_convert_fusion), channel_id=1, source_target_pairs={{0,24},{1,25},{2,26},{3,27},{4,28},{5,29},{6,30},{7,31},{8,16},{9,... | collective-permute-start | bytes 294920 | tf_op jit(solution)/shard_map/ppermute | solution.py:489
  108.4 15.5 %copy-start.1 = (f32[16,192]{1,0:T(8,128)S(1)}, f32[16,192]{1,0:T(8,128)}, u32[]{:S(2)}) copy-start(f32[16,192]{1,0:T(8,128)} %prompt_ref.1) | copy-start | bytes 36868
  108.4 15.5 %copy-start.3 = (f32[16,192]{1,0:T(8,128)S(1)}, f32[16,192]{1,0:T(8,128)}, u32[]{:S(2)}) copy-start(f32[16,192]{1,0:T(8,128)} %param.30) | copy-start | bytes 36868
  108.4 15.5 %copy-start.4 = (f32[16,192]{1,0:T(8,128)S(1)}, f32[16,192]{1,0:T(8,128)}, u32[]{:S(2)}) copy-start(f32[16,192]{1,0:T(8,128)} %param.31) | copy-start | bytes 36868
  108.4 4.8 %collective-permute-start.19 = (bf16[64,768]{1,0:T(8,128)(2,1)S(1)}, bf16[64,768]{1,0:T(8,128)(2,1)S(1)}, u32[]{:S(2)}, u32[]{:S(2)}) collective-permute-start(bf16[64,768]{1,0:T(8,128)(2,1)S(1)} %fusion.6), channel_id=1, source_target_pairs={{0,1},{1,0},{2,3},{3,2},{4,5},{5,4},{6,7},{7,6},{8,9},{9,8},{10,11... | collective-permute-start | bytes 294920 | tf_op jit(solution)/shard_map/ppermute | solution.py:489
  110.1 9.2 %collective-permute-start.20 = (bf16[64,768]{1,0:T(8,128)(2,1)S(1)}, bf16[64,768]{1,0:T(8,128)(2,1)S(1)}, u32[]{:S(2)}, u32[]{:S(2)}) collective-permute-start(bf16[64,768]{1,0:T(8,128)(2,1)S(1)} %fusion.6), channel_id=1, source_target_pairs={{0,2},{1,3},{2,0},{3,1},{4,6},{5,7},{6,4},{7,5},{8,10},{9,11},{10,... | collective-permute-start | bytes 294920 | tf_op jit(solution)/shard_map/ppermute | solution.py:489
  111.3 8.1 %collective-permute-start.21 = (bf16[64,768]{1,0:T(8,128)(2,1)S(1)}, bf16[64,768]{1,0:T(8,128)(2,1)S(1)}, u32[]{:S(2)}, u32[]{:S(2)}) collective-permute-start(bf16[64,768]{1,0:T(8,128)(2,1)S(1)} %fusion.6), channel_id=1, source_target_pairs={{0,3},{1,2},{2,1},{3,0},{4,7},{5,6},{6,5},{7,4},{8,11},{9,10},{10,... | collective-permute-start | bytes 294920 | tf_op jit(solution)/shard_map/ppermute | solution.py:489
  120.7 1.2 collective-permute-start.22

commit v3 on v2

v3 whole, which is shorter than its diff:
```python
import functools

import jax
import jax.numpy as jnp
import numpy as np
from jax import lax
from jax.experimental import pallas as pl
from jax.experimental.pallas import tpu as pltpu
from jax.sharding import PartitionSpec as P

PROMPT = 100
HEAD = 64
PAIR = 2 * HEAD
BLK = 128
norm_eps = 1e-06
beta_first = 0.9
beta_second = 0.999
adam_eps = 1e-08
learn_rate = 0.1
first_fix = 1.0 - 0.9**8
second_fix = 1.0 - 0.999**8
far_marks = (12, 16, 23, 32, 46, 64, 91)
f32 = jnp.float32
bf16 = jnp.bfloat16
i32 = jnp.int32
MASKED = -float(2**30)
AXES = ("dp", "ctx")
MIB = 1 << 20
A_MIB, F_MIB, B_MIB = 6, 20, 18


def bucket_table(offset):
    distance = np.abs(offset)
    passed = sum((distance >= mark).astype(np.int32) for mark in far_marks)
    far_ids = np.minimum(8 + passed, 15)
    return np.where(distance < 8, distance, far_ids) + 16 * (offset > 0).astype(np.int32)


def dot_nn(a, b):
    return lax.dot_general(a, b, (((1,), (0,)), ((), ())), preferred_element_type=f32)


def dot_nt(a, b):
    return lax.dot_general(a, b, (((1,), (1,)), ((), ())), preferred_element_type=f32)


def dot_tn(a, b):
    return lax.dot_general(a, b, (((0,), (0,)), ((), ())), preferred_element_type=f32)


def split_two(values):
    high = values.astype(bf16)
    return high, (values - high.astype(f32)).astype(bf16)


def inv_rms(values):
    return lax.rsqrt(jnp.mean(values * values, axis=-1, keepdims=True) + norm_eps)


def segment_of(place, first, second):
    seg = (place >= first).astype(i32) + (place >= second).astype(i32)
    start = jnp.where(seg == 0, 0, jnp.where(seg == 1, first, second))
    return seg, place - start


def vmem_spec():
    return pl.BlockSpec(memory_space=pltpu.VMEM)


def smem_spec():
    return pl.BlockSpec(memory_space=pltpu.SMEM)


def any_spec():
    return pl.BlockSpec(memory_space=pl.ANY)


def out(shape, dtype):
    return jax.ShapeDtypeStruct(shape, dtype)


def held(shape, dtype):
    return pltpu.VMEM(shape, dtype)


def in_vmem(value):
    return pltpu.with_memory_space_constraint(value, pltpu.VMEM)


def in_hbm(value):
    return pltpu.with_memory_space_constraint(value, pltpu.HBM)


def params(mib):
    return pltpu.CompilerParams(vmem_limit_bytes=mib * MIB)


def cost(flops, nbytes, trans=0):
    return pl.CostEstimate(flops=int(flops), bytes_accessed=int(nbytes), transcendentals=int(trans))


def pick_piece(pieces, turn, j):
    count = len(pieces)
    place = lax.rem(turn - j + count, count)
    picked = pieces[0][...]
    for k in range(1, count):
        picked = jnp.where(place == k, pieces[k][...], picked)
    return picked


def slot_of(index, count):
    return lax.rem(index + 2 * count, count)


def pack_kernel(count, tokens_ref, seg_hbm, prompt_hbm, *refs):
    pieces, (block_ref, seg_ref, prompt_ref, wide_ref, sems) = refs[:count], refs[count:]
    ctx = lax.axis_index("ctx")
    copies = [
        pltpu.make_async_copy(tokens_ref.at[slot_of(ctx + k, count)], pieces[k], sems.at[k]) for k in range(count)
    ]
    small = [
        pltpu.make_async_copy(seg_hbm, seg_ref, sems.at[count]),
        pltpu.make_async_copy(prompt_hbm, prompt_ref, sems.at[count + 1]),
    ]
    for copy in small + copies:
        copy.start()
    for copy in small:
        copy.wait()
    rows = prompt_ref.shape[0]
    wide_ref[...] = jnp.zeros_like(wide_ref)
    wide_ref[0:rows, :] = prompt_ref[...]
    for n in range(2):
        tally = jnp.sum((seg_ref[...] <= n).astype(f32), axis=1, keepdims=True)
        wide_ref[rows + n * count : rows + (n + 1) * count, :] = jnp.broadcast_to(tally, (count, prompt_ref.shape[1]))
    block_ref[...] = wide_ref[...].astype(bf16)
    for copy in copies:
        copy.wait()


def prepare_kernel(count, base_ref, gain_first_ref, gain_second_ref, cot_ref, *refs):
    weights, (tile_ref, table_ref, first_ref, second_ref) = refs[:6], refs[6:10]
    pieces, kept, sems = refs[10 : 10 + count], refs[10 + count : 16 + count], refs[16 + count]
    first_ref[...] = gain_first_ref[...]
    second_ref[...] = gain_second_ref[...]
    ctx = lax.axis_index("ctx")
    copies = [pltpu.make_async_copy(weights[n], kept[n], sems.at[n]) for n in range(6)] + [
        pltpu.make_async_copy(cot_ref.at[slot_of(ctx + k, count)], pieces[k], sems.at[6 + k]) for k in range(count)
    ]
    for copy in copies:
        copy.start()
    heads = tile_ref.shape[0]
    for h in range(heads):
        row = jnp.broadcast_to(base_ref[h : h + 1, :], (BLK, 4 * BLK))
        spread = pltpu.roll(row, 0, 1, stride=1, stride_axis=0)
        low, mid, top = (spread[:, k * BLK : (k + 1) * BLK] for k in (3, 2, 1))
        tile_ref[h, 0] = low
        tile_ref[h, 1] = mid
        tile_ref[h, 2] = top
        rows = slice(h * BLK, (h + 1) * BLK)
        parts = [part for pair in zip(split_two(mid), split_two(low)) for part in pair]
        for k in range(4):
            table_ref[rows, k * BLK : (k + 1) * BLK] = parts[k]
    for copy in copies:
        copy.wait()


def places(count):
    return lax.rem(lax.axis_index("dp"), 2), lax.rem(lax.axis_index("ctx"), count)


def first_kernel(count, piece, *refs):
    own = refs[:count]
    gain_ref, wk_ref, wv_ref, kall_ref, vall_ref, norm_ref = refs[count:]
    turn = places(count)[1]
    half_len = count * piece
    gain = gain_ref[...]
    for j in range(count):
        tok = pick_piece(own, turn, j).astype(f32)
        norm_ref[j * piece : (j + 1) * piece, :] = (tok * inv_rms(tok) * gain).astype(bf16)
    wide = 2 * BLK

    @pl.loop(0, gain.shape[1] // wide)
    def _(t):
        cols = pl.ds(pl.multiple_of(t * wide, wide), wide)
        kall_ref[0:half_len, cols] = dot_nn(norm_ref[...], wk_ref[:, cols]).astype(bf16)
        vall_ref[0:half_len, cols] = dot_nn(norm_ref[...], wv_ref[:, cols]).astype(bf16)


def forward_kernel(count, piece, rows_own, *refs):
    own, partner = refs[:count], refs[count : 2 * count]
    (
        block_ref, other_ref, prompt_ref, kown_ref, vown_ref, gain_first_ref, gain_second_ref, wq_ref, wk_ref, wv_ref,
        wo_ref, wi_ref, wout_ref, tile_ref, table_ref,
    ) = refs[2 * count : 2 * count + 15]
    refs = refs[2 * count + 15 :]
    e_ref, marks_ref, q_ref, kall_ref, vall_ref, mixed_ref, inv_ref, after_ref, act_ref = refs[:9]
    going, (norm_ref, hid_ref, slot_bias_ref, e_buf, sems) = refs[9 : 9 + count], refs[9 + count :]
    half, turn = places(count)
    half_len = count * piece
    width = q_ref.shape[1]
    mine = lax.div(lax.axis_index("ctx"), count) == half
    line = jnp.where(mine, block_ref[...], other_ref[...]).astype(f32)
    line_row = lax.broadcasted_iota(i32, (line.shape[0], 1), 0)
    marks = []
    for n in range(2):
        tally = jnp.where(line_row == rows_own + n * count + turn, line, 0.0)
        tally = jnp.sum(jnp.sum(tally, axis=1, keepdims=True), axis=0, keepdims=True)
        marks.append((tally * (1.0 / (width // lax.axis_size("ctx"))) + 0.5).astype(i32))
        marks_ref[n : n + 1, :] = jnp.broadcast_to(marks[n], (1, BLK))
    first, second = marks
    gain = gain_first_ref[...]
    slots = lax.broadcasted_iota(i32, (1, BLK), 1)
    for j in range(count):
        rows = slice(j * piece, (j + 1) * piece)
        place = half * half_len + j * piece + lax.broadcasted_iota(i32, (piece, 1), 0)
        inside = segment_of(place, first, second)[1]
        shown = inside < PROMPT
        choose = jnp.where((inside == slots) & shown, 1.0, 0.0).astype(bf16)
        picked = dot_nn(choose, prompt_ref[...])
        hidden = jnp.where(shown, picked, pick_piece(own, turn, j).astype(f32))
        hid_ref[rows, :] = hidden.astype(bf16)
        norm_ref[half_len + BLK + j * piece : half_len + BLK + (j + 1) * piece, :] = (
            hidden * inv_rms(hidden) * gain
        ).astype(bf16)
        tok = pick_piece(partner, turn, j).astype(f32)
        norm_ref[rows, :] = (tok * inv_rms(tok) * gain).astype(bf16)
    hidden = prompt_ref[...].astype(f32)
    norm_ref[half_len : half_len + BLK, :] = (hidden * inv_rms(hidden) * gain).astype(bf16)
    wide = 2 * BLK

    @pl.loop(0, width // wide)
    def _(t):
        cols = pl.ds(pl.multiple_of(t * wide, wide), wide)
        kall_ref[half_len:, cols] = dot_nn(norm_ref[0 : half_len + BLK, :], wk_ref[:, cols]).astype(bf16)
        vall_ref[half_len:, cols] = dot_nn(norm_ref[0 : half_len + BLK, :], wv_ref[:, cols]).astype(bf16)
        q_ref[:, cols] = dot_nn(norm_ref[half_len + BLK :, :], wq_ref[:, cols]).astype(bf16)

    lane = lax.broadcasted_iota(i32, (1, PAIR), 1)
    low_lane = lane < HEAD
    lane_seg = lax.rem(lane, HEAD)
    spot = lax.broadcasted_iota(i32, (half_len, 1), 0)
    own_seg, own_inside = segment_of(half * half_len + spot, first, second)
    par_seg, par_inside = segment_of((1 - half) * half_len + spot, first, second)
    q_aug = jnp.where(own_seg == lane_seg, 1.0, 0.0).astype(bf16)

    def key_aug(seg, inside):
        closed = ((seg != lane_seg) | (inside < PROMPT)) & (lane_seg < 3)
        return jnp.where(closed, MASKED, 0.0).astype(bf16)

    slot = lax.broadcasted_iota(i32, (BLK, 1), 0)
    k_aug = jnp.concatenate(
        [
            key_aug(own_seg, own_inside),
            key_aug(par_seg, par_inside),
            jnp.where((slot >= PROMPT) & (lane_seg < 3), MASKED, 0.0).astype(bf16),
        ],
        axis=0,
    )
    across = segment_of(half * half_len + lax.broadcasted_iota(i32, (1, half_len), 1), first, second)[1]
    far = lax.rem(lax.broadcasted_iota(i32, (4 * BLK, 1), 0), 2 * BLK)
    spread = jnp.where(jnp.minimum(across, 2 * BLK - 1) == far, 1.0, 0.0).astype(bf16)
    slot_bias_ref[...] = dot_nn(table_ref[...], spread)
    blocks = half_len // BLK
    ones = jnp.ones((16, 2 * half_len + BLK), bf16)

    def e_copy(hp):
        at = lax.rem(hp, 2)
        return pltpu.make_async_copy(e_buf.at[at], e_ref.at[hp], sems.at[at])

    @pl.loop(0, width // PAIR)
    def _(hp):
        @pl.when(hp >= 2)
        def _():
            e_copy(hp - 2).wait()

        cols = pl.ds(pl.multiple_of(hp * PAIR, PAIR), PAIR)
        q_pair, k_pair = q_ref[:, cols], kall_ref[:, cols]
        v_turned = vall_ref[:, cols].T
        for s in range(2):
            h = 2 * hp + s
            keep = low_lane if s == 0 else jnp.logical_not(low_lane)
            raw = dot_nt(jnp.where(keep, k_pair, k_aug), jnp.where(keep, q_pair, q_aug))
            back_far, ahead_far = tile_ref[h, 0, 0:1, BLK - 1 :], tile_ref[h, 2, BLK - 1 :, 0:1]
            other_far = jnp.where(half == 0, ahead_far, back_far)
            values = (back_far, ahead_far, other_far)
            slot_bias = slot_bias_ref[pl.ds(pl.multiple_of(h * BLK, BLK), BLK), :]
            columns = []
            for qb in range(blocks):
                here = slice(qb * BLK, (qb + 1) * BLK)
                parts, consts = [], []
                for kb in range(2 * blocks):
                    part = raw[kb * BLK : (kb + 1) * BLK, here]
                    const = None
                    if kb < blocks:
                        gap = kb - qb
                        if abs(gap) <= 1:
                            part = part + tile_ref[h, gap + 1]
                        else:
                            const = 0 if gap < 0 else 1
                    elif qb == blocks - 1 and kb == blocks:
                        part = part + jnp.where(half == 0, tile_ref[h, 2], back_far)
                    elif qb == 0 and kb == 2 * blocks - 1:
                        part = part + jnp.where(half == 0, ahead_far, tile_ref[h, 0])
                    else:
                        const = 2
                    parts.append(part)
                    consts.append(const)
                parts.append(raw[2 * blocks * BLK :, here] + slot_bias[:, here])
                consts.append(None)
                peak = None
                for group in (None, 0, 1, 2):
                    members = [p for p, c in zip(parts, consts) if c == group]
                    if not members:
                        continue
                    top = jnp.max(functools.reduce(jnp.maximum, members), axis=0, keepdims=True)
                    if group is not None:
                        top = top + values[group]
                    peak = top if peak is None else jnp.maximum(peak, top)
                shifts = [peak - value for value in values]
                columns.append(
                    [jnp.exp(p - (peak if c is None else shifts[c])).astype(bf16) for p, c in zip(parts, consts)]
                )
            raised = jnp.concatenate(
                [jnp.concatenate([column[kb] for column in columns], axis=1) for kb in range(2 * blocks + 1)], axis=0
            )
            e_buf[lax.rem(hp, 2), s] = raised
            turned = jnp.concatenate([v_turned[s * HEAD : (s + 1) * HEAD], ones], axis=0)
            total = dot_nn(turned, raised)
            inv = 1.0 / total[HEAD : HEAD + 1]
            inv_ref[pl.ds(h, 1), :] = inv
            mixed_ref[pl.ds(pl.multiple_of(h * HEAD, HEAD), HEAD), :] = (total[:HEAD] * inv).astype(bf16)
        e_copy(hp).start()

    @pl.loop(0, half_len // BLK)
    def _(t):
        rows = pl.ds(pl.multiple_of(t * BLK, BLK), BLK)
        after = hid_ref[rows, :].astype(f32) + dot_tn(mixed_ref[:, rows], wo_ref[...])
        after_ref[rows, :] = after
        norm_ref[rows, :] = (after * inv_rms(after) * gain_second_ref[...]).astype(bf16)

    @pl.loop(0, wi_ref.shape[1] // wide)
    def _(t):
        cols = pl.ds(pl.multiple_of(t * wide, wide), wide)
        act_ref[:, cols] = jnp.maximum(dot_nn(norm_ref[0:half_len, :], wi_ref[:, cols]), 0.0).astype(bf16)

    @pl.loop(0, width // wide)
    def _(t):
        cols = pl.ds(pl.multiple_of(t * wide, wide), wide)
        made = (after_ref[:, cols] + dot_nn(act_ref[...], wout_ref[:, cols])).astype(bf16)
        made = [made[j * piece : (j + 1) * piece] for j in range(count)]
        for k in range(count):
            place = slot_of(turn - k, count)
            sent = made[0]
            for j in range(1, count):
                sent = jnp.where(place == j, made[j], sent)
            going[k][:, cols] = sent

    for hp in range(width // PAIR - 2, width // PAIR):
        e_copy(hp).wait()


def backward_kernel(count, piece, *refs):
    cots = refs[:count]
    (
        marks_ref, act_ref, after_ref, mixed_ref, inv_ref, q_ref, kall_ref, vall_ref, prompt_ref, gain_first_ref, gain_second_ref,
        wout_ref, wi_ref, wo_ref, wq_ref, wk_ref, wv_ref, e_ref,
        grad_ref,
        cot_ref, acc_ref, low_ref, do_ref, dq_ref, gk_ref, gv_ref, e_buf, sems,
    ) = refs[count:]
    half, turn = places(count)
    first, second = marks_ref[0:1, 0:1], marks_ref[1:2, 0:1]
    half_len = count * piece
    width = q_ref.shape[1]
    pairs = width // PAIR

    def e_copy(hp):
        at = lax.rem(hp, 2)
        return pltpu.make_async_copy(e_ref.at[hp], e_buf.at[at], sems.at[at])

    for hp in range(2):
        e_copy(hp).start()
    for j in range(count):
        cot_ref[j * piece : (j + 1) * piece, :] = pick_piece(cots, turn, j)
    wide = 4 * BLK
    acc_ref[...] = jnp.zeros_like(acc_ref)

    @pl.loop(0, wi_ref.shape[1] // wide)
    def _(t):
        cols = pl.ds(pl.multiple_of(t * wide, wide), wide)
        grad_act = dot_nt(cot_ref[...], wout_ref[cols, :])
        grad_inner = jnp.where(act_ref[:, cols] > 0, grad_act, 0.0).astype(bf16)
        acc_ref[...] += dot_nt(grad_inner, wi_ref[:, cols])

    gain = gain_second_ref[...]

    @pl.loop(0, half_len // BLK)
    def _(t):
        rows = pl.ds(pl.multiple_of(t * BLK, BLK), BLK)
        after = after_ref[rows, :]
        scale = inv_rms(after)
        pulled = gain * acc_ref[rows, :]
        along = jnp.mean(after * pulled, axis=-1, keepdims=True)
        grad_after = cot_ref[rows, :].astype(f32) + scale * pulled - after * (scale * scale * scale * along)
        acc_ref[rows, :] = grad_after
        low_ref[rows, :] = grad_after.astype(bf16)

    do_ref[...] = dot_nt(wo_ref[...], low_ref[...])

    low_lane = lax.broadcasted_iota(i32, (1, PAIR), 1) < HEAD
    row = lax.broadcasted_iota(i32, (PAIR, 1), 0)
    row_at = lax.rem(row, HEAD)

    @pl.loop(0, pairs)
    def _(hp):
        e_copy(hp).wait()
        cols = pl.ds(pl.multiple_of(hp * PAIR, PAIR), PAIR)
        q_pair, k_turned, v_pair = q_ref[:, cols], kall_ref[:, cols].T, vall_ref[:, cols]
        inv_both = jnp.where(row < HEAD, inv_ref[pl.ds(2 * hp, 1), :], inv_ref[pl.ds(2 * hp + 1, 1), :])
        do_pair = (do_ref[cols, :] * inv_both).astype(bf16)
        inner = do_pair.astype(f32) * mixed_ref[cols, :].astype(f32)
        slot_scores, slot_raised = [], []
        for s in range(2):
            mine = (row < HEAD) == (s == 0)
            keep = low_lane if s == 0 else jnp.logical_not(low_lane)
            high, low = split_two(-jnp.sum(inner[s * HEAD : (s + 1) * HEAD], axis=0, keepdims=True))
            zero = jnp.zeros((), bf16)
            do_e = jnp.where(mine, do_pair, jnp.where(row_at == 0, high, jnp.where(row_at == 1, low, zero)))
            raised = e_buf[lax.rem(hp, 2), s]
            grad_probs = dot_nn(jnp.where(keep, v_pair, jnp.ones((), bf16)), do_e)
            grad_scores = (raised.astype(f32) * grad_probs).astype(bf16)
            made = dot_nn(k_turned[s * HEAD : (s + 1) * HEAD], grad_scores)
            dq_ref[pl.ds(pl.multiple_of(hp * PAIR + s * HEAD, HEAD), HEAD), :] = made.astype(bf16)
            slot_scores.append(grad_scores[2 * half_len :])
            slot_raised.append(raised[2 * half_len :])
        dk = dot_nn(jnp.concatenate(slot_scores, axis=0), q_pair)
        dv = dot_nt(jnp.concatenate(slot_raised, axis=0), do_pair)
        gk_ref[:, cols] = jnp.where(low_lane, dk[:BLK], dk[BLK:]).astype(bf16)
        gv_ref[:, cols] = jnp.where(low_lane, dv[:BLK], dv[BLK:]).astype(bf16)

        @pl.when(hp + 2 < pairs)
        def _():
            e_copy(hp + 2).start()

    spot = lax.broadcasted_iota(i32, (1, half_len), 1)
    inside = segment_of(half * half_len + spot, first, second)[1]
    slots = lax.broadcasted_iota(i32, (BLK, 1), 0)
    choose = jnp.where((inside == slots) & (inside < PROMPT), 1.0, 0.0).astype(bf16)
    gq = dot_nt(choose, dq_ref[...]).astype(bf16)
    pulled = dot_nt(gq, wq_ref[...]) + dot_nt(gk_ref[...], wk_ref[...]) + dot_nt(gv_ref[...], wv_ref[...])
    high, low = split_two(acc_ref[...])
    direct = dot_nn(choose, high) + dot_nn(choose, low)
    hidden = prompt_ref[...].astype(f32)
    scale = inv_rms(hidden)
    pulled = gain_first_ref[...] * pulled
    along = jnp.mean(hidden * pulled, axis=-1, keepdims=True)
    grad_ref[...] = direct + scale * pulled - hidden * (scale * scale * scale * along)


def on_device(
    sizes, tokens, segment_ids, prompt_slots, cotangent, w_query, w_key, w_value, w_output, w_inner, w_outer,
    gain_first, gain_second, bias_table, prompt, first_moment, second_moment,
):
    n_dp, n_ctx = sizes
    count, piece, width = tokens.shape
    half_len = count * piece
    heads = bias_table.shape[1]
    dp, ctx = lax.axis_index("dp"), lax.axis_index("ctx")
    core = lax.rem(dp, 2)

    def permute(value, target):
        pairs = []
        for d in range(n_dp):
            for z in range(n_ctx):
                d2, z2 = target(d, z)
                pairs.append((d * n_ctx + z, d2 * n_ctx + z2))
        return lax.ppermute(value, AXES, pairs)

    def swap_dp(value, bit):
        return permute(value, lambda d, z: (d ^ bit, z))

    def swap_ctx(value, bit):
        return permute(value, lambda d, z: (d, z ^ bit))

    def there(k):
        return lambda d, z: (2 * (d // 2) + z // count, (d % 2) * count + (z + k) % count)

    def in_order(parts, me, axis):
        ordered = []
        for place in range(len(parts)):
            picked = parts[0]
            for n in range(1, len(parts)):
                picked = jnp.where((me ^ n) == place, parts[n], picked)
            ordered.append(picked)
        return jnp.concatenate(ordered, axis=axis)

    rows_own, cols_own = prompt.shape
    piece_like = held((piece, width), bf16)
    packed = pl.pallas_call(
        functools.partial(pack_kernel, count),
        out_shape=[piece_like] * count + [held((rows_own + 8, cols_own), bf16)],
        in_specs=[any_spec()] * 3,
        out_specs=[vmem_spec()] * (count + 1),
        scratch_shapes=[
            pltpu.VMEM(segment_ids.shape, i32),
            pltpu.VMEM(prompt.shape, f32),
            pltpu.VMEM((rows_own + 8, cols_own), f32),
            pltpu.SemaphoreType.DMA((count + 2,)),
        ],
        compiler_params=params(4),
        cost_estimate=cost(1e5, 2e6),
    )(in_hbm(tokens), in_hbm(segment_ids), in_hbm(prompt))

    block = packed[count]
    blocks = [block] + [swap_ctx(block, n) for n in range(1, n_ctx)]
    own = [permute(packed[k], there(k)) for k in range(count)]
    choose = (np.arange(bias_table.shape[0])[:, None] == bucket_table(2 * BLK - np.arange(4 * BLK))[None]).astype(np.float32)
    base = lax.dot_general(
        bias_table, jnp.asarray(choose), (((0,), (0,)), ((), ())), precision=lax.Precision.HIGHEST
    )
    weights = (w_query, w_key, w_value, w_output, w_inner, w_outer)
    prepared = pl.pallas_call(
        functools.partial(prepare_kernel, count),
        out_shape=[held((heads, 3, BLK, BLK), f32), held((heads * BLK, 4 * BLK), bf16)]
        + [held((1, width), f32)] * 2
        + [piece_like] * count
        + [held(w.shape, bf16) for w in weights],
        in_specs=[vmem_spec()] * 3 + [any_spec()] * 7,
        out_specs=[vmem_spec()] * (10 + count),
        scratch_shapes=[pltpu.SemaphoreType.DMA((6 + count,))],
        compiler_params=params(4),
        cost_estimate=cost(1e6, 1.5e7),
    )(base, gain_first[None], gain_second[None], in_hbm(cotangent), *[in_hbm(w) for w in weights])
    tiles, table, gain_1, gain_2 = prepared[:4]
    cot_pieces = prepared[4 : 4 + count]
    w_q, w_k, w_v, w_o, w_i, w_out = prepared[4 + count :]

    block = in_order(blocks, ctx, 1)
    other = swap_dp(block, 1)
    chip_rows = in_order([block[:rows_own], other[:rows_own]], core, 0)
    sent = in_order([chip_rows] + [swap_dp(chip_rows, 2 * n) for n in range(1, n_dp // 2)], dp // 2, 0)

    keys_all = 2 * half_len + BLK
    hidden_ff = w_inner.shape[1]
    partner = [swap_dp(piece_rows, 1) for piece_rows in own]
    kall, vall = pl.pallas_call(
        functools.partial(first_kernel, count, piece),
        out_shape=[held((keys_all, width), bf16), held((keys_all, width), bf16)],
        in_specs=[vmem_spec()] * (count + 3),
        out_specs=[vmem_spec()] * 2,
        scratch_shapes=[pltpu.VMEM((half_len, width), bf16)],
        compiler_params=params(A_MIB),
        cost_estimate=cost(1e10, 8e6),
    )(*own, gain_1, w_k, w_v)
    cots = [permute(cot_pieces[k], there(k)) for k in range(count)]

    made = pl.pallas_call(
        functools.partial(forward_kernel, count, piece, rows_own),
        out_shape=[
            pltpu.HBM((heads // 2, 2, keys_all, half_len), bf16),
            held((8, BLK), i32),
            held((half_len, width), bf16),
            held((keys_all, width), bf16),
            held((keys_all, width), bf16),
            held((width, half_len), bf16),
            held((heads, half_len), f32),
            held((half_len, width), f32),
            held((half_len, hidden_ff), bf16),
        ]
        + [piece_like] * count,
        in_specs=[vmem_spec()] * (2 * count + 15),
        out_specs=[any_spec()] + [vmem_spec()] * (8 + count),
        scratch_shapes=[
            pltpu.VMEM((2 * half_len + BLK, width), bf16),
            pltpu.VMEM((half_len, width), bf16),
            pltpu.VMEM((heads * BLK, half_len), f32),
            pltpu.VMEM((2, 2, keys_all, half_len), bf16),
            pltpu.SemaphoreType.DMA((2,)),
        ],
        input_output_aliases={2 * count + 3: 3, 2 * count + 4: 4},
        compiler_params=params(F_MIB),
        cost_estimate=cost(3e10, 4e7, heads * half_len * keys_all),
    )(
        *own, *partner, block, other, sent, kall, vall, gain_1, gain_2, w_q, w_k, w_v, w_o, w_i, w_out, tiles,
        table,
    )
    got = [permute(made[9 + k], back_of(count, k)) for k in range(count)]
    e, marks, q, kall, vall, mixed, inv, after, act = made[:9]

    grad = pl.pallas_call(
        functools.partial(backward_kernel, count, piece),
        out_shape=held((BLK, width), f32),
        in_specs=[vmem_spec()] * (count + 17) + [any_spec()],
        out_specs=vmem_spec(),
        scratch_shapes=[
            pltpu.VMEM((half_len, width), bf16),
            pltpu.VMEM((half_len, width), f32),
            pltpu.VMEM((half_len, width), bf16),
            pltpu.VMEM((width, half_len), f32),
            pltpu.VMEM((width, half_len), bf16),
            pltpu.VMEM((BLK, width), bf16),
            pltpu.VMEM((BLK, width), bf16),
            pltpu.VMEM((2, 2, keys_all, half_len), bf16),
            pltpu.SemaphoreType.DMA((2,)),
        ],
        compiler_params=params(B_MIB),
        cost_estimate=cost(3e10, 4e7),
    )(
        *cots, marks, act, after, mixed, inv, q, kall, vall, sent, gain_1, gain_2, w_out, w_i, w_o, w_q, w_k, w_v, in_hbm(e),
    )

    got, grad = lax.optimization_barrier((got, grad))
    order = [lax.rem(ctx + j, count) for j in range(count)]
    output = jnp.stack(
        [functools.reduce(lambda a, k: jnp.where(order[k] == r, got[k], a), range(1, count), got[0]) for r in range(count)]
    )

    per = rows_own
    view = grad.reshape(n_dp // 2, 2, per, width)
    mine = jnp.where(core == 1, view[:, 1], view[:, 0])
    theirs = jnp.where(core == 1, view[:, 0], view[:, 1]).astype(bf16)
    total = (mine + swap_dp(theirs, 1).astype(f32)).reshape(n_dp // 2 * per, width)
    plane = total.astype(bf16)
    for n in range(1, n_dp // 2):
        total = total + swap_dp(plane, 2 * n).astype(f32)
    line = total.astype(bf16)
    for n in range(1, n_ctx):
        total = total + swap_ctx(line, n).astype(f32)
    square = jnp.full((8, BLK), jnp.sum(total * total), f32)
    square = square + swap_dp(square, 1)
    max_norm = 0.5 * jnp.sqrt(f32(PROMPT * width))
    norm_total = jnp.sqrt(square[0, 0])
    grad_own = lax.dynamic_slice(total, (dp // 2 * per, ctx * cols_own), (per, cols_own))
    clipped = grad_own * (max_norm / jnp.maximum(norm_total, max_norm))
    first_new = beta_first * first_moment + (1.0 - beta_first) * clipped
    second_new = beta_second * second_moment + (1.0 - beta_second) * clipped * clipped
    prompt_new = prompt - learn_rate * (first_new / first_fix) / (jnp.sqrt(second_new / second_fix) + adam_eps)
    return (output, prompt_new, first_new, second_new)


def back_of(count, k):
    def target(d, z):
        half, c, r = d % 2, z // count, z % count
        return (2 * (d // 2) + c, half * count + (r - k) % count)

    return target


def solution(mesh):
    rows, cols = P("dp", "ctx", None), P("dp", "ctx")
    placed = (rows, cols, cols, rows) + (P(),) * 9 + (cols,) * 3
    return jax.shard_map(
        functools.partial(on_device, (mesh.shape["dp"], mesh.shape["ctx"])),
        mesh=mesh,
        in_specs=placed,
        out_specs=(rows, cols, cols, cols),
        check_vma=False,
    )
```

time: 125 us -> 114 us (0.912)
  Pallas kernels: 61.8 us -> 56.9 us
  starting transfers between devices: 35 us -> 32.5 us
  local copies, waits for them, and re-layouts: 4.73 us -> 2.57 us
    pallas_call x1, Pallas kernels: 21.7 us -> 18.9 us  [on_device(): pl.pallas_call(functools.partial(backward_kernel, count, piece), out_shap...]
    ppermute x23, starting transfers between devices: 35 us -> 32.5 us  [permute(): return lax.ppermute(value, AXES, pairs)]
    unnamed x11 -> x10, local copies, waits for them, and re-layouts: 2.19 us -> 0.03 us
    pallas_call x2, Pallas kernels: 32.6 us -> 30.6 us  [the longest x1 28.5 us: on_device(): pl.pallas_call(functools.partial(forward_kernel, count, piece, rows_own),...]
where the time goes in v3:
time: 114 us
  Pallas kernels  56.9 us (50%)
  starting transfers between devices  32.5 us (29%)
  waiting for transfers between devices  15.8 us (14%)
  other arithmetic  3.4 us (3%)
  local copies, waits for them, and re-layouts  2.57 us (2%)
  between operations  1.72 us (2%)
    ppermute x23, starting transfers between devices, permute(): return lax.ppermute(value, AXES, pairs)  32.5 us
    pallas_call x1, Pallas kernels, on_device(): pl.pallas_call(functools.partial(forward_kernel, count, piece, rows_own),...  28.5 us
    pallas_call x1, Pallas kernels, on_device(): pl.pallas_call(functools.partial(backward_kernel, count, piece), out_shap...  18.9 us
    ppermute x23, waiting for transfers between devices, permute(): return lax.ppermute(value, AXES, pairs)  15.8 us
    pallas_call x1, Pallas kernels, on_device(): pl.pallas_call(functools.partial(prepare_kernel, count), out_shape=[held(...  6.19 us
  transfers between devices with their start and end apart: 23, of which 10 were waited for; matrix products, arithmetic and copies ran while one was open for 3% of the time, Pallas kernels for 49%

profile of v3, /device:TPU:0, one launch (start us, length us, event | category | flops | bytes accessed | tf_op | source)
XLA Modules:
  0.0 113.8 jit_solution(9504234423025722294)
XLA Ops:
  0.6 1.2 %shard_map.183 = (bf16[256,768]{1,0:T(8,128)(2,1)S(1)}, bf16[256,768]{1,0:T(8,128)(2,1)S(1)}, bf16[24,192]{1,0:T(8,128)(2,1)S(1)}) custom-call(bf16[2,256,768]{2,1,0:T(8,128)(2,1)} %tokens_ref.1, s32[2,256]{1,0:T(2,128)} %seg_hbm.1, f32[16,192]{1,0:T(8,128)} %prompt_hbm.1), custom_call_target="tpu_custom_call" | custom-call | flops 100000 | bytes 2000000 | tf_op jit(solution)/shard_map/pallas_call | solution.py:498
  1.8 5.1 %collective-permute-start.4 = (bf16[24,192]{1,0:T(8,128)(2,1)S(1)}, bf16[24,192]{1,0:T(8,128)(2,1)S(1)}, u32[]{:S(2)}, u32[]{:S(2)}) collective-permute-start(bf16[24,192]{1,0:T(8,128)(2,1)S(1)} %get-tuple-element.37), channel_id=1, source_target_pairs={{0,3},{1,2},{2,1},{3,0},{4,7},{5,6},{6,5},{7,4},{8,11},{9,10},{10,... | collective-permute-start | bytes 27656 | tf_op jit(solution)/shard_map/ppermute | solution.py:476
  7.0 0.6 collective-permute-start.6
  7.6 1.0 collective-permute-done.4
  8.6 2.9 %collective-permute-done.5 = bf16[24,192]{1,0:T(8,128)(2,1)S(1)} collective-permute-done((bf16[24,192]{1,0:T(8,128)(2,1)S(1)}, bf16[24,192]{1,0:T(8,128)(2,1)S(1)}, u32[]{:S(2)}, u32[]{:S(2)}) %collective-permute-start.5) | collective-permute-done | bytes 9248 | tf_op jit(solution)/shard_map/ppermute | solution.py:476
  11.6 0.1 pad_maximum_fusion.3.refs_4_
  11.7 0.7 collective-permute-start
  12.4 0.1 collective-permute-start.1
  12.5 0.4 collective-permute-done.7.refs_5_
  12.9 1.6 %collective-permute-start.10 = (bf16[32,768]{1,0:T(8,128)(2,1)S(1)}, bf16[32,768]{1,0:T(8,128)(2,1)S(1)}, u32[]{:S(2)}, u32[]{:S(2)}) collective-permute-start(bf16[32,768]{1,0:T(8,128)(2,1)S(1)} %pad_maximum_fusion.2), channel_id=1, source_target_pairs={{0,8},{1,9},{2,10},{3,11},{4,12},{5,13},{6,14},{7,15},{8,0},{9,1},... | collective-permute-start | bytes 147464 | tf_op jit(solution)/shard_map/ppermute | solution.py:476
  14.5 1.5 %collective-permute-start.8 = (bf16[32,768]{1,0:T(8,128)(2,1)S(1)}, bf16[32,768]{1,0:T(8,128)(2,1)S(1)}, u32[]{:S(2)}, u32[]{:S(2)}) collective-permute-start(bf16[32,768]{1,0:T(8,128)(2,1)S(1)} %pad_maximum_fusion.2), channel_id=1, source_target_pairs={{0,24},{1,25},{2,26},{3,27},{4,28},{5,29},{6,30},{7,31},{8,16},{9,... | collective-permute-start | bytes 147464 | tf_op jit(solution)/shard_map/ppermute | solution.py:476
  16.0 0.5 collective-permute-start.9
  16.5 1.0 convolution_bitcast_fusion.base_ref
  17.5 0.7 broadcast_in_dim.10.gain_second_ref
  18.2 0.7 broadcast_in_dim.9.gain_first_ref
  18.9 6.2 %shard_map.184 = (f32[12,3,128,128]{3,2,1,0:T(8,128)S(1)}, bf16[1536,512]{1,0:T(8,128)(2,1)S(1)}, f32[1,768]{1,0:T(1,128)S(1)}, f32[1,768]{1,0:T(1,128)S(1)}, bf...) custom-call(f32[12,512]{1,0:T(8,128)S(1)} %convolution_bitcast_fusio, ...), custom_call_target="tpu_custom_call" | custom-call | flops 1000000 | bytes 15000000 | tf_op jit(solution)/shard_map/pallas_call | solution.py:521
  25.1 0.7 collective-permute-start.13
  25.8 1.7 %collective-permute-start.14 = (bf16[256,768]{1,0:T(8,128)(2,1)S(1)}, bf16[256,768]{1,0:T(8,128)(2,1)S(1)}, u32[]{:S(2)}, u32[]{:S(2)}) collective-permute-start(bf16[256,768]{1,0:T(8,128)(2,1)S(1)} %get-tuple-element.53), channel_id=1, source_target_pairs={{0,1},{1,0},{2,5},{3,4},{4,3},{5,2},{6,7},{7,6},{8,9},{9,8},{10,13... | collective-permute-start | bytes 1179656 | tf_op jit(solution)/shard_map/ppermute | solution.py:476
  27.5 0.1 select_select_fusion.3
  27.6 6.2 %collective-permute-start.2 = (bf16[256,768]{1,0:T(8,128)(2,1)S(1)}, bf16[256,768]{1,0:T(8,128)(2,1)S(1)}, u32[]{:S(2)}, u32[]{:S(2)}) collective-permute-start(bf16[256,768]{1,0:T(8,128)(2,1)S(1)} %collective-permute-done.refs_0_), channel_id=1, source_target_pairs={{0,4},{1,5},{2,6},{3,7},{4,0},{5,1},{6,2},{7,3},{8,12},{9,13},{10,... | collective-permute-start | bytes 1179656 | tf_op jit(solution)/shard_map/ppermute | solution.py:476
  33.8 0.1 collective-permute-start.3
  33.9 2.1 %shard_map.185 = (bf16[1152,768]{1,0:T(8,128)(2,1)S(1)}, bf16[1152,768]{1,0:T(8,128)(2,1)S(1)}) custom-call(bf16[256,768]{1,0:T(8,128)(2,1)S(1)} %collective-permute-done.refs_0_, bf16[256,768]{1,0:T(8,128)(2,1)S(1)} %collective-permute-done.1.refs_1_, f32[1,768]{1,0:T(1,128)S(1)} %get-tuple-element.38.refs_2_.refs_9_.refs_11_, ...), custom_call_target="tpu_custom_call" | custom-call | flops 10000000000 | bytes 8000000 | tf_op jit(solution)/shard_map/pallas_call | solution.py:545
  36.0 28.5 %shard_map.186 = (bf16[6,2,1152,512]{3,2,1,0:T(8,128)(2,1)}, s32[8,128]{1,0:T(8,128)S(1)}, bf16[512,768]{1,0:T(8,128)(2,1)S(1)}, bf16[1152,768]{1,0:T(8,128)(2,1...) custom-call(bf16[256,768]{1,0:T(8,128)(2,1)S(1)} %collective-permute, ...), custom_call_target="tpu_custom_call", output_to_operand_aliasing={{3}: (7, {}), {4}: (8, {})} | custom-call | flops 30000001024 | bytes 40000000 | tf_op jit(solution)/shard_map/pallas_call | solution.py:556
  64.5 0.9 collective-permute-start.11
  65.4 1.4 %collective-permute-start.12 = (bf16[256,768]{1,0:T(8,128)(2,1)S(1)}, bf16[256,768]{1,0:T(8,128)(2,1)S(1)}, u32[]{:S(2)}, u32[]{:S(2)}) collective-permute-start(bf16[256,768]{1,0:T(8,128)(2,1)S(1)} %get-tuple-element.51), channel_id=1, source_target_pairs={{0,1},{1,0},{2,5},{3,4},{4,3},{5,2},{6,7},{7,6},{8,9},{9,8},{10,13... | collective-permute-start | bytes 1179656 | tf_op jit(solution)/shard_map/ppermute | solution.py:476
  66.8 18.9 %shard_map.187 = f32[128,768]{1,0:T(8,128)S(1)} custom-call(bf16[256,768]{1,0:T(8,128)(2,1)S(1)} %collective-permute-done.13.refs_0_, bf16[256,768]{1,0:T(8,128)(2,1)S(1)} %collective-permute-done.14.refs_1_, s32[8,128]{1,0:T(8,128)S(1)} %get-tuple-element.54.refs_2_, bf16[512,3072]{1,0:T(8,128)(2,1)S(1)} %get-tuple-element.55.refs_3_, ...), custom_call_target="tpu_custom_call" | custom-call | flops 30000001024 | bytes 40000000 | tf_op jit(solution)/shard_map/pallas_call | solution.py:589
  85.8 3.4 %collective-permute-start.15 = (bf16[4,16,768]{2,1,0:T(8,128)(2,1)S(1)}, bf16[4,16,768]{2,1,0:T(8,128)(2,1)S(1)}, u32[]{:S(2)}, u32[]{:S(2)}) collective-permute-start(bf16[4,16,768]{2,1,0:T(8,128)(2,1)S(1)} %fusion.4), channel_id=1, source_target_pairs={{0,4},{1,5},{2,6},{3,7},{4,0},{5,1},{6,2},{7,3},{8,12},{9,13},{10,... | collective-permute-start | bytes 294920 | tf_op jit(solution)/shard_map/ppermute | solution.py:476
  89.2 0.9 collective-permute-done.15
  90.2 1.6 %collective-permute-start.16 = (bf16[64,768]{1,0:T(8,128)(2,1)S(1)}, bf16[64,768]{1,0:T(8,128)(2,1)S(1)}, u32[]{:S(2)}, u32[]{:S(2)}) collective-permute-start(bf16[64,768]{1,0:T(8,128)(2,1)S(1)} %bitcast_convert_fusion), channel_id=1, source_target_pairs={{0,8},{1,9},{2,10},{3,11},{4,12},{5,13},{6,14},{7,15},{8,0},{9,1},... | collective-permute-start | bytes 294920 | tf_op jit(solution)/shard_map/ppermute | solution.py:476
  91.8 1.5 %collective-permute-start.17 = (bf16[64,768]{1,0:T(8,128)(2,1)S(1)}, bf16[64,768]{1,0:T(8,128)(2,1)S(1)}, u32[]{:S(2)}, u32[]{:S(2)}) collective-permute-start(bf16[64,768]{1,0:T(8,128)(2,1)S(1)} %bitcast_convert_fusion), channel_id=1, source_target_pairs={{0,16},{1,17},{2,18},{3,19},{4,20},{5,21},{6,22},{7,23},{8,24},{9,... | collective-permute-start | bytes 294920 | tf_op jit(solution)/shard_map/ppermute | solution.py:476
  93.3 0.4 collective-permute-start.18
  93.8 1.6 %collective-permute-done.16 = bf16[64,768]{1,0:T(8,128)(2,1)S(1)} collective-permute-done((bf16[64,768]{1,0:T(8,128)(2,1)S(1)}, bf16[64,768]{1,0:T(8,128)(2,1)S(1)}, u32[]{:S(2)}, u32[]{:S(2)}) %collective-permute-start.16) | collective-permute-done | bytes 98336 | tf_op jit(solution)/shard_map/ppermute | solution.py:476
  95.3 2.4 %collective-permute-done.17 = bf16[64,768]{1,0:T(8,128)(2,1)S(1)} collective-permute-done((bf16[64,768]{1,0:T(8,128)(2,1)S(1)}, bf16[64,768]{1,0:T(8,128)(2,1)S(1)}, u32[]{:S(2)}, u32[]{:S(2)}) %collective-permute-start.17) | collective-permute-done | bytes 98336 | tf_op jit(solution)/shard_map/ppermute | solution.py:476
  97.7 1.1 collective-permute-done.18
  98.9 0.2 collective-permute-start.19
  99.1 2.9 %collective-permute-start.20 = (bf16[64,768]{1,0:T(8,128)(2,1)S(1)}, bf16[64,768]{1,0:T(8,128)(2,1)S(1)}, u32[]{:S(2)}, u32[]{:S(2)}) collective-permute-start(bf16[64,768]{1,0:T(8,128)(2,1)S(1)} %fusion.6), channel_id=1, source_target_pairs={{0,2},{1,3},{2,0},{3,1},{4,6},{5,7},{6,4},{7,5},{8,10},{9,11},{10,... | collective-permute-start | bytes 294920 | tf_op jit(solution)/shard_map/ppermute | solution.py:476
  102.0 1.4 %collective-permute-start.21 = (bf16[64,768]{1,0:T(8,128)(2,1)S(1)}, bf16[64,768]{1,0:T(8,128)(2,1)S(1)}, u32[]{:S(2)}, u32[]{:S(2)}) collective-permute-start(bf16[64,768]{1,0:T(8,128)(2,1)S(1)} %fusion.6), channel_id=1, source_target_pairs={{0,3},{1,2},{2,1},{3,0},{4,7},{5,6},{6,5},{7,4},{8,11},{9,10},{10,... | collective-permute-start | bytes 294920 | tf_op jit(solution)/shard_map/ppermute | solution.py:476
  103.4 0.1 select_bitcast_fusion.1
  103.4 0.2 collective-permute-done.19
  103.6 5.0 %collective-permute-done.20 = bf16[64,768]{1,0:T(8,128)(2,1)S(1)} collective-permute-done((bf16[64,768]{1,0:T(8,128)(2,1)S(1)}, bf16[64,768]{1,0:T(8,128)(2,1)S(1)}, u32[]{:S(2)}, u32[]{:S(2)}) %collective-permute-start.20) | collective-permute-done | bytes 98336 | tf_op jit(solution)/shard_map/ppermute | solution.py:476
  108.6 0.7 multiply_reduce_fusion
  109.3 0.6 broadcast_in_dim.11
  110.0 0.1 collective-permute-start.22
  110.0 0.9 pad_maximum_fusion
  111.0 0.2 collective-permute-done.22
  111.2 0.6 broadcast_add_fusion
  111.8 0.5 slice.21
  113.1 0.7 divide_subtract_fusion
  (34 shorter events, 0.3 us)
Async XLA Ops:
  0.6 15.9 %copy-start = (f32[32,12]{0,1:T(8,128)S(1)}, f32[32,12]{0,1:T(8,128)}, u32[]{:S(2)}) copy-start(f32[32,12]{0,1:T(8,128)} %param.28) | copy-start | bytes 4612
  1.8 6.8 %collective-permute-start.4 = (bf16[24,192]{1,0:T(8,128)(2,1)S(1)}, bf16[24,192]{1,0:T(8,128)(2,1)S(1)}, u32[]{:S(2)}, u32[]{:S(2)}) collective-permute-start(bf16[24,192]{1,0:T(8,128)(2,1)S(1)} %get-tuple-element.37), channel_id=1, source_target_pairs={{0,3},{1,2},{2,1},{3,0},{4,7},{5,6},{6,5},{7,4},{8,11},{9,10},{10,... | collective-permute-start | bytes 27656 | tf_op jit(solution)/shard_map/ppermute | solution.py:476
  7.0 4.6 %collective-permute-start.5 = (bf16[24,192]{1,0:T(8,128)(2,1)S(1)}, bf16[24,192]{1,0:T(8,128)(2,1)S(1)}, u32[]{:S(2)}, u32[]{:S(2)}) collective-permute-start(bf16[24,192]{1,0:T(8,128)(2,1)S(1)} %get-tuple-element.37), channel_id=1, source_target_pairs={{0,2},{1,3},{2,0},{3,1},{4,6},{5,7},{6,4},{7,5},{8,10},{9,11},{10,... | collective-permute-start | bytes 27656 | tf_op jit(solution)/shard_map/ppermute | solution.py:476
  7.0 4.6 %collective-permute-start.6 = (bf16[24,192]{1,0:T(8,128)(2,1)S(1)}, bf16[24,192]{1,0:T(8,128)(2,1)S(1)}, u32[]{:S(2)}, u32[]{:S(2)}) collective-permute-start(bf16[24,192]{1,0:T(8,128)(2,1)S(1)} %get-tuple-element.37), channel_id=1, source_target_pairs={{0,1},{1,0},{2,3},{3,2},{4,5},{5,4},{6,7},{7,6},{8,9},{9,8},{10,11... | collective-permute-start | bytes 27656 | tf_op jit(solution)/shard_map/ppermute | solution.py:476
  11.7 1.2 %collective-permute-start.7 = (bf16[24,768]{1,0:T(8,128)(2,1)S(1)}, bf16[24,768]{1,0:T(8,128)(2,1)S(1)}, u32[]{:S(2)}, u32[]{:S(2)}) collective-permute-start(bf16[24,768]{1,0:T(8,128)(2,1)S(1)} %pad_maximum_fusion.3.refs_4_), channel_id=1, source_target_pairs={{0,4},{1,5},{2,6},{3,7},{4,0},{5,1},{6,2},{7,3},{8,12},{9,13},{10,... | collective-permute-start | bytes 110600 | tf_op jit(solution)/shard_map/ppermute | solution.py:476
  11.7 15.9 %collective-permute-start = (bf16[256,768]{1,0:T(8,128)(2,1)S(1)}, bf16[256,768]{1,0:T(8,128)(2,1)S(1)}, u32[]{:S(2)}, u32[]{:S(2)}) collective-permute-start(bf16[256,768]{1,0:T(8,128)(2,1)S(1)} %get-tuple-element.35), channel_id=1, source_target_pairs={{0,0},{1,1},{2,4},{3,5},{4,2},{5,3},{6,6},{7,7},{8,8},{9,9},{10,12... | collective-permute-start | bytes 1179656 | tf_op jit(solution)/shard_map/ppermute | solution.py:476
  12.4 21.4 %collective-permute-start.1 = (bf16[256,768]{1,0:T(8,128)(2,1)S(1)}, bf16[256,768]{1,0:T(8,128)(2,1)S(1)}, u32[]{:S(2)}, u32[]{:S(2)}) collective-permute-start(bf16[256,768]{1,0:T(8,128)(2,1)S(1)} %get-tuple-element.36), channel_id=1, source_target_pairs={{0,1},{1,0},{2,5},{3,4},{4,3},{5,2},{6,7},{7,6},{8,9},{9,8},{10,13... | collective-permute-start | bytes 1179656 | tf_op jit(solution)/shard_map/ppermute | solution.py:476
  12.9 12.2 %collective-permute-start.10 = (bf16[32,768]{1,0:T(8,128)(2,1)S(1)}, bf16[32,768]{1,0:T(8,128)(2,1)S(1)}, u32[]{:S(2)}, u32[]{:S(2)}) collective-permute-start(bf16[32,768]{1,0:T(8,128)(2,1)S(1)} %pad_maximum_fusion.2), channel_id=1, source_target_pairs={{0,8},{1,9},{2,10},{3,11},{4,12},{5,13},{6,14},{7,15},{8,0},{9,1},... | collective-permute-start | bytes 147464 | tf_op jit(solution)/shard_map/ppermute | solution.py:476
  14.5 11.3 %collective-permute-start.8 = (bf16[32,768]{1,0:T(8,128)(2,1)S(1)}, bf16[32,768]{1,0:T(8,128)(2,1)S(1)}, u32[]{:S(2)}, u32[]{:S(2)}) collective-permute-start(bf16[32,768]{1,0:T(8,128)(2,1)S(1)} %pad_maximum_fusion.2), channel_id=1, source_target_pairs={{0,24},{1,25},{2,26},{3,27},{4,28},{5,29},{6,30},{7,31},{8,16},{9,... | collective-permute-start | bytes 147464 | tf_op jit(solution)/shard_map/ppermute | solution.py:476
  16.0 11.5 %collective-permute-start.9 = (bf16[32,768]{1,0:T(8,128)(2,1)S(1)}, bf16[32,768]{1,0:T(8,128)(2,1)S(1)}, u32[]{:S(2)}, u32[]{:S(2)}) collective-permute-start(bf16[32,768]{1,0:T(8,128)(2,1)S(1)} %pad_maximum_fusion.2), channel_id=1, source_target_pairs={{0,16},{1,17},{2,18},{3,19},{4,20},{5,21},{6,22},{7,23},{8,24},{9,... | collective-permute-start | bytes 147464 | tf_op jit(solution)/shard_map/ppermute | solution.py:476
  25.1 41.7 %collective-permute-start.13 = (bf16[256,768]{1,0:T(8,128)(2,1)S(1)}, bf16[256,768]{1,0:T(8,128)(2,1)S(1)}, u32[]{:S(2)}, u32[]{:S(2)}) collective-permute-start(bf16[256,768]{1,0:T(8,128)(2,1)S(1)} %get-tuple-element.52), channel_id=1, source_target_pairs={{0,0},{1,1},{2,4},{3,5},{4,2},{5,3},{6,6},{7,7},{8,8},{9,9},{10,12... | collective-permute-start | bytes 1179656 | tf_op jit(solution)/shard_map/ppermute | solution.py:476
  25.8 41.0 %collective-permute-start.14 = (bf16[256,768]{1,0:T(8,128)(2,1)S(1)}, bf16[256,768]{1,0:T(8,128)(2,1)S(1)}, u32[]{:S(2)}, u32[]{:S(2)}) collective-permute-start(bf16[256,768]{1,0:T(8,128)(2,1)S(1)} %get-tuple-element.53), channel_id=1, source_target_pairs={{0,1},{1,0},{2,5},{3,4},{4,3},{5,2},{6,7},{7,6},{8,9},{9,8},{10,13... | collective-permute-start | bytes 1179656 | tf_op jit(solution)/shard_map/ppermute | solution.py:476
  27.6 8.4 %collective-permute-start.2 = (bf16[256,768]{1,0:T(8,128)(2,1)S(1)}, bf16[256,768]{1,0:T(8,128)(2,1)S(1)}, u32[]{:S(2)}, u32[]{:S(2)}) collective-permute-start(bf16[256,768]{1,0:T(8,128)(2,1)S(1)} %collective-permute-done.refs_0_), channel_id=1, source_target_pairs={{0,4},{1,5},{2,6},{3,7},{4,0},{5,1},{6,2},{7,3},{8,12},{9,13},{10,... | collective-permute-start | bytes 1179656 | tf_op jit(solution)/shard_map/ppermute | solution.py:476
  33.8 2.2 %collective-permute-start.3 = (bf16[256,768]{1,0:T(8,128)(2,1)S(1)}, bf16[256,768]{1,0:T(8,128)(2,1)S(1)}, u32[]{:S(2)}, u32[]{:S(2)}) collective-permute-start(bf16[256,768]{1,0:T(8,128)(2,1)S(1)} %collective-permute-done.1.refs_1_), channel_id=1, source_target_pairs={{0,4},{1,5},{2,6},{3,7},{4,0},{5,1},{6,2},{7,3},{8,12},{9,13},{10,... | collective-permute-start | bytes 1179656 | tf_op jit(solution)/shard_map/ppermute | solution.py:476
  64.5 21.3 %collective-permute-start.11 = (bf16[256,768]{1,0:T(8,128)(2,1)S(1)}, bf16[256,768]{1,0:T(8,128)(2,1)S(1)}, u32[]{:S(2)}, u32[]{:S(2)}) collective-permute-start(bf16[256,768]{1,0:T(8,128)(2,1)S(1)} %get-tuple-element.50), channel_id=1, source_target_pairs={{0,0},{1,1},{2,4},{3,5},{4,2},{5,3},{6,6},{7,7},{8,8},{9,9},{10,12... | collective-permute-start | bytes 1179656 | tf_op jit(solution)/shard_map/ppermute | solution.py:476
  65.4 20.4 %collective-permute-start.12 = (bf16[256,768]{1,0:T(8,128)(2,1)S(1)}, bf16[256,768]{1,0:T(8,128)(2,1)S(1)}, u32[]{:S(2)}, u32[]{:S(2)}) collective-permute-start(bf16[256,768]{1,0:T(8,128)(2,1)S(1)} %get-tuple-element.51), channel_id=1, source_target_pairs={{0,1},{1,0},{2,5},{3,4},{4,3},{5,2},{6,7},{7,6},{8,9},{9,8},{10,13... | collective-permute-start | bytes 1179656 | tf_op jit(solution)/shard_map/ppermute | solution.py:476
  85.8 4.3 %collective-permute-start.15 = (bf16[4,16,768]{2,1,0:T(8,128)(2,1)S(1)}, bf16[4,16,768]{2,1,0:T(8,128)(2,1)S(1)}, u32[]{:S(2)}, u32[]{:S(2)}) collective-permute-start(bf16[4,16,768]{2,1,0:T(8,128)(2,1)S(1)} %fusion.4), channel_id=1, source_target_pairs={{0,4},{1,5},{2,6},{3,7},{4,0},{5,1},{6,2},{7,3},{8,12},{9,13},{10,... | collective-permute-start | bytes 294920 | tf_op jit(solution)/shard_map/ppermute | solution.py:476
  90.2 5.1 %collective-permute-start.16 = (bf16[64,768]{1,0:T(8,128)(2,1)S(1)}, bf16[64,768]{1,0:T(8,128)(2,1)S(1)}, u32[]{:S(2)}, u32[]{:S(2)}) collective-permute-start(bf16[64,768]{1,0:T(8,128)(2,1)S(1)} %bitcast_convert_fusion), channel_id=1, source_target_pairs={{0,8},{1,9},{2,10},{3,11},{4,12},{5,13},{6,14},{7,15},{8,0},{9,1},... | collective-permute-start | bytes 294920 | tf_op jit(solution)/shard_map/ppermute | solution.py:476
  91.8 5.9 %collective-permute-start.17 = (bf16[64,768]{1,0:T(8,128)(2,1)S(1)}, bf16[64,768]{1,0:T(8,128)(2,1)S(1)}, u32[]{:S(2)}, u32[]{:S(2)}) collective-permute-start(bf16[64,768]{1,0:T(8,128)(2,1)S(1)} %bitcast_convert_fusion), channel_id=1, source_target_pairs={{0,16},{1,17},{2,18},{3,19},{4,20},{5,21},{6,22},{7,23},{8,24},{9,... | collective-permute-start | bytes 294920 | tf_op jit(solution)/shard_map/ppermute | solution.py:476
  93.3 5.5 %collective-permute-start.18 = (bf16[64,768]{1,0:T(8,128)(2,1)S(1)}, bf16[64,768]{1,0:T(8,128)(2,1)S(1)}, u32[]{:S(2)}, u32[]{:S(2)}) collective-permute-start(bf16[64,768]{1,0:T(8,128)(2,1)S(1)} %bitcast_convert_fusion), channel_id=1, source_target_pairs={{0,24},{1,25},{2,26},{3,27},{4,28},{5,29},{6,30},{7,31},{8,16},{9,... | collective-permute-start | bytes 294920 | tf_op jit(solution)/shard_map/ppermute | solution.py:476
  98.8 15.0 %copy-start.1 = (f32[32,12]{0,1:T(8,128)S(1)}, f32[32,12]{0,1:T(8,128)}, u32[]{:S(2)}) copy-start(f32[32,12]{0,1:T(8,128)} %param.28) | copy-start | bytes 4612
  98.9 14.2 %copy-start.2 = (f32[16,192]{1,0:T(8,128)S(1)}, f32[16,192]{1,0:T(8,128)}, u32[]{:S(2)}) copy-start(f32[16,192]{1,0:T(8,128)} %prompt_hbm.1) | copy-start | bytes 36868
  98.9 14.2 %copy-start.3 = (f32[16,192]{1,0:T(8,128)S(1)}, f32[16,192]{1,0:T(8,128)}, u32[]{:S(2)}) copy-start(f32[16,192]{1,0:T(8,128)} %param.30) | copy-start | bytes 36868
  98.9 14.2 %copy-start.4 = (f32[16,192]{1,0:T(8,128)S(1)}, f32[16,192]{1,0:T(8,128)}, u32[]{:S(2)}) copy-start(f32[16,192]{1,0:T(8,128)} %param.31) | copy-start | bytes 36868
  98.9 4.7 %collective-permute-start.19 = (bf16[64,768]{1,0:T(8,128)(2,1)S(1)}, bf16[64,768]{1,0:T(8,128)(2,1)S(1)}, u32[]{:S(2)}, u32[]{:S(2)}) collective-permute-start(bf16[64,768]{1,0:T(8,128)(2,1)S(1)} %fusion.6), channel_id=1, source_target_pairs={{0,1},{1,0},{2,3},{3,2},{4,5},{5,4},{6,7},{7,6},{8,9},{9,8},{10,11... | collective-permute-start | bytes 294920 | tf_op jit(solution)/shard_map/ppermute | solution.py:476
  99.1 9.5 %collective-permute-start.20 = (bf16[64,768]{1,0:T(8,128)(2,1)S(1)}, bf16[64,768]{1,0:T(8,128)(2,1)S(1)}, u32[]{:S(2)}, u32[]{:S(2)}) collective-permute-start(bf16[64,768]{1,0:T(8,128)(2,1)S(1)} %fusion.6), channel_id=1, source_target_pairs={{0,2},{1,3},{2,0},{3,1},{4,6},{5,7},{6,4},{7,5},{8,10},{9,11},{10,... | collective-permute-start | bytes 294920 | tf_op jit(solution)/shard_map/ppermute | solution.py:476
  102.0 6.6 %collective-permute-start.21 = (bf16[64,768]{1,0:T(8,128)(2,1)S(1)}, bf16[64,768]{1,0:T(8,128)(2,1)S(1)}, u32[]{:S(2)}, u32[]{:S(2)}) collective-permute-start(bf16[64,768]{1,0:T(8,128)(2,1)S(1)} %fusion.6), channel_id=1, source_target_pairs={{0,3},{1,2},{2,1},{3,0},{4,7},{5,6},{6,5},{7,4},{8,11},{9,10},{10,... | collective-permute-start | bytes 294920 | tf_op jit(solution)/shard_map/ppermute | solution.py:476
  110.0 1.2 %collective-permute-start.22 = (f32[8,128]{1,0:T(8,128)S(1)}, f32[8,128]{1,0:T(8,128)S(1)}, u32[]{:S(2)}, u32[]{:S(2)}) collective-permute-start(f32[8,128]{1,0:T(8,128)S(1)} %broadcast_in_dim.11), channel_id=1, source_target_pairs={{0,4},{1,5},{2,6},{3,7},{4,0},{5,1},{6,2},{7,3},{8,12},{9,13},{10,... | collective-permute-start | bytes 12296 | tf_op jit(solution)/shard_map/ppermute | solution.py:476

commit v4 on v3

--- a/solution.py
+++ b/solution.py
@@ -12,6 +12,7 @@
 HEAD = 64
 PAIR = 2 * HEAD
 BLK = 128
+QCOLS = 256
 norm_eps = 1e-06
 beta_first = 0.9
 beta_second = 0.999
@@ -164,48 +165,65 @@
         copy.wait()
 
 
+def plane_kernel(rows_own, *refs):
+    parts, (out_ref, wide_ref) = refs[:-2], refs[-2:]
+    core, chip = lax.rem(lax.axis_index("dp"), 2), lax.div(lax.axis_index("dp"), 2)
+    high = rows_own + 8
+    parts = [part[...].astype(f32) for part in parts]
+    parts = [[jnp.where(core == c, part[:high], part[high:]) for c in range(2)] for part in parts]
+    for place in range(len(parts)):
+        for c in range(2):
+            picked = parts[0][c]
+            for n in range(1, len(parts)):
+                picked = jnp.where((chip ^ n) == place, parts[n][c], picked)
+            start = (2 * place + c) * rows_own
+            wide_ref[start : start + rows_own, :] = picked[:rows_own]
+    for c in range(2):
+        wide_ref[BLK + 8 * c : BLK + 8 * (c + 1), :] = parts[0][c][rows_own:]
+    out_ref[...] = wide_ref[...].astype(bf16)
+
+
 def places(count):
     return lax.rem(lax.axis_index("dp"), 2), lax.rem(lax.axis_index("ctx"), count)
 
 
 def first_kernel(count, piece, *refs):
-    own = refs[:count]
-    gain_ref, wk_ref, wv_ref, kall_ref, vall_ref, norm_ref = refs[count:]
+    own, (gain_ref, norm_ref) = refs[:count], refs[count:]
     turn = places(count)[1]
-    half_len = count * piece
-    gain = gain_ref[...]
     for j in range(count):
         tok = pick_piece(own, turn, j).astype(f32)
-        norm_ref[j * piece : (j + 1) * piece, :] = (tok * inv_rms(tok) * gain).astype(bf16)
-    wide = 2 * BLK
-
-    @pl.loop(0, gain.shape[1] // wide)
-    def _(t):
-        cols = pl.ds(pl.multiple_of(t * wide, wide), wide)
-        kall_ref[0:half_len, cols] = dot_nn(norm_ref[...], wk_ref[:, cols]).astype(bf16)
-        vall_ref[0:half_len, cols] = dot_nn(norm_ref[...], wv_ref[:, cols]).astype(bf16)
+        norm_ref[j * piece : (j + 1) * piece, :] = (tok * inv_rms(tok) * gain_ref[...]).astype(bf16)
 
 
 def forward_kernel(count, piece, rows_own, *refs):
     own, partner = refs[:count], refs[count : 2 * count]
     (
-        block_ref, other_ref, prompt_ref, kown_ref, vown_ref, gain_first_ref, gain_second_ref, wq_ref, wk_ref, wv_ref,
-        wo_ref, wi_ref, wout_ref, tile_ref, table_ref,
-    ) = refs[2 * count : 2 * count + 15]
-    refs = refs[2 * count + 15 :]
-    e_ref, marks_ref, q_ref, kall_ref, vall_ref, mixed_ref, inv_ref, after_ref, act_ref = refs[:9]
-    going, (norm_ref, hid_ref, slot_bias_ref, e_buf, sems) = refs[9 : 9 + count], refs[9 + count :]
+        normed_ref, gain_first_ref, gain_second_ref, wq_ref, wk_ref, wv_ref, wo_ref, wi_ref, wout_ref,
+        tile_ref, table_ref,
+    ) = refs[2 * count : 2 * count + 11]
+    refs = refs[2 * count + 11 :]
+    cols_of, refs = refs[: 2 * count], refs[2 * count :]
+    e_ref, marks_ref, prompt_ref, q_ref, kall_ref, vall_ref, mixed_ref, inv_ref, after_ref, act_ref = refs[:10]
+    going, refs = refs[10 : 10 + count], refs[10 + count :]
+    norm_ref, hid_ref, slot_bias_ref, score_ref, aug_ref, shown_ref, e_buf, sems = refs
+    ctx = lax.axis_index("ctx")
+    few = cols_of[0].shape[1]
+    for place in range(2 * count):
+        picked = cols_of[0][0:BLK]
+        for n in range(1, 2 * count):
+            picked = jnp.where((ctx ^ n) == place, cols_of[n][0:BLK], picked)
+        shown_ref[:, place * few : (place + 1) * few] = picked.astype(f32)
+    prompt_ref[...] = shown_ref[...].astype(bf16)
     half, turn = places(count)
     half_len = count * piece
     width = q_ref.shape[1]
-    mine = lax.div(lax.axis_index("ctx"), count) == half
-    line = jnp.where(mine, block_ref[...], other_ref[...]).astype(f32)
-    line_row = lax.broadcasted_iota(i32, (line.shape[0], 1), 0)
+    tally = functools.reduce(jnp.add, [cols[BLK:].astype(f32) for cols in cols_of])
+    tally_row = lax.broadcasted_iota(i32, (tally.shape[0], 1), 0)
     marks = []
     for n in range(2):
-        tally = jnp.where(line_row == rows_own + n * count + turn, line, 0.0)
-        tally = jnp.sum(jnp.sum(tally, axis=1, keepdims=True), axis=0, keepdims=True)
-        marks.append((tally * (1.0 / (width // lax.axis_size("ctx"))) + 0.5).astype(i32))
+        here = tally_row == 8 * lax.div(ctx, count) + n * count + turn
+        total = jnp.sum(jnp.where(here, tally, 0.0), axis=0, keepdims=True)[:, 0:1]
+        marks.append((total + 0.5).astype(i32))
         marks_ref[n : n + 1, :] = jnp.broadcast_to(marks[n], (1, BLK))
     first, second = marks
     gain = gain_first_ref[...]
@@ -231,13 +249,14 @@
     @pl.loop(0, width // wide)
     def _(t):
         cols = pl.ds(pl.multiple_of(t * wide, wide), wide)
-        kall_ref[half_len:, cols] = dot_nn(norm_ref[0 : half_len + BLK, :], wk_ref[:, cols]).astype(bf16)
-        vall_ref[half_len:, cols] = dot_nn(norm_ref[0 : half_len + BLK, :], wv_ref[:, cols]).astype(bf16)
+        normed = jnp.concatenate([normed_ref[...], norm_ref[0 : half_len + BLK, :]], axis=0)
+        kall_ref[:, cols] = dot_nn(normed, wk_ref[:, cols]).astype(bf16)
+        vall_ref[:, cols] = dot_nn(normed, wv_ref[:, cols]).astype(bf16)
         q_ref[:, cols] = dot_nn(norm_ref[half_len + BLK :, :], wq_ref[:, cols]).astype(bf16)
 
     lane = lax.broadcasted_iota(i32, (1, PAIR), 1)
     low_lane = lane < HEAD
-    lane_seg = lax.rem(lane, HEAD)
+    lane_seg = lane
     spot = lax.broadcasted_iota(i32, (half_len, 1), 0)
     own_seg, own_inside = segment_of(half * half_len + spot, first, second)
     par_seg, par_inside = segment_of((1 - half) * half_len + spot, first, second)
@@ -248,14 +267,9 @@
         return jnp.where(closed, MASKED, 0.0).astype(bf16)
 
     slot = lax.broadcasted_iota(i32, (BLK, 1), 0)
-    k_aug = jnp.concatenate(
-        [
-            key_aug(own_seg, own_inside),
-            key_aug(par_seg, par_inside),
-            jnp.where((slot >= PROMPT) & (lane_seg < 3), MASKED, 0.0).astype(bf16),
-        ],
-        axis=0,
-    )
+    aug_ref[0:half_len] = key_aug(own_seg, own_inside)
+    aug_ref[half_len : 2 * half_len] = key_aug(par_seg, par_inside)
+    aug_ref[2 * half_len :] = jnp.where((slot >= PROMPT) & (lane_seg < 3), MASKED, 0.0).astype(bf16)
     across = segment_of(half * half_len + lax.broadcasted_iota(i32, (1, half_len), 1), first, second)[1]
     far = lax.rem(lax.broadcasted_iota(i32, (4 * BLK, 1), 0), 2 * BLK)
     spread = jnp.where(jnp.minimum(across, 2 * BLK - 1) == far, 1.0, 0.0).astype(bf16)
@@ -267,6 +281,28 @@
         at = lax.rem(hp, 2)
         return pltpu.make_async_copy(e_buf.at[at], e_ref.at[hp], sems.at[at])
 
+    keys_all = 2 * half_len + BLK
+    tiles_q = half_len // QCOLS
+    chunk = keys_all // 3
+    units = [(s, qt) for s in range(2) for qt in range(tiles_q)]
+
+    def kept(s):
+        return low_lane if s == 0 else jnp.logical_not(low_lane)
+
+    def score_steps(hp, s, qt, slot):
+        cols = pl.ds(pl.multiple_of(hp * PAIR, PAIR), PAIR)
+        here = slice(qt * QCOLS, (qt + 1) * QCOLS)
+        q_e = jnp.concatenate([jnp.where(kept(s), q_ref[here, cols], jnp.zeros((), bf16)), q_aug[here]], axis=1)
+
+        def step(n):
+            rows = slice(n * chunk, (n + 1) * chunk)
+            score_ref[slot, rows, :] = dot_nt(jnp.concatenate([kall_ref[rows, cols], aug_ref[rows]], axis=1), q_e)
+
+        return [functools.partial(step, n) for n in range(3)]
+
+    for step in score_steps(0, 0, 0, 0):
+        step()
+
     @pl.loop(0, width // PAIR)
     def _(hp):
         @pl.when(hp >= 2)
@@ -274,61 +310,68 @@
             e_copy(hp - 2).wait()
 
         cols = pl.ds(pl.multiple_of(hp * PAIR, PAIR), PAIR)
-        q_pair, k_pair = q_ref[:, cols], kall_ref[:, cols]
         v_turned = vall_ref[:, cols].T
-        for s in range(2):
+        for u, (s, qt) in enumerate(units):
             h = 2 * hp + s
-            keep = low_lane if s == 0 else jnp.logical_not(low_lane)
-            raw = dot_nt(jnp.where(keep, k_pair, k_aug), jnp.where(keep, q_pair, q_aug))
+            coming = units[(u + 1) % len(units)]
+            at = hp if u + 1 < len(units) else jnp.minimum(hp + 1, width // PAIR - 1)
+            steps = score_steps(at, *coming, (u + 1) % 2)
             back_far, ahead_far = tile_ref[h, 0, 0:1, BLK - 1 :], tile_ref[h, 2, BLK - 1 :, 0:1]
             other_far = jnp.where(half == 0, ahead_far, back_far)
             values = (back_far, ahead_far, other_far)
-            slot_bias = slot_bias_ref[pl.ds(pl.multiple_of(h * BLK, BLK), BLK), :]
             columns = []
-            for qb in range(blocks):
-                here = slice(qb * BLK, (qb + 1) * BLK)
-                parts, consts = [], []
-                for kb in range(2 * blocks):
-                    part = raw[kb * BLK : (kb + 1) * BLK, here]
-                    const = None
+            for sub in range(QCOLS // BLK):
+                qb = qt * (QCOLS // BLK) + sub
+                here = slice(sub * BLK, (sub + 1) * BLK)
+
+                def part_of(kb):
+                    part = score_ref[u % 2, kb * BLK : (kb + 1) * BLK, here]
+                    if kb == 2 * blocks:
+                        slot_rows = pl.ds(pl.multiple_of(h * BLK, BLK), BLK)
+                        return part + slot_bias_ref[slot_rows, qb * BLK : (qb + 1) * BLK], None
+                    gap = kb - qb
+                    if kb < blocks and abs(gap) <= 1:
+                        return part + tile_ref[h, gap + 1], None
                     if kb < blocks:
-                        gap = kb - qb
-                        if abs(gap) <= 1:
-                            part = part + tile_ref[h, gap + 1]
-                        else:
-                            const = 0 if gap < 0 else 1
-                    elif qb == blocks - 1 and kb == blocks:
-                        part = part + jnp.where(half == 0, tile_ref[h, 2], back_far)
-                    elif qb == 0 and kb == 2 * blocks - 1:
-                        part = part + jnp.where(half == 0, ahead_far, tile_ref[h, 0])
-                    else:
-                        const = 2
-                    parts.append(part)
-                    consts.append(const)
-                parts.append(raw[2 * blocks * BLK :, here] + slot_bias[:, here])
-                consts.append(None)
-                peak = None
-                for group in (None, 0, 1, 2):
-                    members = [p for p, c in zip(parts, consts) if c == group]
-                    if not members:
-                        continue
-                    top = jnp.max(functools.reduce(jnp.maximum, members), axis=0, keepdims=True)
-                    if group is not None:
-                        top = top + values[group]
-                    peak = top if peak is None else jnp.maximum(peak, top)
+                        return part, 0 if gap < 0 else 1
+                    if qb == blocks - 1 and kb == blocks:
+                        return part + jnp.where(half == 0, tile_ref[h, 2], back_far), None
+                    if qb == 0 and kb == 2 * blocks - 1:
+                        return part + jnp.where(half == 0, ahead_far, tile_ref[h, 0]), None
+                    return part, 2
+
+                tops, group = {}, {}
+                for kb in range(2 * blocks + 1):
+                    part, const = part_of(kb)
+                    if const is None:
+                        score_ref[u % 2, kb * BLK : (kb + 1) * BLK, here] = part
+                    group[kb] = const
+                    top = jnp.max(part.reshape(BLK // 8, 8, BLK), axis=0)
+                    tops[const] = top if const not in tops else jnp.maximum(tops[const], top)
+                    if steps and kb == 4:
+                        steps.pop(0)()
+                peak = functools.reduce(
+                    jnp.maximum, [top if const is None else top + values[const] for const, top in tops.items()]
+                )
+                peak = jnp.max(peak, axis=0, keepdims=True)
                 shifts = [peak - value for value in values]
-                columns.append(
-                    [jnp.exp(p - (peak if c is None else shifts[c])).astype(bf16) for p, c in zip(parts, consts)]
-                )
-            raised = jnp.concatenate(
-                [jnp.concatenate([column[kb] for column in columns], axis=1) for kb in range(2 * blocks + 1)], axis=0
-            )
-            e_buf[lax.rem(hp, 2), s] = raised
-            turned = jnp.concatenate([v_turned[s * HEAD : (s + 1) * HEAD], ones], axis=0)
-            total = dot_nn(turned, raised)
+                column = []
+                for kb in range(2 * blocks + 1):
+                    part = score_ref[u % 2, kb * BLK : (kb + 1) * BLK, here]
+                    shift = peak if group[kb] is None else shifts[group[kb]]
+                    column.append(jnp.exp(part - shift).astype(bf16))
+                    if steps and kb == 4:
+                        steps.pop(0)()
+                columns.append(jnp.concatenate(column, axis=0))
+            for step in steps:
+                step()
+            raised = jnp.concatenate(columns, axis=1)
+            qcols = slice(qt * QCOLS, (qt + 1) * QCOLS)
+            e_buf[lax.rem(hp, 2), s, :, qcols] = raised
+            total = dot_nn(jnp.concatenate([v_turned[s * HEAD : (s + 1) * HEAD], ones], axis=0), raised)
             inv = 1.0 / total[HEAD : HEAD + 1]
-            inv_ref[pl.ds(h, 1), :] = inv
-            mixed_ref[pl.ds(pl.multiple_of(h * HEAD, HEAD), HEAD), :] = (total[:HEAD] * inv).astype(bf16)
+            inv_ref[pl.ds(h, 1), qcols] = inv
+            mixed_ref[pl.ds(pl.multiple_of(h * HEAD, HEAD), HEAD), qcols] = (total[:HEAD] * inv).astype(bf16)
         e_copy(hp).start()
 
     @pl.loop(0, half_len // BLK)
@@ -359,13 +402,13 @@
         e_copy(hp).wait()
 
 
-def backward_kernel(count, piece, *refs):
+def backward_kernel(count, piece, rows_own, *refs):
     cots = refs[:count]
     (
         marks_ref, act_ref, after_ref, mixed_ref, inv_ref, q_ref, kall_ref, vall_ref, prompt_ref, gain_first_ref, gain_second_ref,
         wout_ref, wi_ref, wo_ref, wq_ref, wk_ref, wv_ref, e_ref,
-        grad_ref,
-        cot_ref, acc_ref, low_ref, do_ref, dq_ref, gk_ref, gv_ref, e_buf, sems,
+        kept_ref, sent_ref,
+        cot_ref, acc_ref, low_ref, do_ref, dq_ref, gk_ref, gv_ref, cast_ref, e_buf, sems,
     ) = refs[count:]
     half, turn = places(count)
     first, second = marks_ref[0:1, 0:1], marks_ref[1:2, 0:1]
@@ -408,7 +451,7 @@
 
     low_lane = lax.broadcasted_iota(i32, (1, PAIR), 1) < HEAD
     row = lax.broadcasted_iota(i32, (PAIR, 1), 0)
-    row_at = lax.rem(row, HEAD)
+    ones = jnp.ones((2 * half_len + BLK, PAIR), bf16)
 
     @pl.loop(0, pairs)
     def _(hp):
@@ -421,12 +464,12 @@
         slot_scores, slot_raised = [], []
         for s in range(2):
             mine = (row < HEAD) == (s == 0)
-            keep = low_lane if s == 0 else jnp.logical_not(low_lane)
             high, low = split_two(-jnp.sum(inner[s * HEAD : (s + 1) * HEAD], axis=0, keepdims=True))
             zero = jnp.zeros((), bf16)
-            do_e = jnp.where(mine, do_pair, jnp.where(row_at == 0, high, jnp.where(row_at == 1, low, zero)))
+            shift = jnp.where(row == 0, high, jnp.where(row == 1, low, zero))
+            do_e = jnp.concatenate([jnp.where(mine, do_pair, zero), shift], axis=0)
             raised = e_buf[lax.rem(hp, 2), s]
-            grad_probs = dot_nn(jnp.where(keep, v_pair, jnp.ones((), bf16)), do_e)
+            grad_probs = dot_nn(jnp.concatenate([v_pair, ones], axis=1), do_e)
             grad_scores = (raised.astype(f32) * grad_probs).astype(bf16)
             made = dot_nn(k_turned[s * HEAD : (s + 1) * HEAD], grad_scores)
             dq_ref[pl.ds(pl.multiple_of(hp * PAIR + s * HEAD, HEAD), HEAD), :] = made.astype(bf16)
@@ -453,7 +496,50 @@
     scale = inv_rms(hidden)
     pulled = gain_first_ref[...] * pulled
     along = jnp.mean(hidden * pulled, axis=-1, keepdims=True)
-    grad_ref[...] = direct + scale * pulled - hidden * (scale * scale * scale * along)
+    grad = direct + scale * pulled - hidden * (scale * scale * scale * along)
+    for place in range(BLK // (2 * rows_own)):
+        rows = slice(place * rows_own, (place + 1) * rows_own)
+        low, high = (grad[(2 * place + c) * rows_own : (2 * place + c + 1) * rows_own] for c in range(2))
+        kept_ref[rows, :] = jnp.where(half == 0, low, high)
+        cast_ref[rows, :] = jnp.where(half == 0, high, low)
+    sent_ref[...] = cast_ref[...].astype(bf16)
+
+
+def share_kernel(rows_own, kept_ref, came_ref, mine_ref, *refs):
+    parts, (total_ref,) = refs[:-1], refs[-1:]
+    chip = lax.div(lax.axis_index("dp"), 2)
+    total = kept_ref[...] + came_ref[...].astype(f32)
+    for place in range(len(parts) + 1):
+        total_ref[place] = total[place * rows_own : (place + 1) * rows_own]
+    mine_ref[...] = total_ref[chip]
+    for n in range(1, len(parts) + 1):
+        parts[n - 1][...] = total_ref[chip ^ n].astype(bf16)
+
+
+def square_kernel(total_ref, *refs):
+    parts, (own_ref, square_ref) = refs[:-2], refs[-2:]
+    total = total_ref[...]
+    for part in parts:
+        total = total + part[...].astype(f32)
+    few = own_ref.shape[1]
+    own = total[:, 0:few]
+    for place in range(1, len(parts) + 1):
+        own = jnp.where(lax.axis_index("ctx") == place, total[:, place * few : (place + 1) * few], own)
+    own_ref[...] = own
+    square = jnp.sum(jnp.sum(total * total, axis=1, keepdims=True), axis=0, keepdims=True)
+    square_ref[...] = jnp.broadcast_to(square, square_ref.shape)
+
+
+def update_kernel(max_norm, grad_ref, prompt_ref, first_ref, second_ref, *refs):
+    squares, (prompt_out, first_out, second_out) = refs[:-3], refs[-3:]
+    square = functools.reduce(jnp.add, [square[0:1, 0:1] for square in squares])
+    clipped = grad_ref[...] * (max_norm / jnp.maximum(jnp.sqrt(square), max_norm))
+    first_new = beta_first * first_ref[...] + (1.0 - beta_first) * clipped
+    second_new = beta_second * second_ref[...] + (1.0 - beta_second) * clipped * clipped
+    step = learn_rate * (first_new / first_fix) / (jnp.sqrt(second_new / second_fix) + adam_eps)
+    prompt_out[...] = prompt_ref[...] - step
+    first_out[...] = first_new
+    second_out[...] = second_new
 
 
 def on_device(
@@ -483,15 +569,6 @@
 
     def there(k):
         return lambda d, z: (2 * (d // 2) + z // count, (d % 2) * count + (z + k) % count)
-
-    def in_order(parts, me, axis):
-        ordered = []
-        for place in range(len(parts)):
-            picked = parts[0]
-            for n in range(1, len(parts)):
-                picked = jnp.where((me ^ n) == place, parts[n], picked)
-            ordered.append(picked)
-        return jnp.concatenate(ordered, axis=axis)
 
     rows_own, cols_own = prompt.shape
     piece_like = held((piece, width), bf16)
@@ -510,9 +587,20 @@
         cost_estimate=cost(1e5, 2e6),
     )(in_hbm(tokens), in_hbm(segment_ids), in_hbm(prompt))
 
-    block = packed[count]
-    blocks = [block] + [swap_ctx(block, n) for n in range(1, n_ctx)]
     own = [permute(packed[k], there(k)) for k in range(count)]
+    chip_rows = jnp.concatenate([packed[count], swap_dp(packed[count], 1)], axis=0)
+    chip_parts = [chip_rows] + [swap_dp(chip_rows, 2 * n) for n in range(1, n_dp // 2)]
+    plane = pl.pallas_call(
+        functools.partial(plane_kernel, rows_own),
+        out_shape=held((BLK + 16, cols_own), bf16),
+        in_specs=[vmem_spec()] * len(chip_parts),
+        out_specs=vmem_spec(),
+        scratch_shapes=[pltpu.VMEM((BLK + 16, cols_own), f32)],
+        compiler_params=params(4),
+        cost_estimate=cost(1e5, 1e5),
+    )(*chip_parts)
+    cols_of = [plane] + [swap_ctx(plane, n) for n in range(1, n_ctx)]
+
     choose = (np.arange(bias_table.shape[0])[:, None] == bucket_table(2 * BLK - np.arange(4 * BLK))[None]).astype(np.float32)
     base = lax.dot_general(
         bias_table, jnp.asarray(choose), (((0,), (0,)), ((), ())), precision=lax.Precision.HIGHEST
@@ -534,23 +622,17 @@
     cot_pieces = prepared[4 : 4 + count]
     w_q, w_k, w_v, w_o, w_i, w_out = prepared[4 + count :]
 
-    block = in_order(blocks, ctx, 1)
-    other = swap_dp(block, 1)
-    chip_rows = in_order([block[:rows_own], other[:rows_own]], core, 0)
-    sent = in_order([chip_rows] + [swap_dp(chip_rows, 2 * n) for n in range(1, n_dp // 2)], dp // 2, 0)
-
     keys_all = 2 * half_len + BLK
     hidden_ff = w_inner.shape[1]
     partner = [swap_dp(piece_rows, 1) for piece_rows in own]
-    kall, vall = pl.pallas_call(
+    normed = pl.pallas_call(
         functools.partial(first_kernel, count, piece),
-        out_shape=[held((keys_all, width), bf16), held((keys_all, width), bf16)],
-        in_specs=[vmem_spec()] * (count + 3),
-        out_specs=[vmem_spec()] * 2,
-        scratch_shapes=[pltpu.VMEM((half_len, width), bf16)],
+        out_shape=held((half_len, width), bf16),
+        in_specs=[vmem_spec()] * (count + 1),
+        out_specs=vmem_spec(),
         compiler_params=params(A_MIB),
         cost_estimate=cost(1e10, 8e6),
-    )(*own, gain_1, w_k, w_v)
+    )(*own, gain_1)
     cots = [permute(cot_pieces[k], there(k)) for k in range(count)]
 
     made = pl.pallas_call(
@@ -558,6 +640,7 @@
         out_shape=[
             pltpu.HBM((heads // 2, 2, keys_all, half_len), bf16),
             held((8, BLK), i32),
+            held((BLK, width), bf16),
             held((half_len, width), bf16),
             held((keys_all, width), bf16),
             held((keys_all, width), bf16),
@@ -567,30 +650,32 @@
             held((half_len, hidden_ff), bf16),
         ]
         + [piece_like] * count,
-        in_specs=[vmem_spec()] * (2 * count + 15),
-        out_specs=[any_spec()] + [vmem_spec()] * (8 + count),
+        in_specs=[vmem_spec()] * (4 * count + 11),
+        out_specs=[any_spec()] + [vmem_spec()] * (9 + count),
         scratch_shapes=[
             pltpu.VMEM((2 * half_len + BLK, width), bf16),
             pltpu.VMEM((half_len, width), bf16),
             pltpu.VMEM((heads * BLK, half_len), f32),
+            pltpu.VMEM((2, keys_all, QCOLS), f32),
+            pltpu.VMEM((keys_all, PAIR), bf16),
+            pltpu.VMEM((BLK, width), f32),
             pltpu.VMEM((2, 2, keys_all, half_len), bf16),
             pltpu.SemaphoreType.DMA((2,)),
         ],
-        input_output_aliases={2 * count + 3: 3, 2 * count + 4: 4},
         compiler_params=params(F_MIB),
         cost_estimate=cost(3e10, 4e7, heads * half_len * keys_all),
     )(
-        *own, *partner, block, other, sent, kall, vall, gain_1, gain_2, w_q, w_k, w_v, w_o, w_i, w_out, tiles,
-        table,
+        *own, *partner, normed, gain_1, gain_2, w_q, w_k, w_v, w_o, w_i, w_out, tiles, table, *cols_of,
     )
-    got = [permute(made[9 + k], back_of(count, k)) for k in range(count)]
-    e, marks, q, kall, vall, mixed, inv, after, act = made[:9]
-
-    grad = pl.pallas_call(
-        functools.partial(backward_kernel, count, piece),
-        out_shape=held((BLK, width), f32),
+    got = [permute(made[10 + k], back_of(count, k)) for k in range(count)]
+    e, marks, sent, q, kall, vall, mixed, inv, after, act = made[:10]
+
+    half_rows = n_dp // 2 * rows_own
+    kept, leaving = pl.pallas_call(
+        functools.partial(backward_kernel, count, piece, rows_own),
+        out_shape=[held((half_rows, width), f32), held((half_rows, width), bf16)],
         in_specs=[vmem_spec()] * (count + 17) + [any_spec()],
-        out_specs=vmem_spec(),
+        out_specs=[vmem_spec()] * 2,
         scratch_shapes=[
             pltpu.VMEM((half_len, width), bf16),
             pltpu.VMEM((half_len, width), f32),
@@ -599,6 +684,7 @@
             pltpu.VMEM((width, half_len), bf16),
             pltpu.VMEM((BLK, width), bf16),
             pltpu.VMEM((BLK, width), bf16),
+            pltpu.VMEM((half_rows, width), f32),
             pltpu.VMEM((2, 2, keys_all, half_len), bf16),
             pltpu.SemaphoreType.DMA((2,)),
         ],
@@ -608,32 +694,47 @@
         *cots, marks, act, after, mixed, inv, q, kall, vall, sent, gain_1, gain_2, w_out, w_i, w_o, w_q, w_k, w_v, in_hbm(e),
     )
 
-    got, grad = lax.optimization_barrier((got, grad))
+    got, leaving = lax.optimization_barrier((got, leaving))
     order = [lax.rem(ctx + j, count) for j in range(count)]
     output = jnp.stack(
         [functools.reduce(lambda a, k: jnp.where(order[k] == r, got[k], a), range(1, count), got[0]) for r in range(count)]
     )
 
-    per = rows_own
-    view = grad.reshape(n_dp // 2, 2, per, width)
-    mine = jnp.where(core == 1, view[:, 1], view[:, 0])
-    theirs = jnp.where(core == 1, view[:, 0], view[:, 1]).astype(bf16)
-    total = (mine + swap_dp(theirs, 1).astype(f32)).reshape(n_dp // 2 * per, width)
-    plane = total.astype(bf16)
-    for n in range(1, n_dp // 2):
-        total = total + swap_dp(plane, 2 * n).astype(f32)
-    line = total.astype(bf16)
-    for n in range(1, n_ctx):
-        total = total + swap_ctx(line, n).astype(f32)
-    square = jnp.full((8, BLK), jnp.sum(total * total), f32)
+    chips = n_dp // 2
+    own_like = held((rows_own, width), f32)
+    mine, *parts = pl.pallas_call(
+        functools.partial(share_kernel, rows_own),
+        out_shape=[own_like] + [held((rows_own, width), bf16)] * (chips - 1),
+        in_specs=[vmem_spec()] * 2,
+        out_specs=[vmem_spec()] * chips,
+        scratch_shapes=[pltpu.VMEM((chips, rows_own, width), f32)],
+        compiler_params=params(4),
+        cost_estimate=cost(1e5, 1e5),
+    )(kept, swap_dp(leaving, 1))
+    for n in range(1, chips):
+        mine = mine + swap_dp(parts[n - 1], 2 * n).astype(f32)
+    line = mine.astype(bf16)
+    line_parts = [swap_ctx(line, n) for n in range(1, n_ctx)]
+    line_parts, output = lax.optimization_barrier((line_parts, output))
+    grad_own, square = pl.pallas_call(
+        square_kernel,
+        out_shape=[held((rows_own, cols_own), f32), held((8, BLK), f32)],
+        in_specs=[vmem_spec()] * n_ctx,
+        out_specs=[vmem_spec()] * 2,
+        compiler_params=params(4),
+        cost_estimate=cost(1e5, 1e5),
+    )(mine, *line_parts)
     square = square + swap_dp(square, 1)
-    max_norm = 0.5 * jnp.sqrt(f32(PROMPT * width))
-    norm_total = jnp.sqrt(square[0, 0])
-    grad_own = lax.dynamic_slice(total, (dp // 2 * per, ctx * cols_own), (per, cols_own))
-    clipped = grad_own * (max_norm / jnp.maximum(norm_total, max_norm))
-    first_new = beta_first * first_moment + (1.0 - beta_first) * clipped
-    second_new = beta_second * second_moment + (1.0 - beta_second) * clipped * clipped
-    prompt_new = prompt - learn_rate * (first_new / first_fix) / (jnp.sqrt(second_new / second_fix) + adam_eps)
+    squares = [square] + [swap_dp(square, 2 * n) for n in range(1, chips)]
+    own_out = out((rows_own, cols_own), f32)
+    prompt_new, first_new, second_new = pl.pallas_call(
+        functools.partial(update_kernel, float(0.5 * np.sqrt(np.float32(PROMPT * width)))),
+        out_shape=[own_out] * 3,
+        in_specs=[vmem_spec()] * (4 + chips),
+        out_specs=[vmem_spec()] * 3,
+        compiler_params=params(4),
+        cost_estimate=cost(1e5, 1e5),
+    )(grad_own, prompt, first_moment, second_moment, *squares)
     return (output, prompt_new, first_new, second_new)
 
 

time: 114 us -> 110 us (0.965)
  starting transfers between devices: 32.5 us -> 36.6 us
  Pallas kernels: 56.9 us -> 53 us
  other arithmetic: 3.4 us -> 1.02 us
  local copies, waits for them, and re-layouts: 2.57 us -> 1.41 us
    ppermute x23 -> x26, starting transfers between devices: 32.5 us -> 36.6 us  [permute(): return lax.ppermute(value, AXES, pairs)]
    pallas_call x1, Pallas kernels: 28.5 us -> 25.2 us  [on_device(): pl.pallas_call(functools.partial(forward_kernel, count, piece, rows_own),...]
    pallas_call x2 -> x6, Pallas kernels: 21 us -> 20.4 us  [the longest x1 19.1 us: on_device(): pl.pallas_call(functools.partial(backward_kernel, count, piece, rows_own)...]
    ppermute x23 -> x26, waiting for transfers between devices: 15.8 us -> 15.3 us  [permute(): return lax.ppermute(value, AXES, pairs)]
  transfers between devices with their start and end apart: 23 -> 26, of which waited for: 10 -> 11; matrix products, arithmetic and copies ran while one was open for 3% -> 3% of each run, Pallas kernels for 49% -> 47%
where the time goes in v4:
time: 110 us; the launch traced here: 109 us
  Pallas kernels  53 us (48%)
  starting transfers between devices  36.6 us (33%)
  waiting for transfers between devices  15.3 us (14%)
  local copies, waits for them, and re-layouts  1.41 us (1%)
    ppermute x26, starting transfers between devices, permute(): return lax.ppermute(value, AXES, pairs)  36.6 us
    pallas_call x1, Pallas kernels, on_device(): pl.pallas_call(functools.partial(forward_kernel, count, piece, rows_own),...  25.2 us
    pallas_call x1, Pallas kernels, on_device(): pl.pallas_call(functools.partial(backward_kernel, count, piece, rows_own)...  19.1 us
    ppermute x26, waiting for transfers between devices, permute(): return lax.ppermute(value, AXES, pairs)  15.3 us
    pallas_call x1, Pallas kernels, on_device(): pl.pallas_call(functools.partial(prepare_kernel, count), out_shape=[held(...  6.19 us
  transfers between devices with their start and end apart: 26, of which 11 were waited for; matrix products, arithmetic and copies ran while one was open for 3% of the time, Pallas kernels for 47%

profile of v4, /device:TPU:0, one launch (start us, length us, event | category | flops | bytes accessed | tf_op | source)
XLA Modules:
  0.0 109.2 jit_solution(1062933764809285028)
XLA Ops:
  0.6 0.0 copy-start
  0.6 1.2 %shard_map.184 = (bf16[256,768]{1,0:T(8,128)(2,1)S(1)}, bf16[256,768]{1,0:T(8,128)(2,1)S(1)}, bf16[24,192]{1,0:T(8,128)(2,1)S(1)}) custom-call(bf16[2,256,768]{2,1,0:T(8,128)(2,1)} %tokens_ref.1, s32[2,256]{1,0:T(2,128)} %seg_hbm.1, f32[16,192]{1,0:T(8,128)} %prompt_ref.1), custom_call_target="tpu_custom_call" | custom-call | flops 100000 | bytes 2000000 | tf_op jit(solution)/shard_map/pallas_call | solution.py:575
  1.8 0.7 collective-permute-start.2
  2.5 3.1 %collective-permute-start.3 = (bf16[256,768]{1,0:T(8,128)(2,1)S(1)}, bf16[256,768]{1,0:T(8,128)(2,1)S(1)}, u32[]{:S(2)}, u32[]{:S(2)}) collective-permute-start(bf16[256,768]{1,0:T(8,128)(2,1)S(1)} %get-tuple-element.52), channel_id=1, source_target_pairs={{0,1},{1,0},{2,5},{3,4},{4,3},{5,2},{6,7},{7,6},{8,9},{9,8},{10,13... | collective-permute-start | bytes 1179656 | tf_op jit(solution)/shard_map/ppermute | solution.py:562
  5.6 3.4 %collective-permute-start.6 = (bf16[24,192]{1,0:T(8,128)(2,1)S(1)}, bf16[24,192]{1,0:T(8,128)(2,1)S(1)}, u32[]{:S(2)}, u32[]{:S(2)}) collective-permute-start(bf16[24,192]{1,0:T(8,128)(2,1)S(1)} %get-tuple-element.63), channel_id=1, source_target_pairs={{0,4},{1,5},{2,6},{3,7},{4,0},{5,1},{6,2},{7,3},{8,12},{9,13},{10,... | collective-permute-start | bytes 27656 | tf_op jit(solution)/shard_map/ppermute | solution.py:562
  9.0 0.8 collective-permute-done.6
  9.8 1.5 %collective-permute-start.7 = (bf16[48,192]{1,0:T(8,128)(2,1)S(1)}, bf16[48,192]{1,0:T(8,128)(2,1)S(1)}, u32[]{:S(2)}, u32[]{:S(2)}) collective-permute-start(bf16[48,192]{1,0:T(8,128)(2,1)S(1)} %constant_dynamic-update-slice_fusion.refs_0_), channel_id=1, source_target_pairs={{0,8},{1,9},{2,10},{3,11},{4,12},{5,13},{6,14},{7,15},{8,0},{9,1},... | collective-permute-start | bytes 55304 | tf_op jit(solution)/shard_map/ppermute | solution.py:562
  11.3 1.5 %collective-permute-start.8 = (bf16[48,192]{1,0:T(8,128)(2,1)S(1)}, bf16[48,192]{1,0:T(8,128)(2,1)S(1)}, u32[]{:S(2)}, u32[]{:S(2)}) collective-permute-start(bf16[48,192]{1,0:T(8,128)(2,1)S(1)} %constant_dynamic-update-slice_fusion.refs_0_), channel_id=1, source_target_pairs={{0,16},{1,17},{2,18},{3,19},{4,20},{5,21},{6,22},{7,23},{8,24},{9,... | collective-permute-start | bytes 55304 | tf_op jit(solution)/shard_map/ppermute | solution.py:562
  12.8 0.5 collective-permute-start.9
  13.3 1.0 convolution_bitcast_fusion.base_ref
  14.3 0.7 broadcast_in_dim.6.gain_first_ref
  15.0 0.7 broadcast_in_dim.7.gain_second_ref
  15.7 6.2 %shard_map.183 = (f32[12,3,128,128]{3,2,1,0:T(8,128)S(1)}, bf16[1536,512]{1,0:T(8,128)(2,1)S(1)}, f32[1,768]{1,0:T(1,128)S(1)}, f32[1,768]{1,0:T(1,128)S(1)}, bf...) custom-call(f32[12,512]{1,0:T(8,128)S(1)} %convolution_bitcast_fusio, ...), custom_call_target="tpu_custom_call" | custom-call | flops 1000000 | bytes 15000000 | tf_op jit(solution)/shard_map/pallas_call | solution.py:609
  22.0 0.7 collective-permute-start.10
  22.7 2.7 %collective-permute-start.11 = (bf16[144,192]{1,0:T(8,128)(2,1)S(1)}, bf16[144,192]{1,0:T(8,128)(2,1)S(1)}, u32[]{:S(2)}, u32[]{:S(2)}) collective-permute-start(bf16[144,192]{1,0:T(8,128)(2,1)S(1)} %shard_map.186.refs_15_), channel_id=1, source_target_pairs={{0,2},{1,3},{2,0},{3,1},{4,6},{5,7},{6,4},{7,5},{8,10},{9,11},{10,... | collective-permute-start | bytes 165896 | tf_op jit(solution)/shard_map/ppermute | solution.py:562
  25.4 1.1 collective-permute-start.12
  26.5 0.5 collective-permute-start.5
  27.0 0.3 shard_map.185.refs_4_
  27.3 0.7 collective-permute-start
  28.0 3.7 %collective-permute-done.11.refs_17_ = bf16[144,192]{1,0:T(8,128)(2,1)S(1)} collective-permute-done((bf16[144,192]{1,0:T(8,128)(2,1)S(1)}, bf16[144,192]{1,0:T(8,128)(2,1)S(1)}, u32[]{:S(2)}, u32[]{:S(2)}) %collective-permute-start.11) | collective-permute-done | bytes 55328 | tf_op jit(solution)/shard_map/ppermute | solution.py:562
  31.7 25.2 %shard_map.187 = (bf16[6,2,1152,512]{3,2,1,0:T(8,128)(2,1)}, s32[8,128]{1,0:T(8,128)S(1)}, bf16[128,768]{1,0:T(8,128)(2,1)S(1)}, bf16[512,768]{1,0:T(8,128)(2,1)...) custom-call(bf16[256,768]{1,0:T(8,128)(2,1)S(1)} %collective-permute, ...), custom_call_target="tpu_custom_call" | custom-call | flops 30000001024 | bytes 40000000 | tf_op jit(solution)/shard_map/pallas_call | solution.py:638
  56.9 0.9 collective-permute-start.13
  57.8 2.1 %collective-permute-start.14 = (bf16[256,768]{1,0:T(8,128)(2,1)S(1)}, bf16[256,768]{1,0:T(8,128)(2,1)S(1)}, u32[]{:S(2)}, u32[]{:S(2)}) collective-permute-start(bf16[256,768]{1,0:T(8,128)(2,1)S(1)} %get-tuple-element.76), channel_id=1, source_target_pairs={{0,1},{1,0},{2,5},{3,4},{4,3},{5,2},{6,7},{7,6},{8,9},{9,8},{10,13... | collective-permute-start | bytes 1179656 | tf_op jit(solution)/shard_map/ppermute | solution.py:562
  59.9 19.1 %shard_map.188 = (f32[64,768]{1,0:T(8,128)S(1)}, bf16[64,768]{1,0:T(8,128)(2,1)S(1)}) custom-call(bf16[256,768]{1,0:T(8,128)(2,1)S(1)} %collective-permute-done.refs_0_, bf16[256,768]{1,0:T(8,128)(2,1)S(1)} %collective-permute-done.1.refs_1_, s32[8,128]{1,0:T(8,128)S(1)} %get-tuple-element.64.refs_2_, bf16[512,3072]{1,0:T(8,128)(2,1)S(1)} %get-tuple-element.65.refs_3_, ...), custom_call_target="tpu_custom_call" | custom-call | flops 30000001024 | bytes 40000000 | tf_op jit(solution)/shard_map/pallas_call | solution.py:674
  79.0 5.8 %collective-permute-start.15 = (bf16[64,768]{1,0:T(8,128)(2,1)S(1)}, bf16[64,768]{1,0:T(8,128)(2,1)S(1)}, u32[]{:S(2)}, u32[]{:S(2)}) collective-permute-start(bf16[64,768]{1,0:T(8,128)(2,1)S(1)} %get-tuple-element.78), channel_id=1, source_target_pairs={{0,4},{1,5},{2,6},{3,7},{4,0},{5,1},{6,2},{7,3},{8,12},{9,13},{10,... | collective-permute-start | bytes 294920 | tf_op jit(solution)/shard_map/ppermute | solution.py:562
  84.7 0.9 collective-permute-done.15.came_ref
  85.7 2.5 %collective-permute-start.18 = (bf16[16,768]{1,0:T(8,128)(2,1)S(1)}, bf16[16,768]{1,0:T(8,128)(2,1)S(1)}, u32[]{:S(2)}, u32[]{:S(2)}) collective-permute-start(bf16[16,768]{1,0:T(8,128)(2,1)S(1)} %get-tuple-element.82), channel_id=1, source_target_pairs={{0,24},{1,25},{2,26},{3,27},{4,28},{5,29},{6,30},{7,31},{8,16},{9,... | collective-permute-start | bytes 73736 | tf_op jit(solution)/shard_map/ppermute | solution.py:562
  88.3 0.5 collective-permute-start.17
  88.8 0.6 collective-permute-start.16
  89.4 0.1 select_bitcast_fusion.1
  89.4 1.1 %collective-permute-done.18 = bf16[16,768]{1,0:T(8,128)(2,1)S(1)} collective-permute-done((bf16[16,768]{1,0:T(8,128)(2,1)S(1)}, bf16[16,768]{1,0:T(8,128)(2,1)S(1)}, u32[]{:S(2)}, u32[]{:S(2)}) %collective-permute-start.18) | collective-permute-done | bytes 24608 | tf_op jit(solution)/shard_map/ppermute | solution.py:562
  90.5 1.6 %collective-permute-done.17 = bf16[16,768]{1,0:T(8,128)(2,1)S(1)} collective-permute-done((bf16[16,768]{1,0:T(8,128)(2,1)S(1)}, bf16[16,768]{1,0:T(8,128)(2,1)S(1)}, u32[]{:S(2)}, u32[]{:S(2)}) %collective-permute-start.17) | collective-permute-done | bytes 24608 | tf_op jit(solution)/shard_map/ppermute | solution.py:562
  92.1 0.6 collective-permute-done.16
  92.7 0.6 collective-permute-start.19
  93.3 1.5 %collective-permute-start.20 = (bf16[16,768]{1,0:T(8,128)(2,1)S(1)}, bf16[16,768]{1,0:T(8,128)(2,1)S(1)}, u32[]{:S(2)}, u32[]{:S(2)}) collective-permute-start(bf16[16,768]{1,0:T(8,128)(2,1)S(1)} %get-tuple-element.94), channel_id=1, source_target_pairs={{0,2},{1,3},{2,0},{3,1},{4,6},{5,7},{6,4},{7,5},{8,10},{9,11},{10,... | collective-permute-start | bytes 73736 | tf_op jit(solution)/shard_map/ppermute | solution.py:562
  94.8 2.3 %collective-permute-start.21 = (bf16[16,768]{1,0:T(8,128)(2,1)S(1)}, bf16[16,768]{1,0:T(8,128)(2,1)S(1)}, u32[]{:S(2)}, u32[]{:S(2)}) collective-permute-start(bf16[16,768]{1,0:T(8,128)(2,1)S(1)} %get-tuple-element.94), channel_id=1, source_target_pairs={{0,3},{1,2},{2,1},{3,0},{4,7},{5,6},{6,5},{7,4},{8,11},{9,10},{10,... | collective-permute-start | bytes 73736 | tf_op jit(solution)/shard_map/ppermute | solution.py:562
  97.1 0.9 pad_maximum_fusion
  98.1 2.3 %collective-permute-done.21.refs_2_ = bf16[16,768]{1,0:T(8,128)(2,1)S(1)} collective-permute-done((bf16[16,768]{1,0:T(8,128)(2,1)S(1)}, bf16[16,768]{1,0:T(8,128)(2,1)S(1)}, u32[]{:S(2)}, u32[]{:S(2)}) %collective-permute-start.21) | collective-permute-done | bytes 24608 | tf_op jit(solution)/shard_map/ppermute | solution.py:562
  100.4 0.3 shard_map.190
  100.7 0.1 collective-permute-start.22
  100.7 1.2 %collective-permute-done.22 = f32[8,128]{1,0:T(8,128)S(1)} collective-permute-done((f32[8,128]{1,0:T(8,128)S(1)}, f32[8,128]{1,0:T(8,128)S(1)}, u32[]{:S(2)}, u32[]{:S(2)}) %collective-permute-start.22) | collective-permute-done | bytes 4128 | tf_op jit(solution)/shard_map/ppermute | solution.py:562
  101.9 0.5 collective-permute-start.23
  102.4 1.5 %collective-permute-start.24 = (f32[8,128]{1,0:T(8,128)S(1)}, f32[8,128]{1,0:T(8,128)S(1)}, u32[]{:S(2)}, u32[]{:S(2)}) collective-permute-start(f32[8,128]{1,0:T(8,128)S(1)} %add.19.refs_0_), channel_id=1, source_target_pairs={{0,16},{1,17},{2,18},{3,19},{4,20},{5,21},{6,22},{7,23},{8,24},{9,... | collective-permute-start | bytes 12296 | tf_op jit(solution)/shard_map/ppermute | solution.py:562
  103.9 1.4 %collective-permute-start.25 = (f32[8,128]{1,0:T(8,128)S(1)}, f32[8,128]{1,0:T(8,128)S(1)}, u32[]{:S(2)}, u32[]{:S(2)}) collective-permute-start(f32[8,128]{1,0:T(8,128)S(1)} %add.19.refs_0_), channel_id=1, source_target_pairs={{0,24},{1,25},{2,26},{3,27},{4,28},{5,29},{6,30},{7,31},{8,16},{9,... | collective-permute-start | bytes 12296 | tf_op jit(solution)/shard_map/ppermute | solution.py:562
  105.4 0.1 collective-permute-done.23.refs_1_
  105.5 0.5 collective-permute-done.24.refs_2_
  106.0 2.4 %collective-permute-done.25.refs_3_ = f32[8,128]{1,0:T(8,128)S(1)} collective-permute-done((f32[8,128]{1,0:T(8,128)S(1)}, f32[8,128]{1,0:T(8,128)S(1)}, u32[]{:S(2)}, u32[]{:S(2)}) %collective-permute-start.25) | collective-permute-done | bytes 4128 | tf_op jit(solution)/shard_map/ppermute | solution.py:562
  108.5 0.7 shard_map.191
  (32 shorter events, 0.2 us)
Async XLA Ops:
  0.6 12.7 %copy-start = (f32[32,12]{0,1:T(8,128)S(1)}, f32[32,12]{0,1:T(8,128)}, u32[]{:S(2)}) copy-start(f32[32,12]{0,1:T(8,128)} %param.28) | copy-start | bytes 4612
  1.8 24.6 %collective-permute-start.2 = (bf16[256,768]{1,0:T(8,128)(2,1)S(1)}, bf16[256,768]{1,0:T(8,128)(2,1)S(1)}, u32[]{:S(2)}, u32[]{:S(2)}) collective-permute-start(bf16[256,768]{1,0:T(8,128)(2,1)S(1)} %get-tuple-element.51), channel_id=1, source_target_pairs={{0,0},{1,1},{2,4},{3,5},{4,2},{5,3},{6,6},{7,7},{8,8},{9,9},{10,12... | collective-permute-start | bytes 1179656 | tf_op jit(solution)/shard_map/ppermute | solution.py:562
  2.5 23.9 %collective-permute-start.3 = (bf16[256,768]{1,0:T(8,128)(2,1)S(1)}, bf16[256,768]{1,0:T(8,128)(2,1)S(1)}, u32[]{:S(2)}, u32[]{:S(2)}) collective-permute-start(bf16[256,768]{1,0:T(8,128)(2,1)S(1)} %get-tuple-element.52), channel_id=1, source_target_pairs={{0,1},{1,0},{2,5},{3,4},{4,3},{5,2},{6,7},{7,6},{8,9},{9,8},{10,13... | collective-permute-start | bytes 1179656 | tf_op jit(solution)/shard_map/ppermute | solution.py:562
  5.6 4.2 %collective-permute-start.6 = (bf16[24,192]{1,0:T(8,128)(2,1)S(1)}, bf16[24,192]{1,0:T(8,128)(2,1)S(1)}, u32[]{:S(2)}, u32[]{:S(2)}) collective-permute-start(bf16[24,192]{1,0:T(8,128)(2,1)S(1)} %get-tuple-element.63), channel_id=1, source_target_pairs={{0,4},{1,5},{2,6},{3,7},{4,0},{5,1},{6,2},{7,3},{8,12},{9,13},{10,... | collective-permute-start | bytes 27656 | tf_op jit(solution)/shard_map/ppermute | solution.py:562
  9.8 12.1 %collective-permute-start.7 = (bf16[48,192]{1,0:T(8,128)(2,1)S(1)}, bf16[48,192]{1,0:T(8,128)(2,1)S(1)}, u32[]{:S(2)}, u32[]{:S(2)}) collective-permute-start(bf16[48,192]{1,0:T(8,128)(2,1)S(1)} %constant_dynamic-update-slice_fusion.refs_0_), channel_id=1, source_target_pairs={{0,8},{1,9},{2,10},{3,11},{4,12},{5,13},{6,14},{7,15},{8,0},{9,1},... | collective-permute-start | bytes 55304 | tf_op jit(solution)/shard_map/ppermute | solution.py:562
  11.3 10.6 %collective-permute-start.8 = (bf16[48,192]{1,0:T(8,128)(2,1)S(1)}, bf16[48,192]{1,0:T(8,128)(2,1)S(1)}, u32[]{:S(2)}, u32[]{:S(2)}) collective-permute-start(bf16[48,192]{1,0:T(8,128)(2,1)S(1)} %constant_dynamic-update-slice_fusion.refs_0_), channel_id=1, source_target_pairs={{0,16},{1,17},{2,18},{3,19},{4,20},{5,21},{6,22},{7,23},{8,24},{9,... | collective-permute-start | bytes 55304 | tf_op jit(solution)/shard_map/ppermute | solution.py:562
  12.8 9.1 %collective-permute-start.9 = (bf16[48,192]{1,0:T(8,128)(2,1)S(1)}, bf16[48,192]{1,0:T(8,128)(2,1)S(1)}, u32[]{:S(2)}, u32[]{:S(2)}) collective-permute-start(bf16[48,192]{1,0:T(8,128)(2,1)S(1)} %constant_dynamic-update-slice_fusion.refs_0_), channel_id=1, source_target_pairs={{0,24},{1,25},{2,26},{3,27},{4,28},{5,29},{6,30},{7,31},{8,16},{9,... | collective-permute-start | bytes 55304 | tf_op jit(solution)/shard_map/ppermute | solution.py:562
  22.0 5.3 %collective-permute-start.10 = (bf16[144,192]{1,0:T(8,128)(2,1)S(1)}, bf16[144,192]{1,0:T(8,128)(2,1)S(1)}, u32[]{:S(2)}, u32[]{:S(2)}) collective-permute-start(bf16[144,192]{1,0:T(8,128)(2,1)S(1)} %shard_map.186.refs_15_), channel_id=1, source_target_pairs={{0,1},{1,0},{2,3},{3,2},{4,5},{5,4},{6,7},{7,6},{8,9},{9,8},{10,11... | collective-permute-start | bytes 165896 | tf_op jit(solution)/shard_map/ppermute | solution.py:562
  22.7 9.0 %collective-permute-start.11 = (bf16[144,192]{1,0:T(8,128)(2,1)S(1)}, bf16[144,192]{1,0:T(8,128)(2,1)S(1)}, u32[]{:S(2)}, u32[]{:S(2)}) collective-permute-start(bf16[144,192]{1,0:T(8,128)(2,1)S(1)} %shard_map.186.refs_15_), channel_id=1, source_target_pairs={{0,2},{1,3},{2,0},{3,1},{4,6},{5,7},{6,4},{7,5},{8,10},{9,11},{10,... | collective-permute-start | bytes 165896 | tf_op jit(solution)/shard_map/ppermute | solution.py:562
  25.4 6.3 %collective-permute-start.12 = (bf16[144,192]{1,0:T(8,128)(2,1)S(1)}, bf16[144,192]{1,0:T(8,128)(2,1)S(1)}, u32[]{:S(2)}, u32[]{:S(2)}) collective-permute-start(bf16[144,192]{1,0:T(8,128)(2,1)S(1)} %shard_map.186.refs_15_), channel_id=1, source_target_pairs={{0,3},{1,2},{2,1},{3,0},{4,7},{5,6},{6,5},{7,4},{8,11},{9,10},{10,... | collective-permute-start | bytes 165896 | tf_op jit(solution)/shard_map/ppermute | solution.py:562
  26.5 5.2 %collective-permute-start.4 = (bf16[256,768]{1,0:T(8,128)(2,1)S(1)}, bf16[256,768]{1,0:T(8,128)(2,1)S(1)}, u32[]{:S(2)}, u32[]{:S(2)}) collective-permute-start(bf16[256,768]{1,0:T(8,128)(2,1)S(1)} %collective-permute-done.2.refs_0_), channel_id=1, source_target_pairs={{0,4},{1,5},{2,6},{3,7},{4,0},{5,1},{6,2},{7,3},{8,12},{9,13},{10,... | collective-permute-start | bytes 1179656 | tf_op jit(solution)/shard_map/ppermute | solution.py:562
  26.5 5.2 %collective-permute-start.5 = (bf16[256,768]{1,0:T(8,128)(2,1)S(1)}, bf16[256,768]{1,0:T(8,128)(2,1)S(1)}, u32[]{:S(2)}, u32[]{:S(2)}) collective-permute-start(bf16[256,768]{1,0:T(8,128)(2,1)S(1)} %collective-permute-done.3.refs_1_), channel_id=1, source_target_pairs={{0,4},{1,5},{2,6},{3,7},{4,0},{5,1},{6,2},{7,3},{8,12},{9,13},{10,... | collective-permute-start | bytes 1179656 | tf_op jit(solution)/shard_map/ppermute | solution.py:562
  27.3 32.5 %collective-permute-start = (bf16[256,768]{1,0:T(8,128)(2,1)S(1)}, bf16[256,768]{1,0:T(8,128)(2,1)S(1)}, u32[]{:S(2)}, u32[]{:S(2)}) collective-permute-start(bf16[256,768]{1,0:T(8,128)(2,1)S(1)} %get-tuple-element.49), channel_id=1, source_target_pairs={{0,0},{1,1},{2,4},{3,5},{4,2},{5,3},{6,6},{7,7},{8,8},{9,9},{10,12... | collective-permute-start | bytes 1179656 | tf_op jit(solution)/shard_map/ppermute | solution.py:562
  31.7 28.2 %collective-permute-start.1 = (bf16[256,768]{1,0:T(8,128)(2,1)S(1)}, bf16[256,768]{1,0:T(8,128)(2,1)S(1)}, u32[]{:S(2)}, u32[]{:S(2)}) collective-permute-start(bf16[256,768]{1,0:T(8,128)(2,1)S(1)} %get-tuple-element.50), channel_id=1, source_target_pairs={{0,1},{1,0},{2,5},{3,4},{4,3},{5,2},{6,7},{7,6},{8,9},{9,8},{10,13... | collective-permute-start | bytes 1179656 | tf_op jit(solution)/shard_map/ppermute | solution.py:562
  56.9 22.0 %collective-permute-start.13 = (bf16[256,768]{1,0:T(8,128)(2,1)S(1)}, bf16[256,768]{1,0:T(8,128)(2,1)S(1)}, u32[]{:S(2)}, u32[]{:S(2)}) collective-permute-start(bf16[256,768]{1,0:T(8,128)(2,1)S(1)} %get-tuple-element.75), channel_id=1, source_target_pairs={{0,0},{1,1},{2,4},{3,5},{4,2},{5,3},{6,6},{7,7},{8,8},{9,9},{10,12... | collective-permute-start | bytes 1179656 | tf_op jit(solution)/shard_map/ppermute | solution.py:562
  57.8 21.2 %collective-permute-start.14 = (bf16[256,768]{1,0:T(8,128)(2,1)S(1)}, bf16[256,768]{1,0:T(8,128)(2,1)S(1)}, u32[]{:S(2)}, u32[]{:S(2)}) collective-permute-start(bf16[256,768]{1,0:T(8,128)(2,1)S(1)} %get-tuple-element.76), channel_id=1, source_target_pairs={{0,1},{1,0},{2,5},{3,4},{4,3},{5,2},{6,7},{7,6},{8,9},{9,8},{10,13... | collective-permute-start | bytes 1179656 | tf_op jit(solution)/shard_map/ppermute | solution.py:562
  79.0 6.7 %collective-permute-start.15 = (bf16[64,768]{1,0:T(8,128)(2,1)S(1)}, bf16[64,768]{1,0:T(8,128)(2,1)S(1)}, u32[]{:S(2)}, u32[]{:S(2)}) collective-permute-start(bf16[64,768]{1,0:T(8,128)(2,1)S(1)} %get-tuple-element.78), channel_id=1, source_target_pairs={{0,4},{1,5},{2,6},{3,7},{4,0},{5,1},{6,2},{7,3},{8,12},{9,13},{10,... | collective-permute-start | bytes 294920 | tf_op jit(solution)/shard_map/ppermute | solution.py:562
  85.7 4.8 %collective-permute-start.18 = (bf16[16,768]{1,0:T(8,128)(2,1)S(1)}, bf16[16,768]{1,0:T(8,128)(2,1)S(1)}, u32[]{:S(2)}, u32[]{:S(2)}) collective-permute-start(bf16[16,768]{1,0:T(8,128)(2,1)S(1)} %get-tuple-element.82), channel_id=1, source_target_pairs={{0,24},{1,25},{2,26},{3,27},{4,28},{5,29},{6,30},{7,31},{8,16},{9,... | collective-permute-start | bytes 73736 | tf_op jit(solution)/shard_map/ppermute | solution.py:562
  88.3 3.8 %collective-permute-start.17 = (bf16[16,768]{1,0:T(8,128)(2,1)S(1)}, bf16[16,768]{1,0:T(8,128)(2,1)S(1)}, u32[]{:S(2)}, u32[]{:S(2)}) collective-permute-start(bf16[16,768]{1,0:T(8,128)(2,1)S(1)} %get-tuple-element.81), channel_id=1, source_target_pairs={{0,16},{1,17},{2,18},{3,19},{4,20},{5,21},{6,22},{7,23},{8,24},{9,... | collective-permute-start | bytes 73736 | tf_op jit(solution)/shard_map/ppermute | solution.py:562
  88.7 20.4 %copy-start.1 = (f32[32,12]{0,1:T(8,128)S(1)}, f32[32,12]{0,1:T(8,128)}, u32[]{:S(2)}) copy-start(f32[32,12]{0,1:T(8,128)} %param.28) | copy-start | bytes 4612
  88.8 19.7 %copy-start.2 = (f32[16,192]{1,0:T(8,128)S(1)}, f32[16,192]{1,0:T(8,128)}, u32[]{:S(2)}) copy-start(f32[16,192]{1,0:T(8,128)} %prompt_ref.1) | copy-start | bytes 36868
  88.8 19.7 %copy-start.3 = (f32[16,192]{1,0:T(8,128)S(1)}, f32[16,192]{1,0:T(8,128)}, u32[]{:S(2)}) copy-start(f32[16,192]{1,0:T(8,128)} %first_ref.1) | copy-start | bytes 36868
  88.8 19.7 %copy-start.4 = (f32[16,192]{1,0:T(8,128)S(1)}, f32[16,192]{1,0:T(8,128)}, u32[]{:S(2)}) copy-start(f32[16,192]{1,0:T(8,128)} %second_ref.1) | copy-start | bytes 36868
  88.8 3.9 %collective-permute-start.16 = (bf16[16,768]{1,0:T(8,128)(2,1)S(1)}, bf16[16,768]{1,0:T(8,128)(2,1)S(1)}, u32[]{:S(2)}, u32[]{:S(2)}) collective-permute-start(bf16[16,768]{1,0:T(8,128)(2,1)S(1)} %get-tuple-element.80), channel_id=1, source_target_pairs={{0,8},{1,9},{2,10},{3,11},{4,12},{5,13},{6,14},{7,15},{8,0},{9,1},... | collective-permute-start | bytes 73736 | tf_op jit(solution)/shard_map/ppermute | solution.py:562
  92.7 5.4 %collective-permute-start.19 = (bf16[16,768]{1,0:T(8,128)(2,1)S(1)}, bf16[16,768]{1,0:T(8,128)(2,1)S(1)}, u32[]{:S(2)}, u32[]{:S(2)}) collective-permute-start(bf16[16,768]{1,0:T(8,128)(2,1)S(1)} %get-tuple-element.94), channel_id=1, source_target_pairs={{0,1},{1,0},{2,3},{3,2},{4,5},{5,4},{6,7},{7,6},{8,9},{9,8},{10,11... | collective-permute-start | bytes 73736 | tf_op jit(solution)/shard_map/ppermute | solution.py:562
  93.3 4.8 %collective-permute-start.20 = (bf16[16,768]{1,0:T(8,128)(2,1)S(1)}, bf16[16,768]{1,0:T(8,128)(2,1)S(1)}, u32[]{:S(2)}, u32[]{:S(2)}) collective-permute-start(bf16[16,768]{1,0:T(8,128)(2,1)S(1)} %get-tuple-element.94), channel_id=1, source_target_pairs={{0,2},{1,3},{2,0},{3,1},{4,6},{5,7},{6,4},{7,5},{8,10},{9,11},{10,... | collective-permute-start | bytes 73736 | tf_op jit(solution)/shard_map/ppermute | solution.py:562
  94.8 5.6 %collective-permute-start.21 = (bf16[16,768]{1,0:T(8,128)(2,1)S(1)}, bf16[16,768]{1,0:T(8,128)(2,1)S(1)}, u32[]{:S(2)}, u32[]{:S(2)}) collective-permute-start(bf16[16,768]{1,0:T(8,128)(2,1)S(1)} %get-tuple-element.94), channel_id=1, source_target_pairs={{0,3},{1,2},{2,1},{3,0},{4,7},{5,6},{6,5},{7,4},{8,11},{9,10},{10,... | collective-permute-start | bytes 73736 | tf_op jit(solution)/shard_map/ppermute | solution.py:562
  100.7 1.2 %collective-permute-start.22 = (f32[8,128]{1,0:T(8,128)S(1)}, f32[8,128]{1,0:T(8,128)S(1)}, u32[]{:S(2)}, u32[]{:S(2)}) collective-permute-start(f32[8,128]{1,0:T(8,128)S(1)} %get-tuple-element.90), channel_id=1, source_target_pairs={{0,4},{1,5},{2,6},{3,7},{4,0},{5,1},{6,2},{7,3},{8,12},{9,13},{10,... | collective-permute-start | bytes 12296 | tf_op jit(solution)/shard_map/ppermute | solution.py:562
  101.9 3.6 %collective-permute-start.23 = (f32[8,128]{1,0:T(8,128)S(1)}, f32[8,128]{1,0:T(8,128)S(1)}, u32[]{:S(2)}, u32[]{:S(2)}) collective-permute-start(f32[8,128]{1,0:T(8,128)S(1)} %add.19.refs_0_), channel_id=1, source_target_pairs={{0,8},{1,9},{2,10},{3,11},{4,12},{5,13},{6,14},{7,15},{8,0},{9,1},... | collective-permute-start | bytes 12296 | tf_op jit(solution)/shard_map/ppermute | solution.py:562
  102.4 3.6 %collective-permute-start.24 = (f32[8,128]{1,0:T(8,128)S(1)}, f32[8,128]{1,0:T(8,128)S(1)}, u32[]{:S(2)}, u32[]{:S(2)}) collective-permute-start(f32[8,128]{1,0:T(8,128)S(1)} %add.19.refs_0_), channel_id=1, source_target_pairs={{0,16},{1,17},{2,18},{3,19},{4,20},{5,21},{6,22},{7,23},{8,24},{9,... | collective-permute-start | bytes 12296 | tf_op jit(solution)/shard_map/ppermute | solution.py:562
  103.9 4.5 %collective-permute-start.25 = (f32[8,128]{1,0:T(8,128)S(1)}, f32[8,128]{1,0:T(8,128)S(1)}, u32[]{:S(2)}, u32[]{:S(2)}) collective-permute-start(f32[8,128]{1,0:T(8,128)S(1)} %add.19.refs_0_), channel_id=1, source_target_pairs={{0,24},{1,25},{2,26},{3,27},{4,28},{5,29},{6,30},{7,31},{8,16},{9,... | collective-permute-start | bytes 12296 | tf_op jit(solution)/shard_map/ppermute | solution.py:562

commit v5 on v4

--- a/solution.py
+++ b/solution.py
@@ -12,6 +12,7 @@
 HEAD = 64
 PAIR = 2 * HEAD
 BLK = 128
+SHOWN = 112
 QCOLS = 256
 norm_eps = 1e-06
 beta_first = 0.9
@@ -102,7 +103,7 @@
 
 def pick_piece(pieces, turn, j):
     count = len(pieces)
-    place = lax.rem(turn - j + count, count)
+    place = lax.rem(turn - j - 1 + count, count)
     picked = pieces[0][...]
     for k in range(1, count):
         picked = jnp.where(place == k, pieces[k][...], picked)
@@ -117,7 +118,7 @@
     pieces, (block_ref, seg_ref, prompt_ref, wide_ref, sems) = refs[:count], refs[count:]
     ctx = lax.axis_index("ctx")
     copies = [
-        pltpu.make_async_copy(tokens_ref.at[slot_of(ctx + k, count)], pieces[k], sems.at[k]) for k in range(count)
+        pltpu.make_async_copy(tokens_ref.at[slot_of(ctx + k + 1, count)], pieces[k], sems.at[k]) for k in range(count)
     ]
     small = [
         pltpu.make_async_copy(seg_hbm, seg_ref, sems.at[count]),
@@ -139,13 +140,13 @@
 
 
 def prepare_kernel(count, base_ref, gain_first_ref, gain_second_ref, cot_ref, *refs):
-    weights, (tile_ref, table_ref, first_ref, second_ref) = refs[:6], refs[6:10]
-    pieces, kept, sems = refs[10 : 10 + count], refs[10 + count : 16 + count], refs[16 + count]
+    weights, (tile_ref, table_ref, first_ref, second_ref) = refs[:3], refs[3:7]
+    pieces, kept, sems = refs[7 : 7 + count], refs[7 + count : 10 + count], refs[10 + count]
     first_ref[...] = gain_first_ref[...]
     second_ref[...] = gain_second_ref[...]
     ctx = lax.axis_index("ctx")
-    copies = [pltpu.make_async_copy(weights[n], kept[n], sems.at[n]) for n in range(6)] + [
-        pltpu.make_async_copy(cot_ref.at[slot_of(ctx + k, count)], pieces[k], sems.at[6 + k]) for k in range(count)
+    copies = [pltpu.make_async_copy(weights[n], kept[n], sems.at[n]) for n in range(3)] + [
+        pltpu.make_async_copy(cot_ref.at[slot_of(ctx + k + 1, count)], pieces[k], sems.at[3 + k]) for k in range(count)
     ]
     for copy in copies:
         copy.start()
@@ -179,8 +180,8 @@
             start = (2 * place + c) * rows_own
             wide_ref[start : start + rows_own, :] = picked[:rows_own]
     for c in range(2):
-        wide_ref[BLK + 8 * c : BLK + 8 * (c + 1), :] = parts[0][c][rows_own:]
-    out_ref[...] = wide_ref[...].astype(bf16)
+        wide_ref[SHOWN + 8 * c : SHOWN + 8 * (c + 1), :] = parts[0][c][rows_own:]
+    out_ref[...] = wide_ref[0 : SHOWN + 16, :].astype(bf16)
 
 
 def places(count):
@@ -198,26 +199,31 @@
 def forward_kernel(count, piece, rows_own, *refs):
     own, partner = refs[:count], refs[count : 2 * count]
     (
-        normed_ref, gain_first_ref, gain_second_ref, wq_ref, wk_ref, wv_ref, wo_ref, wi_ref, wout_ref,
-        tile_ref, table_ref,
-    ) = refs[2 * count : 2 * count + 11]
-    refs = refs[2 * count + 11 :]
-    cols_of, refs = refs[: 2 * count], refs[2 * count :]
+        normed_ref, gain_first_ref, gain_second_ref, wq_ref, wk_ref, wv_ref, tile_ref, table_ref,
+    ) = refs[2 * count : 2 * count + 8]
+    refs = refs[2 * count + 8 :]
+    cols_of, later, refs = refs[: 2 * count], refs[2 * count : 2 * count + 3], refs[2 * count + 3 :]
     e_ref, marks_ref, prompt_ref, q_ref, kall_ref, vall_ref, mixed_ref, inv_ref, after_ref, act_ref = refs[:10]
-    going, refs = refs[10 : 10 + count], refs[10 + count :]
-    norm_ref, hid_ref, slot_bias_ref, score_ref, aug_ref, shown_ref, e_buf, sems = refs
+    kept, refs = refs[10:13], refs[13:]
+    wo_ref, wi_ref, wout_ref = kept
+    going, refs = refs[:count], refs[count:]
+    norm_ref, hid_ref, slot_bias_ref, score_ref, aug_ref, shown_ref, e_buf, sems, weight_sems = refs
+    fetches = [pltpu.make_async_copy(later[n], kept[n], weight_sems.at[n]) for n in range(3)]
+    for fetch in fetches:
+        fetch.start()
     ctx = lax.axis_index("ctx")
     few = cols_of[0].shape[1]
     for place in range(2 * count):
-        picked = cols_of[0][0:BLK]
+        picked = cols_of[0][0:SHOWN]
         for n in range(1, 2 * count):
-            picked = jnp.where((ctx ^ n) == place, cols_of[n][0:BLK], picked)
-        shown_ref[:, place * few : (place + 1) * few] = picked.astype(f32)
+            picked = jnp.where((ctx ^ n) == place, cols_of[n][0:SHOWN], picked)
+        shown_ref[0:SHOWN, place * few : (place + 1) * few] = picked.astype(f32)
+    shown_ref[SHOWN:, :] = jnp.zeros((BLK - SHOWN, shown_ref.shape[1]), f32)
     prompt_ref[...] = shown_ref[...].astype(bf16)
     half, turn = places(count)
     half_len = count * piece
     width = q_ref.shape[1]
-    tally = functools.reduce(jnp.add, [cols[BLK:].astype(f32) for cols in cols_of])
+    tally = functools.reduce(jnp.add, [cols[SHOWN:].astype(f32) for cols in cols_of])
     tally_row = lax.broadcasted_iota(i32, (tally.shape[0], 1), 0)
     marks = []
     for n in range(2):
@@ -374,10 +380,14 @@
             mixed_ref[pl.ds(pl.multiple_of(h * HEAD, HEAD), HEAD), qcols] = (total[:HEAD] * inv).astype(bf16)
         e_copy(hp).start()
 
+    for fetch in fetches:
+        fetch.wait()
+    after_ref[...] = dot_tn(mixed_ref[...], wo_ref[...])
+
     @pl.loop(0, half_len // BLK)
     def _(t):
         rows = pl.ds(pl.multiple_of(t * BLK, BLK), BLK)
-        after = hid_ref[rows, :].astype(f32) + dot_tn(mixed_ref[:, rows], wo_ref[...])
+        after = hid_ref[rows, :].astype(f32) + after_ref[rows, :]
         after_ref[rows, :] = after
         norm_ref[rows, :] = (after * inv_rms(after) * gain_second_ref[...]).astype(bf16)
 
@@ -392,7 +402,7 @@
         made = (after_ref[:, cols] + dot_nn(act_ref[...], wout_ref[:, cols])).astype(bf16)
         made = [made[j * piece : (j + 1) * piece] for j in range(count)]
         for k in range(count):
-            place = slot_of(turn - k, count)
+            place = slot_of(turn - k - 1, count)
             sent = made[0]
             for j in range(1, count):
                 sent = jnp.where(place == j, made[j], sent)
@@ -568,7 +578,7 @@
         return permute(value, lambda d, z: (d, z ^ bit))
 
     def there(k):
-        return lambda d, z: (2 * (d // 2) + z // count, (d % 2) * count + (z + k) % count)
+        return lambda d, z: (2 * (d // 2) + z // count, (d % 2) * count + (z + k + 1) % count)
 
     rows_own, cols_own = prompt.shape
     piece_like = held((piece, width), bf16)
@@ -592,35 +602,36 @@
     chip_parts = [chip_rows] + [swap_dp(chip_rows, 2 * n) for n in range(1, n_dp // 2)]
     plane = pl.pallas_call(
         functools.partial(plane_kernel, rows_own),
-        out_shape=held((BLK + 16, cols_own), bf16),
+        out_shape=held((SHOWN + 16, cols_own), bf16),
         in_specs=[vmem_spec()] * len(chip_parts),
         out_specs=vmem_spec(),
         scratch_shapes=[pltpu.VMEM((BLK + 16, cols_own), f32)],
         compiler_params=params(4),
         cost_estimate=cost(1e5, 1e5),
     )(*chip_parts)
-    cols_of = [plane] + [swap_ctx(plane, n) for n in range(1, n_ctx)]
 
     choose = (np.arange(bias_table.shape[0])[:, None] == bucket_table(2 * BLK - np.arange(4 * BLK))[None]).astype(np.float32)
     base = lax.dot_general(
         bias_table, jnp.asarray(choose), (((0,), (0,)), ((), ())), precision=lax.Precision.HIGHEST
     )
-    weights = (w_query, w_key, w_value, w_output, w_inner, w_outer)
+    base, plane = lax.optimization_barrier((base, plane))
+    cols_of = [plane] + [swap_ctx(plane, n) for n in range(1, n_ctx)]
+    weights = (w_query, w_key, w_value)
     prepared = pl.pallas_call(
         functools.partial(prepare_kernel, count),
         out_shape=[held((heads, 3, BLK, BLK), f32), held((heads * BLK, 4 * BLK), bf16)]
         + [held((1, width), f32)] * 2
         + [piece_like] * count
         + [held(w.shape, bf16) for w in weights],
-        in_specs=[vmem_spec()] * 3 + [any_spec()] * 7,
-        out_specs=[vmem_spec()] * (10 + count),
-        scratch_shapes=[pltpu.SemaphoreType.DMA((6 + count,))],
+        in_specs=[vmem_spec()] * 3 + [any_spec()] * 4,
+        out_specs=[vmem_spec()] * (7 + count),
+        scratch_shapes=[pltpu.SemaphoreType.DMA((3 + count,))],
         compiler_params=params(4),
-        cost_estimate=cost(1e6, 1.5e7),
+        cost_estimate=cost(1e6, 5e6),
     )(base, gain_first[None], gain_second[None], in_hbm(cotangent), *[in_hbm(w) for w in weights])
     tiles, table, gain_1, gain_2 = prepared[:4]
     cot_pieces = prepared[4 : 4 + count]
-    w_q, w_k, w_v, w_o, w_i, w_out = prepared[4 + count :]
+    w_q, w_k, w_v = prepared[4 + count :]
 
     keys_all = 2 * half_len + BLK
     hidden_ff = w_inner.shape[1]
@@ -649,9 +660,10 @@
             held((half_len, width), f32),
             held((half_len, hidden_ff), bf16),
         ]
+        + [held(w.shape, bf16) for w in (w_output, w_inner, w_outer)]
         + [piece_like] * count,
-        in_specs=[vmem_spec()] * (4 * count + 11),
-        out_specs=[any_spec()] + [vmem_spec()] * (9 + count),
+        in_specs=[vmem_spec()] * (4 * count + 8) + [any_spec()] * 3,
+        out_specs=[any_spec()] + [vmem_spec()] * (12 + count),
         scratch_shapes=[
             pltpu.VMEM((2 * half_len + BLK, width), bf16),
             pltpu.VMEM((half_len, width), bf16),
@@ -661,13 +673,16 @@
             pltpu.VMEM((BLK, width), f32),
             pltpu.VMEM((2, 2, keys_all, half_len), bf16),
             pltpu.SemaphoreType.DMA((2,)),
+            pltpu.SemaphoreType.DMA((3,)),
         ],
         compiler_params=params(F_MIB),
         cost_estimate=cost(3e10, 4e7, heads * half_len * keys_all),
     )(
-        *own, *partner, normed, gain_1, gain_2, w_q, w_k, w_v, w_o, w_i, w_out, tiles, table, *cols_of,
+        *own, *partner, normed, gain_1, gain_2, w_q, w_k, w_v, tiles, table, *cols_of,
+        *[in_hbm(w) for w in (w_output, w_inner, w_outer)],
     )
-    got = [permute(made[10 + k], back_of(count, k)) for k in range(count)]
+    got = [permute(made[13 + k], back_of(count, k)) for k in range(count)]
+    w_o, w_i, w_out = made[10:13]
     e, marks, sent, q, kall, vall, mixed, inv, after, act = made[:10]
 
     half_rows = n_dp // 2 * rows_own
@@ -695,7 +710,7 @@
     )
 
     got, leaving = lax.optimization_barrier((got, leaving))
-    order = [lax.rem(ctx + j, count) for j in range(count)]
+    order = [lax.rem(ctx + j + 1, count) for j in range(count)]
     output = jnp.stack(
         [functools.reduce(lambda a, k: jnp.where(order[k] == r, got[k], a), range(1, count), got[0]) for r in range(count)]
     )
@@ -741,7 +756,7 @@
 def back_of(count, k):
     def target(d, z):
         half, c, r = d % 2, z // count, z % count
-        return (2 * (d // 2) + c, half * count + (r - k) % count)
+        return (2 * (d // 2) + c, half * count + (r - k - 1) % count)
 
     return target
 

time: 110 us -> 108 us (0.982)
  Pallas kernels: 53 us -> 49.2 us
  starting transfers between devices: 36.6 us -> 40.3 us
  waiting for transfers between devices: 15.3 us -> 14 us
    ppermute x26, starting transfers between devices: 36.6 us -> 40.3 us  [permute(): return lax.ppermute(value, AXES, pairs)]
    pallas_call x1, Pallas kernels: 6.19 us -> 3.03 us  [on_device(): pl.pallas_call(functools.partial(prepare_kernel, count), out_shape=[held(...]
    ppermute x26, waiting for transfers between devices: 15.3 us -> 14 us  [permute(): return lax.ppermute(value, AXES, pairs)]
  transfers between devices with their start and end apart: 26 -> 26, of which waited for: 11 -> 12; matrix products, arithmetic and copies ran while one was open for 3% -> 3% of each run, Pallas kernels for 47% -> 44%
where the time goes in v5:
time: 108 us
  Pallas kernels  49.2 us (46%)
  starting transfers between devices  40.3 us (37%)
  waiting for transfers between devices  14 us (13%)
  local copies, waits for them, and re-layouts  1.41 us (1%)
    ppermute x26, starting transfers between devices, permute(): return lax.ppermute(value, AXES, pairs)  40.3 us
    pallas_call x1, Pallas kernels, on_device(): pl.pallas_call(functools.partial(forward_kernel, count, piece, rows_own),...  24.5 us
    pallas_call x1, Pallas kernels, on_device(): pl.pallas_call(functools.partial(backward_kernel, count, piece, rows_own)...  19 us
    ppermute x26, waiting for transfers between devices, permute(): return lax.ppermute(value, AXES, pairs)  14 us
    pallas_call x1, Pallas kernels, on_device(): pl.pallas_call(functools.partial(prepare_kernel, count), out_shape=[held(...  3.03 us
  transfers between devices with their start and end apart: 26, of which 12 were waited for; matrix products, arithmetic and copies ran while one was open for 3% of the time, Pallas kernels for 44%

profile of v5, /device:TPU:0, one launch (start us, length us, event | category | flops | bytes accessed | tf_op | source)
XLA Modules:
  0.0 107.8 jit_solution(9488460210969306006)
XLA Ops:
  0.6 1.2 %shard_map.183 = (bf16[256,768]{1,0:T(8,128)(2,1)S(1)}, bf16[256,768]{1,0:T(8,128)(2,1)S(1)}, bf16[24,192]{1,0:T(8,128)(2,1)S(1)}) custom-call(bf16[2,256,768]{2,1,0:T(8,128)(2,1)} %tokens_ref.1, s32[2,256]{1,0:T(2,128)} %seg_hbm.1, f32[16,192]{1,0:T(8,128)} %prompt_ref.1), custom_call_target="tpu_custom_call" | custom-call | flops 100000 | bytes 2000000 | tf_op jit(solution)/shard_map/pallas_call | solution.py:585
  1.8 0.5 collective-permute-start
  2.4 2.6 %collective-permute-start.6 = (bf16[256,768]{1,0:T(8,128)(2,1)S(1)}, bf16[256,768]{1,0:T(8,128)(2,1)S(1)}, u32[]{:S(2)}, u32[]{:S(2)}) collective-permute-start(bf16[256,768]{1,0:T(8,128)(2,1)S(1)} %get-tuple-element.55), channel_id=1, source_target_pairs={{0,1},{1,0},{2,5},{3,4},{4,3},{5,2},{6,7},{7,6},{8,9},{9,8},{10,13... | collective-permute-start | bytes 1179656 | tf_op jit(solution)/shard_map/ppermute | solution.py:572
  5.0 0.7 collective-permute-start.7
  5.7 1.6 %collective-permute-start.1 = (bf16[48,192]{1,0:T(8,128)(2,1)S(1)}, bf16[48,192]{1,0:T(8,128)(2,1)S(1)}, u32[]{:S(2)}, u32[]{:S(2)}) collective-permute-start(bf16[48,192]{1,0:T(8,128)(2,1)S(1)} %constant_dynamic-update-slice_fusion.refs_0_), channel_id=1, source_target_pairs={{0,8},{1,9},{2,10},{3,11},{4,12},{5,13},{6,14},{7,15},{8,0},{9,1},... | collective-permute-start | bytes 55304 | tf_op jit(solution)/shard_map/ppermute | solution.py:572
  7.3 1.5 %collective-permute-start.2 = (bf16[48,192]{1,0:T(8,128)(2,1)S(1)}, bf16[48,192]{1,0:T(8,128)(2,1)S(1)}, u32[]{:S(2)}, u32[]{:S(2)}) collective-permute-start(bf16[48,192]{1,0:T(8,128)(2,1)S(1)} %constant_dynamic-update-slice_fusion.refs_0_), channel_id=1, source_target_pairs={{0,16},{1,17},{2,18},{3,19},{4,20},{5,21},{6,22},{7,23},{8,24},{9,... | collective-permute-start | bytes 55304 | tf_op jit(solution)/shard_map/ppermute | solution.py:572
  8.8 0.5 collective-permute-start.3
  9.3 1.0 convolution_bitcast_fusion.base_ref
  10.3 0.7 broadcast_in_dim.6.gain_first_ref
  11.0 0.7 broadcast_in_dim.7.gain_second_ref
  11.7 1.8 %collective-permute-done.3.refs_3_ = bf16[48,192]{1,0:T(8,128)(2,1)S(1)} collective-permute-done((bf16[48,192]{1,0:T(8,128)(2,1)S(1)}, bf16[48,192]{1,0:T(8,128)(2,1)S(1)}, u32[]{:S(2)}, u32[]{:S(2)}) %collective-permute-start.3) | collective-permute-done | bytes 18464 | tf_op jit(solution)/shard_map/ppermute | solution.py:572
  13.6 0.7 collective-permute-start.10
  14.3 5.3 %collective-permute-start.11 = (bf16[128,192]{1,0:T(8,128)(2,1)S(1)}, bf16[128,192]{1,0:T(8,128)(2,1)S(1)}, u32[]{:S(2)}, u32[]{:S(2)}) collective-permute-start(bf16[128,192]{1,0:T(8,128)(2,1)S(1)} %shard_map.184.refs_12_), channel_id=1, source_target_pairs={{0,2},{1,3},{2,0},{3,1},{4,6},{5,7},{6,4},{7,5},{8,10},{9,11},{10,... | collective-permute-start | bytes 147464 | tf_op jit(solution)/shard_map/ppermute | solution.py:572
  19.6 1.4 %collective-permute-start.12 = (bf16[128,192]{1,0:T(8,128)(2,1)S(1)}, bf16[128,192]{1,0:T(8,128)(2,1)S(1)}, u32[]{:S(2)}, u32[]{:S(2)}) collective-permute-start(bf16[128,192]{1,0:T(8,128)(2,1)S(1)} %shard_map.184.refs_12_), channel_id=1, source_target_pairs={{0,3},{1,2},{2,1},{3,0},{4,7},{5,6},{6,5},{7,4},{8,11},{9,10},{10,... | collective-permute-start | bytes 147464 | tf_op jit(solution)/shard_map/ppermute | solution.py:572
  21.0 3.0 %shard_map.185 = (f32[12,3,128,128]{3,2,1,0:T(8,128)S(1)}, bf16[1536,512]{1,0:T(8,128)(2,1)S(1)}, f32[1,768]{1,0:T(1,128)S(1)}, f32[1,768]{1,0:T(1,128)S(1)}, bf...) custom-call(f32[12,512]{1,0:T(8,128)S(1)} %convolution_bitcast_fusio, ...), custom_call_target="tpu_custom_call" | custom-call | flops 1000000 | bytes 5000000 | tf_op jit(solution)/shard_map/pallas_call | solution.py:620
  24.0 0.1 collective-permute-start.8
  24.1 4.8 %collective-permute-start.9 = (bf16[256,768]{1,0:T(8,128)(2,1)S(1)}, bf16[256,768]{1,0:T(8,128)(2,1)S(1)}, u32[]{:S(2)}, u32[]{:S(2)}) collective-permute-start(bf16[256,768]{1,0:T(8,128)(2,1)S(1)} %collective-permute-done.7.refs_1_), channel_id=1, source_target_pairs={{0,4},{1,5},{2,6},{3,7},{4,0},{5,1},{6,2},{7,3},{8,12},{9,13},{10,... | collective-permute-start | bytes 1179656 | tf_op jit(solution)/shard_map/ppermute | solution.py:572
  28.9 0.3 shard_map.186.refs_4_
  29.3 0.1 collective-permute-start.4
  29.4 0.4 collective-permute-done.11.refs_14_
  29.8 0.7 collective-permute-start.5
  30.5 24.5 %shard_map.187 = (bf16[6,2,1152,512]{3,2,1,0:T(8,128)(2,1)}, s32[8,128]{1,0:T(8,128)S(1)}, bf16[128,768]{1,0:T(8,128)(2,1)S(1)}, bf16[512,768]{1,0:T(8,128)(2,1)...) custom-call(bf16[256,768]{1,0:T(8,128)(2,1)S(1)} %collective-permute, ...), custom_call_target="tpu_custom_call" | custom-call | flops 30000001024 | bytes 40000000 | tf_op jit(solution)/shard_map/pallas_call | solution.py:649
  55.1 1.7 %collective-permute-start.13 = (bf16[256,768]{1,0:T(8,128)(2,1)S(1)}, bf16[256,768]{1,0:T(8,128)(2,1)S(1)}, u32[]{:S(2)}, u32[]{:S(2)}) collective-permute-start(bf16[256,768]{1,0:T(8,128)(2,1)S(1)} %get-tuple-element.79), channel_id=1, source_target_pairs={{0,1},{1,0},{2,5},{3,4},{4,3},{5,2},{6,7},{7,6},{8,9},{9,8},{10,13... | collective-permute-start | bytes 1179656 | tf_op jit(solution)/shard_map/ppermute | solution.py:572
  56.7 0.9 collective-permute-start.14
  57.6 19.0 %shard_map.188 = (f32[64,768]{1,0:T(8,128)S(1)}, bf16[64,768]{1,0:T(8,128)(2,1)S(1)}) custom-call(bf16[256,768]{1,0:T(8,128)(2,1)S(1)} %collective-permute-done.4.refs_0_, bf16[256,768]{1,0:T(8,128)(2,1)S(1)} %collective-permute-done.5.refs_1_, s32[8,128]{1,0:T(8,128)S(1)} %get-tuple-element.65.refs_2_, bf16[512,3072]{1,0:T(8,128)(2,1)S(1)} %get-tuple-element.66.refs_3_, ...), custom_call_target="tpu_custom_call" | custom-call | flops 30000001024 | bytes 40000000 | tf_op jit(solution)/shard_map/pallas_call | solution.py:689
  76.7 5.8 %collective-permute-start.15 = (bf16[64,768]{1,0:T(8,128)(2,1)S(1)}, bf16[64,768]{1,0:T(8,128)(2,1)S(1)}, u32[]{:S(2)}, u32[]{:S(2)}) collective-permute-start(bf16[64,768]{1,0:T(8,128)(2,1)S(1)} %get-tuple-element.82), channel_id=1, source_target_pairs={{0,4},{1,5},{2,6},{3,7},{4,0},{5,1},{6,2},{7,3},{8,12},{9,13},{10,... | collective-permute-start | bytes 294920 | tf_op jit(solution)/shard_map/ppermute | solution.py:572
  82.4 0.9 collective-permute-done.15.came_ref
  83.4 2.5 %collective-permute-start.18 = (bf16[16,768]{1,0:T(8,128)(2,1)S(1)}, bf16[16,768]{1,0:T(8,128)(2,1)S(1)}, u32[]{:S(2)}, u32[]{:S(2)}) collective-permute-start(bf16[16,768]{1,0:T(8,128)(2,1)S(1)} %get-tuple-element.86), channel_id=1, source_target_pairs={{0,24},{1,25},{2,26},{3,27},{4,28},{5,29},{6,30},{7,31},{8,16},{9,... | collective-permute-start | bytes 73736 | tf_op jit(solution)/shard_map/ppermute | solution.py:572
  86.0 0.5 collective-permute-start.17
  86.5 0.6 collective-permute-start.16
  87.1 1.1 %collective-permute-done.18 = bf16[16,768]{1,0:T(8,128)(2,1)S(1)} collective-permute-done((bf16[16,768]{1,0:T(8,128)(2,1)S(1)}, bf16[16,768]{1,0:T(8,128)(2,1)S(1)}, u32[]{:S(2)}, u32[]{:S(2)}) %collective-permute-start.18) | collective-permute-done | bytes 24608 | tf_op jit(solution)/shard_map/ppermute | solution.py:572
  88.2 1.6 %collective-permute-done.17 = bf16[16,768]{1,0:T(8,128)(2,1)S(1)} collective-permute-done((bf16[16,768]{1,0:T(8,128)(2,1)S(1)}, bf16[16,768]{1,0:T(8,128)(2,1)S(1)}, u32[]{:S(2)}, u32[]{:S(2)}) %collective-permute-start.17) | collective-permute-done | bytes 24608 | tf_op jit(solution)/shard_map/ppermute | solution.py:572
  89.8 0.6 collective-permute-done.16
  90.4 1.1 %collective-permute-start.19 = (bf16[16,768]{1,0:T(8,128)(2,1)S(1)}, bf16[16,768]{1,0:T(8,128)(2,1)S(1)}, u32[]{:S(2)}, u32[]{:S(2)}) collective-permute-start(bf16[16,768]{1,0:T(8,128)(2,1)S(1)} %get-tuple-element.98), channel_id=1, source_target_pairs={{0,1},{1,0},{2,3},{3,2},{4,5},{5,4},{6,7},{7,6},{8,9},{9,8},{10,11... | collective-permute-start | bytes 73736 | tf_op jit(solution)/shard_map/ppermute | solution.py:572
  91.5 2.0 %collective-permute-start.20 = (bf16[16,768]{1,0:T(8,128)(2,1)S(1)}, bf16[16,768]{1,0:T(8,128)(2,1)S(1)}, u32[]{:S(2)}, u32[]{:S(2)}) collective-permute-start(bf16[16,768]{1,0:T(8,128)(2,1)S(1)} %get-tuple-element.98), channel_id=1, source_target_pairs={{0,2},{1,3},{2,0},{3,1},{4,6},{5,7},{6,4},{7,5},{8,10},{9,11},{10,... | collective-permute-start | bytes 73736 | tf_op jit(solution)/shard_map/ppermute | solution.py:572
  93.4 1.4 %collective-permute-start.21 = (bf16[16,768]{1,0:T(8,128)(2,1)S(1)}, bf16[16,768]{1,0:T(8,128)(2,1)S(1)}, u32[]{:S(2)}, u32[]{:S(2)}) collective-permute-start(bf16[16,768]{1,0:T(8,128)(2,1)S(1)} %get-tuple-element.98), channel_id=1, source_target_pairs={{0,3},{1,2},{2,1},{3,0},{4,7},{5,6},{6,5},{7,4},{8,11},{9,10},{10,... | collective-permute-start | bytes 73736 | tf_op jit(solution)/shard_map/ppermute | solution.py:572
  94.8 0.9 pad_maximum_fusion
  95.8 0.5 collective-permute-done.20.refs_1_
  96.2 2.8 %collective-permute-done.21.refs_2_ = bf16[16,768]{1,0:T(8,128)(2,1)S(1)} collective-permute-done((bf16[16,768]{1,0:T(8,128)(2,1)S(1)}, bf16[16,768]{1,0:T(8,128)(2,1)S(1)}, u32[]{:S(2)}, u32[]{:S(2)}) %collective-permute-start.21) | collective-permute-done | bytes 24608 | tf_op jit(solution)/shard_map/ppermute | solution.py:572
  99.1 0.3 shard_map.190
  99.4 1.2 %collective-permute-done.22 = f32[8,128]{1,0:T(8,128)S(1)} collective-permute-done((f32[8,128]{1,0:T(8,128)S(1)}, f32[8,128]{1,0:T(8,128)S(1)}, u32[]{:S(2)}, u32[]{:S(2)}) %collective-permute-start.22) | collective-permute-done | bytes 4128 | tf_op jit(solution)/shard_map/ppermute | solution.py:572
  100.6 0.5 collective-permute-start.23
  101.1 1.5 %collective-permute-start.24 = (f32[8,128]{1,0:T(8,128)S(1)}, f32[8,128]{1,0:T(8,128)S(1)}, u32[]{:S(2)}, u32[]{:S(2)}) collective-permute-start(f32[8,128]{1,0:T(8,128)S(1)} %add.22.refs_0_), channel_id=1, source_target_pairs={{0,16},{1,17},{2,18},{3,19},{4,20},{5,21},{6,22},{7,23},{8,24},{9,... | collective-permute-start | bytes 12296 | tf_op jit(solution)/shard_map/ppermute | solution.py:572
  102.6 1.4 %collective-permute-start.25 = (f32[8,128]{1,0:T(8,128)S(1)}, f32[8,128]{1,0:T(8,128)S(1)}, u32[]{:S(2)}, u32[]{:S(2)}) collective-permute-start(f32[8,128]{1,0:T(8,128)S(1)} %add.22.refs_0_), channel_id=1, source_target_pairs={{0,24},{1,25},{2,26},{3,27},{4,28},{5,29},{6,30},{7,31},{8,16},{9,... | collective-permute-start | bytes 12296 | tf_op jit(solution)/shard_map/ppermute | solution.py:572
  104.0 0.1 collective-permute-done.23.refs_1_
  104.2 0.5 collective-permute-done.24.refs_2_
  104.7 2.4 %collective-permute-done.25.refs_3_ = f32[8,128]{1,0:T(8,128)S(1)} collective-permute-done((f32[8,128]{1,0:T(8,128)S(1)}, f32[8,128]{1,0:T(8,128)S(1)}, u32[]{:S(2)}, u32[]{:S(2)}) %collective-permute-start.25) | collective-permute-done | bytes 4128 | tf_op jit(solution)/shard_map/ppermute | solution.py:572
  107.1 0.7 shard_map.191
  (32 shorter events, 0.3 us)
Async XLA Ops:
  0.6 8.7 %copy-start = (f32[32,12]{0,1:T(8,128)S(1)}, f32[32,12]{0,1:T(8,128)}, u32[]{:S(2)}) copy-start(f32[32,12]{0,1:T(8,128)} %param.28) | copy-start | bytes 4612
  1.8 3.9 %collective-permute-start = (bf16[24,192]{1,0:T(8,128)(2,1)S(1)}, bf16[24,192]{1,0:T(8,128)(2,1)S(1)}, u32[]{:S(2)}, u32[]{:S(2)}) collective-permute-start(bf16[24,192]{1,0:T(8,128)(2,1)S(1)} %get-tuple-element.51), channel_id=1, source_target_pairs={{0,4},{1,5},{2,6},{3,7},{4,0},{5,1},{6,2},{7,3},{8,12},{9,13},{10,... | collective-permute-start | bytes 27656 | tf_op jit(solution)/shard_map/ppermute | solution.py:572
  2.4 21.7 %collective-permute-start.6 = (bf16[256,768]{1,0:T(8,128)(2,1)S(1)}, bf16[256,768]{1,0:T(8,128)(2,1)S(1)}, u32[]{:S(2)}, u32[]{:S(2)}) collective-permute-start(bf16[256,768]{1,0:T(8,128)(2,1)S(1)} %get-tuple-element.55), channel_id=1, source_target_pairs={{0,1},{1,0},{2,5},{3,4},{4,3},{5,2},{6,7},{7,6},{8,9},{9,8},{10,13... | collective-permute-start | bytes 1179656 | tf_op jit(solution)/shard_map/ppermute | solution.py:572
  5.0 19.1 %collective-permute-start.7 = (bf16[256,768]{1,0:T(8,128)(2,1)S(1)}, bf16[256,768]{1,0:T(8,128)(2,1)S(1)}, u32[]{:S(2)}, u32[]{:S(2)}) collective-permute-start(bf16[256,768]{1,0:T(8,128)(2,1)S(1)} %get-tuple-element.56), channel_id=1, source_target_pairs={{0,0},{1,1},{2,4},{3,5},{4,2},{5,3},{6,6},{7,7},{8,8},{9,9},{10,12... | collective-permute-start | bytes 1179656 | tf_op jit(solution)/shard_map/ppermute | solution.py:572
  5.7 6.0 %collective-permute-start.1 = (bf16[48,192]{1,0:T(8,128)(2,1)S(1)}, bf16[48,192]{1,0:T(8,128)(2,1)S(1)}, u32[]{:S(2)}, u32[]{:S(2)}) collective-permute-start(bf16[48,192]{1,0:T(8,128)(2,1)S(1)} %constant_dynamic-update-slice_fusion.refs_0_), channel_id=1, source_target_pairs={{0,8},{1,9},{2,10},{3,11},{4,12},{5,13},{6,14},{7,15},{8,0},{9,1},... | collective-permute-start | bytes 55304 | tf_op jit(solution)/shard_map/ppermute | solution.py:572
  7.3 4.4 %collective-permute-start.2 = (bf16[48,192]{1,0:T(8,128)(2,1)S(1)}, bf16[48,192]{1,0:T(8,128)(2,1)S(1)}, u32[]{:S(2)}, u32[]{:S(2)}) collective-permute-start(bf16[48,192]{1,0:T(8,128)(2,1)S(1)} %constant_dynamic-update-slice_fusion.refs_0_), channel_id=1, source_target_pairs={{0,16},{1,17},{2,18},{3,19},{4,20},{5,21},{6,22},{7,23},{8,24},{9,... | collective-permute-start | bytes 55304 | tf_op jit(solution)/shard_map/ppermute | solution.py:572
  8.8 4.7 %collective-permute-start.3 = (bf16[48,192]{1,0:T(8,128)(2,1)S(1)}, bf16[48,192]{1,0:T(8,128)(2,1)S(1)}, u32[]{:S(2)}, u32[]{:S(2)}) collective-permute-start(bf16[48,192]{1,0:T(8,128)(2,1)S(1)} %constant_dynamic-update-slice_fusion.refs_0_), channel_id=1, source_target_pairs={{0,24},{1,25},{2,26},{3,27},{4,28},{5,29},{6,30},{7,31},{8,16},{9,... | collective-permute-start | bytes 55304 | tf_op jit(solution)/shard_map/ppermute | solution.py:572
  13.6 15.7 %collective-permute-start.10 = (bf16[128,192]{1,0:T(8,128)(2,1)S(1)}, bf16[128,192]{1,0:T(8,128)(2,1)S(1)}, u32[]{:S(2)}, u32[]{:S(2)}) collective-permute-start(bf16[128,192]{1,0:T(8,128)(2,1)S(1)} %shard_map.184.refs_12_), channel_id=1, source_target_pairs={{0,1},{1,0},{2,3},{3,2},{4,5},{5,4},{6,7},{7,6},{8,9},{9,8},{10,11... | collective-permute-start | bytes 147464 | tf_op jit(solution)/shard_map/ppermute | solution.py:572
  14.3 15.6 %collective-permute-start.11 = (bf16[128,192]{1,0:T(8,128)(2,1)S(1)}, bf16[128,192]{1,0:T(8,128)(2,1)S(1)}, u32[]{:S(2)}, u32[]{:S(2)}) collective-permute-start(bf16[128,192]{1,0:T(8,128)(2,1)S(1)} %shard_map.184.refs_12_), channel_id=1, source_target_pairs={{0,2},{1,3},{2,0},{3,1},{4,6},{5,7},{6,4},{7,5},{8,10},{9,11},{10,... | collective-permute-start | bytes 147464 | tf_op jit(solution)/shard_map/ppermute | solution.py:572
  19.6 10.9 %collective-permute-start.12 = (bf16[128,192]{1,0:T(8,128)(2,1)S(1)}, bf16[128,192]{1,0:T(8,128)(2,1)S(1)}, u32[]{:S(2)}, u32[]{:S(2)}) collective-permute-start(bf16[128,192]{1,0:T(8,128)(2,1)S(1)} %shard_map.184.refs_12_), channel_id=1, source_target_pairs={{0,3},{1,2},{2,1},{3,0},{4,7},{5,6},{6,5},{7,4},{8,11},{9,10},{10,... | collective-permute-start | bytes 147464 | tf_op jit(solution)/shard_map/ppermute | solution.py:572
  24.0 6.5 %collective-permute-start.8 = (bf16[256,768]{1,0:T(8,128)(2,1)S(1)}, bf16[256,768]{1,0:T(8,128)(2,1)S(1)}, u32[]{:S(2)}, u32[]{:S(2)}) collective-permute-start(bf16[256,768]{1,0:T(8,128)(2,1)S(1)} %collective-permute-done.6.refs_0_), channel_id=1, source_target_pairs={{0,4},{1,5},{2,6},{3,7},{4,0},{5,1},{6,2},{7,3},{8,12},{9,13},{10,... | collective-permute-start | bytes 1179656 | tf_op jit(solution)/shard_map/ppermute | solution.py:572
  24.1 6.4 %collective-permute-start.9 = (bf16[256,768]{1,0:T(8,128)(2,1)S(1)}, bf16[256,768]{1,0:T(8,128)(2,1)S(1)}, u32[]{:S(2)}, u32[]{:S(2)}) collective-permute-start(bf16[256,768]{1,0:T(8,128)(2,1)S(1)} %collective-permute-done.7.refs_1_), channel_id=1, source_target_pairs={{0,4},{1,5},{2,6},{3,7},{4,0},{5,1},{6,2},{7,3},{8,12},{9,13},{10,... | collective-permute-start | bytes 1179656 | tf_op jit(solution)/shard_map/ppermute | solution.py:572
  29.3 28.3 %collective-permute-start.4 = (bf16[256,768]{1,0:T(8,128)(2,1)S(1)}, bf16[256,768]{1,0:T(8,128)(2,1)S(1)}, u32[]{:S(2)}, u32[]{:S(2)}) collective-permute-start(bf16[256,768]{1,0:T(8,128)(2,1)S(1)} %get-tuple-element.53), channel_id=1, source_target_pairs={{0,1},{1,0},{2,5},{3,4},{4,3},{5,2},{6,7},{7,6},{8,9},{9,8},{10,13... | collective-permute-start | bytes 1179656 | tf_op jit(solution)/shard_map/ppermute | solution.py:572
  29.8 27.8 %collective-permute-start.5 = (bf16[256,768]{1,0:T(8,128)(2,1)S(1)}, bf16[256,768]{1,0:T(8,128)(2,1)S(1)}, u32[]{:S(2)}, u32[]{:S(2)}) collective-permute-start(bf16[256,768]{1,0:T(8,128)(2,1)S(1)} %get-tuple-element.54), channel_id=1, source_target_pairs={{0,0},{1,1},{2,4},{3,5},{4,2},{5,3},{6,6},{7,7},{8,8},{9,9},{10,12... | collective-permute-start | bytes 1179656 | tf_op jit(solution)/shard_map/ppermute | solution.py:572
  55.1 21.6 %collective-permute-start.13 = (bf16[256,768]{1,0:T(8,128)(2,1)S(1)}, bf16[256,768]{1,0:T(8,128)(2,1)S(1)}, u32[]{:S(2)}, u32[]{:S(2)}) collective-permute-start(bf16[256,768]{1,0:T(8,128)(2,1)S(1)} %get-tuple-element.79), channel_id=1, source_target_pairs={{0,1},{1,0},{2,5},{3,4},{4,3},{5,2},{6,7},{7,6},{8,9},{9,8},{10,13... | collective-permute-start | bytes 1179656 | tf_op jit(solution)/shard_map/ppermute | solution.py:572
  56.7 19.9 %collective-permute-start.14 = (bf16[256,768]{1,0:T(8,128)(2,1)S(1)}, bf16[256,768]{1,0:T(8,128)(2,1)S(1)}, u32[]{:S(2)}, u32[]{:S(2)}) collective-permute-start(bf16[256,768]{1,0:T(8,128)(2,1)S(1)} %get-tuple-element.80), channel_id=1, source_target_pairs={{0,0},{1,1},{2,4},{3,5},{4,2},{5,3},{6,6},{7,7},{8,8},{9,9},{10,12... | collective-permute-start | bytes 1179656 | tf_op jit(solution)/shard_map/ppermute | solution.py:572
  76.7 6.7 %collective-permute-start.15 = (bf16[64,768]{1,0:T(8,128)(2,1)S(1)}, bf16[64,768]{1,0:T(8,128)(2,1)S(1)}, u32[]{:S(2)}, u32[]{:S(2)}) collective-permute-start(bf16[64,768]{1,0:T(8,128)(2,1)S(1)} %get-tuple-element.82), channel_id=1, source_target_pairs={{0,4},{1,5},{2,6},{3,7},{4,0},{5,1},{6,2},{7,3},{8,12},{9,13},{10,... | collective-permute-start | bytes 294920 | tf_op jit(solution)/shard_map/ppermute | solution.py:572
  83.4 4.8 %collective-permute-start.18 = (bf16[16,768]{1,0:T(8,128)(2,1)S(1)}, bf16[16,768]{1,0:T(8,128)(2,1)S(1)}, u32[]{:S(2)}, u32[]{:S(2)}) collective-permute-start(bf16[16,768]{1,0:T(8,128)(2,1)S(1)} %get-tuple-element.86), channel_id=1, source_target_pairs={{0,24},{1,25},{2,26},{3,27},{4,28},{5,29},{6,30},{7,31},{8,16},{9,... | collective-permute-start | bytes 73736 | tf_op jit(solution)/shard_map/ppermute | solution.py:572
  86.0 3.8 %collective-permute-start.17 = (bf16[16,768]{1,0:T(8,128)(2,1)S(1)}, bf16[16,768]{1,0:T(8,128)(2,1)S(1)}, u32[]{:S(2)}, u32[]{:S(2)}) collective-permute-start(bf16[16,768]{1,0:T(8,128)(2,1)S(1)} %get-tuple-element.85), channel_id=1, source_target_pairs={{0,16},{1,17},{2,18},{3,19},{4,20},{5,21},{6,22},{7,23},{8,24},{9,... | collective-permute-start | bytes 73736 | tf_op jit(solution)/shard_map/ppermute | solution.py:572
  86.5 21.4 %copy-start.1 = (f32[32,12]{0,1:T(8,128)S(1)}, f32[32,12]{0,1:T(8,128)}, u32[]{:S(2)}) copy-start(f32[32,12]{0,1:T(8,128)} %param.28) | copy-start | bytes 4612
  86.5 20.6 %copy-start.2 = (f32[16,192]{1,0:T(8,128)S(1)}, f32[16,192]{1,0:T(8,128)}, u32[]{:S(2)}) copy-start(f32[16,192]{1,0:T(8,128)} %prompt_ref.1) | copy-start | bytes 36868
  86.5 20.7 %copy-start.3 = (f32[16,192]{1,0:T(8,128)S(1)}, f32[16,192]{1,0:T(8,128)}, u32[]{:S(2)}) copy-start(f32[16,192]{1,0:T(8,128)} %first_ref.1) | copy-start | bytes 36868
  86.5 20.7 %copy-start.4 = (f32[16,192]{1,0:T(8,128)S(1)}, f32[16,192]{1,0:T(8,128)}, u32[]{:S(2)}) copy-start(f32[16,192]{1,0:T(8,128)} %second_ref.1) | copy-start | bytes 36868
  86.5 3.9 %collective-permute-start.16 = (bf16[16,768]{1,0:T(8,128)(2,1)S(1)}, bf16[16,768]{1,0:T(8,128)(2,1)S(1)}, u32[]{:S(2)}, u32[]{:S(2)}) collective-permute-start(bf16[16,768]{1,0:T(8,128)(2,1)S(1)} %get-tuple-element.84), channel_id=1, source_target_pairs={{0,8},{1,9},{2,10},{3,11},{4,12},{5,13},{6,14},{7,15},{8,0},{9,1},... | collective-permute-start | bytes 73736 | tf_op jit(solution)/shard_map/ppermute | solution.py:572
  90.4 5.4 %collective-permute-start.19 = (bf16[16,768]{1,0:T(8,128)(2,1)S(1)}, bf16[16,768]{1,0:T(8,128)(2,1)S(1)}, u32[]{:S(2)}, u32[]{:S(2)}) collective-permute-start(bf16[16,768]{1,0:T(8,128)(2,1)S(1)} %get-tuple-element.98), channel_id=1, source_target_pairs={{0,1},{1,0},{2,3},{3,2},{4,5},{5,4},{6,7},{7,6},{8,9},{9,8},{10,11... | collective-permute-start | bytes 73736 | tf_op jit(solution)/shard_map/ppermute | solution.py:572
  91.5 4.8 %collective-permute-start.20 = (bf16[16,768]{1,0:T(8,128)(2,1)S(1)}, bf16[16,768]{1,0:T(8,128)(2,1)S(1)}, u32[]{:S(2)}, u32[]{:S(2)}) collective-permute-start(bf16[16,768]{1,0:T(8,128)(2,1)S(1)} %get-tuple-element.98), channel_id=1, source_target_pairs={{0,2},{1,3},{2,0},{3,1},{4,6},{5,7},{6,4},{7,5},{8,10},{9,11},{10,... | collective-permute-start | bytes 73736 | tf_op jit(solution)/shard_map/ppermute | solution.py:572
  93.4 5.6 %collective-permute-start.21 = (bf16[16,768]{1,0:T(8,128)(2,1)S(1)}, bf16[16,768]{1,0:T(8,128)(2,1)S(1)}, u32[]{:S(2)}, u32[]{:S(2)}) collective-permute-start(bf16[16,768]{1,0:T(8,128)(2,1)S(1)} %get-tuple-element.98), channel_id=1, source_target_pairs={{0,3},{1,2},{2,1},{3,0},{4,7},{5,6},{6,5},{7,4},{8,11},{9,10},{10,... | collective-permute-start | bytes 73736 | tf_op jit(solution)/shard_map/ppermute | solution.py:572
  99.3 1.2 %collective-permute-start.22 = (f32[8,128]{1,0:T(8,128)S(1)}, f32[8,128]{1,0:T(8,128)S(1)}, u32[]{:S(2)}, u32[]{:S(2)}) collective-permute-start(f32[8,128]{1,0:T(8,128)S(1)} %get-tuple-element.94), channel_id=1, source_target_pairs={{0,4},{1,5},{2,6},{3,7},{4,0},{5,1},{6,2},{7,3},{8,12},{9,13},{10,... | collective-permute-start | bytes 12296 | tf_op jit(solution)/shard_map/ppermute | solution.py:572
  100.6 3.6 %collective-permute-start.23 = (f32[8,128]{1,0:T(8,128)S(1)}, f32[8,128]{1,0:T(8,128)S(1)}, u32[]{:S(2)}, u32[]{:S(2)}) collective-permute-start(f32[8,128]{1,0:T(8,128)S(1)} %add.22.refs_0_), channel_id=1, source_target_pairs={{0,8},{1,9},{2,10},{3,11},{4,12},{5,13},{6,14},{7,15},{8,0},{9,1},... | collective-permute-start | bytes 12296 | tf_op jit(solution)/shard_map/ppermute | solution.py:572
  101.1 3.6 %collective-permute-start.24 = (f32[8,128]{1,0:T(8,128)S(1)}, f32[8,128]{1,0:T(8,128)S(1)}, u32[]{:S(2)}, u32[]{:S(2)}) collective-permute-start(f32[8,128]{1,0:T(8,128)S(1)} %add.22.refs_0_), channel_id=1, source_target_pairs={{0,16},{1,17},{2,18},{3,19},{4,20},{5,21},{6,22},{7,23},{8,24},{9,... | collective-permute-start | bytes 12296 | tf_op jit(solution)/shard_map/ppermute | solution.py:572
  102.6 4.5 %collective-permute-start.25 = (f32[8,128]{1,0:T(8,128)S(1)}, f32[8,128]{1,0:T(8,128)S(1)}, u32[]{:S(2)}, u32[]{:S(2)}) collective-permute-start(f32[8,128]{1,0:T(8,128)S(1)} %add.22.refs_0_), channel_id=1, source_target_pairs={{0,24},{1,25},{2,26},{3,27},{4,28},{5,29},{6,30},{7,31},{8,16},{9,... | collective-permute-start | bytes 12296 | tf_op jit(solution)/shard_map/ppermute | solution.py:572

commit v6 on v5

--- a/solution.py
+++ b/solution.py
@@ -13,6 +13,7 @@
 PAIR = 2 * HEAD
 BLK = 128
 SHOWN = 112
+HELD = (SHOWN + 16) // 2
 QCOLS = 256
 norm_eps = 1e-06
 beta_first = 0.9
@@ -181,7 +182,7 @@
             wide_ref[start : start + rows_own, :] = picked[:rows_own]
     for c in range(2):
         wide_ref[SHOWN + 8 * c : SHOWN + 8 * (c + 1), :] = parts[0][c][rows_own:]
-    out_ref[...] = wide_ref[0 : SHOWN + 16, :].astype(bf16)
+    out_ref[...] = jnp.where(core == 0, wide_ref[0:HELD, :], wide_ref[HELD : 2 * HELD, :]).astype(bf16)
 
 
 def places(count):
@@ -202,7 +203,7 @@
         normed_ref, gain_first_ref, gain_second_ref, wq_ref, wk_ref, wv_ref, tile_ref, table_ref,
     ) = refs[2 * count : 2 * count + 8]
     refs = refs[2 * count + 8 :]
-    cols_of, later, refs = refs[: 2 * count], refs[2 * count : 2 * count + 3], refs[2 * count + 3 :]
+    (mine_ref, other_ref), later, refs = refs[:2], refs[2:5], refs[5:]
     e_ref, marks_ref, prompt_ref, q_ref, kall_ref, vall_ref, mixed_ref, inv_ref, after_ref, act_ref = refs[:10]
     kept, refs = refs[10:13], refs[13:]
     wo_ref, wi_ref, wout_ref = kept
@@ -212,18 +213,21 @@
     for fetch in fetches:
         fetch.start()
     ctx = lax.axis_index("ctx")
-    few = cols_of[0].shape[1]
+    half, turn = places(count)
+    few = mine_ref.shape[1]
+    low = jnp.where(half == 0, mine_ref[...], other_ref[...]).astype(f32)
+    high = jnp.where(half == 0, other_ref[...], mine_ref[...]).astype(f32)
     for place in range(2 * count):
-        picked = cols_of[0][0:SHOWN]
-        for n in range(1, 2 * count):
-            picked = jnp.where((ctx ^ n) == place, cols_of[n][0:SHOWN], picked)
-        shown_ref[0:SHOWN, place * few : (place + 1) * few] = picked.astype(f32)
+        for part, start, stop in ((low, 0, HELD), (high, HELD, SHOWN)):
+            picked = part[0 : stop - start]
+            for n in range(1, 2 * count):
+                picked = jnp.where((ctx ^ n) == place, part[n * HELD : n * HELD + stop - start], picked)
+            shown_ref[start:stop, place * few : (place + 1) * few] = picked
     shown_ref[SHOWN:, :] = jnp.zeros((BLK - SHOWN, shown_ref.shape[1]), f32)
     prompt_ref[...] = shown_ref[...].astype(bf16)
-    half, turn = places(count)
     half_len = count * piece
     width = q_ref.shape[1]
-    tally = functools.reduce(jnp.add, [cols[SHOWN:].astype(f32) for cols in cols_of])
+    tally = functools.reduce(jnp.add, [high[(n + 1) * HELD - 16 : (n + 1) * HELD] for n in range(2 * count)])
     tally_row = lax.broadcasted_iota(i32, (tally.shape[0], 1), 0)
     marks = []
     for n in range(2):
@@ -602,7 +606,7 @@
     chip_parts = [chip_rows] + [swap_dp(chip_rows, 2 * n) for n in range(1, n_dp // 2)]
     plane = pl.pallas_call(
         functools.partial(plane_kernel, rows_own),
-        out_shape=held((SHOWN + 16, cols_own), bf16),
+        out_shape=held((HELD, cols_own), bf16),
         in_specs=[vmem_spec()] * len(chip_parts),
         out_specs=vmem_spec(),
         scratch_shapes=[pltpu.VMEM((BLK + 16, cols_own), f32)],
@@ -615,7 +619,8 @@
         bias_table, jnp.asarray(choose), (((0,), (0,)), ((), ())), precision=lax.Precision.HIGHEST
     )
     base, plane = lax.optimization_barrier((base, plane))
-    cols_of = [plane] + [swap_ctx(plane, n) for n in range(1, n_ctx)]
+    cols_mine = jnp.concatenate([plane] + [swap_ctx(plane, n) for n in range(1, n_ctx)], axis=0)
+    cols_other = swap_dp(cols_mine, 1)
     weights = (w_query, w_key, w_value)
     prepared = pl.pallas_call(
         functools.partial(prepare_kernel, count),
@@ -662,7 +667,7 @@
         ]
         + [held(w.shape, bf16) for w in (w_output, w_inner, w_outer)]
         + [piece_like] * count,
-        in_specs=[vmem_spec()] * (4 * count + 8) + [any_spec()] * 3,
+        in_specs=[vmem_spec()] * (2 * count + 10) + [any_spec()] * 3,
         out_specs=[any_spec()] + [vmem_spec()] * (12 + count),
         scratch_shapes=[
             pltpu.VMEM((2 * half_len + BLK, width), bf16),
@@ -678,7 +683,7 @@
         compiler_params=params(F_MIB),
         cost_estimate=cost(3e10, 4e7, heads * half_len * keys_all),
     )(
-        *own, *partner, normed, gain_1, gain_2, w_q, w_k, w_v, tiles, table, *cols_of,
+        *own, *partner, normed, gain_1, gain_2, w_q, w_k, w_v, tiles, table, cols_mine, cols_other,
         *[in_hbm(w) for w in (w_output, w_inner, w_outer)],
     )
     got = [permute(made[13 + k], back_of(count, k)) for k in range(count)]

time: 108 us -> 107 us (level)
  starting transfers between devices: 40.3 us -> 36.2 us
  waiting for transfers between devices: 14 us -> 16.7 us
    ppermute x26 -> x27, starting transfers between devices: 40.3 us -> 36.2 us  [permute(): return lax.ppermute(value, AXES, pairs)]
    ppermute x26 -> x27, waiting for transfers between devices: 14 us -> 16.7 us  [permute(): return lax.ppermute(value, AXES, pairs)]
  transfers between devices with their start and end apart: 26 -> 27, of which waited for: 12 -> 14; matrix products, arithmetic and copies ran while one was open for 3% -> 3% of each run, Pallas kernels for 44% -> 44%
where the time goes in v6:
time: 107 us; the launch traced here: 106 us
  Pallas kernels  49.2 us (46%)
  starting transfers between devices  36.2 us (34%)
  waiting for transfers between devices  16.7 us (16%)
  local copies, waits for them, and re-layouts  1.43 us (1%)
    ppermute x27, starting transfers between devices, permute(): return lax.ppermute(value, AXES, pairs)  36.2 us
    pallas_call x1, Pallas kernels, on_device(): pl.pallas_call(functools.partial(forward_kernel, count, piece, rows_own),...  24.5 us
    pallas_call x1, Pallas kernels, on_device(): pl.pallas_call(functools.partial(backward_kernel, count, piece, rows_own)...  19 us
    ppermute x27, waiting for transfers between devices, permute(): return lax.ppermute(value, AXES, pairs)  16.7 us
    pallas_call x1, Pallas kernels, on_device(): pl.pallas_call(functools.partial(prepare_kernel, count), out_shape=[held(...  3.03 us
  transfers between devices with their start and end apart: 27, of which 14 were waited for; matrix products, arithmetic and copies ran while one was open for 3% of the time, Pallas kernels for 44%

profile of v6, /device:TPU:0, one launch (start us, length us, event | category | flops | bytes accessed | tf_op | source)
XLA Modules:
  0.0 106.4 jit_solution(17294853875606450058)
XLA Ops:
  0.6 1.2 %shard_map.183 = (bf16[256,768]{1,0:T(8,128)(2,1)S(1)}, bf16[256,768]{1,0:T(8,128)(2,1)S(1)}, bf16[24,192]{1,0:T(8,128)(2,1)S(1)}) custom-call(bf16[2,256,768]{2,1,0:T(8,128)(2,1)} %tokens_ref.1, s32[2,256]{1,0:T(2,128)} %seg_hbm.1, f32[16,192]{1,0:T(8,128)} %prompt_ref.1), custom_call_target="tpu_custom_call" | custom-call | flops 100000 | bytes 2000000 | tf_op jit(solution)/shard_map/pallas_call | solution.py:589
  1.8 0.5 collective-permute-start
  2.4 2.6 %collective-permute-start.6 = (bf16[256,768]{1,0:T(8,128)(2,1)S(1)}, bf16[256,768]{1,0:T(8,128)(2,1)S(1)}, u32[]{:S(2)}, u32[]{:S(2)}) collective-permute-start(bf16[256,768]{1,0:T(8,128)(2,1)S(1)} %get-tuple-element.55), channel_id=1, source_target_pairs={{0,1},{1,0},{2,5},{3,4},{4,3},{5,2},{6,7},{7,6},{8,9},{9,8},{10,13... | collective-permute-start | bytes 1179656 | tf_op jit(solution)/shard_map/ppermute | solution.py:576
  5.0 0.7 collective-permute-start.7
  5.7 1.6 %collective-permute-start.1 = (bf16[48,192]{1,0:T(8,128)(2,1)S(1)}, bf16[48,192]{1,0:T(8,128)(2,1)S(1)}, u32[]{:S(2)}, u32[]{:S(2)}) collective-permute-start(bf16[48,192]{1,0:T(8,128)(2,1)S(1)} %constant_dynamic-update-slice_fusion.refs_0_), channel_id=1, source_target_pairs={{0,8},{1,9},{2,10},{3,11},{4,12},{5,13},{6,14},{7,15},{8,0},{9,1},... | collective-permute-start | bytes 55304 | tf_op jit(solution)/shard_map/ppermute | solution.py:576
  7.3 1.5 %collective-permute-start.2 = (bf16[48,192]{1,0:T(8,128)(2,1)S(1)}, bf16[48,192]{1,0:T(8,128)(2,1)S(1)}, u32[]{:S(2)}, u32[]{:S(2)}) collective-permute-start(bf16[48,192]{1,0:T(8,128)(2,1)S(1)} %constant_dynamic-update-slice_fusion.refs_0_), channel_id=1, source_target_pairs={{0,16},{1,17},{2,18},{3,19},{4,20},{5,21},{6,22},{7,23},{8,24},{9,... | collective-permute-start | bytes 55304 | tf_op jit(solution)/shard_map/ppermute | solution.py:576
  8.8 0.5 collective-permute-start.3
  9.3 1.0 convolution_bitcast_fusion.base_ref
  10.3 0.7 broadcast_in_dim.6.gain_first_ref
  11.0 0.7 broadcast_in_dim.7.gain_second_ref
  11.7 1.8 %collective-permute-done.3.refs_3_ = bf16[48,192]{1,0:T(8,128)(2,1)S(1)} collective-permute-done((bf16[48,192]{1,0:T(8,128)(2,1)S(1)}, bf16[48,192]{1,0:T(8,128)(2,1)S(1)}, u32[]{:S(2)}, u32[]{:S(2)}) %collective-permute-start.3) | collective-permute-done | bytes 18464 | tf_op jit(solution)/shard_map/ppermute | solution.py:576
  13.6 0.7 collective-permute-start.10
  14.3 5.3 %collective-permute-start.11 = (bf16[64,192]{1,0:T(8,128)(2,1)S(1)}, bf16[64,192]{1,0:T(8,128)(2,1)S(1)}, u32[]{:S(2)}, u32[]{:S(2)}) collective-permute-start(bf16[64,192]{1,0:T(8,128)(2,1)S(1)} %shard_map.184), channel_id=1, source_target_pairs={{0,2},{1,3},{2,0},{3,1},{4,6},{5,7},{6,4},{7,5},{8,10},{9,11},{10,... | collective-permute-start | bytes 73736 | tf_op jit(solution)/shard_map/ppermute | solution.py:576
  19.6 1.4 %collective-permute-start.12 = (bf16[64,192]{1,0:T(8,128)(2,1)S(1)}, bf16[64,192]{1,0:T(8,128)(2,1)S(1)}, u32[]{:S(2)}, u32[]{:S(2)}) collective-permute-start(bf16[64,192]{1,0:T(8,128)(2,1)S(1)} %shard_map.184), channel_id=1, source_target_pairs={{0,3},{1,2},{2,1},{3,0},{4,7},{5,6},{6,5},{7,4},{8,11},{9,10},{10,... | collective-permute-start | bytes 73736 | tf_op jit(solution)/shard_map/ppermute | solution.py:576
  21.0 3.0 %shard_map.185 = (f32[12,3,128,128]{3,2,1,0:T(8,128)S(1)}, bf16[1536,512]{1,0:T(8,128)(2,1)S(1)}, f32[1,768]{1,0:T(1,128)S(1)}, f32[1,768]{1,0:T(1,128)S(1)}, bf...) custom-call(f32[12,512]{1,0:T(8,128)S(1)} %convolution_bitcast_fusio, ...), custom_call_target="tpu_custom_call" | custom-call | flops 1000000 | bytes 5000000 | tf_op jit(solution)/shard_map/pallas_call | solution.py:625
  24.0 0.6 collective-permute-start.4
  24.7 2.7 %collective-permute-done.11 = bf16[64,192]{1,0:T(8,128)(2,1)S(1)} collective-permute-done((bf16[64,192]{1,0:T(8,128)(2,1)S(1)}, bf16[64,192]{1,0:T(8,128)(2,1)S(1)}, u32[]{:S(2)}, u32[]{:S(2)}) %collective-permute-start.11) | collective-permute-done | bytes 24608 | tf_op jit(solution)/shard_map/ppermute | solution.py:576
  27.4 0.7 collective-permute-start.5
  28.1 0.9 collective-permute-start.13
  29.1 0.4 collective-permute-start.9
  29.5 0.3 shard_map.186.refs_4_
  30.0 0.7 collective-permute-done.8.refs_2_
  30.8 0.6 collective-permute-done.9.refs_3_
  31.3 24.5 %shard_map.187 = (bf16[6,2,1152,512]{3,2,1,0:T(8,128)(2,1)}, s32[8,128]{1,0:T(8,128)S(1)}, bf16[128,768]{1,0:T(8,128)(2,1)S(1)}, bf16[512,768]{1,0:T(8,128)(2,1)...) custom-call(bf16[256,768]{1,0:T(8,128)(2,1)S(1)} %collective-permute, ...), custom_call_target="tpu_custom_call" | custom-call | flops 30000001024 | bytes 40000000 | tf_op jit(solution)/shard_map/pallas_call | solution.py:654
  55.9 0.3 collective-permute-start.14
  56.2 0.9 collective-permute-start.15
  57.1 19.0 %shard_map.188 = (f32[64,768]{1,0:T(8,128)S(1)}, bf16[64,768]{1,0:T(8,128)(2,1)S(1)}) custom-call(bf16[256,768]{1,0:T(8,128)(2,1)S(1)} %collective-permute-done.4.refs_0_, bf16[256,768]{1,0:T(8,128)(2,1)S(1)} %collective-permute-done.5.refs_1_, s32[8,128]{1,0:T(8,128)S(1)} %get-tuple-element.65.refs_2_, bf16[512,3072]{1,0:T(8,128)(2,1)S(1)} %get-tuple-element.66.refs_3_, ...), custom_call_target="tpu_custom_call" | custom-call | flops 30000001024 | bytes 40000000 | tf_op jit(solution)/shard_map/pallas_call | solution.py:694
  76.1 3.5 %collective-permute-start.16 = (bf16[64,768]{1,0:T(8,128)(2,1)S(1)}, bf16[64,768]{1,0:T(8,128)(2,1)S(1)}, u32[]{:S(2)}, u32[]{:S(2)}) collective-permute-start(bf16[64,768]{1,0:T(8,128)(2,1)S(1)} %get-tuple-element.82), channel_id=1, source_target_pairs={{0,4},{1,5},{2,6},{3,7},{4,0},{5,1},{6,2},{7,3},{8,12},{9,13},{10,... | collective-permute-start | bytes 294920 | tf_op jit(solution)/shard_map/ppermute | solution.py:576
  79.7 0.9 collective-permute-done.16.came_ref
  80.6 5.2 %collective-permute-start.19 = (bf16[16,768]{1,0:T(8,128)(2,1)S(1)}, bf16[16,768]{1,0:T(8,128)(2,1)S(1)}, u32[]{:S(2)}, u32[]{:S(2)}) collective-permute-start(bf16[16,768]{1,0:T(8,128)(2,1)S(1)} %get-tuple-element.86), channel_id=1, source_target_pairs={{0,24},{1,25},{2,26},{3,27},{4,28},{5,29},{6,30},{7,31},{8,16},{9,... | collective-permute-start | bytes 73736 | tf_op jit(solution)/shard_map/ppermute | solution.py:576
  85.9 0.5 collective-permute-start.18
  86.3 0.2 collective-permute-start.17
  86.6 1.0 collective-permute-done.19
  87.7 2.0 %collective-permute-done.18 = bf16[16,768]{1,0:T(8,128)(2,1)S(1)} collective-permute-done((bf16[16,768]{1,0:T(8,128)(2,1)S(1)}, bf16[16,768]{1,0:T(8,128)(2,1)S(1)}, u32[]{:S(2)}, u32[]{:S(2)}) %collective-permute-start.18) | collective-permute-done | bytes 24608 | tf_op jit(solution)/shard_map/ppermute | solution.py:576
  89.7 0.5 collective-permute-done.17
  90.3 1.7 %collective-permute-start.21 = (bf16[16,768]{1,0:T(8,128)(2,1)S(1)}, bf16[16,768]{1,0:T(8,128)(2,1)S(1)}, u32[]{:S(2)}, u32[]{:S(2)}) collective-permute-start(bf16[16,768]{1,0:T(8,128)(2,1)S(1)} %get-tuple-element.98), channel_id=1, source_target_pairs={{0,2},{1,3},{2,0},{3,1},{4,6},{5,7},{6,4},{7,5},{8,10},{9,11},{10,... | collective-permute-start | bytes 73736 | tf_op jit(solution)/shard_map/ppermute | solution.py:576
  92.0 2.7 %collective-permute-start.22 = (bf16[16,768]{1,0:T(8,128)(2,1)S(1)}, bf16[16,768]{1,0:T(8,128)(2,1)S(1)}, u32[]{:S(2)}, u32[]{:S(2)}) collective-permute-start(bf16[16,768]{1,0:T(8,128)(2,1)S(1)} %get-tuple-element.98), channel_id=1, source_target_pairs={{0,3},{1,2},{2,1},{3,0},{4,7},{5,6},{6,5},{7,4},{8,11},{9,10},{10,... | collective-permute-start | bytes 73736 | tf_op jit(solution)/shard_map/ppermute | solution.py:576
  94.7 0.9 pad_maximum_fusion
  95.7 2.0 %collective-permute-done.22.refs_2_ = bf16[16,768]{1,0:T(8,128)(2,1)S(1)} collective-permute-done((bf16[16,768]{1,0:T(8,128)(2,1)S(1)}, bf16[16,768]{1,0:T(8,128)(2,1)S(1)}, u32[]{:S(2)}, u32[]{:S(2)}) %collective-permute-start.22) | collective-permute-done | bytes 24608 | tf_op jit(solution)/shard_map/ppermute | solution.py:576
  97.7 0.3 shard_map.190
  98.0 1.2 %collective-permute-done.23 = f32[8,128]{1,0:T(8,128)S(1)} collective-permute-done((f32[8,128]{1,0:T(8,128)S(1)}, f32[8,128]{1,0:T(8,128)S(1)}, u32[]{:S(2)}, u32[]{:S(2)}) %collective-permute-start.23) | collective-permute-done | bytes 4128 | tf_op jit(solution)/shard_map/ppermute | solution.py:576
  99.1 0.2 collective-permute-start.24
  99.3 1.9 %collective-permute-start.25 = (f32[8,128]{1,0:T(8,128)S(1)}, f32[8,128]{1,0:T(8,128)S(1)}, u32[]{:S(2)}, u32[]{:S(2)}) collective-permute-start(f32[8,128]{1,0:T(8,128)S(1)} %add.22.refs_0_), channel_id=1, source_target_pairs={{0,16},{1,17},{2,18},{3,19},{4,20},{5,21},{6,22},{7,23},{8,24},{9,... | collective-permute-start | bytes 12296 | tf_op jit(solution)/shard_map/ppermute | solution.py:576
  101.2 1.4 %collective-permute-start.26 = (f32[8,128]{1,0:T(8,128)S(1)}, f32[8,128]{1,0:T(8,128)S(1)}, u32[]{:S(2)}, u32[]{:S(2)}) collective-permute-start(f32[8,128]{1,0:T(8,128)S(1)} %add.22.refs_0_), channel_id=1, source_target_pairs={{0,24},{1,25},{2,26},{3,27},{4,28},{5,29},{6,30},{7,31},{8,16},{9,... | collective-permute-start | bytes 12296 | tf_op jit(solution)/shard_map/ppermute | solution.py:576
  102.6 0.1 collective-permute-done.24.refs_1_
  102.7 0.2 collective-permute-done.25.refs_2_
  102.9 2.8 %collective-permute-done.26.refs_3_ = f32[8,128]{1,0:T(8,128)S(1)} collective-permute-done((f32[8,128]{1,0:T(8,128)S(1)}, f32[8,128]{1,0:T(8,128)S(1)}, u32[]{:S(2)}, u32[]{:S(2)}) %collective-permute-start.26) | collective-permute-done | bytes 4128 | tf_op jit(solution)/shard_map/ppermute | solution.py:576
  105.7 0.7 shard_map.191
  (38 shorter events, 0.6 us)
Async XLA Ops:
  0.6 8.7 %copy-start = (f32[32,12]{0,1:T(8,128)S(1)}, f32[32,12]{0,1:T(8,128)}, u32[]{:S(2)}) copy-start(f32[32,12]{0,1:T(8,128)} %param.28) | copy-start | bytes 4612
  1.8 3.9 %collective-permute-start = (bf16[24,192]{1,0:T(8,128)(2,1)S(1)}, bf16[24,192]{1,0:T(8,128)(2,1)S(1)}, u32[]{:S(2)}, u32[]{:S(2)}) collective-permute-start(bf16[24,192]{1,0:T(8,128)(2,1)S(1)} %get-tuple-element.51), channel_id=1, source_target_pairs={{0,4},{1,5},{2,6},{3,7},{4,0},{5,1},{6,2},{7,3},{8,12},{9,13},{10,... | collective-permute-start | bytes 27656 | tf_op jit(solution)/shard_map/ppermute | solution.py:576
  2.4 26.7 %collective-permute-start.6 = (bf16[256,768]{1,0:T(8,128)(2,1)S(1)}, bf16[256,768]{1,0:T(8,128)(2,1)S(1)}, u32[]{:S(2)}, u32[]{:S(2)}) collective-permute-start(bf16[256,768]{1,0:T(8,128)(2,1)S(1)} %get-tuple-element.55), channel_id=1, source_target_pairs={{0,1},{1,0},{2,5},{3,4},{4,3},{5,2},{6,7},{7,6},{8,9},{9,8},{10,13... | collective-permute-start | bytes 1179656 | tf_op jit(solution)/shard_map/ppermute | solution.py:576
  5.0 24.1 %collective-permute-start.7 = (bf16[256,768]{1,0:T(8,128)(2,1)S(1)}, bf16[256,768]{1,0:T(8,128)(2,1)S(1)}, u32[]{:S(2)}, u32[]{:S(2)}) collective-permute-start(bf16[256,768]{1,0:T(8,128)(2,1)S(1)} %get-tuple-element.56), channel_id=1, source_target_pairs={{0,0},{1,1},{2,4},{3,5},{4,2},{5,3},{6,6},{7,7},{8,8},{9,9},{10,12... | collective-permute-start | bytes 1179656 | tf_op jit(solution)/shard_map/ppermute | solution.py:576
  5.7 6.0 %collective-permute-start.1 = (bf16[48,192]{1,0:T(8,128)(2,1)S(1)}, bf16[48,192]{1,0:T(8,128)(2,1)S(1)}, u32[]{:S(2)}, u32[]{:S(2)}) collective-permute-start(bf16[48,192]{1,0:T(8,128)(2,1)S(1)} %constant_dynamic-update-slice_fusion.refs_0_), channel_id=1, source_target_pairs={{0,8},{1,9},{2,10},{3,11},{4,12},{5,13},{6,14},{7,15},{8,0},{9,1},... | collective-permute-start | bytes 55304 | tf_op jit(solution)/shard_map/ppermute | solution.py:576
  7.3 4.4 %collective-permute-start.2 = (bf16[48,192]{1,0:T(8,128)(2,1)S(1)}, bf16[48,192]{1,0:T(8,128)(2,1)S(1)}, u32[]{:S(2)}, u32[]{:S(2)}) collective-permute-start(bf16[48,192]{1,0:T(8,128)(2,1)S(1)} %constant_dynamic-update-slice_fusion.refs_0_), channel_id=1, source_target_pairs={{0,16},{1,17},{2,18},{3,19},{4,20},{5,21},{6,22},{7,23},{8,24},{9,... | collective-permute-start | bytes 55304 | tf_op jit(solution)/shard_map/ppermute | solution.py:576
  8.8 4.7 %collective-permute-start.3 = (bf16[48,192]{1,0:T(8,128)(2,1)S(1)}, bf16[48,192]{1,0:T(8,128)(2,1)S(1)}, u32[]{:S(2)}, u32[]{:S(2)}) collective-permute-start(bf16[48,192]{1,0:T(8,128)(2,1)S(1)} %constant_dynamic-update-slice_fusion.refs_0_), channel_id=1, source_target_pairs={{0,24},{1,25},{2,26},{3,27},{4,28},{5,29},{6,30},{7,31},{8,16},{9,... | collective-permute-start | bytes 55304 | tf_op jit(solution)/shard_map/ppermute | solution.py:576
  13.6 10.5 %collective-permute-start.10 = (bf16[64,192]{1,0:T(8,128)(2,1)S(1)}, bf16[64,192]{1,0:T(8,128)(2,1)S(1)}, u32[]{:S(2)}, u32[]{:S(2)}) collective-permute-start(bf16[64,192]{1,0:T(8,128)(2,1)S(1)} %shard_map.184), channel_id=1, source_target_pairs={{0,1},{1,0},{2,3},{3,2},{4,5},{5,4},{6,7},{7,6},{8,9},{9,8},{10,11... | collective-permute-start | bytes 73736 | tf_op jit(solution)/shard_map/ppermute | solution.py:576
  14.3 13.1 %collective-permute-start.11 = (bf16[64,192]{1,0:T(8,128)(2,1)S(1)}, bf16[64,192]{1,0:T(8,128)(2,1)S(1)}, u32[]{:S(2)}, u32[]{:S(2)}) collective-permute-start(bf16[64,192]{1,0:T(8,128)(2,1)S(1)} %shard_map.184), channel_id=1, source_target_pairs={{0,2},{1,3},{2,0},{3,1},{4,6},{5,7},{6,4},{7,5},{8,10},{9,11},{10,... | collective-permute-start | bytes 73736 | tf_op jit(solution)/shard_map/ppermute | solution.py:576
  19.6 8.4 %collective-permute-start.12 = (bf16[64,192]{1,0:T(8,128)(2,1)S(1)}, bf16[64,192]{1,0:T(8,128)(2,1)S(1)}, u32[]{:S(2)}, u32[]{:S(2)}) collective-permute-start(bf16[64,192]{1,0:T(8,128)(2,1)S(1)} %shard_map.184), channel_id=1, source_target_pairs={{0,3},{1,2},{2,1},{3,0},{4,7},{5,6},{6,5},{7,4},{8,11},{9,10},{10,... | collective-permute-start | bytes 73736 | tf_op jit(solution)/shard_map/ppermute | solution.py:576
  24.0 33.0 %collective-permute-start.4 = (bf16[256,768]{1,0:T(8,128)(2,1)S(1)}, bf16[256,768]{1,0:T(8,128)(2,1)S(1)}, u32[]{:S(2)}, u32[]{:S(2)}) collective-permute-start(bf16[256,768]{1,0:T(8,128)(2,1)S(1)} %get-tuple-element.53), channel_id=1, source_target_pairs={{0,1},{1,0},{2,5},{3,4},{4,3},{5,2},{6,7},{7,6},{8,9},{9,8},{10,13... | collective-permute-start | bytes 1179656 | tf_op jit(solution)/shard_map/ppermute | solution.py:576
  27.4 29.7 %collective-permute-start.5 = (bf16[256,768]{1,0:T(8,128)(2,1)S(1)}, bf16[256,768]{1,0:T(8,128)(2,1)S(1)}, u32[]{:S(2)}, u32[]{:S(2)}) collective-permute-start(bf16[256,768]{1,0:T(8,128)(2,1)S(1)} %get-tuple-element.54), channel_id=1, source_target_pairs={{0,0},{1,1},{2,4},{3,5},{4,2},{5,3},{6,6},{7,7},{8,8},{9,9},{10,12... | collective-permute-start | bytes 1179656 | tf_op jit(solution)/shard_map/ppermute | solution.py:576
  28.1 1.9 %collective-permute-start.13 = (bf16[256,192]{1,0:T(8,128)(2,1)S(1)}, bf16[256,192]{1,0:T(8,128)(2,1)S(1)}, u32[]{:S(2)}, u32[]{:S(2)}) collective-permute-start(bf16[256,192]{1,0:T(8,128)(2,1)S(1)} %constant_dynamic-update-slice_fusion.2.refs_12_), channel_id=1, source_target_pairs={{0,4},{1,5},{2,6},{3,7},{4,0},{5,1},{6,2},{7,3},{8,12},{9,13},{10,... | collective-permute-start | bytes 294920 | tf_op jit(solution)/shard_map/ppermute | solution.py:576
  29.0 1.7 %collective-permute-start.8 = (bf16[256,768]{1,0:T(8,128)(2,1)S(1)}, bf16[256,768]{1,0:T(8,128)(2,1)S(1)}, u32[]{:S(2)}, u32[]{:S(2)}) collective-permute-start(bf16[256,768]{1,0:T(8,128)(2,1)S(1)} %collective-permute-done.6.refs_0_), channel_id=1, source_target_pairs={{0,4},{1,5},{2,6},{3,7},{4,0},{5,1},{6,2},{7,3},{8,12},{9,13},{10,... | collective-permute-start | bytes 1179656 | tf_op jit(solution)/shard_map/ppermute | solution.py:576
  29.1 2.2 %collective-permute-start.9 = (bf16[256,768]{1,0:T(8,128)(2,1)S(1)}, bf16[256,768]{1,0:T(8,128)(2,1)S(1)}, u32[]{:S(2)}, u32[]{:S(2)}) collective-permute-start(bf16[256,768]{1,0:T(8,128)(2,1)S(1)} %collective-permute-done.7.refs_1_), channel_id=1, source_target_pairs={{0,4},{1,5},{2,6},{3,7},{4,0},{5,1},{6,2},{7,3},{8,12},{9,13},{10,... | collective-permute-start | bytes 1179656 | tf_op jit(solution)/shard_map/ppermute | solution.py:576
  55.9 20.2 %collective-permute-start.14 = (bf16[256,768]{1,0:T(8,128)(2,1)S(1)}, bf16[256,768]{1,0:T(8,128)(2,1)S(1)}, u32[]{:S(2)}, u32[]{:S(2)}) collective-permute-start(bf16[256,768]{1,0:T(8,128)(2,1)S(1)} %get-tuple-element.79), channel_id=1, source_target_pairs={{0,1},{1,0},{2,5},{3,4},{4,3},{5,2},{6,7},{7,6},{8,9},{9,8},{10,13... | collective-permute-start | bytes 1179656 | tf_op jit(solution)/shard_map/ppermute | solution.py:576
  56.2 19.9 %collective-permute-start.15 = (bf16[256,768]{1,0:T(8,128)(2,1)S(1)}, bf16[256,768]{1,0:T(8,128)(2,1)S(1)}, u32[]{:S(2)}, u32[]{:S(2)}) collective-permute-start(bf16[256,768]{1,0:T(8,128)(2,1)S(1)} %get-tuple-element.80), channel_id=1, source_target_pairs={{0,0},{1,1},{2,4},{3,5},{4,2},{5,3},{6,6},{7,7},{8,8},{9,9},{10,12... | collective-permute-start | bytes 1179656 | tf_op jit(solution)/shard_map/ppermute | solution.py:576
  76.1 4.5 %collective-permute-start.16 = (bf16[64,768]{1,0:T(8,128)(2,1)S(1)}, bf16[64,768]{1,0:T(8,128)(2,1)S(1)}, u32[]{:S(2)}, u32[]{:S(2)}) collective-permute-start(bf16[64,768]{1,0:T(8,128)(2,1)S(1)} %get-tuple-element.82), channel_id=1, source_target_pairs={{0,4},{1,5},{2,6},{3,7},{4,0},{5,1},{6,2},{7,3},{8,12},{9,13},{10,... | collective-permute-start | bytes 294920 | tf_op jit(solution)/shard_map/ppermute | solution.py:576
  80.6 7.0 %collective-permute-start.19 = (bf16[16,768]{1,0:T(8,128)(2,1)S(1)}, bf16[16,768]{1,0:T(8,128)(2,1)S(1)}, u32[]{:S(2)}, u32[]{:S(2)}) collective-permute-start(bf16[16,768]{1,0:T(8,128)(2,1)S(1)} %get-tuple-element.86), channel_id=1, source_target_pairs={{0,24},{1,25},{2,26},{3,27},{4,28},{5,29},{6,30},{7,31},{8,16},{9,... | collective-permute-start | bytes 73736 | tf_op jit(solution)/shard_map/ppermute | solution.py:576
  85.9 3.8 %collective-permute-start.18 = (bf16[16,768]{1,0:T(8,128)(2,1)S(1)}, bf16[16,768]{1,0:T(8,128)(2,1)S(1)}, u32[]{:S(2)}, u32[]{:S(2)}) collective-permute-start(bf16[16,768]{1,0:T(8,128)(2,1)S(1)} %get-tuple-element.85), channel_id=1, source_target_pairs={{0,16},{1,17},{2,18},{3,19},{4,20},{5,21},{6,22},{7,23},{8,24},{9,... | collective-permute-start | bytes 73736 | tf_op jit(solution)/shard_map/ppermute | solution.py:576
  86.3 20.1 %copy-start.1 = (f32[32,12]{0,1:T(8,128)S(1)}, f32[32,12]{0,1:T(8,128)}, u32[]{:S(2)}) copy-start(f32[32,12]{0,1:T(8,128)} %param.28) | copy-start | bytes 4612
  86.3 19.4 %copy-start.2 = (f32[16,192]{1,0:T(8,128)S(1)}, f32[16,192]{1,0:T(8,128)}, u32[]{:S(2)}) copy-start(f32[16,192]{1,0:T(8,128)} %prompt_ref.1) | copy-start | bytes 36868
  86.3 19.4 %copy-start.3 = (f32[16,192]{1,0:T(8,128)S(1)}, f32[16,192]{1,0:T(8,128)}, u32[]{:S(2)}) copy-start(f32[16,192]{1,0:T(8,128)} %first_ref.1) | copy-start | bytes 36868
  86.3 19.4 %copy-start.4 = (f32[16,192]{1,0:T(8,128)S(1)}, f32[16,192]{1,0:T(8,128)}, u32[]{:S(2)}) copy-start(f32[16,192]{1,0:T(8,128)} %second_ref.1) | copy-start | bytes 36868
  86.3 3.9 %collective-permute-start.17 = (bf16[16,768]{1,0:T(8,128)(2,1)S(1)}, bf16[16,768]{1,0:T(8,128)(2,1)S(1)}, u32[]{:S(2)}, u32[]{:S(2)}) collective-permute-start(bf16[16,768]{1,0:T(8,128)(2,1)S(1)} %get-tuple-element.84), channel_id=1, source_target_pairs={{0,8},{1,9},{2,10},{3,11},{4,12},{5,13},{6,14},{7,15},{8,0},{9,1},... | collective-permute-start | bytes 73736 | tf_op jit(solution)/shard_map/ppermute | solution.py:576
  90.2 5.4 %collective-permute-start.20 = (bf16[16,768]{1,0:T(8,128)(2,1)S(1)}, bf16[16,768]{1,0:T(8,128)(2,1)S(1)}, u32[]{:S(2)}, u32[]{:S(2)}) collective-permute-start(bf16[16,768]{1,0:T(8,128)(2,1)S(1)} %get-tuple-element.98), channel_id=1, source_target_pairs={{0,1},{1,0},{2,3},{3,2},{4,5},{5,4},{6,7},{7,6},{8,9},{9,8},{10,11... | collective-permute-start | bytes 73736 | tf_op jit(solution)/shard_map/ppermute | solution.py:576
  90.3 5.3 %collective-permute-start.21 = (bf16[16,768]{1,0:T(8,128)(2,1)S(1)}, bf16[16,768]{1,0:T(8,128)(2,1)S(1)}, u32[]{:S(2)}, u32[]{:S(2)}) collective-permute-start(bf16[16,768]{1,0:T(8,128)(2,1)S(1)} %get-tuple-element.98), channel_id=1, source_target_pairs={{0,2},{1,3},{2,0},{3,1},{4,6},{5,7},{6,4},{7,5},{8,10},{9,11},{10,... | collective-permute-start | bytes 73736 | tf_op jit(solution)/shard_map/ppermute | solution.py:576
  92.0 5.6 %collective-permute-start.22 = (bf16[16,768]{1,0:T(8,128)(2,1)S(1)}, bf16[16,768]{1,0:T(8,128)(2,1)S(1)}, u32[]{:S(2)}, u32[]{:S(2)}) collective-permute-start(bf16[16,768]{1,0:T(8,128)(2,1)S(1)} %get-tuple-element.98), channel_id=1, source_target_pairs={{0,3},{1,2},{2,1},{3,0},{4,7},{5,6},{6,5},{7,4},{8,11},{9,10},{10,... | collective-permute-start | bytes 73736 | tf_op jit(solution)/shard_map/ppermute | solution.py:576
  97.9 1.2 %collective-permute-start.23 = (f32[8,128]{1,0:T(8,128)S(1)}, f32[8,128]{1,0:T(8,128)S(1)}, u32[]{:S(2)}, u32[]{:S(2)}) collective-permute-start(f32[8,128]{1,0:T(8,128)S(1)} %get-tuple-element.94), channel_id=1, source_target_pairs={{0,4},{1,5},{2,6},{3,7},{4,0},{5,1},{6,2},{7,3},{8,12},{9,13},{10,... | collective-permute-start | bytes 12296 | tf_op jit(solution)/shard_map/ppermute | solution.py:576
  99.1 3.6 %collective-permute-start.24 = (f32[8,128]{1,0:T(8,128)S(1)}, f32[8,128]{1,0:T(8,128)S(1)}, u32[]{:S(2)}, u32[]{:S(2)}) collective-permute-start(f32[8,128]{1,0:T(8,128)S(1)} %add.22.refs_0_), channel_id=1, source_target_pairs={{0,8},{1,9},{2,10},{3,11},{4,12},{5,13},{6,14},{7,15},{8,0},{9,1},... | collective-permute-start | bytes 12296 | tf_op jit(solution)/shard_map/ppermute | solution.py:576
  99.3 3.6 %collective-permute-start.25 = (f32[8,128]{1,0:T(8,128)S(1)}, f32[8,128]{1,0:T(8,128)S(1)}, u32[]{:S(2)}, u32[]{:S(2)}) collective-permute-start(f32[8,128]{1,0:T(8,128)S(1)} %add.22.refs_0_), channel_id=1, source_target_pairs={{0,16},{1,17},{2,18},{3,19},{4,20},{5,21},{6,22},{7,23},{8,24},{9,... | collective-permute-start | bytes 12296 | tf_op jit(solution)/shard_map/ppermute | solution.py:576
  101.2 4.5 %collective-permute-start.26 = (f32[8,128]{1,0:T(8,128)S(1)}, f32[8,128]{1,0:T(8,128)S(1)}, u32[]{:S(2)}, u32[]{:S(2)}) collective-permute-start(f32[8,128]{1,0:T(8,128)S(1)} %add.22.refs_0_), channel_id=1, source_target_pairs={{0,24},{1,25},{2,26},{3,27},{4,28},{5,29},{6,30},{7,31},{8,16},{9,... | collective-permute-start | bytes 12296 | tf_op jit(solution)/shard_map/ppermute | solution.py:576

commit v7 on v6

--- a/solution.py
+++ b/solution.py
@@ -15,6 +15,7 @@
 SHOWN = 112
 HELD = (SHOWN + 16) // 2
 QCOLS = 256
+UNITS = 1536
 norm_eps = 1e-06
 beta_first = 0.9
 beta_second = 0.999
@@ -395,22 +396,22 @@
         after_ref[rows, :] = after
         norm_ref[rows, :] = (after * inv_rms(after) * gain_second_ref[...]).astype(bf16)
 
-    @pl.loop(0, wi_ref.shape[1] // wide)
+    @pl.loop(0, wi_ref.shape[1] // UNITS)
     def _(t):
-        cols = pl.ds(pl.multiple_of(t * wide, wide), wide)
-        act_ref[:, cols] = jnp.maximum(dot_nn(norm_ref[0:half_len, :], wi_ref[:, cols]), 0.0).astype(bf16)
-
-    @pl.loop(0, width // wide)
-    def _(t):
-        cols = pl.ds(pl.multiple_of(t * wide, wide), wide)
-        made = (after_ref[:, cols] + dot_nn(act_ref[...], wout_ref[:, cols])).astype(bf16)
-        made = [made[j * piece : (j + 1) * piece] for j in range(count)]
-        for k in range(count):
-            place = slot_of(turn - k - 1, count)
-            sent = made[0]
-            for j in range(1, count):
-                sent = jnp.where(place == j, made[j], sent)
-            going[k][:, cols] = sent
+        units = pl.ds(pl.multiple_of(t * UNITS, UNITS), UNITS)
+        inner = lax.dot_general(
+            wi_ref[:, units], norm_ref[0:half_len, :], (((0,), (1,)), ((), ())), preferred_element_type=f32
+        )
+        act_ref[units, :] = jnp.maximum(inner, 0.0).astype(bf16)
+
+    made = (after_ref[...] + dot_tn(act_ref[...], wout_ref[...])).astype(bf16)
+    made = [made[j * piece : (j + 1) * piece] for j in range(count)]
+    for k in range(count):
+        place = slot_of(turn - k - 1, count)
+        sent = made[0]
+        for j in range(1, count):
+            sent = jnp.where(place == j, made[j], sent)
+        going[k][...] = sent
 
     for hp in range(width // PAIR - 2, width // PAIR):
         e_copy(hp).wait()
@@ -438,16 +439,16 @@
         e_copy(hp).start()
     for j in range(count):
         cot_ref[j * piece : (j + 1) * piece, :] = pick_piece(cots, turn, j)
-    wide = 4 * BLK
-    acc_ref[...] = jnp.zeros_like(acc_ref)
-
-    @pl.loop(0, wi_ref.shape[1] // wide)
+    do_ref[...] = jnp.zeros_like(do_ref)
+
+    @pl.loop(0, wi_ref.shape[1] // UNITS)
     def _(t):
-        cols = pl.ds(pl.multiple_of(t * wide, wide), wide)
-        grad_act = dot_nt(cot_ref[...], wout_ref[cols, :])
-        grad_inner = jnp.where(act_ref[:, cols] > 0, grad_act, 0.0).astype(bf16)
-        acc_ref[...] += dot_nt(grad_inner, wi_ref[:, cols])
-
+        units = pl.ds(pl.multiple_of(t * UNITS, UNITS), UNITS)
+        grad_act = dot_nt(wout_ref[units, :], cot_ref[...])
+        grad_inner = jnp.where(act_ref[units, :] > 0, grad_act, 0.0).astype(bf16)
+        do_ref[...] += dot_nn(wi_ref[:, units], grad_inner)
+
+    acc_ref[...] = do_ref[...].T
     gain = gain_second_ref[...]
 
     @pl.loop(0, half_len // BLK)
@@ -663,7 +664,7 @@
             held((width, half_len), bf16),
             held((heads, half_len), f32),
             held((half_len, width), f32),
-            held((half_len, hidden_ff), bf16),
+            held((hidden_ff, half_len), bf16),
         ]
         + [held(w.shape, bf16) for w in (w_output, w_inner, w_outer)]
         + [piece_like] * count,

time: 107 us -> 104 us (0.972)
  Pallas kernels: 49.2 us -> 46.7 us
    pallas_call x1, Pallas kernels: 24.5 us -> 22.5 us  [on_device(): pl.pallas_call(functools.partial(forward_kernel, count, piece, rows_own),...]
  transfers between devices with their start and end apart: 27 -> 27, of which waited for: 14 -> 14; matrix products, arithmetic and copies ran while one was open for 3% -> 3% of each run, Pallas kernels for 44% -> 43%
where the time goes in v7:
time: 104 us
  Pallas kernels  46.7 us (45%)
  starting transfers between devices  36.2 us (35%)
  waiting for transfers between devices  16.7 us (16%)
  local copies, waits for them, and re-layouts  1.43 us (1%)
    ppermute x27, starting transfers between devices, permute(): return lax.ppermute(value, AXES, pairs)  36.2 us
    pallas_call x1, Pallas kernels, on_device(): pl.pallas_call(functools.partial(forward_kernel, count, piece, rows_own),...  22.5 us
    pallas_call x1, Pallas kernels, on_device(): pl.pallas_call(functools.partial(backward_kernel, count, piece, rows_own)...  18.7 us
    ppermute x27, waiting for transfers between devices, permute(): return lax.ppermute(value, AXES, pairs)  16.7 us
    pallas_call x1, Pallas kernels, on_device(): pl.pallas_call(functools.partial(prepare_kernel, count), out_shape=[held(...  3.03 us
  transfers between devices with their start and end apart: 27, of which 14 were waited for; matrix products, arithmetic and copies ran while one was open for 3% of the time, Pallas kernels for 43%

profile of v7, /device:TPU:0, one launch (start us, length us, event | category | flops | bytes accessed | tf_op | source)
XLA Modules:
  0.0 103.9 jit_solution(8957770678534525755)
XLA Ops:
  0.6 1.2 %shard_map.183 = (bf16[256,768]{1,0:T(8,128)(2,1)S(1)}, bf16[256,768]{1,0:T(8,128)(2,1)S(1)}, bf16[24,192]{1,0:T(8,128)(2,1)S(1)}) custom-call(bf16[2,256,768]{2,1,0:T(8,128)(2,1)} %tokens_ref.1, s32[2,256]{1,0:T(2,128)} %seg_hbm.1, f32[16,192]{1,0:T(8,128)} %prompt_ref.1), custom_call_target="tpu_custom_call" | custom-call | flops 100000 | bytes 2000000 | tf_op jit(solution)/shard_map/pallas_call | solution.py:590
  1.8 0.5 collective-permute-start
  2.4 2.6 %collective-permute-start.6 = (bf16[256,768]{1,0:T(8,128)(2,1)S(1)}, bf16[256,768]{1,0:T(8,128)(2,1)S(1)}, u32[]{:S(2)}, u32[]{:S(2)}) collective-permute-start(bf16[256,768]{1,0:T(8,128)(2,1)S(1)} %get-tuple-element.55), channel_id=1, source_target_pairs={{0,1},{1,0},{2,5},{3,4},{4,3},{5,2},{6,7},{7,6},{8,9},{9,8},{10,13... | collective-permute-start | bytes 1179656 | tf_op jit(solution)/shard_map/ppermute | solution.py:577
  5.0 0.7 collective-permute-start.7
  5.7 1.6 %collective-permute-start.1 = (bf16[48,192]{1,0:T(8,128)(2,1)S(1)}, bf16[48,192]{1,0:T(8,128)(2,1)S(1)}, u32[]{:S(2)}, u32[]{:S(2)}) collective-permute-start(bf16[48,192]{1,0:T(8,128)(2,1)S(1)} %constant_dynamic-update-slice_fusion.refs_0_), channel_id=1, source_target_pairs={{0,8},{1,9},{2,10},{3,11},{4,12},{5,13},{6,14},{7,15},{8,0},{9,1},... | collective-permute-start | bytes 55304 | tf_op jit(solution)/shard_map/ppermute | solution.py:577
  7.3 1.5 %collective-permute-start.2 = (bf16[48,192]{1,0:T(8,128)(2,1)S(1)}, bf16[48,192]{1,0:T(8,128)(2,1)S(1)}, u32[]{:S(2)}, u32[]{:S(2)}) collective-permute-start(bf16[48,192]{1,0:T(8,128)(2,1)S(1)} %constant_dynamic-update-slice_fusion.refs_0_), channel_id=1, source_target_pairs={{0,16},{1,17},{2,18},{3,19},{4,20},{5,21},{6,22},{7,23},{8,24},{9,... | collective-permute-start | bytes 55304 | tf_op jit(solution)/shard_map/ppermute | solution.py:577
  8.8 0.5 collective-permute-start.3
  9.3 1.0 convolution_bitcast_fusion.base_ref
  10.3 0.7 broadcast_in_dim.6.gain_first_ref
  11.0 0.7 broadcast_in_dim.7.gain_second_ref
  11.7 1.8 %collective-permute-done.3.refs_3_ = bf16[48,192]{1,0:T(8,128)(2,1)S(1)} collective-permute-done((bf16[48,192]{1,0:T(8,128)(2,1)S(1)}, bf16[48,192]{1,0:T(8,128)(2,1)S(1)}, u32[]{:S(2)}, u32[]{:S(2)}) %collective-permute-start.3) | collective-permute-done | bytes 18464 | tf_op jit(solution)/shard_map/ppermute | solution.py:577
  13.6 0.7 collective-permute-start.10
  14.3 5.3 %collective-permute-start.11 = (bf16[64,192]{1,0:T(8,128)(2,1)S(1)}, bf16[64,192]{1,0:T(8,128)(2,1)S(1)}, u32[]{:S(2)}, u32[]{:S(2)}) collective-permute-start(bf16[64,192]{1,0:T(8,128)(2,1)S(1)} %shard_map.184), channel_id=1, source_target_pairs={{0,2},{1,3},{2,0},{3,1},{4,6},{5,7},{6,4},{7,5},{8,10},{9,11},{10,... | collective-permute-start | bytes 73736 | tf_op jit(solution)/shard_map/ppermute | solution.py:577
  19.6 1.4 %collective-permute-start.12 = (bf16[64,192]{1,0:T(8,128)(2,1)S(1)}, bf16[64,192]{1,0:T(8,128)(2,1)S(1)}, u32[]{:S(2)}, u32[]{:S(2)}) collective-permute-start(bf16[64,192]{1,0:T(8,128)(2,1)S(1)} %shard_map.184), channel_id=1, source_target_pairs={{0,3},{1,2},{2,1},{3,0},{4,7},{5,6},{6,5},{7,4},{8,11},{9,10},{10,... | collective-permute-start | bytes 73736 | tf_op jit(solution)/shard_map/ppermute | solution.py:577
  21.0 3.0 %shard_map.185 = (f32[12,3,128,128]{3,2,1,0:T(8,128)S(1)}, bf16[1536,512]{1,0:T(8,128)(2,1)S(1)}, f32[1,768]{1,0:T(1,128)S(1)}, f32[1,768]{1,0:T(1,128)S(1)}, bf...) custom-call(f32[12,512]{1,0:T(8,128)S(1)} %convolution_bitcast_fusio, ...), custom_call_target="tpu_custom_call" | custom-call | flops 1000000 | bytes 5000000 | tf_op jit(solution)/shard_map/pallas_call | solution.py:626
  24.0 0.6 collective-permute-start.4
  24.7 2.7 %collective-permute-done.11 = bf16[64,192]{1,0:T(8,128)(2,1)S(1)} collective-permute-done((bf16[64,192]{1,0:T(8,128)(2,1)S(1)}, bf16[64,192]{1,0:T(8,128)(2,1)S(1)}, u32[]{:S(2)}, u32[]{:S(2)}) %collective-permute-start.11) | collective-permute-done | bytes 24608 | tf_op jit(solution)/shard_map/ppermute | solution.py:577
  27.4 0.7 collective-permute-start.5
  28.1 0.9 collective-permute-start.13
  29.1 0.4 collective-permute-start.9
  29.5 0.3 shard_map.186.refs_4_
  30.0 0.7 collective-permute-done.8.refs_2_
  30.8 0.6 collective-permute-done.9.refs_3_
  31.3 22.5 %shard_map.187 = (bf16[6,2,1152,512]{3,2,1,0:T(8,128)(2,1)}, s32[8,128]{1,0:T(8,128)S(1)}, bf16[128,768]{1,0:T(8,128)(2,1)S(1)}, bf16[512,768]{1,0:T(8,128)(2,1)...) custom-call(bf16[256,768]{1,0:T(8,128)(2,1)S(1)} %collective-permute, ...), custom_call_target="tpu_custom_call" | custom-call | flops 30000001024 | bytes 40000000 | tf_op jit(solution)/shard_map/pallas_call | solution.py:655
  53.8 0.3 collective-permute-start.14
  54.1 0.9 collective-permute-start.15
  55.0 18.7 %shard_map.188 = (f32[64,768]{1,0:T(8,128)S(1)}, bf16[64,768]{1,0:T(8,128)(2,1)S(1)}) custom-call(bf16[256,768]{1,0:T(8,128)(2,1)S(1)} %collective-permute-done.4.refs_0_, bf16[256,768]{1,0:T(8,128)(2,1)S(1)} %collective-permute-done.5.refs_1_, s32[8,128]{1,0:T(8,128)S(1)} %get-tuple-element.65.refs_2_, bf16[3072,512]{1,0:T(8,128)(2,1)S(1)} %get-tuple-element.66.refs_3_, ...), custom_call_target="tpu_custom_call" | custom-call | flops 30000001024 | bytes 40000000 | tf_op jit(solution)/shard_map/pallas_call | solution.py:695
  73.7 3.5 %collective-permute-start.16 = (bf16[64,768]{1,0:T(8,128)(2,1)S(1)}, bf16[64,768]{1,0:T(8,128)(2,1)S(1)}, u32[]{:S(2)}, u32[]{:S(2)}) collective-permute-start(bf16[64,768]{1,0:T(8,128)(2,1)S(1)} %get-tuple-element.82), channel_id=1, source_target_pairs={{0,4},{1,5},{2,6},{3,7},{4,0},{5,1},{6,2},{7,3},{8,12},{9,13},{10,... | collective-permute-start | bytes 294920 | tf_op jit(solution)/shard_map/ppermute | solution.py:577
  77.2 0.9 collective-permute-done.16.came_ref
  78.2 5.2 %collective-permute-start.19 = (bf16[16,768]{1,0:T(8,128)(2,1)S(1)}, bf16[16,768]{1,0:T(8,128)(2,1)S(1)}, u32[]{:S(2)}, u32[]{:S(2)}) collective-permute-start(bf16[16,768]{1,0:T(8,128)(2,1)S(1)} %get-tuple-element.86), channel_id=1, source_target_pairs={{0,24},{1,25},{2,26},{3,27},{4,28},{5,29},{6,30},{7,31},{8,16},{9,... | collective-permute-start | bytes 73736 | tf_op jit(solution)/shard_map/ppermute | solution.py:577
  83.4 0.5 collective-permute-start.18
  83.9 0.3 collective-permute-start.17
  84.2 1.0 collective-permute-done.19
  85.2 2.0 %collective-permute-done.18 = bf16[16,768]{1,0:T(8,128)(2,1)S(1)} collective-permute-done((bf16[16,768]{1,0:T(8,128)(2,1)S(1)}, bf16[16,768]{1,0:T(8,128)(2,1)S(1)}, u32[]{:S(2)}, u32[]{:S(2)}) %collective-permute-start.18) | collective-permute-done | bytes 24608 | tf_op jit(solution)/shard_map/ppermute | solution.py:577
  87.2 0.5 collective-permute-done.17
  87.8 1.7 %collective-permute-start.21 = (bf16[16,768]{1,0:T(8,128)(2,1)S(1)}, bf16[16,768]{1,0:T(8,128)(2,1)S(1)}, u32[]{:S(2)}, u32[]{:S(2)}) collective-permute-start(bf16[16,768]{1,0:T(8,128)(2,1)S(1)} %get-tuple-element.98), channel_id=1, source_target_pairs={{0,2},{1,3},{2,0},{3,1},{4,6},{5,7},{6,4},{7,5},{8,10},{9,11},{10,... | collective-permute-start | bytes 73736 | tf_op jit(solution)/shard_map/ppermute | solution.py:577
  89.6 2.7 %collective-permute-start.22 = (bf16[16,768]{1,0:T(8,128)(2,1)S(1)}, bf16[16,768]{1,0:T(8,128)(2,1)S(1)}, u32[]{:S(2)}, u32[]{:S(2)}) collective-permute-start(bf16[16,768]{1,0:T(8,128)(2,1)S(1)} %get-tuple-element.98), channel_id=1, source_target_pairs={{0,3},{1,2},{2,1},{3,0},{4,7},{5,6},{6,5},{7,4},{8,11},{9,10},{10,... | collective-permute-start | bytes 73736 | tf_op jit(solution)/shard_map/ppermute | solution.py:577
  92.2 0.9 pad_maximum_fusion
  93.2 2.0 %collective-permute-done.22.refs_2_ = bf16[16,768]{1,0:T(8,128)(2,1)S(1)} collective-permute-done((bf16[16,768]{1,0:T(8,128)(2,1)S(1)}, bf16[16,768]{1,0:T(8,128)(2,1)S(1)}, u32[]{:S(2)}, u32[]{:S(2)}) %collective-permute-start.22) | collective-permute-done | bytes 24608 | tf_op jit(solution)/shard_map/ppermute | solution.py:577
  95.2 0.3 shard_map.190
  95.5 1.2 %collective-permute-done.23 = f32[8,128]{1,0:T(8,128)S(1)} collective-permute-done((f32[8,128]{1,0:T(8,128)S(1)}, f32[8,128]{1,0:T(8,128)S(1)}, u32[]{:S(2)}, u32[]{:S(2)}) %collective-permute-start.23) | collective-permute-done | bytes 4128 | tf_op jit(solution)/shard_map/ppermute | solution.py:577
  96.7 0.2 collective-permute-start.24
  96.9 1.9 %collective-permute-start.25 = (f32[8,128]{1,0:T(8,128)S(1)}, f32[8,128]{1,0:T(8,128)S(1)}, u32[]{:S(2)}, u32[]{:S(2)}) collective-permute-start(f32[8,128]{1,0:T(8,128)S(1)} %add.22.refs_0_), channel_id=1, source_target_pairs={{0,16},{1,17},{2,18},{3,19},{4,20},{5,21},{6,22},{7,23},{8,24},{9,... | collective-permute-start | bytes 12296 | tf_op jit(solution)/shard_map/ppermute | solution.py:577
  98.7 1.4 %collective-permute-start.26 = (f32[8,128]{1,0:T(8,128)S(1)}, f32[8,128]{1,0:T(8,128)S(1)}, u32[]{:S(2)}, u32[]{:S(2)}) collective-permute-start(f32[8,128]{1,0:T(8,128)S(1)} %add.22.refs_0_), channel_id=1, source_target_pairs={{0,24},{1,25},{2,26},{3,27},{4,28},{5,29},{6,30},{7,31},{8,16},{9,... | collective-permute-start | bytes 12296 | tf_op jit(solution)/shard_map/ppermute | solution.py:577
  100.2 0.1 collective-permute-done.24.refs_1_
  100.3 0.2 collective-permute-done.25.refs_2_
  100.5 2.8 %collective-permute-done.26.refs_3_ = f32[8,128]{1,0:T(8,128)S(1)} collective-permute-done((f32[8,128]{1,0:T(8,128)S(1)}, f32[8,128]{1,0:T(8,128)S(1)}, u32[]{:S(2)}, u32[]{:S(2)}) %collective-permute-start.26) | collective-permute-done | bytes 4128 | tf_op jit(solution)/shard_map/ppermute | solution.py:577
  103.2 0.7 shard_map.191
  (38 shorter events, 0.6 us)
Async XLA Ops:
  0.6 8.7 %copy-start = (f32[32,12]{0,1:T(8,128)S(1)}, f32[32,12]{0,1:T(8,128)}, u32[]{:S(2)}) copy-start(f32[32,12]{0,1:T(8,128)} %param.28) | copy-start | bytes 4612
  1.8 3.9 %collective-permute-start = (bf16[24,192]{1,0:T(8,128)(2,1)S(1)}, bf16[24,192]{1,0:T(8,128)(2,1)S(1)}, u32[]{:S(2)}, u32[]{:S(2)}) collective-permute-start(bf16[24,192]{1,0:T(8,128)(2,1)S(1)} %get-tuple-element.51), channel_id=1, source_target_pairs={{0,4},{1,5},{2,6},{3,7},{4,0},{5,1},{6,2},{7,3},{8,12},{9,13},{10,... | collective-permute-start | bytes 27656 | tf_op jit(solution)/shard_map/ppermute | solution.py:577
  2.4 26.7 %collective-permute-start.6 = (bf16[256,768]{1,0:T(8,128)(2,1)S(1)}, bf16[256,768]{1,0:T(8,128)(2,1)S(1)}, u32[]{:S(2)}, u32[]{:S(2)}) collective-permute-start(bf16[256,768]{1,0:T(8,128)(2,1)S(1)} %get-tuple-element.55), channel_id=1, source_target_pairs={{0,1},{1,0},{2,5},{3,4},{4,3},{5,2},{6,7},{7,6},{8,9},{9,8},{10,13... | collective-permute-start | bytes 1179656 | tf_op jit(solution)/shard_map/ppermute | solution.py:577
  5.0 24.1 %collective-permute-start.7 = (bf16[256,768]{1,0:T(8,128)(2,1)S(1)}, bf16[256,768]{1,0:T(8,128)(2,1)S(1)}, u32[]{:S(2)}, u32[]{:S(2)}) collective-permute-start(bf16[256,768]{1,0:T(8,128)(2,1)S(1)} %get-tuple-element.56), channel_id=1, source_target_pairs={{0,0},{1,1},{2,4},{3,5},{4,2},{5,3},{6,6},{7,7},{8,8},{9,9},{10,12... | collective-permute-start | bytes 1179656 | tf_op jit(solution)/shard_map/ppermute | solution.py:577
  5.7 6.0 %collective-permute-start.1 = (bf16[48,192]{1,0:T(8,128)(2,1)S(1)}, bf16[48,192]{1,0:T(8,128)(2,1)S(1)}, u32[]{:S(2)}, u32[]{:S(2)}) collective-permute-start(bf16[48,192]{1,0:T(8,128)(2,1)S(1)} %constant_dynamic-update-slice_fusion.refs_0_), channel_id=1, source_target_pairs={{0,8},{1,9},{2,10},{3,11},{4,12},{5,13},{6,14},{7,15},{8,0},{9,1},... | collective-permute-start | bytes 55304 | tf_op jit(solution)/shard_map/ppermute | solution.py:577
  7.3 4.4 %collective-permute-start.2 = (bf16[48,192]{1,0:T(8,128)(2,1)S(1)}, bf16[48,192]{1,0:T(8,128)(2,1)S(1)}, u32[]{:S(2)}, u32[]{:S(2)}) collective-permute-start(bf16[48,192]{1,0:T(8,128)(2,1)S(1)} %constant_dynamic-update-slice_fusion.refs_0_), channel_id=1, source_target_pairs={{0,16},{1,17},{2,18},{3,19},{4,20},{5,21},{6,22},{7,23},{8,24},{9,... | collective-permute-start | bytes 55304 | tf_op jit(solution)/shard_map/ppermute | solution.py:577
  8.8 4.7 %collective-permute-start.3 = (bf16[48,192]{1,0:T(8,128)(2,1)S(1)}, bf16[48,192]{1,0:T(8,128)(2,1)S(1)}, u32[]{:S(2)}, u32[]{:S(2)}) collective-permute-start(bf16[48,192]{1,0:T(8,128)(2,1)S(1)} %constant_dynamic-update-slice_fusion.refs_0_), channel_id=1, source_target_pairs={{0,24},{1,25},{2,26},{3,27},{4,28},{5,29},{6,30},{7,31},{8,16},{9,... | collective-permute-start | bytes 55304 | tf_op jit(solution)/shard_map/ppermute | solution.py:577
  13.6 10.5 %collective-permute-start.10 = (bf16[64,192]{1,0:T(8,128)(2,1)S(1)}, bf16[64,192]{1,0:T(8,128)(2,1)S(1)}, u32[]{:S(2)}, u32[]{:S(2)}) collective-permute-start(bf16[64,192]{1,0:T(8,128)(2,1)S(1)} %shard_map.184), channel_id=1, source_target_pairs={{0,1},{1,0},{2,3},{3,2},{4,5},{5,4},{6,7},{7,6},{8,9},{9,8},{10,11... | collective-permute-start | bytes 73736 | tf_op jit(solution)/shard_map/ppermute | solution.py:577
  14.3 13.1 %collective-permute-start.11 = (bf16[64,192]{1,0:T(8,128)(2,1)S(1)}, bf16[64,192]{1,0:T(8,128)(2,1)S(1)}, u32[]{:S(2)}, u32[]{:S(2)}) collective-permute-start(bf16[64,192]{1,0:T(8,128)(2,1)S(1)} %shard_map.184), channel_id=1, source_target_pairs={{0,2},{1,3},{2,0},{3,1},{4,6},{5,7},{6,4},{7,5},{8,10},{9,11},{10,... | collective-permute-start | bytes 73736 | tf_op jit(solution)/shard_map/ppermute | solution.py:577
  19.6 8.4 %collective-permute-start.12 = (bf16[64,192]{1,0:T(8,128)(2,1)S(1)}, bf16[64,192]{1,0:T(8,128)(2,1)S(1)}, u32[]{:S(2)}, u32[]{:S(2)}) collective-permute-start(bf16[64,192]{1,0:T(8,128)(2,1)S(1)} %shard_map.184), channel_id=1, source_target_pairs={{0,3},{1,2},{2,1},{3,0},{4,7},{5,6},{6,5},{7,4},{8,11},{9,10},{10,... | collective-permute-start | bytes 73736 | tf_op jit(solution)/shard_map/ppermute | solution.py:577
  24.0 30.9 %collective-permute-start.4 = (bf16[256,768]{1,0:T(8,128)(2,1)S(1)}, bf16[256,768]{1,0:T(8,128)(2,1)S(1)}, u32[]{:S(2)}, u32[]{:S(2)}) collective-permute-start(bf16[256,768]{1,0:T(8,128)(2,1)S(1)} %get-tuple-element.53), channel_id=1, source_target_pairs={{0,1},{1,0},{2,5},{3,4},{4,3},{5,2},{6,7},{7,6},{8,9},{9,8},{10,13... | collective-permute-start | bytes 1179656 | tf_op jit(solution)/shard_map/ppermute | solution.py:577
  27.4 27.6 %collective-permute-start.5 = (bf16[256,768]{1,0:T(8,128)(2,1)S(1)}, bf16[256,768]{1,0:T(8,128)(2,1)S(1)}, u32[]{:S(2)}, u32[]{:S(2)}) collective-permute-start(bf16[256,768]{1,0:T(8,128)(2,1)S(1)} %get-tuple-element.54), channel_id=1, source_target_pairs={{0,0},{1,1},{2,4},{3,5},{4,2},{5,3},{6,6},{7,7},{8,8},{9,9},{10,12... | collective-permute-start | bytes 1179656 | tf_op jit(solution)/shard_map/ppermute | solution.py:577
  28.1 1.9 %collective-permute-start.13 = (bf16[256,192]{1,0:T(8,128)(2,1)S(1)}, bf16[256,192]{1,0:T(8,128)(2,1)S(1)}, u32[]{:S(2)}, u32[]{:S(2)}) collective-permute-start(bf16[256,192]{1,0:T(8,128)(2,1)S(1)} %constant_dynamic-update-slice_fusion.2.refs_12_), channel_id=1, source_target_pairs={{0,4},{1,5},{2,6},{3,7},{4,0},{5,1},{6,2},{7,3},{8,12},{9,13},{10,... | collective-permute-start | bytes 294920 | tf_op jit(solution)/shard_map/ppermute | solution.py:577
  29.0 1.7 %collective-permute-start.8 = (bf16[256,768]{1,0:T(8,128)(2,1)S(1)}, bf16[256,768]{1,0:T(8,128)(2,1)S(1)}, u32[]{:S(2)}, u32[]{:S(2)}) collective-permute-start(bf16[256,768]{1,0:T(8,128)(2,1)S(1)} %collective-permute-done.6.refs_0_), channel_id=1, source_target_pairs={{0,4},{1,5},{2,6},{3,7},{4,0},{5,1},{6,2},{7,3},{8,12},{9,13},{10,... | collective-permute-start | bytes 1179656 | tf_op jit(solution)/shard_map/ppermute | solution.py:577
  29.1 2.2 %collective-permute-start.9 = (bf16[256,768]{1,0:T(8,128)(2,1)S(1)}, bf16[256,768]{1,0:T(8,128)(2,1)S(1)}, u32[]{:S(2)}, u32[]{:S(2)}) collective-permute-start(bf16[256,768]{1,0:T(8,128)(2,1)S(1)} %collective-permute-done.7.refs_1_), channel_id=1, source_target_pairs={{0,4},{1,5},{2,6},{3,7},{4,0},{5,1},{6,2},{7,3},{8,12},{9,13},{10,... | collective-permute-start | bytes 1179656 | tf_op jit(solution)/shard_map/ppermute | solution.py:577
  53.8 19.9 %collective-permute-start.14 = (bf16[256,768]{1,0:T(8,128)(2,1)S(1)}, bf16[256,768]{1,0:T(8,128)(2,1)S(1)}, u32[]{:S(2)}, u32[]{:S(2)}) collective-permute-start(bf16[256,768]{1,0:T(8,128)(2,1)S(1)} %get-tuple-element.79), channel_id=1, source_target_pairs={{0,1},{1,0},{2,5},{3,4},{4,3},{5,2},{6,7},{7,6},{8,9},{9,8},{10,13... | collective-permute-start | bytes 1179656 | tf_op jit(solution)/shard_map/ppermute | solution.py:577
  54.1 19.6 %collective-permute-start.15 = (bf16[256,768]{1,0:T(8,128)(2,1)S(1)}, bf16[256,768]{1,0:T(8,128)(2,1)S(1)}, u32[]{:S(2)}, u32[]{:S(2)}) collective-permute-start(bf16[256,768]{1,0:T(8,128)(2,1)S(1)} %get-tuple-element.80), channel_id=1, source_target_pairs={{0,0},{1,1},{2,4},{3,5},{4,2},{5,3},{6,6},{7,7},{8,8},{9,9},{10,12... | collective-permute-start | bytes 1179656 | tf_op jit(solution)/shard_map/ppermute | solution.py:577
  73.7 4.5 %collective-permute-start.16 = (bf16[64,768]{1,0:T(8,128)(2,1)S(1)}, bf16[64,768]{1,0:T(8,128)(2,1)S(1)}, u32[]{:S(2)}, u32[]{:S(2)}) collective-permute-start(bf16[64,768]{1,0:T(8,128)(2,1)S(1)} %get-tuple-element.82), channel_id=1, source_target_pairs={{0,4},{1,5},{2,6},{3,7},{4,0},{5,1},{6,2},{7,3},{8,12},{9,13},{10,... | collective-permute-start | bytes 294920 | tf_op jit(solution)/shard_map/ppermute | solution.py:577
  78.2 7.0 %collective-permute-start.19 = (bf16[16,768]{1,0:T(8,128)(2,1)S(1)}, bf16[16,768]{1,0:T(8,128)(2,1)S(1)}, u32[]{:S(2)}, u32[]{:S(2)}) collective-permute-start(bf16[16,768]{1,0:T(8,128)(2,1)S(1)} %get-tuple-element.86), channel_id=1, source_target_pairs={{0,24},{1,25},{2,26},{3,27},{4,28},{5,29},{6,30},{7,31},{8,16},{9,... | collective-permute-start | bytes 73736 | tf_op jit(solution)/shard_map/ppermute | solution.py:577
  83.4 3.8 %collective-permute-start.18 = (bf16[16,768]{1,0:T(8,128)(2,1)S(1)}, bf16[16,768]{1,0:T(8,128)(2,1)S(1)}, u32[]{:S(2)}, u32[]{:S(2)}) collective-permute-start(bf16[16,768]{1,0:T(8,128)(2,1)S(1)} %get-tuple-element.85), channel_id=1, source_target_pairs={{0,16},{1,17},{2,18},{3,19},{4,20},{5,21},{6,22},{7,23},{8,24},{9,... | collective-permute-start | bytes 73736 | tf_op jit(solution)/shard_map/ppermute | solution.py:577
  83.8 20.1 %copy-start.1 = (f32[32,12]{0,1:T(8,128)S(1)}, f32[32,12]{0,1:T(8,128)}, u32[]{:S(2)}) copy-start(f32[32,12]{0,1:T(8,128)} %param.28) | copy-start | bytes 4612
  83.8 19.4 %copy-start.2 = (f32[16,192]{1,0:T(8,128)S(1)}, f32[16,192]{1,0:T(8,128)}, u32[]{:S(2)}) copy-start(f32[16,192]{1,0:T(8,128)} %prompt_ref.1) | copy-start | bytes 36868
  83.8 19.4 %copy-start.3 = (f32[16,192]{1,0:T(8,128)S(1)}, f32[16,192]{1,0:T(8,128)}, u32[]{:S(2)}) copy-start(f32[16,192]{1,0:T(8,128)} %first_ref.1) | copy-start | bytes 36868
  83.8 19.4 %copy-start.4 = (f32[16,192]{1,0:T(8,128)S(1)}, f32[16,192]{1,0:T(8,128)}, u32[]{:S(2)}) copy-start(f32[16,192]{1,0:T(8,128)} %second_ref.1) | copy-start | bytes 36868
  83.9 3.9 %collective-permute-start.17 = (bf16[16,768]{1,0:T(8,128)(2,1)S(1)}, bf16[16,768]{1,0:T(8,128)(2,1)S(1)}, u32[]{:S(2)}, u32[]{:S(2)}) collective-permute-start(bf16[16,768]{1,0:T(8,128)(2,1)S(1)} %get-tuple-element.84), channel_id=1, source_target_pairs={{0,8},{1,9},{2,10},{3,11},{4,12},{5,13},{6,14},{7,15},{8,0},{9,1},... | collective-permute-start | bytes 73736 | tf_op jit(solution)/shard_map/ppermute | solution.py:577
  87.8 5.4 %collective-permute-start.20 = (bf16[16,768]{1,0:T(8,128)(2,1)S(1)}, bf16[16,768]{1,0:T(8,128)(2,1)S(1)}, u32[]{:S(2)}, u32[]{:S(2)}) collective-permute-start(bf16[16,768]{1,0:T(8,128)(2,1)S(1)} %get-tuple-element.98), channel_id=1, source_target_pairs={{0,1},{1,0},{2,3},{3,2},{4,5},{5,4},{6,7},{7,6},{8,9},{9,8},{10,11... | collective-permute-start | bytes 73736 | tf_op jit(solution)/shard_map/ppermute | solution.py:577
  87.8 5.3 %collective-permute-start.21 = (bf16[16,768]{1,0:T(8,128)(2,1)S(1)}, bf16[16,768]{1,0:T(8,128)(2,1)S(1)}, u32[]{:S(2)}, u32[]{:S(2)}) collective-permute-start(bf16[16,768]{1,0:T(8,128)(2,1)S(1)} %get-tuple-element.98), channel_id=1, source_target_pairs={{0,2},{1,3},{2,0},{3,1},{4,6},{5,7},{6,4},{7,5},{8,10},{9,11},{10,... | collective-permute-start | bytes 73736 | tf_op jit(solution)/shard_map/ppermute | solution.py:577
  89.6 5.6 %collective-permute-start.22 = (bf16[16,768]{1,0:T(8,128)(2,1)S(1)}, bf16[16,768]{1,0:T(8,128)(2,1)S(1)}, u32[]{:S(2)}, u32[]{:S(2)}) collective-permute-start(bf16[16,768]{1,0:T(8,128)(2,1)S(1)} %get-tuple-element.98), channel_id=1, source_target_pairs={{0,3},{1,2},{2,1},{3,0},{4,7},{5,6},{6,5},{7,4},{8,11},{9,10},{10,... | collective-permute-start | bytes 73736 | tf_op jit(solution)/shard_map/ppermute | solution.py:577
  95.4 1.2 %collective-permute-start.23 = (f32[8,128]{1,0:T(8,128)S(1)}, f32[8,128]{1,0:T(8,128)S(1)}, u32[]{:S(2)}, u32[]{:S(2)}) collective-permute-start(f32[8,128]{1,0:T(8,128)S(1)} %get-tuple-element.94), channel_id=1, source_target_pairs={{0,4},{1,5},{2,6},{3,7},{4,0},{5,1},{6,2},{7,3},{8,12},{9,13},{10,... | collective-permute-start | bytes 12296 | tf_op jit(solution)/shard_map/ppermute | solution.py:577
  96.7 3.6 %collective-permute-start.24 = (f32[8,128]{1,0:T(8,128)S(1)}, f32[8,128]{1,0:T(8,128)S(1)}, u32[]{:S(2)}, u32[]{:S(2)}) collective-permute-start(f32[8,128]{1,0:T(8,128)S(1)} %add.22.refs_0_), channel_id=1, source_target_pairs={{0,8},{1,9},{2,10},{3,11},{4,12},{5,13},{6,14},{7,15},{8,0},{9,1},... | collective-permute-start | bytes 12296 | tf_op jit(solution)/shard_map/ppermute | solution.py:577
  96.9 3.6 %collective-permute-start.25 = (f32[8,128]{1,0:T(8,128)S(1)}, f32[8,128]{1,0:T(8,128)S(1)}, u32[]{:S(2)}, u32[]{:S(2)}) collective-permute-start(f32[8,128]{1,0:T(8,128)S(1)} %add.22.refs_0_), channel_id=1, source_target_pairs={{0,16},{1,17},{2,18},{3,19},{4,20},{5,21},{6,22},{7,23},{8,24},{9,... | collective-permute-start | bytes 12296 | tf_op jit(solution)/shard_map/ppermute | solution.py:577
  98.7 4.5 %collective-permute-start.26 = (f32[8,128]{1,0:T(8,128)S(1)}, f32[8,128]{1,0:T(8,128)S(1)}, u32[]{:S(2)}, u32[]{:S(2)}) collective-permute-start(f32[8,128]{1,0:T(8,128)S(1)} %add.22.refs_0_), channel_id=1, source_target_pairs={{0,24},{1,25},{2,26},{3,27},{4,28},{5,29},{6,30},{7,31},{8,16},{9,... | collective-permute-start | bytes 12296 | tf_op jit(solution)/shard_map/ppermute | solution.py:577

commit v8 on v7

--- a/solution.py
+++ b/solution.py
@@ -256,10 +256,8 @@
     hidden = prompt_ref[...].astype(f32)
     norm_ref[half_len : half_len + BLK, :] = (hidden * inv_rms(hidden) * gain).astype(bf16)
     wide = 2 * BLK
-
-    @pl.loop(0, width // wide)
-    def _(t):
-        cols = pl.ds(pl.multiple_of(t * wide, wide), wide)
+    for t in range(width // wide):
+        cols = slice(t * wide, (t + 1) * wide)
         normed = jnp.concatenate([normed_ref[...], norm_ref[0 : half_len + BLK, :]], axis=0)
         kall_ref[:, cols] = dot_nn(normed, wk_ref[:, cols]).astype(bf16)
         vall_ref[:, cols] = dot_nn(normed, wv_ref[:, cols]).astype(bf16)
@@ -389,9 +387,8 @@
         fetch.wait()
     after_ref[...] = dot_tn(mixed_ref[...], wo_ref[...])
 
-    @pl.loop(0, half_len // BLK)
-    def _(t):
-        rows = pl.ds(pl.multiple_of(t * BLK, BLK), BLK)
+    for t in range(half_len // BLK):
+        rows = slice(t * BLK, (t + 1) * BLK)
         after = hid_ref[rows, :].astype(f32) + after_ref[rows, :]
         after_ref[rows, :] = after
         norm_ref[rows, :] = (after * inv_rms(after) * gain_second_ref[...]).astype(bf16)
@@ -441,9 +438,8 @@
         cot_ref[j * piece : (j + 1) * piece, :] = pick_piece(cots, turn, j)
     do_ref[...] = jnp.zeros_like(do_ref)
 
-    @pl.loop(0, wi_ref.shape[1] // UNITS)
-    def _(t):
-        units = pl.ds(pl.multiple_of(t * UNITS, UNITS), UNITS)
+    for t in range(wi_ref.shape[1] // UNITS):
+        units = slice(t * UNITS, (t + 1) * UNITS)
         grad_act = dot_nt(wout_ref[units, :], cot_ref[...])
         grad_inner = jnp.where(act_ref[units, :] > 0, grad_act, 0.0).astype(bf16)
         do_ref[...] += dot_nn(wi_ref[:, units], grad_inner)
@@ -451,9 +447,8 @@
     acc_ref[...] = do_ref[...].T
     gain = gain_second_ref[...]
 
-    @pl.loop(0, half_len // BLK)
-    def _(t):
-        rows = pl.ds(pl.multiple_of(t * BLK, BLK), BLK)
+    for t in range(half_len // BLK):
+        rows = slice(t * BLK, (t + 1) * BLK)
         after = after_ref[rows, :]
         scale = inv_rms(after)
         pulled = gain * acc_ref[rows, :]

time: 104 us -> 102 us (0.981)
  Pallas kernels: 46.7 us -> 44.5 us
    pallas_call x1, Pallas kernels: 22.5 us -> 21.3 us  [on_device(): pl.pallas_call(functools.partial(forward_kernel, count, piece, rows_own),...]
  transfers between devices with their start and end apart: 27 -> 27, of which waited for: 14 -> 14; matrix products, arithmetic and copies ran while one was open for 3% -> 3% of each run, Pallas kernels for 43% -> 42%
where the time goes in v8:
time: 102 us
  Pallas kernels  44.5 us (44%)
  starting transfers between devices  36.2 us (35%)
  waiting for transfers between devices  16.7 us (16%)
  local copies, waits for them, and re-layouts  1.43 us (1%)
  other arithmetic  1.02 us (1%)
    ppermute x27, starting transfers between devices, permute(): return lax.ppermute(value, AXES, pairs)  36.2 us
    pallas_call x1, Pallas kernels, on_device(): pl.pallas_call(functools.partial(forward_kernel, count, piece, rows_own),...  21.3 us
    pallas_call x1, Pallas kernels, on_device(): pl.pallas_call(functools.partial(backward_kernel, count, piece, rows_own)...  17.7 us
    ppermute x27, waiting for transfers between devices, permute(): return lax.ppermute(value, AXES, pairs)  16.7 us
    pallas_call x1, Pallas kernels, on_device(): pl.pallas_call(functools.partial(prepare_kernel, count), out_shape=[held(...  3.03 us
  transfers between devices with their start and end apart: 27, of which 14 were waited for; matrix products, arithmetic and copies ran while one was open for 3% of the time, Pallas kernels for 42%

profile of v8, /device:TPU:0, one launch (start us, length us, event | category | flops | bytes accessed | tf_op | source)
XLA Modules:
  0.0 101.8 jit_solution(15351638822321840520)
XLA Ops:
  0.6 1.2 %shard_map.183 = (bf16[256,768]{1,0:T(8,128)(2,1)S(1)}, bf16[256,768]{1,0:T(8,128)(2,1)S(1)}, bf16[24,192]{1,0:T(8,128)(2,1)S(1)}) custom-call(bf16[2,256,768]{2,1,0:T(8,128)(2,1)} %tokens_ref.1, s32[2,256]{1,0:T(2,128)} %seg_hbm.1, f32[16,192]{1,0:T(8,128)} %prompt_ref.1), custom_call_target="tpu_custom_call" | custom-call | flops 100000 | bytes 2000000 | tf_op jit(solution)/shard_map/pallas_call | solution.py:585
  1.8 0.5 collective-permute-start
  2.4 2.6 %collective-permute-start.6 = (bf16[256,768]{1,0:T(8,128)(2,1)S(1)}, bf16[256,768]{1,0:T(8,128)(2,1)S(1)}, u32[]{:S(2)}, u32[]{:S(2)}) collective-permute-start(bf16[256,768]{1,0:T(8,128)(2,1)S(1)} %get-tuple-element.55), channel_id=1, source_target_pairs={{0,1},{1,0},{2,5},{3,4},{4,3},{5,2},{6,7},{7,6},{8,9},{9,8},{10,13... | collective-permute-start | bytes 1179656 | tf_op jit(solution)/shard_map/ppermute | solution.py:572
  5.0 0.7 collective-permute-start.7
  5.7 1.6 %collective-permute-start.1 = (bf16[48,192]{1,0:T(8,128)(2,1)S(1)}, bf16[48,192]{1,0:T(8,128)(2,1)S(1)}, u32[]{:S(2)}, u32[]{:S(2)}) collective-permute-start(bf16[48,192]{1,0:T(8,128)(2,1)S(1)} %constant_dynamic-update-slice_fusion.refs_0_), channel_id=1, source_target_pairs={{0,8},{1,9},{2,10},{3,11},{4,12},{5,13},{6,14},{7,15},{8,0},{9,1},... | collective-permute-start | bytes 55304 | tf_op jit(solution)/shard_map/ppermute | solution.py:572
  7.3 1.5 %collective-permute-start.2 = (bf16[48,192]{1,0:T(8,128)(2,1)S(1)}, bf16[48,192]{1,0:T(8,128)(2,1)S(1)}, u32[]{:S(2)}, u32[]{:S(2)}) collective-permute-start(bf16[48,192]{1,0:T(8,128)(2,1)S(1)} %constant_dynamic-update-slice_fusion.refs_0_), channel_id=1, source_target_pairs={{0,16},{1,17},{2,18},{3,19},{4,20},{5,21},{6,22},{7,23},{8,24},{9,... | collective-permute-start | bytes 55304 | tf_op jit(solution)/shard_map/ppermute | solution.py:572
  8.8 0.5 collective-permute-start.3
  9.3 1.0 convolution_bitcast_fusion.base_ref
  10.3 0.7 broadcast_in_dim.6.gain_first_ref
  11.0 0.7 broadcast_in_dim.7.gain_second_ref
  11.7 1.8 %collective-permute-done.3.refs_3_ = bf16[48,192]{1,0:T(8,128)(2,1)S(1)} collective-permute-done((bf16[48,192]{1,0:T(8,128)(2,1)S(1)}, bf16[48,192]{1,0:T(8,128)(2,1)S(1)}, u32[]{:S(2)}, u32[]{:S(2)}) %collective-permute-start.3) | collective-permute-done | bytes 18464 | tf_op jit(solution)/shard_map/ppermute | solution.py:572
  13.6 0.7 collective-permute-start.10
  14.3 5.3 %collective-permute-start.11 = (bf16[64,192]{1,0:T(8,128)(2,1)S(1)}, bf16[64,192]{1,0:T(8,128)(2,1)S(1)}, u32[]{:S(2)}, u32[]{:S(2)}) collective-permute-start(bf16[64,192]{1,0:T(8,128)(2,1)S(1)} %shard_map.184), channel_id=1, source_target_pairs={{0,2},{1,3},{2,0},{3,1},{4,6},{5,7},{6,4},{7,5},{8,10},{9,11},{10,... | collective-permute-start | bytes 73736 | tf_op jit(solution)/shard_map/ppermute | solution.py:572
  19.6 1.4 %collective-permute-start.12 = (bf16[64,192]{1,0:T(8,128)(2,1)S(1)}, bf16[64,192]{1,0:T(8,128)(2,1)S(1)}, u32[]{:S(2)}, u32[]{:S(2)}) collective-permute-start(bf16[64,192]{1,0:T(8,128)(2,1)S(1)} %shard_map.184), channel_id=1, source_target_pairs={{0,3},{1,2},{2,1},{3,0},{4,7},{5,6},{6,5},{7,4},{8,11},{9,10},{10,... | collective-permute-start | bytes 73736 | tf_op jit(solution)/shard_map/ppermute | solution.py:572
  21.0 3.0 %shard_map.185 = (f32[12,3,128,128]{3,2,1,0:T(8,128)S(1)}, bf16[1536,512]{1,0:T(8,128)(2,1)S(1)}, f32[1,768]{1,0:T(1,128)S(1)}, f32[1,768]{1,0:T(1,128)S(1)}, bf...) custom-call(f32[12,512]{1,0:T(8,128)S(1)} %convolution_bitcast_fusio, ...), custom_call_target="tpu_custom_call" | custom-call | flops 1000000 | bytes 5000000 | tf_op jit(solution)/shard_map/pallas_call | solution.py:621
  24.0 0.6 collective-permute-start.4
  24.7 2.7 %collective-permute-done.11 = bf16[64,192]{1,0:T(8,128)(2,1)S(1)} collective-permute-done((bf16[64,192]{1,0:T(8,128)(2,1)S(1)}, bf16[64,192]{1,0:T(8,128)(2,1)S(1)}, u32[]{:S(2)}, u32[]{:S(2)}) %collective-permute-start.11) | collective-permute-done | bytes 24608 | tf_op jit(solution)/shard_map/ppermute | solution.py:572
  27.4 0.7 collective-permute-start.5
  28.1 0.9 collective-permute-start.13
  29.1 0.4 collective-permute-start.9
  29.5 0.3 shard_map.186.refs_4_
  30.0 0.7 collective-permute-done.8.refs_2_
  30.8 0.6 collective-permute-done.9.refs_3_
  31.3 21.3 %shard_map.187 = (bf16[6,2,1152,512]{3,2,1,0:T(8,128)(2,1)}, s32[8,128]{1,0:T(8,128)S(1)}, bf16[128,768]{1,0:T(8,128)(2,1)S(1)}, bf16[512,768]{1,0:T(8,128)(2,1)...) custom-call(bf16[256,768]{1,0:T(8,128)(2,1)S(1)} %collective-permute, ...), custom_call_target="tpu_custom_call" | custom-call | flops 30000001024 | bytes 40000000 | tf_op jit(solution)/shard_map/pallas_call | solution.py:650
  52.6 0.3 collective-permute-start.14
  52.9 0.9 collective-permute-start.15
  53.8 17.7 %shard_map.188 = (f32[64,768]{1,0:T(8,128)S(1)}, bf16[64,768]{1,0:T(8,128)(2,1)S(1)}) custom-call(bf16[256,768]{1,0:T(8,128)(2,1)S(1)} %collective-permute-done.4.refs_0_, bf16[256,768]{1,0:T(8,128)(2,1)S(1)} %collective-permute-done.5.refs_1_, s32[8,128]{1,0:T(8,128)S(1)} %get-tuple-element.65.refs_2_, bf16[3072,512]{1,0:T(8,128)(2,1)S(1)} %get-tuple-element.66.refs_3_, ...), custom_call_target="tpu_custom_call" | custom-call | flops 30000001024 | bytes 40000000 | tf_op jit(solution)/shard_map/pallas_call | solution.py:690
  71.5 3.5 %collective-permute-start.16 = (bf16[64,768]{1,0:T(8,128)(2,1)S(1)}, bf16[64,768]{1,0:T(8,128)(2,1)S(1)}, u32[]{:S(2)}, u32[]{:S(2)}) collective-permute-start(bf16[64,768]{1,0:T(8,128)(2,1)S(1)} %get-tuple-element.82), channel_id=1, source_target_pairs={{0,4},{1,5},{2,6},{3,7},{4,0},{5,1},{6,2},{7,3},{8,12},{9,13},{10,... | collective-permute-start | bytes 294920 | tf_op jit(solution)/shard_map/ppermute | solution.py:572
  75.1 0.9 collective-permute-done.16.came_ref
  76.0 5.2 %collective-permute-start.19 = (bf16[16,768]{1,0:T(8,128)(2,1)S(1)}, bf16[16,768]{1,0:T(8,128)(2,1)S(1)}, u32[]{:S(2)}, u32[]{:S(2)}) collective-permute-start(bf16[16,768]{1,0:T(8,128)(2,1)S(1)} %get-tuple-element.86), channel_id=1, source_target_pairs={{0,24},{1,25},{2,26},{3,27},{4,28},{5,29},{6,30},{7,31},{8,16},{9,... | collective-permute-start | bytes 73736 | tf_op jit(solution)/shard_map/ppermute | solution.py:572
  81.3 0.4 collective-permute-start.18
  81.7 0.3 collective-permute-start.17
  82.0 1.0 collective-permute-done.19
  83.1 2.0 %collective-permute-done.18 = bf16[16,768]{1,0:T(8,128)(2,1)S(1)} collective-permute-done((bf16[16,768]{1,0:T(8,128)(2,1)S(1)}, bf16[16,768]{1,0:T(8,128)(2,1)S(1)}, u32[]{:S(2)}, u32[]{:S(2)}) %collective-permute-start.18) | collective-permute-done | bytes 24608 | tf_op jit(solution)/shard_map/ppermute | solution.py:572
  85.1 0.5 collective-permute-done.17
  85.7 1.7 %collective-permute-start.21 = (bf16[16,768]{1,0:T(8,128)(2,1)S(1)}, bf16[16,768]{1,0:T(8,128)(2,1)S(1)}, u32[]{:S(2)}, u32[]{:S(2)}) collective-permute-start(bf16[16,768]{1,0:T(8,128)(2,1)S(1)} %get-tuple-element.98), channel_id=1, source_target_pairs={{0,2},{1,3},{2,0},{3,1},{4,6},{5,7},{6,4},{7,5},{8,10},{9,11},{10,... | collective-permute-start | bytes 73736 | tf_op jit(solution)/shard_map/ppermute | solution.py:572
  87.4 2.7 %collective-permute-start.22 = (bf16[16,768]{1,0:T(8,128)(2,1)S(1)}, bf16[16,768]{1,0:T(8,128)(2,1)S(1)}, u32[]{:S(2)}, u32[]{:S(2)}) collective-permute-start(bf16[16,768]{1,0:T(8,128)(2,1)S(1)} %get-tuple-element.98), channel_id=1, source_target_pairs={{0,3},{1,2},{2,1},{3,0},{4,7},{5,6},{6,5},{7,4},{8,11},{9,10},{10,... | collective-permute-start | bytes 73736 | tf_op jit(solution)/shard_map/ppermute | solution.py:572
  90.1 0.9 pad_maximum_fusion
  91.0 2.0 %collective-permute-done.22.refs_2_ = bf16[16,768]{1,0:T(8,128)(2,1)S(1)} collective-permute-done((bf16[16,768]{1,0:T(8,128)(2,1)S(1)}, bf16[16,768]{1,0:T(8,128)(2,1)S(1)}, u32[]{:S(2)}, u32[]{:S(2)}) %collective-permute-start.22) | collective-permute-done | bytes 24608 | tf_op jit(solution)/shard_map/ppermute | solution.py:572
  93.0 0.3 shard_map.190
  93.4 1.2 %collective-permute-done.23 = f32[8,128]{1,0:T(8,128)S(1)} collective-permute-done((f32[8,128]{1,0:T(8,128)S(1)}, f32[8,128]{1,0:T(8,128)S(1)}, u32[]{:S(2)}, u32[]{:S(2)}) %collective-permute-start.23) | collective-permute-done | bytes 4128 | tf_op jit(solution)/shard_map/ppermute | solution.py:572
  94.5 0.2 collective-permute-start.24
  94.7 1.9 %collective-permute-start.25 = (f32[8,128]{1,0:T(8,128)S(1)}, f32[8,128]{1,0:T(8,128)S(1)}, u32[]{:S(2)}, u32[]{:S(2)}) collective-permute-start(f32[8,128]{1,0:T(8,128)S(1)} %add.22.refs_0_), channel_id=1, source_target_pairs={{0,16},{1,17},{2,18},{3,19},{4,20},{5,21},{6,22},{7,23},{8,24},{9,... | collective-permute-start | bytes 12296 | tf_op jit(solution)/shard_map/ppermute | solution.py:572
  96.6 1.4 %collective-permute-start.26 = (f32[8,128]{1,0:T(8,128)S(1)}, f32[8,128]{1,0:T(8,128)S(1)}, u32[]{:S(2)}, u32[]{:S(2)}) collective-permute-start(f32[8,128]{1,0:T(8,128)S(1)} %add.22.refs_0_), channel_id=1, source_target_pairs={{0,24},{1,25},{2,26},{3,27},{4,28},{5,29},{6,30},{7,31},{8,16},{9,... | collective-permute-start | bytes 12296 | tf_op jit(solution)/shard_map/ppermute | solution.py:572
  98.0 0.1 collective-permute-done.24.refs_1_
  98.1 0.2 collective-permute-done.25.refs_2_
  98.3 2.8 %collective-permute-done.26.refs_3_ = f32[8,128]{1,0:T(8,128)S(1)} collective-permute-done((f32[8,128]{1,0:T(8,128)S(1)}, f32[8,128]{1,0:T(8,128)S(1)}, u32[]{:S(2)}, u32[]{:S(2)}) %collective-permute-start.26) | collective-permute-done | bytes 4128 | tf_op jit(solution)/shard_map/ppermute | solution.py:572
  101.1 0.7 shard_map.191
  (38 shorter events, 0.6 us)
Async XLA Ops:
  0.6 8.7 %copy-start = (f32[32,12]{0,1:T(8,128)S(1)}, f32[32,12]{0,1:T(8,128)}, u32[]{:S(2)}) copy-start(f32[32,12]{0,1:T(8,128)} %param.28) | copy-start | bytes 4612
  1.8 3.9 %collective-permute-start = (bf16[24,192]{1,0:T(8,128)(2,1)S(1)}, bf16[24,192]{1,0:T(8,128)(2,1)S(1)}, u32[]{:S(2)}, u32[]{:S(2)}) collective-permute-start(bf16[24,192]{1,0:T(8,128)(2,1)S(1)} %get-tuple-element.51), channel_id=1, source_target_pairs={{0,4},{1,5},{2,6},{3,7},{4,0},{5,1},{6,2},{7,3},{8,12},{9,13},{10,... | collective-permute-start | bytes 27656 | tf_op jit(solution)/shard_map/ppermute | solution.py:572
  2.4 26.7 %collective-permute-start.6 = (bf16[256,768]{1,0:T(8,128)(2,1)S(1)}, bf16[256,768]{1,0:T(8,128)(2,1)S(1)}, u32[]{:S(2)}, u32[]{:S(2)}) collective-permute-start(bf16[256,768]{1,0:T(8,128)(2,1)S(1)} %get-tuple-element.55), channel_id=1, source_target_pairs={{0,1},{1,0},{2,5},{3,4},{4,3},{5,2},{6,7},{7,6},{8,9},{9,8},{10,13... | collective-permute-start | bytes 1179656 | tf_op jit(solution)/shard_map/ppermute | solution.py:572
  5.0 24.1 %collective-permute-start.7 = (bf16[256,768]{1,0:T(8,128)(2,1)S(1)}, bf16[256,768]{1,0:T(8,128)(2,1)S(1)}, u32[]{:S(2)}, u32[]{:S(2)}) collective-permute-start(bf16[256,768]{1,0:T(8,128)(2,1)S(1)} %get-tuple-element.56), channel_id=1, source_target_pairs={{0,0},{1,1},{2,4},{3,5},{4,2},{5,3},{6,6},{7,7},{8,8},{9,9},{10,12... | collective-permute-start | bytes 1179656 | tf_op jit(solution)/shard_map/ppermute | solution.py:572
  5.7 6.0 %collective-permute-start.1 = (bf16[48,192]{1,0:T(8,128)(2,1)S(1)}, bf16[48,192]{1,0:T(8,128)(2,1)S(1)}, u32[]{:S(2)}, u32[]{:S(2)}) collective-permute-start(bf16[48,192]{1,0:T(8,128)(2,1)S(1)} %constant_dynamic-update-slice_fusion.refs_0_), channel_id=1, source_target_pairs={{0,8},{1,9},{2,10},{3,11},{4,12},{5,13},{6,14},{7,15},{8,0},{9,1},... | collective-permute-start | bytes 55304 | tf_op jit(solution)/shard_map/ppermute | solution.py:572
  7.3 4.4 %collective-permute-start.2 = (bf16[48,192]{1,0:T(8,128)(2,1)S(1)}, bf16[48,192]{1,0:T(8,128)(2,1)S(1)}, u32[]{:S(2)}, u32[]{:S(2)}) collective-permute-start(bf16[48,192]{1,0:T(8,128)(2,1)S(1)} %constant_dynamic-update-slice_fusion.refs_0_), channel_id=1, source_target_pairs={{0,16},{1,17},{2,18},{3,19},{4,20},{5,21},{6,22},{7,23},{8,24},{9,... | collective-permute-start | bytes 55304 | tf_op jit(solution)/shard_map/ppermute | solution.py:572
  8.8 4.7 %collective-permute-start.3 = (bf16[48,192]{1,0:T(8,128)(2,1)S(1)}, bf16[48,192]{1,0:T(8,128)(2,1)S(1)}, u32[]{:S(2)}, u32[]{:S(2)}) collective-permute-start(bf16[48,192]{1,0:T(8,128)(2,1)S(1)} %constant_dynamic-update-slice_fusion.refs_0_), channel_id=1, source_target_pairs={{0,24},{1,25},{2,26},{3,27},{4,28},{5,29},{6,30},{7,31},{8,16},{9,... | collective-permute-start | bytes 55304 | tf_op jit(solution)/shard_map/ppermute | solution.py:572
  13.6 10.5 %collective-permute-start.10 = (bf16[64,192]{1,0:T(8,128)(2,1)S(1)}, bf16[64,192]{1,0:T(8,128)(2,1)S(1)}, u32[]{:S(2)}, u32[]{:S(2)}) collective-permute-start(bf16[64,192]{1,0:T(8,128)(2,1)S(1)} %shard_map.184), channel_id=1, source_target_pairs={{0,1},{1,0},{2,3},{3,2},{4,5},{5,4},{6,7},{7,6},{8,9},{9,8},{10,11... | collective-permute-start | bytes 73736 | tf_op jit(solution)/shard_map/ppermute | solution.py:572
  14.3 13.1 %collective-permute-start.11 = (bf16[64,192]{1,0:T(8,128)(2,1)S(1)}, bf16[64,192]{1,0:T(8,128)(2,1)S(1)}, u32[]{:S(2)}, u32[]{:S(2)}) collective-permute-start(bf16[64,192]{1,0:T(8,128)(2,1)S(1)} %shard_map.184), channel_id=1, source_target_pairs={{0,2},{1,3},{2,0},{3,1},{4,6},{5,7},{6,4},{7,5},{8,10},{9,11},{10,... | collective-permute-start | bytes 73736 | tf_op jit(solution)/shard_map/ppermute | solution.py:572
  19.6 8.4 %collective-permute-start.12 = (bf16[64,192]{1,0:T(8,128)(2,1)S(1)}, bf16[64,192]{1,0:T(8,128)(2,1)S(1)}, u32[]{:S(2)}, u32[]{:S(2)}) collective-permute-start(bf16[64,192]{1,0:T(8,128)(2,1)S(1)} %shard_map.184), channel_id=1, source_target_pairs={{0,3},{1,2},{2,1},{3,0},{4,7},{5,6},{6,5},{7,4},{8,11},{9,10},{10,... | collective-permute-start | bytes 73736 | tf_op jit(solution)/shard_map/ppermute | solution.py:572
  24.0 29.7 %collective-permute-start.4 = (bf16[256,768]{1,0:T(8,128)(2,1)S(1)}, bf16[256,768]{1,0:T(8,128)(2,1)S(1)}, u32[]{:S(2)}, u32[]{:S(2)}) collective-permute-start(bf16[256,768]{1,0:T(8,128)(2,1)S(1)} %get-tuple-element.53), channel_id=1, source_target_pairs={{0,1},{1,0},{2,5},{3,4},{4,3},{5,2},{6,7},{7,6},{8,9},{9,8},{10,13... | collective-permute-start | bytes 1179656 | tf_op jit(solution)/shard_map/ppermute | solution.py:572
  27.4 26.4 %collective-permute-start.5 = (bf16[256,768]{1,0:T(8,128)(2,1)S(1)}, bf16[256,768]{1,0:T(8,128)(2,1)S(1)}, u32[]{:S(2)}, u32[]{:S(2)}) collective-permute-start(bf16[256,768]{1,0:T(8,128)(2,1)S(1)} %get-tuple-element.54), channel_id=1, source_target_pairs={{0,0},{1,1},{2,4},{3,5},{4,2},{5,3},{6,6},{7,7},{8,8},{9,9},{10,12... | collective-permute-start | bytes 1179656 | tf_op jit(solution)/shard_map/ppermute | solution.py:572
  28.1 1.9 %collective-permute-start.13 = (bf16[256,192]{1,0:T(8,128)(2,1)S(1)}, bf16[256,192]{1,0:T(8,128)(2,1)S(1)}, u32[]{:S(2)}, u32[]{:S(2)}) collective-permute-start(bf16[256,192]{1,0:T(8,128)(2,1)S(1)} %constant_dynamic-update-slice_fusion.2.refs_12_), channel_id=1, source_target_pairs={{0,4},{1,5},{2,6},{3,7},{4,0},{5,1},{6,2},{7,3},{8,12},{9,13},{10,... | collective-permute-start | bytes 294920 | tf_op jit(solution)/shard_map/ppermute | solution.py:572
  29.0 1.7 %collective-permute-start.8 = (bf16[256,768]{1,0:T(8,128)(2,1)S(1)}, bf16[256,768]{1,0:T(8,128)(2,1)S(1)}, u32[]{:S(2)}, u32[]{:S(2)}) collective-permute-start(bf16[256,768]{1,0:T(8,128)(2,1)S(1)} %collective-permute-done.6.refs_0_), channel_id=1, source_target_pairs={{0,4},{1,5},{2,6},{3,7},{4,0},{5,1},{6,2},{7,3},{8,12},{9,13},{10,... | collective-permute-start | bytes 1179656 | tf_op jit(solution)/shard_map/ppermute | solution.py:572
  29.1 2.2 %collective-permute-start.9 = (bf16[256,768]{1,0:T(8,128)(2,1)S(1)}, bf16[256,768]{1,0:T(8,128)(2,1)S(1)}, u32[]{:S(2)}, u32[]{:S(2)}) collective-permute-start(bf16[256,768]{1,0:T(8,128)(2,1)S(1)} %collective-permute-done.7.refs_1_), channel_id=1, source_target_pairs={{0,4},{1,5},{2,6},{3,7},{4,0},{5,1},{6,2},{7,3},{8,12},{9,13},{10,... | collective-permute-start | bytes 1179656 | tf_op jit(solution)/shard_map/ppermute | solution.py:572
  52.6 18.9 %collective-permute-start.14 = (bf16[256,768]{1,0:T(8,128)(2,1)S(1)}, bf16[256,768]{1,0:T(8,128)(2,1)S(1)}, u32[]{:S(2)}, u32[]{:S(2)}) collective-permute-start(bf16[256,768]{1,0:T(8,128)(2,1)S(1)} %get-tuple-element.79), channel_id=1, source_target_pairs={{0,1},{1,0},{2,5},{3,4},{4,3},{5,2},{6,7},{7,6},{8,9},{9,8},{10,13... | collective-permute-start | bytes 1179656 | tf_op jit(solution)/shard_map/ppermute | solution.py:572
  52.9 18.6 %collective-permute-start.15 = (bf16[256,768]{1,0:T(8,128)(2,1)S(1)}, bf16[256,768]{1,0:T(8,128)(2,1)S(1)}, u32[]{:S(2)}, u32[]{:S(2)}) collective-permute-start(bf16[256,768]{1,0:T(8,128)(2,1)S(1)} %get-tuple-element.80), channel_id=1, source_target_pairs={{0,0},{1,1},{2,4},{3,5},{4,2},{5,3},{6,6},{7,7},{8,8},{9,9},{10,12... | collective-permute-start | bytes 1179656 | tf_op jit(solution)/shard_map/ppermute | solution.py:572
  71.5 4.5 %collective-permute-start.16 = (bf16[64,768]{1,0:T(8,128)(2,1)S(1)}, bf16[64,768]{1,0:T(8,128)(2,1)S(1)}, u32[]{:S(2)}, u32[]{:S(2)}) collective-permute-start(bf16[64,768]{1,0:T(8,128)(2,1)S(1)} %get-tuple-element.82), channel_id=1, source_target_pairs={{0,4},{1,5},{2,6},{3,7},{4,0},{5,1},{6,2},{7,3},{8,12},{9,13},{10,... | collective-permute-start | bytes 294920 | tf_op jit(solution)/shard_map/ppermute | solution.py:572
  76.0 7.0 %collective-permute-start.19 = (bf16[16,768]{1,0:T(8,128)(2,1)S(1)}, bf16[16,768]{1,0:T(8,128)(2,1)S(1)}, u32[]{:S(2)}, u32[]{:S(2)}) collective-permute-start(bf16[16,768]{1,0:T(8,128)(2,1)S(1)} %get-tuple-element.86), channel_id=1, source_target_pairs={{0,24},{1,25},{2,26},{3,27},{4,28},{5,29},{6,30},{7,31},{8,16},{9,... | collective-permute-start | bytes 73736 | tf_op jit(solution)/shard_map/ppermute | solution.py:572
  81.3 3.8 %collective-permute-start.18 = (bf16[16,768]{1,0:T(8,128)(2,1)S(1)}, bf16[16,768]{1,0:T(8,128)(2,1)S(1)}, u32[]{:S(2)}, u32[]{:S(2)}) collective-permute-start(bf16[16,768]{1,0:T(8,128)(2,1)S(1)} %get-tuple-element.85), channel_id=1, source_target_pairs={{0,16},{1,17},{2,18},{3,19},{4,20},{5,21},{6,22},{7,23},{8,24},{9,... | collective-permute-start | bytes 73736 | tf_op jit(solution)/shard_map/ppermute | solution.py:572
  81.7 20.1 %copy-start.1 = (f32[32,12]{0,1:T(8,128)S(1)}, f32[32,12]{0,1:T(8,128)}, u32[]{:S(2)}) copy-start(f32[32,12]{0,1:T(8,128)} %param.28) | copy-start | bytes 4612
  81.7 19.4 %copy-start.2 = (f32[16,192]{1,0:T(8,128)S(1)}, f32[16,192]{1,0:T(8,128)}, u32[]{:S(2)}) copy-start(f32[16,192]{1,0:T(8,128)} %prompt_ref.1) | copy-start | bytes 36868
  81.7 19.4 %copy-start.3 = (f32[16,192]{1,0:T(8,128)S(1)}, f32[16,192]{1,0:T(8,128)}, u32[]{:S(2)}) copy-start(f32[16,192]{1,0:T(8,128)} %first_ref.1) | copy-start | bytes 36868
  81.7 19.4 %copy-start.4 = (f32[16,192]{1,0:T(8,128)S(1)}, f32[16,192]{1,0:T(8,128)}, u32[]{:S(2)}) copy-start(f32[16,192]{1,0:T(8,128)} %second_ref.1) | copy-start | bytes 36868
  81.7 3.9 %collective-permute-start.17 = (bf16[16,768]{1,0:T(8,128)(2,1)S(1)}, bf16[16,768]{1,0:T(8,128)(2,1)S(1)}, u32[]{:S(2)}, u32[]{:S(2)}) collective-permute-start(bf16[16,768]{1,0:T(8,128)(2,1)S(1)} %get-tuple-element.84), channel_id=1, source_target_pairs={{0,8},{1,9},{2,10},{3,11},{4,12},{5,13},{6,14},{7,15},{8,0},{9,1},... | collective-permute-start | bytes 73736 | tf_op jit(solution)/shard_map/ppermute | solution.py:572
  85.6 5.4 %collective-permute-start.20 = (bf16[16,768]{1,0:T(8,128)(2,1)S(1)}, bf16[16,768]{1,0:T(8,128)(2,1)S(1)}, u32[]{:S(2)}, u32[]{:S(2)}) collective-permute-start(bf16[16,768]{1,0:T(8,128)(2,1)S(1)} %get-tuple-element.98), channel_id=1, source_target_pairs={{0,1},{1,0},{2,3},{3,2},{4,5},{5,4},{6,7},{7,6},{8,9},{9,8},{10,11... | collective-permute-start | bytes 73736 | tf_op jit(solution)/shard_map/ppermute | solution.py:572
  85.7 5.3 %collective-permute-start.21 = (bf16[16,768]{1,0:T(8,128)(2,1)S(1)}, bf16[16,768]{1,0:T(8,128)(2,1)S(1)}, u32[]{:S(2)}, u32[]{:S(2)}) collective-permute-start(bf16[16,768]{1,0:T(8,128)(2,1)S(1)} %get-tuple-element.98), channel_id=1, source_target_pairs={{0,2},{1,3},{2,0},{3,1},{4,6},{5,7},{6,4},{7,5},{8,10},{9,11},{10,... | collective-permute-start | bytes 73736 | tf_op jit(solution)/shard_map/ppermute | solution.py:572
  87.4 5.6 %collective-permute-start.22 = (bf16[16,768]{1,0:T(8,128)(2,1)S(1)}, bf16[16,768]{1,0:T(8,128)(2,1)S(1)}, u32[]{:S(2)}, u32[]{:S(2)}) collective-permute-start(bf16[16,768]{1,0:T(8,128)(2,1)S(1)} %get-tuple-element.98), channel_id=1, source_target_pairs={{0,3},{1,2},{2,1},{3,0},{4,7},{5,6},{6,5},{7,4},{8,11},{9,10},{10,... | collective-permute-start | bytes 73736 | tf_op jit(solution)/shard_map/ppermute | solution.py:572
  93.3 1.2 %collective-permute-start.23 = (f32[8,128]{1,0:T(8,128)S(1)}, f32[8,128]{1,0:T(8,128)S(1)}, u32[]{:S(2)}, u32[]{:S(2)}) collective-permute-start(f32[8,128]{1,0:T(8,128)S(1)} %get-tuple-element.94), channel_id=1, source_target_pairs={{0,4},{1,5},{2,6},{3,7},{4,0},{5,1},{6,2},{7,3},{8,12},{9,13},{10,... | collective-permute-start | bytes 12296 | tf_op jit(solution)/shard_map/ppermute | solution.py:572
  94.5 3.6 %collective-permute-start.24 = (f32[8,128]{1,0:T(8,128)S(1)}, f32[8,128]{1,0:T(8,128)S(1)}, u32[]{:S(2)}, u32[]{:S(2)}) collective-permute-start(f32[8,128]{1,0:T(8,128)S(1)} %add.22.refs_0_), channel_id=1, source_target_pairs={{0,8},{1,9},{2,10},{3,11},{4,12},{5,13},{6,14},{7,15},{8,0},{9,1},... | collective-permute-start | bytes 12296 | tf_op jit(solution)/shard_map/ppermute | solution.py:572
  94.7 3.6 %collective-permute-start.25 = (f32[8,128]{1,0:T(8,128)S(1)}, f32[8,128]{1,0:T(8,128)S(1)}, u32[]{:S(2)}, u32[]{:S(2)}) collective-permute-start(f32[8,128]{1,0:T(8,128)S(1)} %add.22.refs_0_), channel_id=1, source_target_pairs={{0,16},{1,17},{2,18},{3,19},{4,20},{5,21},{6,22},{7,23},{8,24},{9,... | collective-permute-start | bytes 12296 | tf_op jit(solution)/shard_map/ppermute | solution.py:572
  96.6 4.5 %collective-permute-start.26 = (f32[8,128]{1,0:T(8,128)S(1)}, f32[8,128]{1,0:T(8,128)S(1)}, u32[]{:S(2)}, u32[]{:S(2)}) collective-permute-start(f32[8,128]{1,0:T(8,128)S(1)} %add.22.refs_0_), channel_id=1, source_target_pairs={{0,24},{1,25},{2,26},{3,27},{4,28},{5,29},{6,30},{7,31},{8,16},{9,... | collective-permute-start | bytes 12296 | tf_op jit(solution)/shard_map/ppermute | solution.py:572

commit v9 on v8

--- a/solution.py
+++ b/solution.py
@@ -144,8 +144,8 @@
 def prepare_kernel(count, base_ref, gain_first_ref, gain_second_ref, cot_ref, *refs):
     weights, (tile_ref, table_ref, first_ref, second_ref) = refs[:3], refs[3:7]
     pieces, kept, sems = refs[7 : 7 + count], refs[7 + count : 10 + count], refs[10 + count]
-    first_ref[...] = gain_first_ref[...]
-    second_ref[...] = gain_second_ref[...]
+    first_ref[0, :] = gain_first_ref[...]
+    second_ref[0, :] = gain_second_ref[...]
     ctx = lax.axis_index("ctx")
     copies = [pltpu.make_async_copy(weights[n], kept[n], sems.at[n]) for n in range(3)] + [
         pltpu.make_async_copy(cot_ref.at[slot_of(ctx + k + 1, count)], pieces[k], sems.at[3 + k]) for k in range(count)
@@ -261,6 +261,8 @@
         normed = jnp.concatenate([normed_ref[...], norm_ref[0 : half_len + BLK, :]], axis=0)
         kall_ref[:, cols] = dot_nn(normed, wk_ref[:, cols]).astype(bf16)
         vall_ref[:, cols] = dot_nn(normed, wv_ref[:, cols]).astype(bf16)
+    for t in range(width // wide):
+        cols = slice(t * wide, (t + 1) * wide)
         q_ref[:, cols] = dot_nn(norm_ref[half_len + BLK :, :], wq_ref[:, cols]).astype(bf16)
 
     lane = lax.broadcasted_iota(i32, (1, PAIR), 1)
@@ -629,7 +631,7 @@
         scratch_shapes=[pltpu.SemaphoreType.DMA((3 + count,))],
         compiler_params=params(4),
         cost_estimate=cost(1e6, 5e6),
-    )(base, gain_first[None], gain_second[None], in_hbm(cotangent), *[in_hbm(w) for w in weights])
+    )(base, gain_first, gain_second, in_hbm(cotangent), *[in_hbm(w) for w in weights])
     tiles, table, gain_1, gain_2 = prepared[:4]
     cot_pieces = prepared[4 : 4 + count]
     w_q, w_k, w_v = prepared[4 + count :]

time: 102 us -> 102 us (level)
    broadcast_in_dim x2 -> x0, local copies, waits for them, and re-layouts: 1.38 us -> none  [the longest x1 0.69 us: on_device(): gain_first[None]]
    unnamed x14 -> x18, local copies, waits for them, and re-layouts: 0.04 us -> 1.42 us
  transfers between devices with their start and end apart: 27 -> 27, of which waited for: 14 -> 15; matrix products, arithmetic and copies ran while one was open for 3% -> 2% of each run, Pallas kernels for 42% -> 42%
where the time goes in v9:
time: 102 us; the launch traced here: 101 us
  Pallas kernels  44.5 us (44%)
  starting transfers between devices  36.2 us (35%)
  waiting for transfers between devices  16.2 us (16%)
  local copies, waits for them, and re-layouts  1.42 us (1%)
  other arithmetic  1.02 us (1%)
    ppermute x27, starting transfers between devices, permute(): return lax.ppermute(value, AXES, pairs)  36.2 us
    pallas_call x1, Pallas kernels, on_device(): pl.pallas_call(functools.partial(forward_kernel, count, piece, rows_own),...  21.2 us
    pallas_call x1, Pallas kernels, on_device(): pl.pallas_call(functools.partial(backward_kernel, count, piece, rows_own)...  17.7 us
    ppermute x27, waiting for transfers between devices, permute(): return lax.ppermute(value, AXES, pairs)  16.2 us
    pallas_call x1, Pallas kernels, on_device(): pl.pallas_call(functools.partial(prepare_kernel, count), out_shape=[held(...  3.03 us
  transfers between devices with their start and end apart: 27, of which 15 were waited for; matrix products, arithmetic and copies ran while one was open for 2% of the time, Pallas kernels for 42%

profile of v9, /device:TPU:0, one launch (start us, length us, event | category | flops | bytes accessed | tf_op | source)
XLA Modules:
  0.0 101.2 jit_solution(10657990036232812771)
XLA Ops:
  0.6 1.2 %shard_map.183 = (bf16[256,768]{1,0:T(8,128)(2,1)S(1)}, bf16[256,768]{1,0:T(8,128)(2,1)S(1)}, bf16[24,192]{1,0:T(8,128)(2,1)S(1)}) custom-call(bf16[2,256,768]{2,1,0:T(8,128)(2,1)} %tokens_ref.1, s32[2,256]{1,0:T(2,128)} %seg_hbm.1, f32[16,192]{1,0:T(8,128)} %prompt_ref.1), custom_call_target="tpu_custom_call" | custom-call | flops 100000 | bytes 2000000 | tf_op jit(solution)/shard_map/pallas_call | solution.py:587
  1.8 0.5 collective-permute-start
  2.4 2.6 %collective-permute-start.6 = (bf16[256,768]{1,0:T(8,128)(2,1)S(1)}, bf16[256,768]{1,0:T(8,128)(2,1)S(1)}, u32[]{:S(2)}, u32[]{:S(2)}) collective-permute-start(bf16[256,768]{1,0:T(8,128)(2,1)S(1)} %get-tuple-element.55), channel_id=1, source_target_pairs={{0,1},{1,0},{2,5},{3,4},{4,3},{5,2},{6,7},{7,6},{8,9},{9,8},{10,13... | collective-permute-start | bytes 1179656 | tf_op jit(solution)/shard_map/ppermute | solution.py:574
  5.0 0.7 collective-permute-start.7
  5.7 1.6 %collective-permute-start.1 = (bf16[48,192]{1,0:T(8,128)(2,1)S(1)}, bf16[48,192]{1,0:T(8,128)(2,1)S(1)}, u32[]{:S(2)}, u32[]{:S(2)}) collective-permute-start(bf16[48,192]{1,0:T(8,128)(2,1)S(1)} %constant_dynamic-update-slice_fusion.refs_0_), channel_id=1, source_target_pairs={{0,8},{1,9},{2,10},{3,11},{4,12},{5,13},{6,14},{7,15},{8,0},{9,1},... | collective-permute-start | bytes 55304 | tf_op jit(solution)/shard_map/ppermute | solution.py:574
  7.3 1.5 %collective-permute-start.2 = (bf16[48,192]{1,0:T(8,128)(2,1)S(1)}, bf16[48,192]{1,0:T(8,128)(2,1)S(1)}, u32[]{:S(2)}, u32[]{:S(2)}) collective-permute-start(bf16[48,192]{1,0:T(8,128)(2,1)S(1)} %constant_dynamic-update-slice_fusion.refs_0_), channel_id=1, source_target_pairs={{0,16},{1,17},{2,18},{3,19},{4,20},{5,21},{6,22},{7,23},{8,24},{9,... | collective-permute-start | bytes 55304 | tf_op jit(solution)/shard_map/ppermute | solution.py:574
  8.8 0.5 collective-permute-start.3
  9.3 1.0 convolution_bitcast_fusion.base_ref
  10.3 0.8 collective-permute-done.2.refs_2_
  11.1 2.4 %collective-permute-done.3.refs_3_ = bf16[48,192]{1,0:T(8,128)(2,1)S(1)} collective-permute-done((bf16[48,192]{1,0:T(8,128)(2,1)S(1)}, bf16[48,192]{1,0:T(8,128)(2,1)S(1)}, u32[]{:S(2)}, u32[]{:S(2)}) %collective-permute-start.3) | collective-permute-done | bytes 18464 | tf_op jit(solution)/shard_map/ppermute | solution.py:574
  13.6 0.7 collective-permute-start.10
  14.3 5.3 %collective-permute-start.11 = (bf16[64,192]{1,0:T(8,128)(2,1)S(1)}, bf16[64,192]{1,0:T(8,128)(2,1)S(1)}, u32[]{:S(2)}, u32[]{:S(2)}) collective-permute-start(bf16[64,192]{1,0:T(8,128)(2,1)S(1)} %shard_map.184), channel_id=1, source_target_pairs={{0,2},{1,3},{2,0},{3,1},{4,6},{5,7},{6,4},{7,5},{8,10},{9,11},{10,... | collective-permute-start | bytes 73736 | tf_op jit(solution)/shard_map/ppermute | solution.py:574
  19.6 1.4 %collective-permute-start.12 = (bf16[64,192]{1,0:T(8,128)(2,1)S(1)}, bf16[64,192]{1,0:T(8,128)(2,1)S(1)}, u32[]{:S(2)}, u32[]{:S(2)}) collective-permute-start(bf16[64,192]{1,0:T(8,128)(2,1)S(1)} %shard_map.184), channel_id=1, source_target_pairs={{0,3},{1,2},{2,1},{3,0},{4,7},{5,6},{6,5},{7,4},{8,11},{9,10},{10,... | collective-permute-start | bytes 73736 | tf_op jit(solution)/shard_map/ppermute | solution.py:574
  21.0 0.7 copy-done.5
  21.7 0.7 copy-done.6
  22.4 3.0 %shard_map.185 = (f32[12,3,128,128]{3,2,1,0:T(8,128)S(1)}, bf16[1536,512]{1,0:T(8,128)(2,1)S(1)}, f32[1,768]{1,0:T(1,128)S(1)}, f32[1,768]{1,0:T(1,128)S(1)}, bf...) custom-call(f32[12,512]{1,0:T(8,128)S(1)} %convolution_bitcast_fusio, ...), custom_call_target="tpu_custom_call" | custom-call | flops 1000000 | bytes 5000000 | tf_op jit(solution)/shard_map/pallas_call | solution.py:623
  25.4 0.6 collective-permute-start.4
  26.1 1.3 %collective-permute-done.11 = bf16[64,192]{1,0:T(8,128)(2,1)S(1)} collective-permute-done((bf16[64,192]{1,0:T(8,128)(2,1)S(1)}, bf16[64,192]{1,0:T(8,128)(2,1)S(1)}, u32[]{:S(2)}, u32[]{:S(2)}) %collective-permute-start.11) | collective-permute-done | bytes 24608 | tf_op jit(solution)/shard_map/ppermute | solution.py:574
  27.4 0.7 collective-permute-start.5
  28.1 2.0 %collective-permute-start.13 = (bf16[256,192]{1,0:T(8,128)(2,1)S(1)}, bf16[256,192]{1,0:T(8,128)(2,1)S(1)}, u32[]{:S(2)}, u32[]{:S(2)}) collective-permute-start(bf16[256,192]{1,0:T(8,128)(2,1)S(1)} %constant_dynamic-update-slice_fusion.2.refs_12_), channel_id=1, source_target_pairs={{0,4},{1,5},{2,6},{3,7},{4,0},{5,1},{6,2},{7,3},{8,12},{9,13},{10,... | collective-permute-start | bytes 294920 | tf_op jit(solution)/shard_map/ppermute | solution.py:574
  30.2 0.4 collective-permute-start.9
  30.6 0.3 shard_map.186.refs_4_
  30.9 0.1 collective-permute-done.13.refs_13_
  31.1 0.7 collective-permute-done.8.refs_2_
  31.8 0.6 collective-permute-done.9.refs_3_
  32.4 21.2 %shard_map.187 = (bf16[6,2,1152,512]{3,2,1,0:T(8,128)(2,1)}, s32[8,128]{1,0:T(8,128)S(1)}, bf16[128,768]{1,0:T(8,128)(2,1)S(1)}, bf16[512,768]{1,0:T(8,128)(2,1)...) custom-call(bf16[256,768]{1,0:T(8,128)(2,1)S(1)} %collective-permute, ...), custom_call_target="tpu_custom_call" | custom-call | flops 30000001024 | bytes 40000000 | tf_op jit(solution)/shard_map/pallas_call | solution.py:652
  53.6 0.7 collective-permute-start.14
  54.2 0.9 collective-permute-start.15
  55.1 17.7 %shard_map.188 = (f32[64,768]{1,0:T(8,128)S(1)}, bf16[64,768]{1,0:T(8,128)(2,1)S(1)}) custom-call(bf16[256,768]{1,0:T(8,128)(2,1)S(1)} %collective-permute-done.4.refs_0_, bf16[256,768]{1,0:T(8,128)(2,1)S(1)} %collective-permute-done.5.refs_1_, s32[8,128]{1,0:T(8,128)S(1)} %get-tuple-element.65.refs_2_, bf16[3072,512]{1,0:T(8,128)(2,1)S(1)} %get-tuple-element.66.refs_3_, ...), custom_call_target="tpu_custom_call" | custom-call | flops 30000001024 | bytes 40000000 | tf_op jit(solution)/shard_map/pallas_call | solution.py:692
  72.8 3.5 %collective-permute-start.16 = (bf16[64,768]{1,0:T(8,128)(2,1)S(1)}, bf16[64,768]{1,0:T(8,128)(2,1)S(1)}, u32[]{:S(2)}, u32[]{:S(2)}) collective-permute-start(bf16[64,768]{1,0:T(8,128)(2,1)S(1)} %get-tuple-element.82), channel_id=1, source_target_pairs={{0,4},{1,5},{2,6},{3,7},{4,0},{5,1},{6,2},{7,3},{8,12},{9,13},{10,... | collective-permute-start | bytes 294920 | tf_op jit(solution)/shard_map/ppermute | solution.py:574
  76.4 0.9 collective-permute-done.16.came_ref
  77.3 3.8 %collective-permute-start.19 = (bf16[16,768]{1,0:T(8,128)(2,1)S(1)}, bf16[16,768]{1,0:T(8,128)(2,1)S(1)}, u32[]{:S(2)}, u32[]{:S(2)}) collective-permute-start(bf16[16,768]{1,0:T(8,128)(2,1)S(1)} %get-tuple-element.86), channel_id=1, source_target_pairs={{0,24},{1,25},{2,26},{3,27},{4,28},{5,29},{6,30},{7,31},{8,16},{9,... | collective-permute-start | bytes 73736 | tf_op jit(solution)/shard_map/ppermute | solution.py:574
  81.2 0.7 collective-permute-start.17
  81.9 1.0 %collective-permute-done.19 = bf16[16,768]{1,0:T(8,128)(2,1)S(1)} collective-permute-done((bf16[16,768]{1,0:T(8,128)(2,1)S(1)}, bf16[16,768]{1,0:T(8,128)(2,1)S(1)}, u32[]{:S(2)}, u32[]{:S(2)}) %collective-permute-start.19) | collective-permute-done | bytes 24608 | tf_op jit(solution)/shard_map/ppermute | solution.py:574
  82.9 2.0 %collective-permute-done.18 = bf16[16,768]{1,0:T(8,128)(2,1)S(1)} collective-permute-done((bf16[16,768]{1,0:T(8,128)(2,1)S(1)}, bf16[16,768]{1,0:T(8,128)(2,1)S(1)}, u32[]{:S(2)}, u32[]{:S(2)}) %collective-permute-start.18) | collective-permute-done | bytes 24608 | tf_op jit(solution)/shard_map/ppermute | solution.py:574
  85.2 1.7 %collective-permute-start.21 = (bf16[16,768]{1,0:T(8,128)(2,1)S(1)}, bf16[16,768]{1,0:T(8,128)(2,1)S(1)}, u32[]{:S(2)}, u32[]{:S(2)}) collective-permute-start(bf16[16,768]{1,0:T(8,128)(2,1)S(1)} %get-tuple-element.98), channel_id=1, source_target_pairs={{0,2},{1,3},{2,0},{3,1},{4,6},{5,7},{6,4},{7,5},{8,10},{9,11},{10,... | collective-permute-start | bytes 73736 | tf_op jit(solution)/shard_map/ppermute | solution.py:574
  86.9 2.7 %collective-permute-start.22 = (bf16[16,768]{1,0:T(8,128)(2,1)S(1)}, bf16[16,768]{1,0:T(8,128)(2,1)S(1)}, u32[]{:S(2)}, u32[]{:S(2)}) collective-permute-start(bf16[16,768]{1,0:T(8,128)(2,1)S(1)} %get-tuple-element.98), channel_id=1, source_target_pairs={{0,3},{1,2},{2,1},{3,0},{4,7},{5,6},{6,5},{7,4},{8,11},{9,10},{10,... | collective-permute-start | bytes 73736 | tf_op jit(solution)/shard_map/ppermute | solution.py:574
  89.5 0.9 pad_maximum_fusion
  90.5 2.0 %collective-permute-done.22.refs_2_ = bf16[16,768]{1,0:T(8,128)(2,1)S(1)} collective-permute-done((bf16[16,768]{1,0:T(8,128)(2,1)S(1)}, bf16[16,768]{1,0:T(8,128)(2,1)S(1)}, u32[]{:S(2)}, u32[]{:S(2)}) %collective-permute-start.22) | collective-permute-done | bytes 24608 | tf_op jit(solution)/shard_map/ppermute | solution.py:574
  92.5 0.3 shard_map.190
  92.8 1.2 %collective-permute-done.23 = f32[8,128]{1,0:T(8,128)S(1)} collective-permute-done((f32[8,128]{1,0:T(8,128)S(1)}, f32[8,128]{1,0:T(8,128)S(1)}, u32[]{:S(2)}, u32[]{:S(2)}) %collective-permute-start.23) | collective-permute-done | bytes 4128 | tf_op jit(solution)/shard_map/ppermute | solution.py:574
  94.0 1.5 %collective-permute-start.24 = (f32[8,128]{1,0:T(8,128)S(1)}, f32[8,128]{1,0:T(8,128)S(1)}, u32[]{:S(2)}, u32[]{:S(2)}) collective-permute-start(f32[8,128]{1,0:T(8,128)S(1)} %add.22.refs_0_), channel_id=1, source_target_pairs={{0,8},{1,9},{2,10},{3,11},{4,12},{5,13},{6,14},{7,15},{8,0},{9,1},... | collective-permute-start | bytes 12296 | tf_op jit(solution)/shard_map/ppermute | solution.py:574
  95.4 0.6 collective-permute-start.25
  96.0 1.5 %collective-permute-start.26 = (f32[8,128]{1,0:T(8,128)S(1)}, f32[8,128]{1,0:T(8,128)S(1)}, u32[]{:S(2)}, u32[]{:S(2)}) collective-permute-start(f32[8,128]{1,0:T(8,128)S(1)} %add.22.refs_0_), channel_id=1, source_target_pairs={{0,24},{1,25},{2,26},{3,27},{4,28},{5,29},{6,30},{7,31},{8,16},{9,... | collective-permute-start | bytes 12296 | tf_op jit(solution)/shard_map/ppermute | solution.py:574
  97.4 0.1 collective-permute-done.24.refs_1_
  97.6 1.5 %collective-permute-done.25.refs_2_ = f32[8,128]{1,0:T(8,128)S(1)} collective-permute-done((f32[8,128]{1,0:T(8,128)S(1)}, f32[8,128]{1,0:T(8,128)S(1)}, u32[]{:S(2)}, u32[]{:S(2)}) %collective-permute-start.25) | collective-permute-done | bytes 4128 | tf_op jit(solution)/shard_map/ppermute | solution.py:574
  99.0 1.5 %collective-permute-done.26.refs_3_ = f32[8,128]{1,0:T(8,128)S(1)} collective-permute-done((f32[8,128]{1,0:T(8,128)S(1)}, f32[8,128]{1,0:T(8,128)S(1)}, u32[]{:S(2)}, u32[]{:S(2)}) %collective-permute-start.26) | collective-permute-done | bytes 4128 | tf_op jit(solution)/shard_map/ppermute | solution.py:574
  100.5 0.7 shard_map.191
  (40 shorter events, 0.5 us)
Async XLA Ops:
  0.6 8.7 %copy-start = (f32[32,12]{0,1:T(8,128)S(1)}, f32[32,12]{0,1:T(8,128)}, u32[]{:S(2)}) copy-start(f32[32,12]{0,1:T(8,128)} %param.28) | copy-start | bytes 4612
  1.8 3.9 %collective-permute-start = (bf16[24,192]{1,0:T(8,128)(2,1)S(1)}, bf16[24,192]{1,0:T(8,128)(2,1)S(1)}, u32[]{:S(2)}, u32[]{:S(2)}) collective-permute-start(bf16[24,192]{1,0:T(8,128)(2,1)S(1)} %get-tuple-element.51), channel_id=1, source_target_pairs={{0,4},{1,5},{2,6},{3,7},{4,0},{5,1},{6,2},{7,3},{8,12},{9,13},{10,... | collective-permute-start | bytes 27656 | tf_op jit(solution)/shard_map/ppermute | solution.py:574
  2.4 27.7 %collective-permute-start.6 = (bf16[256,768]{1,0:T(8,128)(2,1)S(1)}, bf16[256,768]{1,0:T(8,128)(2,1)S(1)}, u32[]{:S(2)}, u32[]{:S(2)}) collective-permute-start(bf16[256,768]{1,0:T(8,128)(2,1)S(1)} %get-tuple-element.55), channel_id=1, source_target_pairs={{0,1},{1,0},{2,5},{3,4},{4,3},{5,2},{6,7},{7,6},{8,9},{9,8},{10,13... | collective-permute-start | bytes 1179656 | tf_op jit(solution)/shard_map/ppermute | solution.py:574
  5.0 25.1 %collective-permute-start.7 = (bf16[256,768]{1,0:T(8,128)(2,1)S(1)}, bf16[256,768]{1,0:T(8,128)(2,1)S(1)}, u32[]{:S(2)}, u32[]{:S(2)}) collective-permute-start(bf16[256,768]{1,0:T(8,128)(2,1)S(1)} %get-tuple-element.56), channel_id=1, source_target_pairs={{0,0},{1,1},{2,4},{3,5},{4,2},{5,3},{6,6},{7,7},{8,8},{9,9},{10,12... | collective-permute-start | bytes 1179656 | tf_op jit(solution)/shard_map/ppermute | solution.py:574
  5.7 4.6 %collective-permute-start.1 = (bf16[48,192]{1,0:T(8,128)(2,1)S(1)}, bf16[48,192]{1,0:T(8,128)(2,1)S(1)}, u32[]{:S(2)}, u32[]{:S(2)}) collective-permute-start(bf16[48,192]{1,0:T(8,128)(2,1)S(1)} %constant_dynamic-update-slice_fusion.refs_0_), channel_id=1, source_target_pairs={{0,8},{1,9},{2,10},{3,11},{4,12},{5,13},{6,14},{7,15},{8,0},{9,1},... | collective-permute-start | bytes 55304 | tf_op jit(solution)/shard_map/ppermute | solution.py:574
  7.3 3.8 %collective-permute-start.2 = (bf16[48,192]{1,0:T(8,128)(2,1)S(1)}, bf16[48,192]{1,0:T(8,128)(2,1)S(1)}, u32[]{:S(2)}, u32[]{:S(2)}) collective-permute-start(bf16[48,192]{1,0:T(8,128)(2,1)S(1)} %constant_dynamic-update-slice_fusion.refs_0_), channel_id=1, source_target_pairs={{0,16},{1,17},{2,18},{3,19},{4,20},{5,21},{6,22},{7,23},{8,24},{9,... | collective-permute-start | bytes 55304 | tf_op jit(solution)/shard_map/ppermute | solution.py:574
  8.8 4.7 %collective-permute-start.3 = (bf16[48,192]{1,0:T(8,128)(2,1)S(1)}, bf16[48,192]{1,0:T(8,128)(2,1)S(1)}, u32[]{:S(2)}, u32[]{:S(2)}) collective-permute-start(bf16[48,192]{1,0:T(8,128)(2,1)S(1)} %constant_dynamic-update-slice_fusion.refs_0_), channel_id=1, source_target_pairs={{0,24},{1,25},{2,26},{3,27},{4,28},{5,29},{6,30},{7,31},{8,16},{9,... | collective-permute-start | bytes 55304 | tf_op jit(solution)/shard_map/ppermute | solution.py:574
  13.6 11.8 %collective-permute-start.10 = (bf16[64,192]{1,0:T(8,128)(2,1)S(1)}, bf16[64,192]{1,0:T(8,128)(2,1)S(1)}, u32[]{:S(2)}, u32[]{:S(2)}) collective-permute-start(bf16[64,192]{1,0:T(8,128)(2,1)S(1)} %shard_map.184), channel_id=1, source_target_pairs={{0,1},{1,0},{2,3},{3,2},{4,5},{5,4},{6,7},{7,6},{8,9},{9,8},{10,11... | collective-permute-start | bytes 73736 | tf_op jit(solution)/shard_map/ppermute | solution.py:574
  14.3 13.1 %collective-permute-start.11 = (bf16[64,192]{1,0:T(8,128)(2,1)S(1)}, bf16[64,192]{1,0:T(8,128)(2,1)S(1)}, u32[]{:S(2)}, u32[]{:S(2)}) collective-permute-start(bf16[64,192]{1,0:T(8,128)(2,1)S(1)} %shard_map.184), channel_id=1, source_target_pairs={{0,2},{1,3},{2,0},{3,1},{4,6},{5,7},{6,4},{7,5},{8,10},{9,11},{10,... | collective-permute-start | bytes 73736 | tf_op jit(solution)/shard_map/ppermute | solution.py:574
  19.6 8.4 %collective-permute-start.12 = (bf16[64,192]{1,0:T(8,128)(2,1)S(1)}, bf16[64,192]{1,0:T(8,128)(2,1)S(1)}, u32[]{:S(2)}, u32[]{:S(2)}) collective-permute-start(bf16[64,192]{1,0:T(8,128)(2,1)S(1)} %shard_map.184), channel_id=1, source_target_pairs={{0,3},{1,2},{2,1},{3,0},{4,7},{5,6},{6,5},{7,4},{8,11},{9,10},{10,... | collective-permute-start | bytes 73736 | tf_op jit(solution)/shard_map/ppermute | solution.py:574
  21.0 0.7 copy-start.5
  21.7 0.7 copy-start.6
  25.4 29.7 %collective-permute-start.4 = (bf16[256,768]{1,0:T(8,128)(2,1)S(1)}, bf16[256,768]{1,0:T(8,128)(2,1)S(1)}, u32[]{:S(2)}, u32[]{:S(2)}) collective-permute-start(bf16[256,768]{1,0:T(8,128)(2,1)S(1)} %get-tuple-element.53), channel_id=1, source_target_pairs={{0,1},{1,0},{2,5},{3,4},{4,3},{5,2},{6,7},{7,6},{8,9},{9,8},{10,13... | collective-permute-start | bytes 1179656 | tf_op jit(solution)/shard_map/ppermute | solution.py:574
  27.4 27.7 %collective-permute-start.5 = (bf16[256,768]{1,0:T(8,128)(2,1)S(1)}, bf16[256,768]{1,0:T(8,128)(2,1)S(1)}, u32[]{:S(2)}, u32[]{:S(2)}) collective-permute-start(bf16[256,768]{1,0:T(8,128)(2,1)S(1)} %get-tuple-element.54), channel_id=1, source_target_pairs={{0,0},{1,1},{2,4},{3,5},{4,2},{5,3},{6,6},{7,7},{8,8},{9,9},{10,12... | collective-permute-start | bytes 1179656 | tf_op jit(solution)/shard_map/ppermute | solution.py:574
  28.1 3.0 %collective-permute-start.13 = (bf16[256,192]{1,0:T(8,128)(2,1)S(1)}, bf16[256,192]{1,0:T(8,128)(2,1)S(1)}, u32[]{:S(2)}, u32[]{:S(2)}) collective-permute-start(bf16[256,192]{1,0:T(8,128)(2,1)S(1)} %constant_dynamic-update-slice_fusion.2.refs_12_), channel_id=1, source_target_pairs={{0,4},{1,5},{2,6},{3,7},{4,0},{5,1},{6,2},{7,3},{8,12},{9,13},{10,... | collective-permute-start | bytes 294920 | tf_op jit(solution)/shard_map/ppermute | solution.py:574
  30.1 1.7 %collective-permute-start.8 = (bf16[256,768]{1,0:T(8,128)(2,1)S(1)}, bf16[256,768]{1,0:T(8,128)(2,1)S(1)}, u32[]{:S(2)}, u32[]{:S(2)}) collective-permute-start(bf16[256,768]{1,0:T(8,128)(2,1)S(1)} %collective-permute-done.6.refs_0_), channel_id=1, source_target_pairs={{0,4},{1,5},{2,6},{3,7},{4,0},{5,1},{6,2},{7,3},{8,12},{9,13},{10,... | collective-permute-start | bytes 1179656 | tf_op jit(solution)/shard_map/ppermute | solution.py:574
  30.2 2.2 %collective-permute-start.9 = (bf16[256,768]{1,0:T(8,128)(2,1)S(1)}, bf16[256,768]{1,0:T(8,128)(2,1)S(1)}, u32[]{:S(2)}, u32[]{:S(2)}) collective-permute-start(bf16[256,768]{1,0:T(8,128)(2,1)S(1)} %collective-permute-done.7.refs_1_), channel_id=1, source_target_pairs={{0,4},{1,5},{2,6},{3,7},{4,0},{5,1},{6,2},{7,3},{8,12},{9,13},{10,... | collective-permute-start | bytes 1179656 | tf_op jit(solution)/shard_map/ppermute | solution.py:574
  53.6 19.2 %collective-permute-start.14 = (bf16[256,768]{1,0:T(8,128)(2,1)S(1)}, bf16[256,768]{1,0:T(8,128)(2,1)S(1)}, u32[]{:S(2)}, u32[]{:S(2)}) collective-permute-start(bf16[256,768]{1,0:T(8,128)(2,1)S(1)} %get-tuple-element.79), channel_id=1, source_target_pairs={{0,1},{1,0},{2,5},{3,4},{4,3},{5,2},{6,7},{7,6},{8,9},{9,8},{10,13... | collective-permute-start | bytes 1179656 | tf_op jit(solution)/shard_map/ppermute | solution.py:574
  54.2 18.6 %collective-permute-start.15 = (bf16[256,768]{1,0:T(8,128)(2,1)S(1)}, bf16[256,768]{1,0:T(8,128)(2,1)S(1)}, u32[]{:S(2)}, u32[]{:S(2)}) collective-permute-start(bf16[256,768]{1,0:T(8,128)(2,1)S(1)} %get-tuple-element.80), channel_id=1, source_target_pairs={{0,0},{1,1},{2,4},{3,5},{4,2},{5,3},{6,6},{7,7},{8,8},{9,9},{10,12... | collective-permute-start | bytes 1179656 | tf_op jit(solution)/shard_map/ppermute | solution.py:574
  72.8 4.5 %collective-permute-start.16 = (bf16[64,768]{1,0:T(8,128)(2,1)S(1)}, bf16[64,768]{1,0:T(8,128)(2,1)S(1)}, u32[]{:S(2)}, u32[]{:S(2)}) collective-permute-start(bf16[64,768]{1,0:T(8,128)(2,1)S(1)} %get-tuple-element.82), channel_id=1, source_target_pairs={{0,4},{1,5},{2,6},{3,7},{4,0},{5,1},{6,2},{7,3},{8,12},{9,13},{10,... | collective-permute-start | bytes 294920 | tf_op jit(solution)/shard_map/ppermute | solution.py:574
  77.3 5.6 %collective-permute-start.19 = (bf16[16,768]{1,0:T(8,128)(2,1)S(1)}, bf16[16,768]{1,0:T(8,128)(2,1)S(1)}, u32[]{:S(2)}, u32[]{:S(2)}) collective-permute-start(bf16[16,768]{1,0:T(8,128)(2,1)S(1)} %get-tuple-element.86), channel_id=1, source_target_pairs={{0,24},{1,25},{2,26},{3,27},{4,28},{5,29},{6,30},{7,31},{8,16},{9,... | collective-permute-start | bytes 73736 | tf_op jit(solution)/shard_map/ppermute | solution.py:574
  81.1 3.8 %collective-permute-start.18 = (bf16[16,768]{1,0:T(8,128)(2,1)S(1)}, bf16[16,768]{1,0:T(8,128)(2,1)S(1)}, u32[]{:S(2)}, u32[]{:S(2)}) collective-permute-start(bf16[16,768]{1,0:T(8,128)(2,1)S(1)} %get-tuple-element.85), channel_id=1, source_target_pairs={{0,16},{1,17},{2,18},{3,19},{4,20},{5,21},{6,22},{7,23},{8,24},{9,... | collective-permute-start | bytes 73736 | tf_op jit(solution)/shard_map/ppermute | solution.py:574
  81.1 20.0 %copy-start.1 = (f32[32,12]{0,1:T(8,128)S(1)}, f32[32,12]{0,1:T(8,128)}, u32[]{:S(2)}) copy-start(f32[32,12]{0,1:T(8,128)} %param.28) | copy-start | bytes 4612
  81.2 19.3 %copy-start.2 = (f32[16,192]{1,0:T(8,128)S(1)}, f32[16,192]{1,0:T(8,128)}, u32[]{:S(2)}) copy-start(f32[16,192]{1,0:T(8,128)} %prompt_ref.1) | copy-start | bytes 36868
  81.2 19.3 %copy-start.3 = (f32[16,192]{1,0:T(8,128)S(1)}, f32[16,192]{1,0:T(8,128)}, u32[]{:S(2)}) copy-start(f32[16,192]{1,0:T(8,128)} %first_ref.1) | copy-start | bytes 36868
  81.2 19.3 %copy-start.4 = (f32[16,192]{1,0:T(8,128)S(1)}, f32[16,192]{1,0:T(8,128)}, u32[]{:S(2)}) copy-start(f32[16,192]{1,0:T(8,128)} %second_ref.1) | copy-start | bytes 36868
  81.2 3.9 %collective-permute-start.17 = (bf16[16,768]{1,0:T(8,128)(2,1)S(1)}, bf16[16,768]{1,0:T(8,128)(2,1)S(1)}, u32[]{:S(2)}, u32[]{:S(2)}) collective-permute-start(bf16[16,768]{1,0:T(8,128)(2,1)S(1)} %get-tuple-element.84), channel_id=1, source_target_pairs={{0,8},{1,9},{2,10},{3,11},{4,12},{5,13},{6,14},{7,15},{8,0},{9,1},... | collective-permute-start | bytes 73736 | tf_op jit(solution)/shard_map/ppermute | solution.py:574
  85.1 5.4 %collective-permute-start.20 = (bf16[16,768]{1,0:T(8,128)(2,1)S(1)}, bf16[16,768]{1,0:T(8,128)(2,1)S(1)}, u32[]{:S(2)}, u32[]{:S(2)}) collective-permute-start(bf16[16,768]{1,0:T(8,128)(2,1)S(1)} %get-tuple-element.98), channel_id=1, source_target_pairs={{0,1},{1,0},{2,3},{3,2},{4,5},{5,4},{6,7},{7,6},{8,9},{9,8},{10,11... | collective-permute-start | bytes 73736 | tf_op jit(solution)/shard_map/ppermute | solution.py:574
  85.2 5.3 %collective-permute-start.21 = (bf16[16,768]{1,0:T(8,128)(2,1)S(1)}, bf16[16,768]{1,0:T(8,128)(2,1)S(1)}, u32[]{:S(2)}, u32[]{:S(2)}) collective-permute-start(bf16[16,768]{1,0:T(8,128)(2,1)S(1)} %get-tuple-element.98), channel_id=1, source_target_pairs={{0,2},{1,3},{2,0},{3,1},{4,6},{5,7},{6,4},{7,5},{8,10},{9,11},{10,... | collective-permute-start | bytes 73736 | tf_op jit(solution)/shard_map/ppermute | solution.py:574
  86.9 5.6 %collective-permute-start.22 = (bf16[16,768]{1,0:T(8,128)(2,1)S(1)}, bf16[16,768]{1,0:T(8,128)(2,1)S(1)}, u32[]{:S(2)}, u32[]{:S(2)}) collective-permute-start(bf16[16,768]{1,0:T(8,128)(2,1)S(1)} %get-tuple-element.98), channel_id=1, source_target_pairs={{0,3},{1,2},{2,1},{3,0},{4,7},{5,6},{6,5},{7,4},{8,11},{9,10},{10,... | collective-permute-start | bytes 73736 | tf_op jit(solution)/shard_map/ppermute | solution.py:574
  92.7 1.2 %collective-permute-start.23 = (f32[8,128]{1,0:T(8,128)S(1)}, f32[8,128]{1,0:T(8,128)S(1)}, u32[]{:S(2)}, u32[]{:S(2)}) collective-permute-start(f32[8,128]{1,0:T(8,128)S(1)} %get-tuple-element.94), channel_id=1, source_target_pairs={{0,4},{1,5},{2,6},{3,7},{4,0},{5,1},{6,2},{7,3},{8,12},{9,13},{10,... | collective-permute-start | bytes 12296 | tf_op jit(solution)/shard_map/ppermute | solution.py:574
  94.0 3.6 %collective-permute-start.24 = (f32[8,128]{1,0:T(8,128)S(1)}, f32[8,128]{1,0:T(8,128)S(1)}, u32[]{:S(2)}, u32[]{:S(2)}) collective-permute-start(f32[8,128]{1,0:T(8,128)S(1)} %add.22.refs_0_), channel_id=1, source_target_pairs={{0,8},{1,9},{2,10},{3,11},{4,12},{5,13},{6,14},{7,15},{8,0},{9,1},... | collective-permute-start | bytes 12296 | tf_op jit(solution)/shard_map/ppermute | solution.py:574
  95.4 3.6 %collective-permute-start.25 = (f32[8,128]{1,0:T(8,128)S(1)}, f32[8,128]{1,0:T(8,128)S(1)}, u32[]{:S(2)}, u32[]{:S(2)}) collective-permute-start(f32[8,128]{1,0:T(8,128)S(1)} %add.22.refs_0_), channel_id=1, source_target_pairs={{0,16},{1,17},{2,18},{3,19},{4,20},{5,21},{6,22},{7,23},{8,24},{9,... | collective-permute-start | bytes 12296 | tf_op jit(solution)/shard_map/ppermute | solution.py:574
  96.0 4.5 %collective-permute-start.26 = (f32[8,128]{1,0:T(8,128)S(1)}, f32[8,128]{1,0:T(8,128)S(1)}, u32[]{:S(2)}, u32[]{:S(2)}) collective-permute-start(f32[8,128]{1,0:T(8,128)S(1)} %add.22.refs_0_), channel_id=1, source_target_pairs={{0,24},{1,25},{2,26},{3,27},{4,28},{5,29},{6,30},{7,31},{8,16},{9,... | collective-permute-start | bytes 12296 | tf_op jit(solution)/shard_map/ppermute | solution.py:574
